TPU v7x, 32 devices: a whole 2x2x4 slice. The times are simulated.
32 devices in a mesh: wide: 2 (over core), tensor: 4 (over y, x), expert: 4 (over z).
Axes of the slice: x: 2, y: 2, z: 4, core: 2. Of those that a mesh axis runs over, the one named last changes fastest.
Arguments:
- tokens: bfloat16 [512, 6144], P('expert', 'wide'), may hold values from -6 to 6
- expert_ids: int32 [512, 2], P('expert'), may hold values from 0 to 3, all different within a row; in each aligned block of 128 rows (0 to 127, 128 to 255, ...) at most 96 rows name the same one
- gate_values: float32 [512, 2], P('expert'), may hold values from 0.1 to 1
- w_gate: bfloat16 [4, 6144, 8192], P('expert', 'wide', 'tensor'), may hold values from -0.078125 to 0.078125
- w_up: bfloat16 [4, 6144, 8192], P('expert', 'wide', 'tensor'), may hold values from -0.078125 to 0.078125
- w_down: bfloat16 [4, 8192, 6144], P('expert', 'tensor', 'wide'), may hold values from -0.0625 to 0.0625
- cotangent: bfloat16 [512, 6144], P('expert', 'wide'), may hold values from -6 to 6
Outputs:
- layer_out: bfloat16 [512, 6144], P('expert', 'wide')
- token_grad: bfloat16 [512, 6144], P('expert', 'wide')
- gate_grad: float32 [512, 2], P('expert')
Inputs may be any that keep to these rules, and one draw needn't show every extreme that they name: `expert_ids`: in each block of 128 rows no expert is named by more than 96 rows, a bound that some block reaches; the two experts of a row differ.
All inputs are finite; a program needn't handle non-finite values.
Results may differ from a plain program's by a relative error of at most 0.0066.
Values may be sent and summed in bfloat16 or wider, within the bound.
No kernel may reach another device: no remote copies, remote signals or barrier semaphores. Data moves between devices by JAX's collectives and lax.ppermute only.
A program may use at most 128 MiB of HBM per device.

v0:
```python
import jax
import jax.numpy as jnp
from jax import lax
from jax.sharding import PartitionSpec as P


def slot_index(expert_ids, experts):
    hit_table = (expert_ids[:, :, None] == jnp.arange(experts, dtype=jnp.int32)).astype(jnp.int32)
    per_row = jnp.sum(hit_table, axis=1)
    before = jnp.cumsum(per_row, axis=0) - per_row
    return jnp.sum(hit_table * before[:, None, :], axis=2)


def to_owners(buffer):
    return lax.all_to_all(buffer, "expert", split_axis=0, concat_axis=0, tiled=True)


def local_grads(grad_hidden, gate_pre, up_pre):
    sigmoid_gate = jax.nn.sigmoid(gate_pre)
    grad_gate = (
        grad_hidden * up_pre * (sigmoid_gate * (1.0 + gate_pre * (1.0 - sigmoid_gate)))
    ).astype(jnp.bfloat16)
    grad_up = (grad_hidden * (gate_pre * sigmoid_gate)).astype(jnp.bfloat16)
    return (grad_gate, grad_up)


def send_back(sources, project, groups, cap_rows, owner_order):
    pieces = tuple((source for source in sources))
    shares = lax.psum_scatter(project(pieces), "tensor", scatter_dimension=0, tiled=True).astype(
        jnp.bfloat16
    )
    entire = lax.all_gather(shares, "tensor", axis=0, tiled=True)
    columns = entire.shape[1]
    arrived = lax.all_to_all(
        entire.reshape(groups, cap_rows, columns), "expert", split_axis=0, concat_axis=0, tiled=True
    )
    return (arrived.reshape(groups * cap_rows, columns), owner_order)


def local(tokens, expert_ids, gate_values, w_gate, w_up, w_down, cotangent):
    tok_rows = tokens.shape[0]
    groups = lax.axis_size("expert")
    experts = groups * w_gate.shape[0]
    cap_rows = min(tok_rows, 3 * tok_rows // experts)
    total_rows = groups * cap_rows
    gate_mat = w_gate[0]
    up_mat = w_up[0]
    down_mat = w_down[0]
    slot_of = slot_index(expert_ids, experts)
    owner_order = expert_ids * cap_rows + slot_of
    cells = jnp.arange(experts * cap_rows, dtype=jnp.int32)
    scatter_pick = [owner_order[:, which][None, :] == cells[:, None] for which in range(2)]
    spread = jnp.logical_or(scatter_pick[0], scatter_pick[1]).astype(jnp.bfloat16)
    outgoing = jnp.dot(spread, tokens, preferred_element_type=jnp.float32).astype(jnp.bfloat16)
    arrived = to_owners(outgoing.reshape(experts, cap_rows, tokens.shape[1])).reshape(
        total_rows, tokens.shape[1]
    )
    gate_pre, up_pre = lax.psum(
        (
            jnp.dot(arrived, gate_mat, preferred_element_type=jnp.float32),
            jnp.dot(arrived, up_mat, preferred_element_type=jnp.float32),
        ),
        "wide",
    )
    hidden = (gate_pre * jax.nn.sigmoid(gate_pre) * up_pre).astype(jnp.bfloat16)

    def forward_project(pieces):
        return jnp.einsum("...f,fd->...d", pieces[0], down_mat, preferred_element_type=jnp.float32)

    returned, order_used = send_back((hidden,), forward_project, groups, cap_rows, owner_order)
    gather_pick = [
        (order_used[:, which][:, None] == cells[None, :]).astype(jnp.bfloat16) for which in range(2)
    ]
    chosen = [
        jnp.dot(selector, returned, preferred_element_type=jnp.float32) for selector in gather_pick
    ]
    layer_out = (gate_values[:, 0:1] * chosen[0] + gate_values[:, 1:2] * chosen[1]).astype(
        jnp.bfloat16
    )
    upstream = cotangent.astype(jnp.float32)
    gate_part = jnp.stack([jnp.sum(upstream * chosen[which], axis=1) for which in range(2)], axis=1)
    gate_grad = lax.psum(gate_part, "wide")
    weighted = (
        scatter_pick[0].astype(jnp.float32) * gate_values[:, 0][None, :]
        + scatter_pick[1].astype(jnp.float32) * gate_values[:, 1][None, :]
    )
    grad_outgoing = jnp.dot(
        weighted, upstream, precision=lax.Precision.HIGHEST, preferred_element_type=jnp.float32
    ).astype(jnp.bfloat16)
    grad_arrived = to_owners(grad_outgoing.reshape(experts, cap_rows, tokens.shape[1])).reshape(
        total_rows, tokens.shape[1]
    )
    grad_hidden = lax.psum(
        jnp.einsum("rd,fd->rf", grad_arrived, down_mat, preferred_element_type=jnp.float32), "wide"
    )
    grad_gate, grad_up = local_grads(grad_hidden, gate_pre, up_pre)

    def backward_project(pieces):
        return jnp.einsum(
            "...f,df->...d", pieces[0], gate_mat, preferred_element_type=jnp.float32
        ) + jnp.einsum("...f,df->...d", pieces[1], up_mat, preferred_element_type=jnp.float32)

    grad_returned, order_again = send_back(
        (grad_gate, grad_up), backward_project, groups, cap_rows, owner_order
    )
    grad_chosen = [
        jnp.dot(selector, grad_returned, preferred_element_type=jnp.float32)
        for selector in gather_pick
    ]
    token_grad = (grad_chosen[0] + grad_chosen[1]).astype(jnp.bfloat16)
    return (layer_out, token_grad, gate_grad)


def solution(mesh):
    in_specs = (
        P("expert", "wide"),
        P("expert", None),
        P("expert", None),
        P("expert", "wide", "tensor"),
        P("expert", "wide", "tensor"),
        P("expert", "tensor", "wide"),
        P("expert", "wide"),
    )
    out_specs = (P("expert", "wide"), P("expert", "wide"), P("expert", None))
    return jax.shard_map(local, mesh=mesh, in_specs=in_specs, out_specs=out_specs, check_vma=False)
```

profile of v0, /device:TPU:16, one launch (start us, length us, event | category | flops | bytes accessed | tf_op | source)
XLA Modules:
  0.0 472.1 jit_solution(12170741461714203472)
XLA Ops:
  7.2 0.0 copy-start
  7.2 0.8 convert_reduce_fusion
  7.9 0.1 copy.11
  8.1 0.2 reduce_window_sum.11
  8.2 0.1 copy.13
  8.3 0.7 select_reduce_fusion
  9.0 0.7 multiply_add_fusion
  9.7 0.0 copy-done
  9.7 2.2 convolution_convert_fusion.1
  11.9 5.3 %all-to-all-start = ((bf16[4,96,3072]{2,1,0:T(8,128)(2,1)}), bf16[4,96,3072]{2,1,0:T(8,128)(2,1)S(1)}, u32[]{:S(2)}, u32[]{:S(2)}) async-start(bf16[4,96,3072]{2,1,0:T(8,128)(2,1)} %bitcast.3), calls=%async_computation | async-start | bytes 4718592 | tf_op jit(solution)/shard_map/all_to_all | solution.py:15
  17.2 0.0 copy-done.5
  17.3 3.4 convolution_convert_fusion
  20.7 47.1 %all-to-all-done = bf16[4,96,3072]{2,1,0:T(8,128)(2,1)S(1)} async-done(((bf16[4,96,3072]{2,1,0:T(8,128)(2,1)}), bf16[4,96,3072]{2,1,0:T(8,128)(2,1)S(1)}, u32[]{:S(2)}, u32[]{:S(2)}) %all-to-all-start) | async-done | bytes 2359328 | tf_op jit(solution)/shard_map/all_to_all | solution.py:15
  67.8 7.7 %all-to-all-start.2 = ((bf16[4,96,3072]{2,1,0:T(8,128)(2,1)}), bf16[4,96,3072]{2,1,0:T(8,128)(2,1)}, u32[]{:S(2)}, u32[]{:S(2)}) async-start(bf16[4,96,3072]{2,1,0:T(8,128)(2,1)} %bitcast.11), calls=%async_computation.3 | async-start | bytes 4718592 | tf_op jit(solution)/shard_map/all_to_all | solution.py:15
  75.5 9.7 %fusion.6 = f32[384,2048]{1,0:T(8,128)} fusion(bf16[384,3072]{1,0:T(8,128)(2,1)S(1)} %bitcast.50, bf16[1,3072,2048]{2,1,0:T(8,128)(2,1)} %param.11), kind=kOutput, calls=%fused_computation.6 | convolution fusion | flops 4831838208 | bytes 18087936 | tf_op jit(solution)/shard_map/dot_general | solution.py:61
  85.2 9.7 %fusion.10 = f32[384,2048]{1,0:T(8,128)} fusion(bf16[384,3072]{1,0:T(8,128)(2,1)S(1)} %bitcast.51, bf16[1,3072,2048]{2,1,0:T(8,128)(2,1)} %param.10), kind=kOutput, calls=%fused_computation.10 | convolution fusion | flops 4831838208 | bytes 18087936 | tf_op jit(solution)/shard_map/dot_general | solution.py:60
  94.9 30.7 %all-to-all-done.2 = bf16[4,96,3072]{2,1,0:T(8,128)(2,1)} async-done(((bf16[4,96,3072]{2,1,0:T(8,128)(2,1)}), bf16[4,96,3072]{2,1,0:T(8,128)(2,1)}, u32[]{:S(2)}, u32[]{:S(2)}) %all-to-all-start.2) | async-done | bytes 2359328 | tf_op jit(solution)/shard_map/all_to_all | solution.py:15
  125.6 10.0 %fusion = f32[384,2048]{1,0:T(8,128)} fusion(bf16[384,3072]{1,0:T(8,128)(2,1)} %bitcast.12, bf16[1,2048,3072]{2,1,0:T(8,128)(2,1)} %param.12), kind=kOutput, calls=%fused_computation | convolution fusion | flops 4831838208 | bytes 18087936 | tf_op jit(solution)/shard_map/rd,fd->rf/dot_general | solution.py:94
  135.6 0.0 all-reduce.3.cloned.1.call-update
  135.6 0.0 reduce-scatter.3.cloned.1.call-start
  135.7 43.3 %all-reduce.3.cloned.1.call-done = (f32[384,2048]{1,0:T(8,128)}, f32[384,2048]{1,0:T(8,128)}, f32[384,2048]{1,0:T(8,128)}) async-done(((f32[384,2048]{1,0:T(8,128)}, f32[384,2048]{1,0:T(8,128)}, f32[384,2048]{1,0:T(8,128)}), (f32[384,2048]{1,0:T(8,128)}, f32[384,2048]{1,0:T(8,128)}, f32[384,2048]{1,0:T(8,128)})) %all-reduce.3.cloned.1.call-update) | async-done | bytes 9437200 | tf_op jit(solution)/shard_map/psum | solution.py:58
  179.0 12.3 %fusion.2 = f32[384,3072]{1,0:T(8,128)} fusion(bf16[1,2048,3072]{2,1,0:T(8,128)(2,1)} %param.12, f32[384,2048]{1,0:T(8,128)} %get-tuple-element.5, f32[384,2048]{1,0:T(8,128)} %get-tuple-element.6), kind=kOutput, calls=%fused_computation.2 | convolution fusion | flops 4836556800 | bytes 23592960 | tf_op jit(solution)/shard_map/...f,fd->...d/dot_general | solution.py:68
  191.3 0.0 reduce-scatter.3.cloned.1.call-update
  191.3 0.2 reduce-scatter.5.cloned.1.call-start
  191.5 15.7 %fusion.4 = f32[384,3072]{1,0:T(8,128)} fusion(bf16[1,3072,2048]{2,1,0:T(8,128)(2,1)} %param.11, f32[384,2048]{1,0:T(8,128)} %get-tuple-element.7, f32[384,2048]{1,0:T(8,128)} %get-tuple-element.6), kind=kOutput, calls=%fused_computation.4 | convolution fusion | flops 4836556800 | bytes 23592960 | tf_op jit(solution)/shard_map/...f,df->...d/dot_general | solution.py:101
  207.3 13.6 %fusion.12 = f32[384,3072]{1,0:T(8,128)} fusion(f32[384,3072]{1,0:T(8,128)} %fusion.4, bf16[1,3072,2048]{2,1,0:T(8,128)(2,1)} %param.10, f32[384,2048]{1,0:T(8,128)} %get-tuple-element.6, f32[384,2048]{1,0:T(8,128)} %get-tuple-element.7, f32[384,2048]{1,0:T(8,128)S(1)} %copy-done.6), kind=kOutput, calls=%fused_computation.12 | convolution fusion | flops 4840882176 | bytes 31457280 | tf_op jit(solution)/shard_map/...f,df->...d/dot_general | solution.py:99
  220.9 0.0 reduce-scatter.5.cloned.1.call-update
  220.9 0.0 all-gather.3.cloned.1.call-start
  221.0 28.5 %reduce-scatter.3.cloned.1.call-done = f32[96,3072]{1,0:T(8,128)} async-done(((f32[384,3072]{1,0:T(8,128)}), f32[96,3072]{1,0:T(8,128)}) %reduce-scatter.3.cloned.1.call-update) | async-done | bytes 1179664 | tf_op jit(solution)/shard_map/reduce_scatter | solution.py:29
  249.5 2.2 convert_element_type.41
  251.6 0.0 all-gather.3.cloned.1.call-update
  251.6 0.0 all-gather.5.cloned.1.call-start
  251.7 57.9 %reduce-scatter.5.cloned.1.call-done = f32[96,3072]{1,0:T(8,128)} async-done(((f32[384,3072]{1,0:T(8,128)}), f32[96,3072]{1,0:T(8,128)}) %reduce-scatter.5.cloned.1.call-update) | async-done | bytes 1179664 | tf_op jit(solution)/shard_map/reduce_scatter | solution.py:29
  309.6 2.2 convert_element_type.46
  311.7 0.0 all-gather.5.cloned.1.call-update
  311.8 37.6 %all-gather.3.cloned.1.call-done = bf16[384,3072]{1,0:T(8,128)(2,1)} async-done(((bf16[96,3072]{1,0:T(8,128)(2,1)}), bf16[384,3072]{1,0:T(8,128)(2,1)}) %all-gather.3.cloned.1.call-update) | async-done | bytes 2359312 | tf_op jit(solution)/shard_map/all_gather | solution.py:32
  349.4 5.1 %all-to-all-start.1 = ((bf16[4,96,3072]{2,1,0:T(8,128)(2,1)}), bf16[4,96,3072]{2,1,0:T(8,128)(2,1)S(1)}, u32[]{:S(2)}, u32[]{:S(2)}) async-start(bf16[4,96,3072]{2,1,0:T(8,128)(2,1)} %bitcast.49), calls=%async_computation.2 | async-start | bytes 4718592 | tf_op jit(solution)/shard_map/all_to_all | solution.py:34
  354.5 34.7 %all-gather.5.cloned.1.call-done = bf16[384,3072]{1,0:T(8,128)(2,1)} async-done(((bf16[96,3072]{1,0:T(8,128)(2,1)}), bf16[384,3072]{1,0:T(8,128)(2,1)}) %all-gather.5.cloned.1.call-update) | async-done | bytes 2359312 | tf_op jit(solution)/shard_map/all_gather | solution.py:32
  389.2 15.9 %all-to-all-done.1 = bf16[4,96,3072]{2,1,0:T(8,128)(2,1)S(1)} async-done(((bf16[4,96,3072]{2,1,0:T(8,128)(2,1)}), bf16[4,96,3072]{2,1,0:T(8,128)(2,1)S(1)}, u32[]{:S(2)}, u32[]{:S(2)}) %all-to-all-start.1) | async-done | bytes 2359328 | tf_op jit(solution)/shard_map/all_to_all | solution.py:34
  405.0 1.4 copy-done.2
  406.5 6.9 %all-to-all-start.3 = ((bf16[4,96,3072]{2,1,0:T(8,128)(2,1)}), bf16[4,96,3072]{2,1,0:T(8,128)(2,1)S(1)}, u32[]{:S(2)}, u32[]{:S(2)}) async-start(bf16[4,96,3072]{2,1,0:T(8,128)(2,1)} %bitcast.48), calls=%async_computation.5 | async-start | bytes 4718592 | tf_op jit(solution)/shard_map/all_to_all | solution.py:34
  413.3 2.4 fusion.25
  415.8 1.9 fusion.17
  417.7 3.0 psum.31
  420.7 42.6 %all-to-all-done.3 = bf16[4,96,3072]{2,1,0:T(8,128)(2,1)S(1)} async-done(((bf16[4,96,3072]{2,1,0:T(8,128)(2,1)}), bf16[4,96,3072]{2,1,0:T(8,128)(2,1)S(1)}, u32[]{:S(2)}, u32[]{:S(2)}) %all-to-all-start.3) | async-done | bytes 2359328 | tf_op jit(solution)/shard_map/all_to_all | solution.py:34
  463.4 0.6 fusion.27
  464.0 1.5 fusion.15
  465.5 0.0 copy-done.1
  (14 shorter events, 0.0 us)
Async XLA Ops:
  7.2 2.6 copy-start
  11.9 5.3 %copy-start.5 = (f32[128,2]{0,1:T(2,128)S(1)}, f32[128,2]{0,1:T(2,128)}, u32[]{:S(2)}) copy-start(f32[128,2]{0,1:T(2,128)} %param.9) | copy-start | bytes 3076
  11.9 5.3 %copy-start.4 = (bf16[128,3072]{1,0:T(8,128)(2,1)S(1)}, bf16[128,3072]{1,0:T(8,128)(2,1)}, u32[]{:S(2)}) copy-start(bf16[128,3072]{1,0:T(8,128)(2,1)} %param.13) | copy-start | bytes 2359300
  11.9 55.9 %all-to-all-start = ((bf16[4,96,3072]{2,1,0:T(8,128)(2,1)}), bf16[4,96,3072]{2,1,0:T(8,128)(2,1)S(1)}, u32[]{:S(2)}, u32[]{:S(2)}) async-start(bf16[4,96,3072]{2,1,0:T(8,128)(2,1)} %bitcast.3), calls=%async_computation | async-start | bytes 4718592 | tf_op jit(solution)/shard_map/all_to_all | solution.py:15
  67.8 57.8 %all-to-all-start.2 = ((bf16[4,96,3072]{2,1,0:T(8,128)(2,1)}), bf16[4,96,3072]{2,1,0:T(8,128)(2,1)}, u32[]{:S(2)}, u32[]{:S(2)}) async-start(bf16[4,96,3072]{2,1,0:T(8,128)(2,1)} %bitcast.11), calls=%async_computation.3 | async-start | bytes 4718592 | tf_op jit(solution)/shard_map/all_to_all | solution.py:15
  75.5 103.5 %all-reduce.3.cloned.1.call-start = ((), (), s32[]{:S(2)}) async-start(), calls=%async_computation.10 | async-start | bytes 18874368 | tf_op jit(solution)/shard_map/psum | solution.py:58
  135.6 113.8 %reduce-scatter.3.cloned.1.call-start = ((), (), s32[]{:S(2)}) async-start(), calls=%async_computation.6 | async-start | bytes 5898240 | tf_op jit(solution)/shard_map/reduce_scatter | solution.py:29
  191.3 118.3 %reduce-scatter.5.cloned.1.call-start = ((), (), s32[]{:S(2)}) async-start(), calls=%async_computation.8 | async-start | bytes 5898240 | tf_op jit(solution)/shard_map/reduce_scatter | solution.py:29
  191.5 15.8 %copy-start.6 = (f32[384,2048]{1,0:T(8,128)S(1)}, f32[384,2048]{1,0:T(8,128)}, u32[]{:S(2)}) copy-start(f32[384,2048]{1,0:T(8,128)} %get-tuple-element.5) | copy-start | bytes 9437188
  220.9 128.5 %all-gather.3.cloned.1.call-start = ((), (), s32[]{:S(2)}) async-start(), calls=%async_computation.7 | async-start | bytes 2949120 | tf_op jit(solution)/shard_map/all_gather | solution.py:32
  251.6 137.5 %all-gather.5.cloned.1.call-start = ((), (), s32[]{:S(2)}) async-start(), calls=%async_computation.9 | async-start | bytes 2949120 | tf_op jit(solution)/shard_map/all_gather | solution.py:32
  349.4 55.7 %all-to-all-start.1 = ((bf16[4,96,3072]{2,1,0:T(8,128)(2,1)}), bf16[4,96,3072]{2,1,0:T(8,128)(2,1)S(1)}, u32[]{:S(2)}, u32[]{:S(2)}) async-start(bf16[4,96,3072]{2,1,0:T(8,128)(2,1)} %bitcast.49), calls=%async_computation.2 | async-start | bytes 4718592 | tf_op jit(solution)/shard_map/all_to_all | solution.py:34
  405.0 1.4 copy-start.2
  406.5 56.9 %all-to-all-start.3 = ((bf16[4,96,3072]{2,1,0:T(8,128)(2,1)}), bf16[4,96,3072]{2,1,0:T(8,128)(2,1)S(1)}, u32[]{:S(2)}, u32[]{:S(2)}) async-start(bf16[4,96,3072]{2,1,0:T(8,128)(2,1)} %bitcast.48), calls=%async_computation.5 | async-start | bytes 4718592 | tf_op jit(solution)/shard_map/all_to_all | solution.py:34
  413.3 2.4 copy-start.3
  463.4 2.2 copy-start.1
Sparse Core Ops, SparseCore 0:
  135.7 43.2 all-reduce.2
  191.4 57.9 reduce-scatter.2
  252.4 57.0 reduce-scatter.4
  311.9 37.4 all-gather.2
  351.6 37.4 all-gather.4
where the time goes:
time: 477 us; the launch traced here: 472 us
  waiting for transfers between devices  338 us (71%)
  matrix products  83.2 us (17%)
  starting transfers between devices  25.4 us (5%)
  between operations  13.8 us (3%)
  other arithmetic  6.66 us (1%)
    reduce_scatter x2, waiting for transfers between devices, send_back(): lax.psum_scatter(project(pieces), 'tensor', scatter_dimension=0, tiled=True)  86.4 us
    all_to_all x2, waiting for transfers between devices, to_owners(): lax.all_to_all(buffer, 'expert', split_axis=0, concat_axis=0, tiled=True)  77.8 us
    all_gather x2, waiting for transfers between devices, send_back(): entire = lax.all_gather(shares, 'tensor', axis=0, tiled=True)  72.3 us
    all_to_all x2, waiting for transfers between devices, send_back(): lax.all_to_all(entire.reshape(groups, cap_rows, columns), 'expert', split...  58.5 us
    psum x1, waiting for transfers between devices, local(): lax.psum((jnp.dot(arrived, gate_mat, preferred_element_type=jnp.float32),...  43.3 us
    dot_general x1, matrix products, backward_project(): jnp.einsum('...f,df->...d', pieces[1], up_mat, preferred_element_type=jnp...  15.7 us
    dot_general x1, matrix products, backward_project(): jnp.einsum('...f,df->...d', pieces[0], gate_mat, preferred_element_type=j...  13.6 us
    all_to_all x2, starting transfers between devices, to_owners(): lax.all_to_all(buffer, 'expert', split_axis=0, concat_axis=0, tiled=True)  13.1 us
  transfers between devices with their start and end apart: 9, of which 9 were waited for; matrix products, arithmetic and copies ran while one was open for 13% of the time, Pallas kernels for 0%

commit v1 on v0

v1 whole, which is shorter than its diff:
```python
import jax
import jax.numpy as jnp
from jax import lax
from jax.experimental import pallas as pl
from jax.experimental.pallas import tpu as pltpu
from jax.sharding import PartitionSpec as P

BF = jnp.bfloat16
F32 = jnp.float32
MIB = 1024 * 1024


def slot_index(expert_ids, experts):
    hit_table = (expert_ids[:, :, None] == jnp.arange(experts, dtype=jnp.int32)).astype(jnp.int32)
    per_row = jnp.sum(hit_table, axis=1)
    before = jnp.cumsum(per_row, axis=0) - per_row
    return jnp.sum(hit_table * before[:, None, :], axis=2)


def exchange(array, axis, bit):
    size = lax.axis_size(axis)
    return lax.ppermute(array, axis, [(i, i ^ bit) for i in range(size)])


def dot_nn(a, b):
    return jnp.dot(a, b, preferred_element_type=F32)


def dot_nt(a, b):
    return lax.dot_general(a, b, (((1,), (1,)), ((), ())), preferred_element_type=F32)


def params(mib):
    return pltpu.CompilerParams(vmem_limit_bytes=mib * MIB)


def whole(shape):
    zeros = (0,) * len(shape)
    return pl.BlockSpec(shape, lambda i, *_: zeros, pipeline_mode=pl.Buffered(1))


def sds(shape, dtype):
    return jax.ShapeDtypeStruct(shape, dtype)


def cost(flops, nbytes):
    return pl.CostEstimate(flops=flops, bytes_accessed=nbytes, transcendentals=0)


def gather_rows(t, own_ref, parts, rows_ref):
    cap = own_ref.shape[0]
    n = len(parts)
    quarter = parts[0].shape[1]
    for q in range(n):
        rows_ref[q, :cap, :] = own_ref[:, q * quarter : (q + 1) * quarter]
    for j in range(n):
        rows_ref[t ^ j, cap:, :] = parts[j][...]


def pre_act_kernel(t_ref, own_ref, *refs):
    parts, (gate_w, up_w, gate_o, up_o, gate_s, up_s, rows_ref) = refs[:-7], refs[-7:]

    @pl.when(pl.program_id(0) == 0)
    def _():
        gather_rows(t_ref[0], own_ref, parts, rows_ref)

    n, _, quarter = rows_ref.shape
    for w, out, send in ((gate_w, gate_o, gate_s), (up_w, up_o, up_s)):
        total = dot_nn(rows_ref[0], w[:quarter, :])
        for q in range(1, n):
            total += dot_nn(rows_ref[q], w[q * quarter : (q + 1) * quarter, :])
        out[...] = total
        send[...] = total.astype(BF)


def pre_acts(t, own, parts, gate_mat, up_mat, block):
    depth, hidden = gate_mat.shape
    cap = own.shape[0]
    n = len(parts)
    rows = cap + parts[0].shape[0]
    weight = pl.BlockSpec((depth, block), lambda i, *_: (0, i))
    out = pl.BlockSpec((rows, block), lambda i, *_: (0, i))
    return pl.pallas_call(
        pre_act_kernel,
        grid_spec=pltpu.PrefetchScalarGridSpec(
            num_scalar_prefetch=1,
            grid=(hidden // block,),
            in_specs=[whole(own.shape)] + [whole(p.shape) for p in parts] + [weight, weight],
            out_specs=[out] * 4,
            scratch_shapes=[pltpu.VMEM((n, rows, depth // n), BF)],
        ),
        out_shape=[sds((rows, hidden), F32)] * 2 + [sds((rows, hidden), BF)] * 2,
        compiler_params=params(48),
        cost_estimate=cost(4 * rows * depth * hidden, 4 * depth * hidden),
        name="pre_acts",
    )(t, own, *parts, gate_mat, up_mat)


def grad_hidden_kernel(t_ref, own_ref, *refs):
    parts, (down_w, out, send, rows_ref) = refs[:-4], refs[-4:]

    @pl.when(pl.program_id(0) == 0)
    def _():
        gather_rows(t_ref[0], own_ref, parts, rows_ref)

    n, _, quarter = rows_ref.shape
    total = dot_nt(rows_ref[0], down_w[:, :quarter])
    for q in range(1, n):
        total += dot_nt(rows_ref[q], down_w[:, q * quarter : (q + 1) * quarter])
    out[...] = total
    send[...] = total.astype(BF)


def grad_hiddens(t, own, parts, down_mat, block):
    hidden, depth = down_mat.shape
    n = len(parts)
    rows = own.shape[0] + parts[0].shape[0]
    weight = pl.BlockSpec((block, depth), lambda i, *_: (i, 0))
    out = pl.BlockSpec((rows, block), lambda i, *_: (0, i))
    return pl.pallas_call(
        grad_hidden_kernel,
        grid_spec=pltpu.PrefetchScalarGridSpec(
            num_scalar_prefetch=1,
            grid=(hidden // block,),
            in_specs=[whole(own.shape)] + [whole(p.shape) for p in parts] + [weight],
            out_specs=[out] * 2,
            scratch_shapes=[pltpu.VMEM((n, rows, depth // n), BF)],
        ),
        out_shape=[sds((rows, hidden), F32), sds((rows, hidden), BF)],
        compiler_params=params(48),
        cost_estimate=cost(2 * rows * depth * hidden, 2 * depth * hidden),
        name="grad_hidden",
    )(t, own, *parts, down_mat)


STRIP = 32


def project_kernel(t_ref, gate_o, up_o, gate_r, up_r, down_w, pieces, kept, hidden_ref):
    step = pl.program_id(0)

    @pl.when(step == 0)
    def _():
        @pl.loop(0, hidden_ref.shape[0] // STRIP)
        def _(i):
            here = pl.ds(pl.multiple_of(i * STRIP, STRIP), STRIP)
            gate = gate_o[here, :] + gate_r[here, :].astype(F32)
            up = up_o[here, :] + up_r[here, :].astype(F32)
            hidden_ref[here, :] = (gate * jax.nn.sigmoid(gate) * up).astype(BF)

    total = dot_nn(hidden_ref[...], down_w[...])

    @pl.when(step < pl.num_programs(0) - 1)
    def _():
        pieces[0] = total.astype(BF)

    @pl.when(step == pl.num_programs(0) - 1)
    def _():
        kept[...] = total


def projected(t, n, gate_o, up_o, gate_r, up_r, down_mat):
    hidden, depth = down_mat.shape
    rows = gate_o.shape[0]
    quarter = depth // n

    def which(i, t):
        return t[0] ^ ((i + 1) % n)

    return pl.pallas_call(
        project_kernel,
        grid_spec=pltpu.PrefetchScalarGridSpec(
            num_scalar_prefetch=1,
            grid=(n,),
            in_specs=[whole(gate_o.shape)] * 4
            + [pl.BlockSpec((hidden, quarter), lambda i, t: (0, which(i, t)))],
            out_specs=[
                pl.BlockSpec((1, rows, quarter), lambda i, t: (jnp.minimum(i, n - 2), 0, 0)),
                pl.BlockSpec((rows, quarter), lambda i, t: (0, 0)),
            ],
            scratch_shapes=[pltpu.VMEM((rows, hidden), BF)],
        ),
        out_shape=[sds((n - 1, rows, quarter), BF), sds((rows, quarter), F32)],
        compiler_params=params(48),
        cost_estimate=cost(2 * rows * depth * hidden, 2 * depth * hidden),
        name="project",
    )(t, gate_o, up_o, gate_r, up_r, down_mat)


def grad_rows_kernel(
    t_ref, gate_o, up_o, gate_r, up_r, gh_o, gh_r, gate_w, up_w, pieces, kept, gg_ref, gu_ref
):
    step = pl.program_id(0)

    @pl.when(step == 0)
    def _():
        @pl.loop(0, gg_ref.shape[0] // STRIP)
        def _(i):
            here = pl.ds(pl.multiple_of(i * STRIP, STRIP), STRIP)
            gate = gate_o[here, :] + gate_r[here, :].astype(F32)
            up = up_o[here, :] + up_r[here, :].astype(F32)
            grad = gh_o[here, :] + gh_r[here, :].astype(F32)
            s = jax.nn.sigmoid(gate)
            gg_ref[here, :] = (grad * up * (s * (1.0 + gate * (1.0 - s)))).astype(BF)
            gu_ref[here, :] = (grad * (gate * s)).astype(BF)

    total = dot_nt(gg_ref[...], gate_w[...]) + dot_nt(gu_ref[...], up_w[...])

    @pl.when(step < pl.num_programs(0) - 1)
    def _():
        pieces[0] = total.astype(BF)

    @pl.when(step == pl.num_programs(0) - 1)
    def _():
        kept[...] = total


def grad_rows(t, n, gate_o, up_o, gate_r, up_r, gh_o, gh_r, gate_mat, up_mat):
    depth, hidden = gate_mat.shape
    rows = gate_o.shape[0]
    quarter = depth // n

    def which(i, t):
        return t[0] ^ ((i + 1) % n)

    weight = pl.BlockSpec((quarter, hidden), lambda i, t: (which(i, t), 0))
    return pl.pallas_call(
        grad_rows_kernel,
        grid_spec=pltpu.PrefetchScalarGridSpec(
            num_scalar_prefetch=1,
            grid=(n,),
            in_specs=[whole(gate_o.shape)] * 6 + [weight, weight],
            out_specs=[
                pl.BlockSpec((1, rows, quarter), lambda i, t: (jnp.minimum(i, n - 2), 0, 0)),
                pl.BlockSpec((rows, quarter), lambda i, t: (0, 0)),
            ],
            scratch_shapes=[pltpu.VMEM((rows, hidden), BF)] * 2,
        ),
        out_shape=[sds((n - 1, rows, quarter), BF), sds((rows, quarter), F32)],
        compiler_params=params(52),
        cost_estimate=cost(4 * rows * depth * hidden, 4 * depth * hidden),
        name="grad_rows",
    )(t, gate_o, up_o, gate_r, up_r, gh_o, gh_r, gate_mat, up_mat)


def local(tokens, expert_ids, gate_values, w_gate, w_up, w_down, cotangent):
    tok_rows, depth = tokens.shape
    groups = lax.axis_size("expert")
    n = lax.axis_size("tensor")
    z = lax.axis_index("expert")
    t = lax.axis_index("tensor")
    t_arr = t.astype(jnp.int32).reshape(1)
    experts = groups
    cap = min(tok_rows, 3 * tok_rows // experts)
    quarter = depth // n
    gate_mat, up_mat, down_mat = w_gate[0], w_up[0], w_down[0]

    slot_of = slot_index(expert_ids, experts)
    order = (expert_ids ^ z) * cap + slot_of
    cells = jnp.arange(experts * cap, dtype=jnp.int32)
    pick = [order[:, k][None, :] == cells[:, None] for k in range(2)]
    spread = jnp.logical_or(pick[0], pick[1]).astype(BF)
    slot_gate = jnp.sum(
        jnp.where(pick[0], gate_values[:, 0][None, :], 0.0)
        + jnp.where(pick[1], gate_values[:, 1][None, :], 0.0),
        axis=1,
        keepdims=True,
    )

    def dispatch(source, scale):
        part = lax.dynamic_slice(source, (0, t * quarter), (tok_rows, quarter))
        out = dot_nn(spread[cap:], part)
        own = dot_nn(spread[:cap], source)
        if scale is not None:
            out, own = out * scale[cap:], own * scale[:cap]
        out, own = out.astype(BF), own.astype(BF)
        arrived = jnp.concatenate(
            [exchange(out[(k - 1) * cap : k * cap], "expert", k) for k in range(1, groups)], axis=0
        )
        return own, arrived

    tok_own, tok_part = dispatch(tokens, None)
    tok_parts = [tok_part] + [exchange(tok_part, "tensor", j) for j in range(1, n)]
    cot_own, cot_part = dispatch(cotangent, slot_gate)
    cot_parts = [cot_part] + [exchange(cot_part, "tensor", j) for j in range(1, n)]

    gate_o, up_o, gate_s, up_s = pre_acts(t_arr, tok_own, tok_parts, gate_mat, up_mat, 512)
    gate_r, up_r = exchange(gate_s, "wide", 1), exchange(up_s, "wide", 1)
    gh_o, gh_s = grad_hiddens(t_arr, cot_own, cot_parts, down_mat, 512)
    gh_r = exchange(gh_s, "wide", 1)

    def send_back(pieces, kept):
        total = kept
        for j in range(1, n):
            total = total + exchange(pieces[j - 1], "tensor", j).astype(F32)
        total = total.astype(BF)
        back = [total[:cap]] + [
            exchange(total[k * cap : (k + 1) * cap], "expert", k) for k in range(1, groups)
        ]
        return jnp.concatenate(back, axis=0)

    def spread_out(part):
        got = [part] + [exchange(part, "tensor", j) for j in range(1, n)]
        out = jnp.zeros((tok_rows, depth), part.dtype)
        for j in range(n):
            out = lax.dynamic_update_slice(out, got[j], (0, (t ^ j) * quarter))
        return out

    gather = [(order[:, k][:, None] == cells[None, :]).astype(BF) for k in range(2)]
    pieces, kept = projected(t_arr, n, gate_o, up_o, gate_r, up_r, down_mat)
    returned = send_back(pieces, kept)
    chosen = [dot_nn(g, returned) for g in gather]
    layer_part = (gate_values[:, 0:1] * chosen[0] + gate_values[:, 1:2] * chosen[1]).astype(BF)
    layer_out = spread_out(layer_part)
    cot_here = lax.dynamic_slice(cotangent, (0, t * quarter), (tok_rows, quarter)).astype(F32)
    gate_grad = lax.psum(
        jnp.stack([jnp.sum(cot_here * c, axis=1) for c in chosen], axis=1), ("wide", "tensor")
    )

    gpieces, gkept = grad_rows(
        t_arr, n, gate_o, up_o, gate_r, up_r, gh_o, gh_r, gate_mat, up_mat
    )
    greturned = send_back(gpieces, gkept)
    grad_part = (dot_nn(gather[0], greturned) + dot_nn(gather[1], greturned)).astype(BF)
    token_grad = spread_out(grad_part)
    return (layer_out, token_grad, gate_grad)


def plain_local(tokens, expert_ids, gate_values, w_gate, w_up, w_down, cotangent):
    tok_rows, depth = tokens.shape
    groups = lax.axis_size("expert")
    experts = groups * w_gate.shape[0]
    cap = min(tok_rows, 3 * tok_rows // experts)
    total_rows = groups * cap
    gate_mat, up_mat, down_mat = w_gate[0], w_up[0], w_down[0]
    order = expert_ids * cap + slot_index(expert_ids, experts)
    cells = jnp.arange(experts * cap, dtype=jnp.int32)
    pick = [order[:, k][None, :] == cells[:, None] for k in range(2)]
    gather = [(order[:, k][:, None] == cells[None, :]).astype(BF) for k in range(2)]

    def to_owners(rows):
        out = rows.astype(BF).reshape(groups, cap, depth)
        out = lax.all_to_all(out, "expert", split_axis=0, concat_axis=0, tiled=True)
        return out.reshape(total_rows, depth)

    def send_back(rows):
        share = lax.psum_scatter(rows, "tensor", scatter_dimension=0, tiled=True).astype(BF)
        return to_owners(lax.all_gather(share, "tensor", axis=0, tiled=True))

    spread = jnp.logical_or(pick[0], pick[1]).astype(BF)
    arrived = to_owners(dot_nn(spread, tokens))
    gate_pre, up_pre = lax.psum((dot_nn(arrived, gate_mat), dot_nn(arrived, up_mat)), "wide")
    s = jax.nn.sigmoid(gate_pre)
    returned = send_back(dot_nn((gate_pre * s * up_pre).astype(BF), down_mat))
    chosen = [dot_nn(g, returned) for g in gather]
    layer_out = (gate_values[:, 0:1] * chosen[0] + gate_values[:, 1:2] * chosen[1]).astype(BF)
    upstream = cotangent.astype(F32)
    gate_grad = lax.psum(
        jnp.stack([jnp.sum(upstream * c, axis=1) for c in chosen], axis=1), "wide"
    )
    slot_gate = jnp.sum(
        jnp.where(pick[0], gate_values[:, 0][None, :], 0.0)
        + jnp.where(pick[1], gate_values[:, 1][None, :], 0.0),
        axis=1,
        keepdims=True,
    )
    grad_arrived = to_owners(dot_nn(spread, cotangent) * slot_gate)
    grad_hidden = lax.psum(dot_nt(grad_arrived, down_mat), "wide")
    grad_gate = (grad_hidden * up_pre * (s * (1.0 + gate_pre * (1.0 - s)))).astype(BF)
    grad_up = (grad_hidden * (gate_pre * s)).astype(BF)
    back = send_back(dot_nt(grad_gate, gate_mat) + dot_nt(grad_up, up_mat))
    token_grad = (dot_nn(gather[0], back) + dot_nn(gather[1], back)).astype(BF)
    return (layer_out, token_grad, gate_grad)


def solution(mesh):
    in_specs = (
        P("expert", "wide"),
        P("expert", None),
        P("expert", None),
        P("expert", "wide", "tensor"),
        P("expert", "wide", "tensor"),
        P("expert", "tensor", "wide"),
        P("expert", "wide"),
    )
    out_specs = (P("expert", "wide"), P("expert", "wide"), P("expert", None))
    laid_out = mesh.shape["tensor"] == 4 and mesh.shape["expert"] == 4 and mesh.shape["wide"] == 2
    return jax.shard_map(
        local if laid_out else plain_local,
        mesh=mesh,
        in_specs=in_specs,
        out_specs=out_specs,
        check_vma=False,
    )
```

time: 477 us -> 204 us (0.43)
  waiting for transfers between devices: 338 us -> 73 us
  matrix products: 83.2 us -> 3.77 us
  Pallas kernels: 0 us -> 56.8 us
  starting transfers between devices: 25.4 us -> 38.4 us
  between operations: 13.8 us -> 1.02 us
  blocking collectives: 3.02 us -> 14.4 us
  local copies, waits for them, and re-layouts: 1.63 us -> 9.6 us
    all_to_all x4 -> x0, waiting for transfers between devices: 136 us -> none  [the longest x2 77.8 us: to_owners(): lax.all_to_all(buffer, 'expert', split_axis=0, concat_axis=0, tiled=True)]
    reduce_scatter x2 -> x0, waiting for transfers between devices: 86.4 us -> none  [send_back(): lax.psum_scatter(project(pieces), 'tensor', scatter_dimension=0, tiled=True)]
    dot_general x12 -> x8, matrix products: 83.2 us -> 3.77 us  [dot_nn(): return jnp.dot(a, b, preferred_element_type=F32)]
    ppermute x0 -> x33, waiting for transfers between devices: none -> 73 us  [exchange(): return lax.ppermute(array, axis, [(i, i ^ bit) for i in range(size)])]
    all_gather x2 -> x0, waiting for transfers between devices: 72.3 us -> none  [send_back(): entire = lax.all_gather(shares, 'tensor', axis=0, tiled=True)]
    pallas_call x0 -> x4, Pallas kernels: none -> 56.8 us  [the longest x1 20.9 us: grad_rows(): pl.pallas_call(grad_rows_kernel, grid_spec=pltpu.PrefetchScalarGridSpec(n...]
    psum x1 -> x0, waiting for transfers between devices: 43.3 us -> none  [local(): lax.psum((jnp.dot(arrived, gate_mat, preferred_element_type=jnp.float32),...]
    ppermute x0 -> x33, starting transfers between devices: none -> 38.4 us  [exchange(): return lax.ppermute(array, axis, [(i, i ^ bit) for i in range(size)])]
  transfers between devices with their start and end apart: 9 -> 33, of which waited for: 9 -> 13; matrix products, arithmetic and copies ran while one was open for 13% -> 6% of each run, Pallas kernels for 0% -> 18%
where the time goes in v1:
time: 204 us; the launch traced here: 203 us
  waiting for transfers between devices  73 us (36%)
  Pallas kernels  56.8 us (28%)
  starting transfers between devices  38.4 us (19%)
  blocking collectives  14.4 us (7%)
  local copies, waits for them, and re-layouts  9.6 us (5%)
  other arithmetic  6.08 us (3%)
  matrix products  3.77 us (2%)
    ppermute x33, waiting for transfers between devices, exchange(): return lax.ppermute(array, axis, [(i, i ^ bit) for i in range(size)])  73 us
    ppermute x33, starting transfers between devices, exchange(): return lax.ppermute(array, axis, [(i, i ^ bit) for i in range(size)])  38.4 us
    pallas_call x1, Pallas kernels, grad_rows(): pl.pallas_call(grad_rows_kernel, grid_spec=pltpu.PrefetchScalarGridSpec(n...  20.9 us
    pallas_call x1, Pallas kernels, pre_acts(): pl.pallas_call(pre_act_kernel, grid_spec=pltpu.PrefetchScalarGridSpec(num...  15 us
    psum x1, blocking collectives, local(): lax.psum(jnp.stack([jnp.sum(cot_here * c, axis=1) for c in chosen], axis=...  14.4 us
    pallas_call x1, Pallas kernels, projected(): pl.pallas_call(project_kernel, grid_spec=pltpu.PrefetchScalarGridSpec(num...  11.3 us
    pallas_call x1, Pallas kernels, grad_hiddens(): pl.pallas_call(grad_hidden_kernel, grid_spec=pltpu.PrefetchScalarGridSpec...  9.65 us
  transfers between devices with their start and end apart: 33, of which 13 were waited for; matrix products, arithmetic and copies ran while one was open for 6% of the time, Pallas kernels for 18%

profile of v1, /device:TPU:16, one launch (start us, length us, event | category | flops | bytes accessed | tf_op | source)
XLA Modules:
  0.0 203.2 jit_solution(5573696540871735542)
XLA Ops:
  3.6 1.6 collective-permute-start
  5.6 1.6 collective-permute-start.2
  7.7 2.5 %collective-permute-start.17 = (bf16[96,768]{1,0:T(8,128)(2,1)S(1)}, bf16[96,768]{1,0:T(8,128)(2,1)S(1)}, u32[]{:S(2)}, u32[]{:S(2)}) collective-permute-start(bf16[96,768]{1,0:T(8,128)(2,1)S(1)} %get-tuple-element.43), channel_id=1, source_target_pairs={{0,1},{1,0},{2,3},{3,2},{4,5},{5,4},{6,7},{7,6},{8,9},{9,8},{10,11... | collective-permute-start | bytes 442376 | tf_op jit(solution)/shard_map/ppermute | solution.py:22
  11.2 4.9 %collective-permute-done.1 = bf16[96,768]{1,0:T(8,128)(2,1)S(1)} collective-permute-done((bf16[96,768]{1,0:T(8,128)(2,1)S(1)}, bf16[96,768]{1,0:T(8,128)(2,1)S(1)}, u32[]{:S(2)}, u32[]{:S(2)}) %collective-permute-start.1) | collective-permute-done | bytes 147488 | tf_op jit(solution)/shard_map/ppermute | solution.py:22
  16.1 9.9 %collective-permute-done.2 = bf16[96,768]{1,0:T(8,128)(2,1)S(1)} collective-permute-done((bf16[96,768]{1,0:T(8,128)(2,1)S(1)}, bf16[96,768]{1,0:T(8,128)(2,1)S(1)}, u32[]{:S(2)}, u32[]{:S(2)}) %collective-permute-start.2) | collective-permute-done | bytes 147488 | tf_op jit(solution)/shard_map/ppermute | solution.py:22
  26.0 1.6 collective-permute-start.3
  27.6 1.5 collective-permute-start.4
  30.6 4.5 %collective-permute-done.19 = bf16[96,768]{1,0:T(8,128)(2,1)S(1)} collective-permute-done((bf16[96,768]{1,0:T(8,128)(2,1)S(1)}, bf16[96,768]{1,0:T(8,128)(2,1)S(1)}, u32[]{:S(2)}, u32[]{:S(2)}) %collective-permute-start.19) | collective-permute-done | bytes 147488 | tf_op jit(solution)/shard_map/ppermute | solution.py:22
  35.1 1.6 collective-permute-start.20
  36.7 1.5 collective-permute-start.21
  38.2 1.0 collective-permute-done.3.refs_1_
  39.2 2.4 %collective-permute-start.22 = (bf16[288,768]{1,0:T(8,128)(2,1)S(1)}, bf16[288,768]{1,0:T(8,128)(2,1)S(1)}, u32[]{:S(2)}, u32[]{:S(2)}) collective-permute-start(bf16[288,768]{1,0:T(8,128)(2,1)S(1)} %constant_dynamic-update-slice_fusion.3.refs_0_), channel_id=1, source_target_pairs={{0,12},{4,8},{8,4},{12,0},{1,13},{5,9},{9,5},{13,1},{2,14},{6,10},... | collective-permute-start | bytes 1327112 | tf_op jit(solution)/shard_map/ppermute | solution.py:22
  41.6 7.1 %collective-permute-done.4.refs_2_ = bf16[288,768]{1,0:T(8,128)(2,1)S(1)} collective-permute-done((bf16[288,768]{1,0:T(8,128)(2,1)S(1)}, bf16[288,768]{1,0:T(8,128)(2,1)S(1)}, u32[]{:S(2)}, u32[]{:S(2)}) %collective-permute-start.4) | collective-permute-done | bytes 442400 | tf_op jit(solution)/shard_map/ppermute | solution.py:22
  48.7 1.0 collective-permute-done.5.refs_3_
  49.7 15.0 %pre_acts.1 = (f32[384,2048]{1,0:T(8,128)}, f32[384,2048]{1,0:T(8,128)}, bf16[384,2048]{1,0:T(8,128)(2,1)S(1)}, bf16[384,2048]{1,0:T(8,128)(2,1)S(1)}) custom-call(s32[1]{0:T(128)} %bitcast.2.t_ref, bf16[96,3072]{1,0:T(8,128)(2,1)S(1)} %convolution_convert_fusion.own_ref, bf16[288,768]{1,0:T(8,128)(2,1)S(1)} %constant_dynamic-update-slice_fusion.refs_0_, ...), custom_call_target="tpu_custom_call" | custom-call | flops 9663676416 | bytes 25165824 | tf_op jit(solution)/shard_map/pre_acts/pallas_call | solution.py:83
  65.3 9.6 %grad_hidden.1 = (f32[384,2048]{1,0:T(8,128)}, bf16[384,2048]{1,0:T(8,128)(2,1)S(1)}) custom-call(s32[1]{0:T(128)} %bitcast.2.t_ref, bf16[96,3072]{1,0:T(8,128)(2,1)S(1)} %fusion.own_ref, bf16[288,768]{1,0:T(8,128)(2,1)S(1)} %constant_dynamic-update-slice_fusion.3.refs_0_, bf16[288,768]{1,0:T(8,128)(2,1)S(1)} %collective-permute-done.20.refs_1_, ...), custom_call_target="tpu_custom_call" | custom-call | flops 4831838208 | bytes 12582912 | tf_op jit(solution)/shard_map/grad_hidden/pallas_call | solution.py:120
  75.0 3.4 %collective-permute-done.23.gh_r = bf16[384,2048]{1,0:T(8,128)(2,1)S(1)} collective-permute-done((bf16[384,2048]{1,0:T(8,128)(2,1)S(1)}, bf16[384,2048]{1,0:T(8,128)(2,1)S(1)}, u32[]{:S(2)}, u32[]{:S(2)}) %collective-permute-start.23) | collective-permute-done | bytes 1572896 | tf_op jit(solution)/shard_map/ppermute | solution.py:22
  78.4 1.2 copy-done.7
  79.5 20.9 %grad_rows.1 = (bf16[3,384,768]{2,1,0:T(8,128)(2,1)}, f32[384,768]{1,0:T(8,128)S(1)}) custom-call(s32[1]{0:T(128)} %bitcast.2.t_ref, f32[384,2048]{1,0:T(8,128)} %get-tuple-element.13.gate_o, f32[384,2048]{1,0:T(8,128)} %get-tuple-element.14.up_o, bf16[384,2048]{1,0:T(8,128)(2,1)} %copy-done.2, bf16[384,2048]{1,0:T(8,128)(2,1)} %copy-done.4, ...), custom_call_target="tpu_custom_call" | custom-call | flops 9663676416 | bytes 25165824 | tf_op jit(solution)/shard_map/grad_rows/pallas_call | solution.py:227
  100.4 2.7 %slice_bitcast_fusion.2 = (bf16[384,768]{1,0:T(8,128)(2,1)S(1)}, bf16[384,768]{1,0:T(8,128)(2,1)}, bf16[384,768]{1,0:T(8,128)(2,1)}) fusion(bf16[3,384,768]{2,1,0:T(8,128)(2,1)} %get-tuple-element.22), kind=kLoop, calls=%fused_computation.14 | loop fusion | bytes 3538944 | tf_op jit(solution)/shard_map/squeeze | solution.py:295
  103.1 1.5 collective-permute-start.24
  104.6 1.2 collective-permute-start.25
  105.8 0.9 collective-permute-start.26
  106.7 11.3 %project.1 = (bf16[3,384,768]{2,1,0:T(8,128)(2,1)S(1)}, f32[384,768]{1,0:T(8,128)S(1)}) custom-call(s32[1]{0:T(128)} %bitcast.2.t_ref, f32[384,2048]{1,0:T(8,128)} %get-tuple-element.13.gate_o, f32[384,2048]{1,0:T(8,128)} %get-tuple-element.14.up_o, bf16[384,2048]{1,0:T(8,128)(2,1)S(1)} %copy-done.3, bf16[384,2048]{1,0:T(8,128)(2,1)S(1)} %copy-done.5, ...), custom_call_target="tpu_custom_call" | custom-call | flops 4831838208 | bytes 12582912 | tf_op jit(solution)/shard_map/project/pallas_call | solution.py:170
  118.0 1.2 slice_bitcast_fusion.5
  119.3 2.0 collective-permute-start.10
  121.3 1.5 collective-permute-start.8
  122.7 22.3 %collective-permute-done.25 = bf16[384,768]{1,0:T(8,128)(2,1)} collective-permute-done((bf16[384,768]{1,0:T(8,128)(2,1)}, bf16[384,768]{1,0:T(8,128)(2,1)}, u32[]{:S(2)}, u32[]{:S(2)}) %collective-permute-start.25) | collective-permute-done | bytes 589856 | tf_op jit(solution)/shard_map/ppermute | solution.py:22
  145.1 1.7 add_convert_fusion
  146.9 1.3 collective-permute-start.28
  148.2 2.2 %collective-permute-start.29 = (bf16[96,768]{1,0:T(8,128)(2,1)S(1)}, bf16[96,768]{1,0:T(8,128)(2,1)S(1)}, u32[]{:S(2)}, u32[]{:S(2)}) collective-permute-start(bf16[96,768]{1,0:T(8,128)(2,1)S(1)} %get-tuple-element.34), channel_id=1, source_target_pairs={{0,3},{1,2},{2,1},{3,0},{4,7},{5,6},{6,5},{7,4},{8,11},{9,10},{10,... | collective-permute-start | bytes 442376 | tf_op jit(solution)/shard_map/ppermute | solution.py:22
  150.4 6.2 %collective-permute-done.8 = bf16[384,768]{1,0:T(8,128)(2,1)} collective-permute-done((bf16[384,768]{1,0:T(8,128)(2,1)}, bf16[384,768]{1,0:T(8,128)(2,1)}, u32[]{:S(2)}, u32[]{:S(2)}) %collective-permute-start.8) | collective-permute-done | bytes 589856 | tf_op jit(solution)/shard_map/ppermute | solution.py:22
  156.6 1.6 collective-permute-done.9
  158.1 1.7 add_convert_fusion.1
  160.0 3.4 %collective-permute-start.13 = (bf16[96,768]{1,0:T(8,128)(2,1)S(1)}, bf16[96,768]{1,0:T(8,128)(2,1)S(1)}, u32[]{:S(2)}, u32[]{:S(2)}) collective-permute-start(bf16[96,768]{1,0:T(8,128)(2,1)S(1)} %get-tuple-element.38), channel_id=1, source_target_pairs={{0,3},{1,2},{2,1},{3,0},{4,7},{5,6},{6,5},{7,4},{8,11},{9,10},{10,... | collective-permute-start | bytes 442376 | tf_op jit(solution)/shard_map/ppermute | solution.py:22
  163.8 1.0 constant_dynamic-update-slice_fusion.9
  165.6 1.7 collective-permute-start.31
  167.3 1.3 collective-permute-start.32
  168.6 7.5 %collective-permute-done.13 = bf16[96,768]{1,0:T(8,128)(2,1)S(1)} collective-permute-done((bf16[96,768]{1,0:T(8,128)(2,1)S(1)}, bf16[96,768]{1,0:T(8,128)(2,1)S(1)}, u32[]{:S(2)}, u32[]{:S(2)}) %collective-permute-start.13) | collective-permute-done | bytes 147488 | tf_op jit(solution)/shard_map/ppermute | solution.py:22
  176.5 1.0 constant_dynamic-update-slice_fusion.13
  177.5 0.8 collective-permute-start.14
  179.3 14.4 %psum.7 = f32[128,2]{0,1:T(2,128)} all-reduce(f32[128,2]{0,1:T(2,128)S(1)} %pad_maximum_fusion.6), channel_id=1, replica_groups=mesh['wide'=2,'tensor'=4,'expert'=4] {'wide','tensor'}, use_global_device_ids=true, to_apply=%region_6.7 | all-reduce | flops 256 | bytes 2048 | tf_op jit(solution)/shard_map/psum | solution.py:316
  193.7 2.4 %collective-permute-start.16 = (bf16[128,768]{1,0:T(8,128)(2,1)}, bf16[128,768]{1,0:T(8,128)(2,1)S(1)}, u32[]{:S(2)}, u32[]{:S(2)}) collective-permute-start(bf16[128,768]{1,0:T(8,128)(2,1)} %get-tuple-element.26), channel_id=1, source_target_pairs={{0,12},{4,8},{8,4},{12,0},{1,13},{5,9},{9,5},{13,1},{2,14},{6,10},... | collective-permute-start | bytes 589832 | tf_op jit(solution)/shard_map/ppermute | solution.py:22
  196.1 1.0 constant_dynamic-update-slice_fusion.8
  197.2 0.9 constant_dynamic-update-slice_fusion.12
  198.2 0.9 constant_dynamic-update-slice_fusion.11
  199.2 3.1 %collective-permute-done.16 = bf16[128,768]{1,0:T(8,128)(2,1)S(1)} collective-permute-done((bf16[128,768]{1,0:T(8,128)(2,1)}, bf16[128,768]{1,0:T(8,128)(2,1)S(1)}, u32[]{:S(2)}, u32[]{:S(2)}) %collective-permute-start.16) | collective-permute-done | bytes 196640 | tf_op jit(solution)/shard_map/ppermute | solution.py:22
  202.3 0.9 copy-done.8
  (90 shorter events, 9.7 us)
Async XLA Ops:
  0.6 2.7 %copy-start = (bf16[128,3072]{1,0:T(8,128)(2,1)S(1)}, bf16[128,3072]{1,0:T(8,128)(2,1)}, u32[]{:S(2)}) copy-start(bf16[128,3072]{1,0:T(8,128)(2,1)} %param.7) | copy-start | bytes 2359300
  0.6 6.5 %copy-start.10 = (f32[128,2]{0,1:T(2,128)S(1)}, f32[128,2]{0,1:T(2,128)}, u32[]{:S(2)}) copy-start(f32[128,2]{0,1:T(2,128)} %param.9) | copy-start | bytes 3076
  0.7 6.8 %copy-start.6 = (bf16[128,3072]{1,0:T(8,128)(2,1)S(1)}, bf16[128,3072]{1,0:T(8,128)(2,1)}, u32[]{:S(2)}) copy-start(bf16[128,3072]{1,0:T(8,128)(2,1)} %param.13) | copy-start | bytes 2359300
  3.6 7.6 %collective-permute-start = (bf16[96,768]{1,0:T(8,128)(2,1)S(1)}, bf16[96,768]{1,0:T(8,128)(2,1)S(1)}, u32[]{:S(2)}, u32[]{:S(2)}) collective-permute-start(bf16[96,768]{1,0:T(8,128)(2,1)S(1)} %get-tuple-element.46), channel_id=1, source_target_pairs={{0,1},{1,0},{2,3},{3,2},{4,5},{5,4},{6,7},{7,6},{8,9},{9,8},{10,11... | collective-permute-start | bytes 442376 | tf_op jit(solution)/shard_map/ppermute | solution.py:22
  5.3 10.8 %collective-permute-start.1 = (bf16[96,768]{1,0:T(8,128)(2,1)S(1)}, bf16[96,768]{1,0:T(8,128)(2,1)S(1)}, u32[]{:S(2)}, u32[]{:S(2)}) collective-permute-start(bf16[96,768]{1,0:T(8,128)(2,1)S(1)} %get-tuple-element.45), channel_id=1, source_target_pairs={{0,2},{1,3},{2,0},{3,1},{4,6},{5,7},{6,4},{7,5},{8,10},{9,11},{10,... | collective-permute-start | bytes 442376 | tf_op jit(solution)/shard_map/ppermute | solution.py:22
  5.6 20.4 %collective-permute-start.2 = (bf16[96,768]{1,0:T(8,128)(2,1)S(1)}, bf16[96,768]{1,0:T(8,128)(2,1)S(1)}, u32[]{:S(2)}, u32[]{:S(2)}) collective-permute-start(bf16[96,768]{1,0:T(8,128)(2,1)S(1)} %get-tuple-element.44), channel_id=1, source_target_pairs={{0,3},{1,2},{2,1},{3,0},{4,7},{5,6},{6,5},{7,4},{8,11},{9,10},{10,... | collective-permute-start | bytes 442376 | tf_op jit(solution)/shard_map/ppermute | solution.py:22
  7.7 22.2 %collective-permute-start.17 = (bf16[96,768]{1,0:T(8,128)(2,1)S(1)}, bf16[96,768]{1,0:T(8,128)(2,1)S(1)}, u32[]{:S(2)}, u32[]{:S(2)}) collective-permute-start(bf16[96,768]{1,0:T(8,128)(2,1)S(1)} %get-tuple-element.43), channel_id=1, source_target_pairs={{0,1},{1,0},{2,3},{3,2},{4,5},{5,4},{6,7},{7,6},{8,9},{9,8},{10,11... | collective-permute-start | bytes 442376 | tf_op jit(solution)/shard_map/ppermute | solution.py:22
  10.3 20.3 %collective-permute-start.18 = (bf16[96,768]{1,0:T(8,128)(2,1)S(1)}, bf16[96,768]{1,0:T(8,128)(2,1)S(1)}, u32[]{:S(2)}, u32[]{:S(2)}) collective-permute-start(bf16[96,768]{1,0:T(8,128)(2,1)S(1)} %get-tuple-element.42), channel_id=1, source_target_pairs={{0,2},{1,3},{2,0},{3,1},{4,6},{5,7},{6,4},{7,5},{8,10},{9,11},{10,... | collective-permute-start | bytes 442376 | tf_op jit(solution)/shard_map/ppermute | solution.py:22
  26.0 13.2 %collective-permute-start.3 = (bf16[288,768]{1,0:T(8,128)(2,1)S(1)}, bf16[288,768]{1,0:T(8,128)(2,1)S(1)}, u32[]{:S(2)}, u32[]{:S(2)}) collective-permute-start(bf16[288,768]{1,0:T(8,128)(2,1)S(1)} %constant_dynamic-update-slice_fusion.refs_0_), channel_id=1, source_target_pairs={{0,4},{4,0},{8,12},{12,8},{1,5},{5,1},{9,13},{13,9},{2,6},{6,2},{1... | collective-permute-start | bytes 1327112 | tf_op jit(solution)/shard_map/ppermute | solution.py:22
  27.6 21.1 %collective-permute-start.4 = (bf16[288,768]{1,0:T(8,128)(2,1)S(1)}, bf16[288,768]{1,0:T(8,128)(2,1)S(1)}, u32[]{:S(2)}, u32[]{:S(2)}) collective-permute-start(bf16[288,768]{1,0:T(8,128)(2,1)S(1)} %constant_dynamic-update-slice_fusion.refs_0_), channel_id=1, source_target_pairs={{0,8},{4,12},{8,0},{12,4},{1,9},{5,13},{9,1},{13,5},{2,10},{6,14},... | collective-permute-start | bytes 1327112 | tf_op jit(solution)/shard_map/ppermute | solution.py:22
  29.1 20.6 %collective-permute-start.5 = (bf16[288,768]{1,0:T(8,128)(2,1)S(1)}, bf16[288,768]{1,0:T(8,128)(2,1)S(1)}, u32[]{:S(2)}, u32[]{:S(2)}) collective-permute-start(bf16[288,768]{1,0:T(8,128)(2,1)S(1)} %constant_dynamic-update-slice_fusion.refs_0_), channel_id=1, source_target_pairs={{0,12},{4,8},{8,4},{12,0},{1,13},{5,9},{9,5},{13,1},{2,14},{6,10},... | collective-permute-start | bytes 1327112 | tf_op jit(solution)/shard_map/ppermute | solution.py:22
  29.9 5.2 %collective-permute-start.19 = (bf16[96,768]{1,0:T(8,128)(2,1)S(1)}, bf16[96,768]{1,0:T(8,128)(2,1)S(1)}, u32[]{:S(2)}, u32[]{:S(2)}) collective-permute-start(bf16[96,768]{1,0:T(8,128)(2,1)S(1)} %get-tuple-element.41), channel_id=1, source_target_pairs={{0,3},{1,2},{2,1},{3,0},{4,7},{5,6},{6,5},{7,4},{8,11},{9,10},{10,... | collective-permute-start | bytes 442376 | tf_op jit(solution)/shard_map/ppermute | solution.py:22
  35.1 30.2 %collective-permute-start.20 = (bf16[288,768]{1,0:T(8,128)(2,1)S(1)}, bf16[288,768]{1,0:T(8,128)(2,1)S(1)}, u32[]{:S(2)}, u32[]{:S(2)}) collective-permute-start(bf16[288,768]{1,0:T(8,128)(2,1)S(1)} %constant_dynamic-update-slice_fusion.3.refs_0_), channel_id=1, source_target_pairs={{0,4},{4,0},{8,12},{12,8},{1,5},{5,1},{9,13},{13,9},{2,6},{6,2},{1... | collective-permute-start | bytes 1327112 | tf_op jit(solution)/shard_map/ppermute | solution.py:22
  36.7 28.6 %collective-permute-start.21 = (bf16[288,768]{1,0:T(8,128)(2,1)S(1)}, bf16[288,768]{1,0:T(8,128)(2,1)S(1)}, u32[]{:S(2)}, u32[]{:S(2)}) collective-permute-start(bf16[288,768]{1,0:T(8,128)(2,1)S(1)} %constant_dynamic-update-slice_fusion.3.refs_0_), channel_id=1, source_target_pairs={{0,8},{4,12},{8,0},{12,4},{1,9},{5,13},{9,1},{13,5},{2,10},{6,14},... | collective-permute-start | bytes 1327112 | tf_op jit(solution)/shard_map/ppermute | solution.py:22
  39.2 26.1 %collective-permute-start.22 = (bf16[288,768]{1,0:T(8,128)(2,1)S(1)}, bf16[288,768]{1,0:T(8,128)(2,1)S(1)}, u32[]{:S(2)}, u32[]{:S(2)}) collective-permute-start(bf16[288,768]{1,0:T(8,128)(2,1)S(1)} %constant_dynamic-update-slice_fusion.3.refs_0_), channel_id=1, source_target_pairs={{0,12},{4,8},{8,4},{12,0},{1,13},{5,9},{9,5},{13,1},{2,14},{6,10},... | collective-permute-start | bytes 1327112 | tf_op jit(solution)/shard_map/ppermute | solution.py:22
  64.8 10.2 %collective-permute-start.6 = (bf16[384,2048]{1,0:T(8,128)(2,1)S(1)}, bf16[384,2048]{1,0:T(8,128)(2,1)S(1)}, u32[]{:S(2)}, u32[]{:S(2)}) collective-permute-start(bf16[384,2048]{1,0:T(8,128)(2,1)S(1)} %get-tuple-element.15), channel_id=1, source_target_pairs={{0,16},{16,0},{1,17},{17,1},{2,18},{18,2},{3,19},{19,3},{4,20},{20... | collective-permute-start | bytes 4718600 | tf_op jit(solution)/shard_map/ppermute | solution.py:22
  64.8 10.2 %collective-permute-start.7 = (bf16[384,2048]{1,0:T(8,128)(2,1)S(1)}, bf16[384,2048]{1,0:T(8,128)(2,1)S(1)}, u32[]{:S(2)}, u32[]{:S(2)}) collective-permute-start(bf16[384,2048]{1,0:T(8,128)(2,1)S(1)} %get-tuple-element.16), channel_id=1, source_target_pairs={{0,16},{16,0},{1,17},{17,1},{2,18},{18,2},{3,19},{19,3},{4,20},{20... | collective-permute-start | bytes 4718600 | tf_op jit(solution)/shard_map/ppermute | solution.py:22
  74.9 3.4 %collective-permute-start.23 = (bf16[384,2048]{1,0:T(8,128)(2,1)S(1)}, bf16[384,2048]{1,0:T(8,128)(2,1)S(1)}, u32[]{:S(2)}, u32[]{:S(2)}) collective-permute-start(bf16[384,2048]{1,0:T(8,128)(2,1)S(1)} %get-tuple-element.20), channel_id=1, source_target_pairs={{0,16},{16,0},{1,17},{17,1},{2,18},{18,2},{3,19},{19,3},{4,20},{20... | collective-permute-start | bytes 4718600 | tf_op jit(solution)/shard_map/ppermute | solution.py:22
  74.9 3.4 %copy-start.2 = (bf16[384,2048]{1,0:T(8,128)(2,1)}, bf16[384,2048]{1,0:T(8,128)(2,1)S(1)}, u32[]{:S(2)}) copy-start(bf16[384,2048]{1,0:T(8,128)(2,1)S(1)} %collective-permute-done.6.gate_r) | copy-start | bytes 4718596
  75.0 3.4 %copy-start.4 = (bf16[384,2048]{1,0:T(8,128)(2,1)}, bf16[384,2048]{1,0:T(8,128)(2,1)S(1)}, u32[]{:S(2)}) copy-start(bf16[384,2048]{1,0:T(8,128)(2,1)S(1)} %collective-permute-done.7.up_r) | copy-start | bytes 4718596
  78.3 1.2 copy-start.7
  100.4 6.4 %copy-start.3 = (bf16[384,2048]{1,0:T(8,128)(2,1)S(1)}, bf16[384,2048]{1,0:T(8,128)(2,1)}, u32[]{:S(2)}) copy-start(bf16[384,2048]{1,0:T(8,128)(2,1)} %copy-done.2) | copy-start | bytes 4718596
  100.4 6.4 %copy-start.5 = (bf16[384,2048]{1,0:T(8,128)(2,1)S(1)}, bf16[384,2048]{1,0:T(8,128)(2,1)}, u32[]{:S(2)}) copy-start(bf16[384,2048]{1,0:T(8,128)(2,1)} %copy-done.4) | copy-start | bytes 4718596
  103.1 19.6 %collective-permute-start.24 = (bf16[384,768]{1,0:T(8,128)(2,1)S(1)}, bf16[384,768]{1,0:T(8,128)(2,1)}, u32[]{:S(2)}, u32[]{:S(2)}) collective-permute-start(bf16[384,768]{1,0:T(8,128)(2,1)S(1)} %get-tuple-element.27), channel_id=1, source_target_pairs={{0,4},{4,0},{8,12},{12,8},{1,5},{5,1},{9,13},{13,9},{2,6},{6,2},{1... | collective-permute-start | bytes 1769480 | tf_op jit(solution)/shard_map/ppermute | solution.py:22
  104.6 40.5 %collective-permute-start.25 = (bf16[384,768]{1,0:T(8,128)(2,1)}, bf16[384,768]{1,0:T(8,128)(2,1)}, u32[]{:S(2)}, u32[]{:S(2)}) collective-permute-start(bf16[384,768]{1,0:T(8,128)(2,1)} %get-tuple-element.29), channel_id=1, source_target_pairs={{0,8},{4,12},{8,0},{12,4},{1,9},{5,13},{9,1},{13,5},{2,10},{6,14},... | collective-permute-start | bytes 1769480 | tf_op jit(solution)/shard_map/ppermute | solution.py:22
  105.8 39.2 %collective-permute-start.26 = (bf16[384,768]{1,0:T(8,128)(2,1)}, bf16[384,768]{1,0:T(8,128)(2,1)}, u32[]{:S(2)}, u32[]{:S(2)}) collective-permute-start(bf16[384,768]{1,0:T(8,128)(2,1)} %get-tuple-element.28), channel_id=1, source_target_pairs={{0,12},{4,8},{8,4},{12,0},{1,13},{5,9},{9,5},{13,1},{2,14},{6,10},... | collective-permute-start | bytes 1769480 | tf_op jit(solution)/shard_map/ppermute | solution.py:22
  119.3 28.9 %collective-permute-start.10 = (bf16[384,768]{1,0:T(8,128)(2,1)}, bf16[384,768]{1,0:T(8,128)(2,1)}, u32[]{:S(2)}, u32[]{:S(2)}) collective-permute-start(bf16[384,768]{1,0:T(8,128)(2,1)} %get-tuple-element.31), channel_id=1, source_target_pairs={{0,12},{4,8},{8,4},{12,0},{1,13},{5,9},{9,5},{13,1},{2,14},{6,10},... | collective-permute-start | bytes 1769480 | tf_op jit(solution)/shard_map/ppermute | solution.py:22
  121.3 35.3 %collective-permute-start.8 = (bf16[384,768]{1,0:T(8,128)(2,1)}, bf16[384,768]{1,0:T(8,128)(2,1)}, u32[]{:S(2)}, u32[]{:S(2)}) collective-permute-start(bf16[384,768]{1,0:T(8,128)(2,1)} %get-tuple-element.30), channel_id=1, source_target_pairs={{0,4},{4,0},{8,12},{12,8},{1,5},{5,1},{9,13},{13,9},{2,6},{6,2},{1... | collective-permute-start | bytes 1769480 | tf_op jit(solution)/shard_map/ppermute | solution.py:22
  122.7 35.4 %collective-permute-start.9 = (bf16[384,768]{1,0:T(8,128)(2,1)}, bf16[384,768]{1,0:T(8,128)(2,1)}, u32[]{:S(2)}, u32[]{:S(2)}) collective-permute-start(bf16[384,768]{1,0:T(8,128)(2,1)} %get-tuple-element.32), channel_id=1, source_target_pairs={{0,8},{4,12},{8,0},{12,4},{1,9},{5,13},{9,1},{13,5},{2,10},{6,14},... | collective-permute-start | bytes 1769480 | tf_op jit(solution)/shard_map/ppermute | solution.py:22
  146.8 13.2 %collective-permute-start.27 = (bf16[96,768]{1,0:T(8,128)(2,1)S(1)}, bf16[96,768]{1,0:T(8,128)(2,1)S(1)}, u32[]{:S(2)}, u32[]{:S(2)}) collective-permute-start(bf16[96,768]{1,0:T(8,128)(2,1)S(1)} %get-tuple-element.36), channel_id=1, source_target_pairs={{0,1},{1,0},{2,3},{3,2},{4,5},{5,4},{6,7},{7,6},{8,9},{9,8},{10,11... | collective-permute-start | bytes 442376 | tf_op jit(solution)/shard_map/ppermute | solution.py:22
  146.9 16.5 %collective-permute-start.28 = (bf16[96,768]{1,0:T(8,128)(2,1)S(1)}, bf16[96,768]{1,0:T(8,128)(2,1)S(1)}, u32[]{:S(2)}, u32[]{:S(2)}) collective-permute-start(bf16[96,768]{1,0:T(8,128)(2,1)S(1)} %get-tuple-element.35), channel_id=1, source_target_pairs={{0,2},{1,3},{2,0},{3,1},{4,6},{5,7},{6,4},{7,5},{8,10},{9,11},{10,... | collective-permute-start | bytes 442376 | tf_op jit(solution)/shard_map/ppermute | solution.py:22
  148.2 15.2 %collective-permute-start.29 = (bf16[96,768]{1,0:T(8,128)(2,1)S(1)}, bf16[96,768]{1,0:T(8,128)(2,1)S(1)}, u32[]{:S(2)}, u32[]{:S(2)}) collective-permute-start(bf16[96,768]{1,0:T(8,128)(2,1)S(1)} %get-tuple-element.34), channel_id=1, source_target_pairs={{0,3},{1,2},{2,1},{3,0},{4,7},{5,6},{6,5},{7,4},{8,11},{9,10},{10,... | collective-permute-start | bytes 442376 | tf_op jit(solution)/shard_map/ppermute | solution.py:22
  159.8 7.5 %collective-permute-start.11 = (bf16[96,768]{1,0:T(8,128)(2,1)S(1)}, bf16[96,768]{1,0:T(8,128)(2,1)S(1)}, u32[]{:S(2)}, u32[]{:S(2)}) collective-permute-start(bf16[96,768]{1,0:T(8,128)(2,1)S(1)} %get-tuple-element.40), channel_id=1, source_target_pairs={{0,1},{1,0},{2,3},{3,2},{4,5},{5,4},{6,7},{7,6},{8,9},{9,8},{10,11... | collective-permute-start | bytes 442376 | tf_op jit(solution)/shard_map/ppermute | solution.py:22
  159.9 8.7 %collective-permute-start.12 = (bf16[96,768]{1,0:T(8,128)(2,1)S(1)}, bf16[96,768]{1,0:T(8,128)(2,1)S(1)}, u32[]{:S(2)}, u32[]{:S(2)}) collective-permute-start(bf16[96,768]{1,0:T(8,128)(2,1)S(1)} %get-tuple-element.39), channel_id=1, source_target_pairs={{0,2},{1,3},{2,0},{3,1},{4,6},{5,7},{6,4},{7,5},{8,10},{9,11},{10,... | collective-permute-start | bytes 442376 | tf_op jit(solution)/shard_map/ppermute | solution.py:22
  160.0 16.1 %collective-permute-start.13 = (bf16[96,768]{1,0:T(8,128)(2,1)S(1)}, bf16[96,768]{1,0:T(8,128)(2,1)S(1)}, u32[]{:S(2)}, u32[]{:S(2)}) collective-permute-start(bf16[96,768]{1,0:T(8,128)(2,1)S(1)} %get-tuple-element.38), channel_id=1, source_target_pairs={{0,3},{1,2},{2,1},{3,0},{4,7},{5,6},{6,5},{7,4},{8,11},{9,10},{10,... | collective-permute-start | bytes 442376 | tf_op jit(solution)/shard_map/ppermute | solution.py:22
  164.8 28.9 %collective-permute-start.30 = (bf16[128,768]{1,0:T(8,128)(2,1)}, bf16[128,768]{1,0:T(8,128)(2,1)}, u32[]{:S(2)}, u32[]{:S(2)}) collective-permute-start(bf16[128,768]{1,0:T(8,128)(2,1)} %get-tuple-element.53), channel_id=1, source_target_pairs={{0,4},{4,0},{8,12},{12,8},{1,5},{5,1},{9,13},{13,9},{2,6},{6,2},{1... | collective-permute-start | bytes 589832 | tf_op jit(solution)/shard_map/ppermute | solution.py:22
  165.6 32.6 %collective-permute-start.31 = (bf16[128,768]{1,0:T(8,128)(2,1)}, bf16[128,768]{1,0:T(8,128)(2,1)S(1)}, u32[]{:S(2)}, u32[]{:S(2)}) collective-permute-start(bf16[128,768]{1,0:T(8,128)(2,1)} %get-tuple-element.53), channel_id=1, source_target_pairs={{0,8},{4,12},{8,0},{12,4},{1,9},{5,13},{9,1},{13,5},{2,10},{6,14},... | collective-permute-start | bytes 589832 | tf_op jit(solution)/shard_map/ppermute | solution.py:22
  167.3 31.8 %collective-permute-start.32 = (bf16[128,768]{1,0:T(8,128)(2,1)}, bf16[128,768]{1,0:T(8,128)(2,1)S(1)}, u32[]{:S(2)}, u32[]{:S(2)}) collective-permute-start(bf16[128,768]{1,0:T(8,128)(2,1)} %get-tuple-element.53), channel_id=1, source_target_pairs={{0,12},{4,8},{8,4},{12,0},{1,13},{5,9},{9,5},{13,1},{2,14},{6,10},... | collective-permute-start | bytes 589832 | tf_op jit(solution)/shard_map/ppermute | solution.py:22
  177.5 19.6 %collective-permute-start.14 = (bf16[128,768]{1,0:T(8,128)(2,1)}, bf16[128,768]{1,0:T(8,128)(2,1)}, u32[]{:S(2)}, u32[]{:S(2)}) collective-permute-start(bf16[128,768]{1,0:T(8,128)(2,1)} %get-tuple-element.26), channel_id=1, source_target_pairs={{0,4},{4,0},{8,12},{12,8},{1,5},{5,1},{9,13},{13,9},{2,6},{6,2},{1... | collective-permute-start | bytes 589832 | tf_op jit(solution)/shard_map/ppermute | solution.py:22
  178.3 19.8 %collective-permute-start.15 = (bf16[128,768]{1,0:T(8,128)(2,1)}, bf16[128,768]{1,0:T(8,128)(2,1)}, u32[]{:S(2)}, u32[]{:S(2)}) collective-permute-start(bf16[128,768]{1,0:T(8,128)(2,1)} %get-tuple-element.26), channel_id=1, source_target_pairs={{0,8},{4,12},{8,0},{12,4},{1,9},{5,13},{9,1},{13,5},{2,10},{6,14},... | collective-permute-start | bytes 589832 | tf_op jit(solution)/shard_map/ppermute | solution.py:22
  193.7 8.5 %collective-permute-start.16 = (bf16[128,768]{1,0:T(8,128)(2,1)}, bf16[128,768]{1,0:T(8,128)(2,1)S(1)}, u32[]{:S(2)}, u32[]{:S(2)}) collective-permute-start(bf16[128,768]{1,0:T(8,128)(2,1)} %get-tuple-element.26), channel_id=1, source_target_pairs={{0,12},{4,8},{8,4},{12,0},{1,13},{5,9},{9,5},{13,1},{2,14},{6,10},... | collective-permute-start | bytes 589832 | tf_op jit(solution)/shard_map/ppermute | solution.py:22
  196.1 7.0 %copy-start.1 = (bf16[128,3072]{1,0:T(8,128)(2,1)S(1)}, bf16[128,3072]{1,0:T(8,128)(2,1)}, u32[]{:S(2)}) copy-start(bf16[128,3072]{1,0:T(8,128)(2,1)} %param.7) | copy-start | bytes 2359300
  199.2 3.1 %copy-start.9 = (bf16[128,3072]{1,0:T(8,128)(2,1)}, bf16[128,3072]{1,0:T(8,128)(2,1)S(1)}, u32[]{:S(2)}) copy-start(bf16[128,3072]{1,0:T(8,128)(2,1)S(1)} %constant_dynamic-update-slice_fusion.6) | copy-start | bytes 2359300
  202.3 0.9 copy-start.8

commit v2 on v1

--- a/solution.py
+++ b/solution.py
@@ -73,12 +73,13 @@
         send[...] = total.astype(BF)
 
 
-def pre_acts(t, own, parts, gate_mat, up_mat, block):
-    depth, hidden = gate_mat.shape
+def pre_acts(t, own, parts, gate_mat, up_mat, block, start, stop):
+    depth, hidden = gate_mat.shape[0], stop - start
+    first = start // block
     cap = own.shape[0]
     n = len(parts)
     rows = cap + parts[0].shape[0]
-    weight = pl.BlockSpec((depth, block), lambda i, *_: (0, i))
+    weight = pl.BlockSpec((depth, block), lambda i, *_: (0, first + i))
     out = pl.BlockSpec((rows, block), lambda i, *_: (0, i))
     return pl.pallas_call(
         pre_act_kernel,
@@ -90,7 +91,7 @@
             scratch_shapes=[pltpu.VMEM((n, rows, depth // n), BF)],
         ),
         out_shape=[sds((rows, hidden), F32)] * 2 + [sds((rows, hidden), BF)] * 2,
-        compiler_params=params(48),
+        compiler_params=params(40),
         cost_estimate=cost(4 * rows * depth * hidden, 4 * depth * hidden),
         name="pre_acts",
     )(t, own, *parts, gate_mat, up_mat)
@@ -111,11 +112,12 @@
     send[...] = total.astype(BF)
 
 
-def grad_hiddens(t, own, parts, down_mat, block):
-    hidden, depth = down_mat.shape
+def grad_hiddens(t, own, parts, down_mat, block, start, stop):
+    depth, hidden = down_mat.shape[1], stop - start
+    first = start // block
     n = len(parts)
     rows = own.shape[0] + parts[0].shape[0]
-    weight = pl.BlockSpec((block, depth), lambda i, *_: (i, 0))
+    weight = pl.BlockSpec((block, depth), lambda i, *_: (first + i, 0))
     out = pl.BlockSpec((rows, block), lambda i, *_: (0, i))
     return pl.pallas_call(
         grad_hidden_kernel,
@@ -127,7 +129,7 @@
             scratch_shapes=[pltpu.VMEM((n, rows, depth // n), BF)],
         ),
         out_shape=[sds((rows, hidden), F32), sds((rows, hidden), BF)],
-        compiler_params=params(48),
+        compiler_params=params(40),
         cost_estimate=cost(2 * rows * depth * hidden, 2 * depth * hidden),
         name="grad_hidden",
     )(t, own, *parts, down_mat)
@@ -136,111 +138,182 @@
 STRIP = 32
 
 
-def project_kernel(t_ref, gate_o, up_o, gate_r, up_r, down_w, pieces, kept, hidden_ref):
-    step = pl.program_id(0)
-
-    @pl.when(step == 0)
-    def _():
-        @pl.loop(0, hidden_ref.shape[0] // STRIP)
-        def _(i):
-            here = pl.ds(pl.multiple_of(i * STRIP, STRIP), STRIP)
+def hidden_strips(*refs):
+    groups, hidden_ref = refs[:-1], refs[-1]
+
+    @pl.loop(0, hidden_ref.shape[0] // STRIP)
+    def _(i):
+        here = pl.ds(pl.multiple_of(i * STRIP, STRIP), STRIP)
+        at = 0
+        for g in range(0, len(groups), 4):
+            gate_o, up_o, gate_r, up_r = groups[g : g + 4]
+            width = gate_o.shape[1]
             gate = gate_o[here, :] + gate_r[here, :].astype(F32)
             up = up_o[here, :] + up_r[here, :].astype(F32)
-            hidden_ref[here, :] = (gate * jax.nn.sigmoid(gate) * up).astype(BF)
-
-    total = dot_nn(hidden_ref[...], down_w[...])
-
-    @pl.when(step < pl.num_programs(0) - 1)
-    def _():
-        pieces[0] = total.astype(BF)
-
-    @pl.when(step == pl.num_programs(0) - 1)
-    def _():
-        kept[...] = total
-
-
-def projected(t, n, gate_o, up_o, gate_r, up_r, down_mat):
-    hidden, depth = down_mat.shape
-    rows = gate_o.shape[0]
-    quarter = depth // n
-
-    def which(i, t):
-        return t[0] ^ ((i + 1) % n)
-
-    return pl.pallas_call(
-        project_kernel,
-        grid_spec=pltpu.PrefetchScalarGridSpec(
-            num_scalar_prefetch=1,
-            grid=(n,),
-            in_specs=[whole(gate_o.shape)] * 4
-            + [pl.BlockSpec((hidden, quarter), lambda i, t: (0, which(i, t)))],
-            out_specs=[
-                pl.BlockSpec((1, rows, quarter), lambda i, t: (jnp.minimum(i, n - 2), 0, 0)),
-                pl.BlockSpec((rows, quarter), lambda i, t: (0, 0)),
-            ],
-            scratch_shapes=[pltpu.VMEM((rows, hidden), BF)],
-        ),
-        out_shape=[sds((n - 1, rows, quarter), BF), sds((rows, quarter), F32)],
-        compiler_params=params(48),
-        cost_estimate=cost(2 * rows * depth * hidden, 2 * depth * hidden),
-        name="project",
-    )(t, gate_o, up_o, gate_r, up_r, down_mat)
-
-
-def grad_rows_kernel(
-    t_ref, gate_o, up_o, gate_r, up_r, gh_o, gh_r, gate_w, up_w, pieces, kept, gg_ref, gu_ref
-):
-    step = pl.program_id(0)
-
-    @pl.when(step == 0)
-    def _():
-        @pl.loop(0, gg_ref.shape[0] // STRIP)
-        def _(i):
-            here = pl.ds(pl.multiple_of(i * STRIP, STRIP), STRIP)
+            hidden_ref[here, at : at + width] = (gate * jax.nn.sigmoid(gate) * up).astype(BF)
+            at += width
+
+
+def grad_strips(*refs):
+    refs, (gg_ref, gu_ref) = refs[:-2], refs[-2:]
+    share = len(refs) // 6
+    groups, grads = refs[: 4 * share], refs[4 * share :]
+
+    @pl.loop(0, gg_ref.shape[0] // STRIP)
+    def _(i):
+        here = pl.ds(pl.multiple_of(i * STRIP, STRIP), STRIP)
+        at = 0
+        for g in range(0, len(groups), 4):
+            gate_o, up_o, gate_r, up_r = groups[g : g + 4]
+            gh_o, gh_r = grads[g // 2 : g // 2 + 2]
+            cols = slice(at, at + gate_o.shape[1])
             gate = gate_o[here, :] + gate_r[here, :].astype(F32)
             up = up_o[here, :] + up_r[here, :].astype(F32)
             grad = gh_o[here, :] + gh_r[here, :].astype(F32)
             s = jax.nn.sigmoid(gate)
-            gg_ref[here, :] = (grad * up * (s * (1.0 + gate * (1.0 - s)))).astype(BF)
-            gu_ref[here, :] = (grad * (gate * s)).astype(BF)
-
-    total = dot_nt(gg_ref[...], gate_w[...]) + dot_nt(gu_ref[...], up_w[...])
-
-    @pl.when(step < pl.num_programs(0) - 1)
-    def _():
-        pieces[0] = total.astype(BF)
-
-    @pl.when(step == pl.num_programs(0) - 1)
-    def _():
-        kept[...] = total
-
-
-def grad_rows(t, n, gate_o, up_o, gate_r, up_r, gh_o, gh_r, gate_mat, up_mat):
-    depth, hidden = gate_mat.shape
-    rows = gate_o.shape[0]
-    quarter = depth // n
-
-    def which(i, t):
-        return t[0] ^ ((i + 1) % n)
-
-    weight = pl.BlockSpec((quarter, hidden), lambda i, t: (which(i, t), 0))
+            gg_ref[here, cols] = (grad * up * (s * (1.0 + gate * (1.0 - s)))).astype(BF)
+            gu_ref[here, cols] = (grad * (gate * s)).astype(BF)
+            at += gate_o.shape[1]
+
+
+def first_piece_kernel(make, product, n_in, n_w, n_act):
+    def kernel(t_ref, *refs):
+        ins, refs = refs[:n_in], refs[n_in:]
+        weights, refs = refs[:n_w], refs[n_w:]
+        halves, acts = refs[:2], refs[2:]
+
+        @pl.when(pl.program_id(0) == 0)
+        def _():
+            make(*ins, *acts)
+
+        total = product(acts, weights).astype(BF)
+        for h in range(2):
+
+            @pl.when(pl.program_id(0) == h)
+            def _():
+                halves[h][...] = total
+
+    return kernel
+
+
+def rest_kernel(product, n_act, n_w, order):
+    def kernel(t_ref, *refs):
+        acts, refs = refs[:n_act], refs[n_act:]
+        weights, refs = refs[:n_w], refs[n_w:]
+        added, outs = (refs[:2], refs[2:]) if 1 in order else ((), refs)
+        total = product(acts, weights)
+        half = total.shape[1] // 2
+        for i, j in enumerate(order):
+
+            @pl.when(pl.program_id(0) == i)
+            def _():
+                if j == 0:
+                    outs[i][...] = total
+                elif j == 1:
+                    outs[i][:, :half] = total[:, :half].astype(BF)
+                    outs[i][:, half:] = (total[:, half:] + added[1][...].astype(F32)).astype(BF)
+                else:
+                    outs[i][:, :half] = (total[:, :half] + added[0][...].astype(F32)).astype(BF)
+                    outs[i][:, half:] = total[:, half:].astype(BF)
+
+    return kernel
+
+
+def forward_product(acts, weights):
+    return dot_nn(acts[0][...], weights[0][...])
+
+
+def backward_product(acts, weights):
+    return dot_nt(acts[0][...], weights[0][...]) + dot_nt(acts[1][...], weights[1][...])
+
+
+def weight_specs(mats, nn, block, index):
+    if nn:
+        return [pl.BlockSpec((m.shape[0], block), lambda i, t: (0, index(i, t))) for m in mats]
+    return [pl.BlockSpec((block, m.shape[1]), lambda i, t: (index(i, t), 0)) for m in mats]
+
+
+def sizes(mats, nn):
+    return mats[0].shape if nn else mats[0].shape[::-1]
+
+
+def first_piece(t, n, make, product, nn, ins, mats, mib, name):
+    hidden, depth = sizes(mats, nn)
+    rows = ins[0].shape[0]
+    half = depth // n // 2
+    acts = [sds((rows, hidden), BF)] * len(mats)
     return pl.pallas_call(
-        grad_rows_kernel,
+        first_piece_kernel(make, product, len(ins), len(mats), len(acts)),
         grid_spec=pltpu.PrefetchScalarGridSpec(
             num_scalar_prefetch=1,
-            grid=(n,),
-            in_specs=[whole(gate_o.shape)] * 6 + [weight, weight],
-            out_specs=[
-                pl.BlockSpec((1, rows, quarter), lambda i, t: (jnp.minimum(i, n - 2), 0, 0)),
-                pl.BlockSpec((rows, quarter), lambda i, t: (0, 0)),
-            ],
-            scratch_shapes=[pltpu.VMEM((rows, hidden), BF)] * 2,
+            grid=(2,),
+            in_specs=[whole(x.shape) for x in ins]
+            + weight_specs(mats, nn, half, lambda i, t: (t[0] ^ 3) * 2 + i),
+            out_specs=[pl.BlockSpec((rows, half), lambda i, t: (0, 0))] * 2
+            + [pl.BlockSpec((rows, hidden), lambda i, t: (0, 0))] * len(acts),
         ),
-        out_shape=[sds((n - 1, rows, quarter), BF), sds((rows, quarter), F32)],
-        compiler_params=params(52),
-        cost_estimate=cost(4 * rows * depth * hidden, 4 * depth * hidden),
-        name="grad_rows",
-    )(t, gate_o, up_o, gate_r, up_r, gh_o, gh_r, gate_mat, up_mat)
+        out_shape=[sds((rows, half), BF)] * 2 + acts,
+        compiler_params=params(mib),
+        cost_estimate=cost(2 * rows * depth * hidden * len(mats) // n, 2 * depth * hidden),
+        name=name,
+    )(t, *ins, *mats)
+
+
+def rest_pieces(t, n, product, nn, acts, mats, added, order, mib, name):
+    hidden, depth = sizes(mats, nn)
+    rows = acts[0].shape[0]
+    quarter = depth // n
+
+    def index(i, t):
+        j = order[-1]
+        for k in range(len(order) - 2, -1, -1):
+            j = jnp.where(i == k, order[k], j)
+        return t[0] ^ j
+
+    return pl.pallas_call(
+        rest_kernel(product, len(acts), len(mats), order),
+        grid_spec=pltpu.PrefetchScalarGridSpec(
+            num_scalar_prefetch=1,
+            grid=(len(order),),
+            in_specs=[whole(x.shape) for x in acts]
+            + weight_specs(mats, nn, quarter, index)
+            + [whole(x.shape) for x in added],
+            out_specs=[pl.BlockSpec((rows, quarter), lambda i, t: (0, 0))] * len(order),
+        ),
+        out_shape=[sds((rows, quarter), F32 if j == 0 else BF) for j in order],
+        compiler_params=params(mib),
+        cost_estimate=cost(
+            2 * rows * quarter * len(order) * hidden * len(mats), 2 * quarter * len(order) * hidden
+        ),
+        name=name,
+    )(t, *acts, *mats, *added)
+
+
+def assemble_kernel(t_ref, *refs):
+    parts, out = refs[:-1], refs[-1]
+    width = parts[0].shape[1]
+    for j, part in enumerate(parts):
+        out[:, pl.ds(pl.multiple_of((t_ref[0] ^ j) * width, 128), width)] = part[...]
+
+
+def assemble(t, parts):
+    rows, width = parts[0].shape
+    return pl.pallas_call(
+        assemble_kernel,
+        grid_spec=pltpu.PrefetchScalarGridSpec(
+            num_scalar_prefetch=1,
+            grid=(1,),
+            in_specs=[whole(p.shape) for p in parts],
+            out_specs=pl.BlockSpec((rows, width * len(parts)), lambda i, t: (0, 0)),
+        ),
+        out_shape=sds((rows, width * len(parts)), parts[0].dtype),
+        compiler_params=params(16),
+        name="assemble",
+    )(t, *parts)
+
+
+def after(value, *others):
+    return lax.optimization_barrier((value,) + others)[0]
 
 
 def local(tokens, expert_ids, gate_values, w_gate, w_up, w_down, cotangent):
@@ -253,7 +326,10 @@
     experts = groups
     cap = min(tok_rows, 3 * tok_rows // experts)
     quarter = depth // n
-    gate_mat, up_mat, down_mat = w_gate[0], w_up[0], w_down[0]
+    half = quarter // 2
+    gate_mat, up_mat, down_mat = (
+        pltpu.with_memory_space_constraint(w[0], pltpu.HBM) for w in (w_gate, w_up, w_down)
+    )
 
     slot_of = slot_index(expert_ids, experts)
     order = (expert_ids ^ z) * cap + slot_of
@@ -267,63 +343,99 @@
         keepdims=True,
     )
 
-    def dispatch(source, scale):
+    def outgoing(source, scale):
         part = lax.dynamic_slice(source, (0, t * quarter), (tok_rows, quarter))
         out = dot_nn(spread[cap:], part)
         own = dot_nn(spread[:cap], source)
         if scale is not None:
             out, own = out * scale[cap:], own * scale[:cap]
-        out, own = out.astype(BF), own.astype(BF)
-        arrived = jnp.concatenate(
+        return own.astype(BF), out.astype(BF)
+
+    def over_z(out):
+        return jnp.concatenate(
             [exchange(out[(k - 1) * cap : k * cap], "expert", k) for k in range(1, groups)], axis=0
         )
-        return own, arrived
-
-    tok_own, tok_part = dispatch(tokens, None)
-    tok_parts = [tok_part] + [exchange(tok_part, "tensor", j) for j in range(1, n)]
-    cot_own, cot_part = dispatch(cotangent, slot_gate)
-    cot_parts = [cot_part] + [exchange(cot_part, "tensor", j) for j in range(1, n)]
-
-    gate_o, up_o, gate_s, up_s = pre_acts(t_arr, tok_own, tok_parts, gate_mat, up_mat, 512)
-    gate_r, up_r = exchange(gate_s, "wide", 1), exchange(up_s, "wide", 1)
-    gh_o, gh_s = grad_hiddens(t_arr, cot_own, cot_parts, down_mat, 512)
-    gh_r = exchange(gh_s, "wide", 1)
-
-    def send_back(pieces, kept):
-        total = kept
-        for j in range(1, n):
-            total = total + exchange(pieces[j - 1], "tensor", j).astype(F32)
+
+    tok_own, tok_out = outgoing(tokens, None)
+    cot_own, cot_out = outgoing(cotangent, slot_gate)
+    tok_part = over_z(tok_out)
+    tok_x, tok_y = exchange(tok_part, "tensor", 1), exchange(tok_part, "tensor", 2)
+    cot_part = over_z(after(cot_out, tok_part))
+    tok_d = jnp.concatenate(
+        [exchange(tok_y[:, :half], "tensor", 1), exchange(tok_x[:, half:], "tensor", 2)], axis=1
+    )
+    tok_parts = [tok_part, tok_x, tok_y, tok_d]
+    cot_ready = after(cot_part, tok_d)
+    cot_parts = [cot_part] + [exchange(cot_ready, "tensor", j) for j in range(1, n)]
+
+    acts_in = ()
+    hidden_here = gate_mat.shape[1]
+    turn = after(t_arr, cot_part)
+    for start in range(0, hidden_here, hidden_here // 2):
+        if start:
+            turn = after(t_arr, *cot_parts[1:3])
+        gate_o, up_o, gate_s, up_s = pre_acts(
+            turn, tok_own, tok_parts, gate_mat, up_mat, 512, start, start + hidden_here // 2
+        )
+        acts_in += (gate_o, up_o, exchange(gate_s, "wide", 1), exchange(up_s, "wide", 1))
+
+    def sum_back(rest, keep):
+        total = keep
+        for j, piece in zip((1, 2), rest):
+            total = total + exchange(piece, "tensor", j).astype(F32)
         total = total.astype(BF)
         back = [total[:cap]] + [
             exchange(total[k * cap : (k + 1) * cap], "expert", k) for k in range(1, groups)
         ]
         return jnp.concatenate(back, axis=0)
 
-    def spread_out(part):
-        got = [part] + [exchange(part, "tensor", j) for j in range(1, n)]
-        out = jnp.zeros((tok_rows, depth), part.dtype)
-        for j in range(n):
-            out = lax.dynamic_update_slice(out, got[j], (0, (t ^ j) * quarter))
-        return out
+    def gathered(part):
+        return assemble(t_arr, [part] + [exchange(part, "tensor", j) for j in range(1, n)])
 
     gather = [(order[:, k][:, None] == cells[None, :]).astype(BF) for k in range(2)]
-    pieces, kept = projected(t_arr, n, gate_o, up_o, gate_r, up_r, down_mat)
-    returned = send_back(pieces, kept)
+
+    d_a, d_b, hidden = first_piece(
+        t_arr, n, hidden_strips, forward_product, True, acts_in, [down_mat], 36, "project_first"
+    )
+    added = [exchange(d_a, "tensor", 1), exchange(d_b, "tensor", 2)]
+    gh_in = ()
+    for start in range(0, hidden_here, hidden_here // 2):
+        turn = after(t_arr, *added) if start else after(t_arr, hidden)
+        gh_o, gh_s = grad_hiddens(
+            turn, cot_own, cot_parts, down_mat, 512, start, start + hidden_here // 2
+        )
+        gh_in += (gh_o, exchange(gh_s, "wide", 1))
+    to_x, to_y, keep = rest_pieces(
+        t_arr, n, forward_product, True, [hidden], [down_mat], added, (1, 2, 0), 34, "project_rest"
+    )
+
+    e_a, e_b, grad_g, grad_u = first_piece(
+        t_arr, n, grad_strips, backward_product, False, acts_in + gh_in,
+        [gate_mat, up_mat], 36, "rows_first",
+    )
+    gadded = [exchange(e_a, "tensor", 1), exchange(e_b, "tensor", 2)]
+    (gkeep,) = rest_pieces(
+        t_arr, n, backward_product, False, [grad_g, grad_u], [gate_mat, up_mat], [], (0,), 47,
+        "rows_kept",
+    )
+    gto_x, gto_y = rest_pieces(
+        after(t_arr, gkeep), n, backward_product, False, [grad_g, grad_u], [gate_mat, up_mat], gadded, (1, 2),
+        47, "rows_rest",
+    )
+
+    returned = sum_back((to_x, to_y), after(keep, e_a))
     chosen = [dot_nn(g, returned) for g in gather]
     layer_part = (gate_values[:, 0:1] * chosen[0] + gate_values[:, 1:2] * chosen[1]).astype(BF)
-    layer_out = spread_out(layer_part)
+    layer_out = gathered(layer_part)
     cot_here = lax.dynamic_slice(cotangent, (0, t * quarter), (tok_rows, quarter)).astype(F32)
-    gate_grad = lax.psum(
-        jnp.stack([jnp.sum(cot_here * c, axis=1) for c in chosen], axis=1), ("wide", "tensor")
-    )
-
-    gpieces, gkept = grad_rows(
-        t_arr, n, gate_o, up_o, gate_r, up_r, gh_o, gh_r, gate_mat, up_mat
-    )
-    greturned = send_back(gpieces, gkept)
+    gate_grad = jnp.stack([jnp.sum(cot_here * c, axis=1) for c in chosen], axis=0)
+    for axis, bit in (("wide", 1), ("tensor", 1), ("tensor", 2)):
+        gate_grad = gate_grad + exchange(gate_grad, axis, bit)
+
+    greturned = sum_back((gto_x, gto_y), gkeep)
     grad_part = (dot_nn(gather[0], greturned) + dot_nn(gather[1], greturned)).astype(BF)
-    token_grad = spread_out(grad_part)
-    return (layer_out, token_grad, gate_grad)
+    token_grad = gathered(grad_part)
+    return (layer_out, token_grad, gate_grad.T)
 
 
 def plain_local(tokens, expert_ids, gate_values, w_gate, w_up, w_down, cotangent):

time: 204 us -> 170 us (0.83)
  waiting for transfers between devices: 73 us -> 54.1 us
  blocking collectives: 14.4 us -> 0 us
  local copies, waits for them, and re-layouts: 9.6 us -> 0.6 us
  Pallas kernels: 56.8 us -> 62.2 us
  starting transfers between devices: 38.4 us -> 43.6 us
  other arithmetic: 6.08 us -> 3.59 us
    ppermute x33 -> x42, waiting for transfers between devices: 73 us -> 54.1 us  [exchange(): return lax.ppermute(array, axis, [(i, i ^ bit) for i in range(size)])]
    psum x1 -> x0, blocking collectives: 14.4 us -> none  [local(): lax.psum(jnp.stack([jnp.sum(cot_here * c, axis=1) for c in chosen], axis=...]
    ppermute x33 -> x42, starting transfers between devices: 38.4 us -> 43.6 us  [exchange(): return lax.ppermute(array, axis, [(i, i ^ bit) for i in range(size)])]
    squeeze x2 -> x0, local copies, waits for them, and re-layouts: 3.94 us -> none  [send_back(): total = total + exchange(pieces[j - 1], 'tensor', j).astype(F32)]
    dynamic_update_slice x6 -> x0, local copies, waits for them, and re-layouts: 2.97 us -> none  [spread_out(): out = lax.dynamic_update_slice(out, got[j], (0, (t ^ j) * quarter))]
    convert_element_type x2, other arithmetic: 3.34 us -> 0.42 us  [sum_back(): total = total.astype(BF)]
    pallas_call x2 -> x7, Pallas kernels: 32.1 us -> 34.9 us  [the longest x3 20.8 us: rest_pieces(): pl.pallas_call(rest_kernel(product, len(acts), len(mats), order), grid_sp...]
    pallas_call x1 -> x2, Pallas kernels: 15 us -> 17.2 us  [pre_acts(): pl.pallas_call(pre_act_kernel, grid_spec=pltpu.PrefetchScalarGridSpec(num...]
  transfers between devices with their start and end apart: 33 -> 42, of which waited for: 13 -> 20; matrix products, arithmetic and copies ran while one was open for 6% -> 3% of each run, Pallas kernels for 18% -> 36%
where the time goes in v2:
time: 170 us; the launch traced here: 169 us
  Pallas kernels  62.2 us (37%)
  waiting for transfers between devices  54.1 us (32%)
  starting transfers between devices  43.6 us (26%)
  other arithmetic  3.59 us (2%)
  matrix products  3.42 us (2%)
    ppermute x42, waiting for transfers between devices, exchange(): return lax.ppermute(array, axis, [(i, i ^ bit) for i in range(size)])  54.1 us
    ppermute x42, starting transfers between devices, exchange(): return lax.ppermute(array, axis, [(i, i ^ bit) for i in range(size)])  43.6 us
    pallas_call x3, Pallas kernels, rest_pieces(): pl.pallas_call(rest_kernel(product, len(acts), len(mats), order), grid_sp...  20.8 us
    pallas_call x2, Pallas kernels, pre_acts(): pl.pallas_call(pre_act_kernel, grid_spec=pltpu.PrefetchScalarGridSpec(num...  17.2 us
    pallas_call x2, Pallas kernels, first_piece(): pl.pallas_call(first_piece_kernel(make, product, len(ins), len(mats), len...  12.2 us
    pallas_call x2, Pallas kernels, grad_hiddens(): pl.pallas_call(grad_hidden_kernel, grid_spec=pltpu.PrefetchScalarGridSpec...  10.1 us
    dot_general x8, matrix products, dot_nn(): return jnp.dot(a, b, preferred_element_type=F32)  3.42 us
  transfers between devices with their start and end apart: 42, of which 20 were waited for; matrix products, arithmetic and copies ran while one was open for 3% of the time, Pallas kernels for 36%

profile of v2, /device:TPU:16, one launch (start us, length us, event | category | flops | bytes accessed | tf_op | source)
XLA Modules:
  0.0 168.6 jit_solution(10912464315800386805)
XLA Ops:
  3.6 1.6 collective-permute-start
  5.6 1.6 collective-permute-start.2
  7.7 2.7 %collective-permute-done = bf16[96,768]{1,0:T(8,128)(2,1)S(1)} collective-permute-done((bf16[96,768]{1,0:T(8,128)(2,1)S(1)}, bf16[96,768]{1,0:T(8,128)(2,1)S(1)}, u32[]{:S(2)}, u32[]{:S(2)}) %collective-permute-start) | collective-permute-done | bytes 147488 | tf_op jit(solution)/shard_map/ppermute | solution.py:22
  10.4 5.8 %collective-permute-done.1 = bf16[96,768]{1,0:T(8,128)(2,1)S(1)} collective-permute-done((bf16[96,768]{1,0:T(8,128)(2,1)S(1)}, bf16[96,768]{1,0:T(8,128)(2,1)S(1)}, u32[]{:S(2)}, u32[]{:S(2)}) %collective-permute-start.1) | collective-permute-done | bytes 147488 | tf_op jit(solution)/shard_map/ppermute | solution.py:22
  16.2 3.8 %collective-permute-done.2 = bf16[96,768]{1,0:T(8,128)(2,1)S(1)} collective-permute-done((bf16[96,768]{1,0:T(8,128)(2,1)S(1)}, bf16[96,768]{1,0:T(8,128)(2,1)S(1)}, u32[]{:S(2)}, u32[]{:S(2)}) %collective-permute-start.2) | collective-permute-done | bytes 147488 | tf_op jit(solution)/shard_map/ppermute | solution.py:22
  20.0 1.6 collective-permute-start.7
  21.6 1.5 collective-permute-start.6
  23.2 1.9 %collective-permute-start.4 = (bf16[96,768]{1,0:T(8,128)(2,1)S(1)}, bf16[96,768]{1,0:T(8,128)(2,1)S(1)}, u32[]{:S(2)}, u32[]{:S(2)}) collective-permute-start(bf16[96,768]{1,0:T(8,128)(2,1)S(1)} %get-tuple-element.79), channel_id=1, source_target_pairs={{0,2},{1,3},{2,0},{3,1},{4,6},{5,7},{6,4},{7,5},{8,10},{9,11},{10,... | collective-permute-start | bytes 442376 | tf_op jit(solution)/shard_map/ppermute | solution.py:22
  25.4 1.6 collective-permute-start.5
  27.0 2.9 %collective-permute-done.3 = bf16[96,768]{1,0:T(8,128)(2,1)S(1)} collective-permute-done((bf16[96,768]{1,0:T(8,128)(2,1)S(1)}, bf16[96,768]{1,0:T(8,128)(2,1)S(1)}, u32[]{:S(2)}, u32[]{:S(2)}) %collective-permute-start.3) | collective-permute-done | bytes 147488 | tf_op jit(solution)/shard_map/ppermute | solution.py:22
  30.0 1.0 collective-permute-done.7.refs_2_
  31.0 1.6 collective-permute-start.8
  32.6 1.5 collective-permute-done.4
  34.8 3.2 %collective-permute-done.5 = bf16[96,768]{1,0:T(8,128)(2,1)S(1)} collective-permute-done((bf16[96,768]{1,0:T(8,128)(2,1)S(1)}, bf16[96,768]{1,0:T(8,128)(2,1)S(1)}, u32[]{:S(2)}, u32[]{:S(2)}) %collective-permute-start.5) | collective-permute-done | bytes 147488 | tf_op jit(solution)/shard_map/ppermute | solution.py:22
  38.0 2.2 %collective-permute-done.9 = bf16[288,384]{1,0:T(8,128)(2,1)S(1)} collective-permute-done((bf16[288,384]{1,0:T(8,128)(2,1)S(1)}, bf16[288,384]{1,0:T(8,128)(2,1)S(1)}, u32[]{:S(2)}, u32[]{:S(2)}) %collective-permute-start.9) | collective-permute-done | bytes 221216 | tf_op jit(solution)/shard_map/ppermute | solution.py:22
  41.3 8.6 %pre_acts.2 = (f32[384,1024]{1,0:T(8,128)S(1)}, f32[384,1024]{1,0:T(8,128)S(1)}, bf16[384,1024]{1,0:T(8,128)(2,1)S(1)}, bf16[384,1024]{1,0:T(8,128)(2,1)S(1)}) custom-call(s32[1]{0:T(128)} %bitcast.t_ref, bf16[96,3072]{1,0:T(8,128)(2,1)S(1)} %convolution_convert_fusion.own_ref, bf16[288,768]{1,0:T(8,128)(2,1)S(1)} %constant_dynamic-update-slice_fusion.refs_0_, ...), custom_call_target="tpu_custom_call" | custom-call | flops 4831838208 | bytes 12582912 | tf_op jit(solution)/shard_map/pre_acts/pallas_call | solution.py:84
  50.5 8.6 %pre_acts.3 = (f32[384,1024]{1,0:T(8,128)S(1)}, f32[384,1024]{1,0:T(8,128)S(1)}, bf16[384,1024]{1,0:T(8,128)(2,1)S(1)}, bf16[384,1024]{1,0:T(8,128)(2,1)S(1)}) custom-call(s32[1]{0:T(128)} %bitcast.t_ref, bf16[96,3072]{1,0:T(8,128)(2,1)S(1)} %convolution_convert_fusion.own_ref, bf16[288,768]{1,0:T(8,128)(2,1)S(1)} %constant_dynamic-update-slice_fusion.refs_0_, ...), custom_call_target="tpu_custom_call" | custom-call | flops 4831838208 | bytes 12582912 | tf_op jit(solution)/shard_map/pre_acts/pallas_call | solution.py:84
  59.7 2.5 %collective-permute-start.18 = (bf16[288,768]{1,0:T(8,128)(2,1)S(1)}, bf16[288,768]{1,0:T(8,128)(2,1)S(1)}, u32[]{:S(2)}, u32[]{:S(2)}) collective-permute-start(bf16[288,768]{1,0:T(8,128)(2,1)S(1)} %constant_dynamic-update-slice_fusion.3.refs_0_), channel_id=1, source_target_pairs={{0,12},{4,8},{8,4},{12,0},{1,13},{5,9},{9,5},{13,1},{2,14},{6,10},... | collective-permute-start | bytes 1327112 | tf_op jit(solution)/shard_map/ppermute | solution.py:22
  62.6 4.5 %project_first.1 = (bf16[384,384]{1,0:T(8,128)(2,1)S(1)}, bf16[384,384]{1,0:T(8,128)(2,1)S(1)}, bf16[384,2048]{1,0:T(8,128)(2,1)S(1)}) custom-call(s32[1]{0:T(128)} %bitcast.t_ref, f32[384,1024]{1,0:T(8,128)S(1)} %get-tuple-element.37.refs_0_, f32[384,1024]{1,0:T(8,128)S(1)} %get-tuple-element.38.refs_1_, ...), custom_call_target="tpu_custom_call" | custom-call | flops 1207959552 | bytes 12582912 | tf_op jit(solution)/shard_map/project_first/pallas_call | solution.py:245
  67.1 1.6 collective-permute-start.16
  68.6 1.5 collective-permute-start.17
  70.5 3.1 %collective-permute-done.18.refs_3_ = bf16[288,768]{1,0:T(8,128)(2,1)S(1)} collective-permute-done((bf16[288,768]{1,0:T(8,128)(2,1)S(1)}, bf16[288,768]{1,0:T(8,128)(2,1)S(1)}, u32[]{:S(2)}, u32[]{:S(2)}) %collective-permute-start.18) | collective-permute-done | bytes 442400 | tf_op jit(solution)/shard_map/ppermute | solution.py:22
  73.6 5.1 %grad_hidden.2 = (f32[384,1024]{1,0:T(8,128)S(1)}, bf16[384,1024]{1,0:T(8,128)(2,1)S(1)}) custom-call(s32[1]{0:T(128)} %bitcast.t_ref, bf16[96,3072]{1,0:T(8,128)(2,1)S(1)} %fusion.own_ref, bf16[288,768]{1,0:T(8,128)(2,1)S(1)} %constant_dynamic-update-slice_fusion.3.refs_0_, bf16[288,768]{1,0:T(8,128)(2,1)S(1)} %collective-permute-done.12.refs_1_, ...), custom_call_target="tpu_custom_call" | custom-call | flops 2415919104 | bytes 6291456 | tf_op jit(solution)/shard_map/grad_hidden/pallas_call | solution.py:122
  79.1 5.1 %grad_hidden.3 = (f32[384,1024]{1,0:T(8,128)S(1)}, bf16[384,1024]{1,0:T(8,128)(2,1)S(1)}) custom-call(s32[1]{0:T(128)} %bitcast.t_ref, bf16[96,3072]{1,0:T(8,128)(2,1)S(1)} %fusion.own_ref, bf16[288,768]{1,0:T(8,128)(2,1)S(1)} %constant_dynamic-update-slice_fusion.3.refs_0_, bf16[288,768]{1,0:T(8,128)(2,1)S(1)} %collective-permute-done.12.refs_1_, ...), custom_call_target="tpu_custom_call" | custom-call | flops 2415919104 | bytes 6291456 | tf_op jit(solution)/shard_map/grad_hidden/pallas_call | solution.py:122
  84.4 6.8 %project_rest.1 = (bf16[384,768]{1,0:T(8,128)(2,1)S(1)}, bf16[384,768]{1,0:T(8,128)(2,1)S(1)}, f32[384,768]{1,0:T(8,128)S(1)}) custom-call(s32[1]{0:T(128)} %bitcast.t_ref, bf16[384,2048]{1,0:T(8,128)(2,1)S(1)} %get-tuple-element.47.refs_0_, bf16[2048,3072]{1,0:T(8,128)(2,1)} %bitcast.31, bf16[384,384]{1,0:T(8,128)(2,1)S(1)} %collective-permute-done.16.refs_2_, ...), custom_call_target="tpu_custom_call" | custom-call | flops 3623878656 | bytes 9437184 | tf_op jit(solution)/shard_map/project_rest/pallas_call | solution.py:273
  91.2 1.6 collective-permute-start.21
  92.8 1.5 collective-permute-start.22
  94.3 7.8 %rows_first.1 = (bf16[384,384]{1,0:T(8,128)(2,1)S(1)}, bf16[384,384]{1,0:T(8,128)(2,1)S(1)}, bf16[384,2048]{1,0:T(8,128)(2,1)S(1)}, bf16[384,2048]{1,0:T(8,128)(2,1)S(1)}) custom-call(s32[1]{0:T(128)} %bitcast.t_ref, f32[384,1024]{1,0:T(8,128)S(1)} %get-tuple-element.37.refs_0_, f32[384,1024]{1,0:T(8,128)S(1)} %get-tuple-element.38.refs_1_, ...), custom_call_target="tpu_custom_call" | custom-call | flops 2415919104 | bytes 12582912 | tf_op jit(solution)/shard_map/rows_first/pallas_call | solution.py:245
  103.2 4.2 %collective-permute-done.21 = bf16[384,768]{1,0:T(8,128)(2,1)S(1)} collective-permute-done((bf16[384,768]{1,0:T(8,128)(2,1)S(1)}, bf16[384,768]{1,0:T(8,128)(2,1)S(1)}, u32[]{:S(2)}, u32[]{:S(2)}) %collective-permute-start.21) | collective-permute-done | bytes 589856 | tf_op jit(solution)/shard_map/ppermute | solution.py:22
  107.4 1.6 collective-permute-done.22
  109.2 3.1 %collective-permute-start.23 = (bf16[96,768]{1,0:T(8,128)(2,1)S(1)}, bf16[96,768]{1,0:T(8,128)(2,1)S(1)}, u32[]{:S(2)}, u32[]{:S(2)}) collective-permute-start(bf16[96,768]{1,0:T(8,128)(2,1)S(1)} %get-tuple-element.77), channel_id=1, source_target_pairs={{0,1},{1,0},{2,3},{3,2},{4,5},{5,4},{6,7},{7,6},{8,9},{9,8},{10,11... | collective-permute-start | bytes 442376 | tf_op jit(solution)/shard_map/ppermute | solution.py:22
  113.8 5.6 %rows_kept.1 = f32[384,768]{1,0:T(8,128)S(1)} custom-call(s32[1]{0:T(128)} %bitcast.t_ref, bf16[384,2048]{1,0:T(8,128)(2,1)S(1)} %get-tuple-element.61.refs_0_, bf16[384,2048]{1,0:T(8,128)(2,1)S(1)} %get-tuple-element.62.refs_1_, bf16[3072,2048]{1,0:T(8,128)(2,1)} %bitcast.21, bf16[3072,2048]{1,0:T(8,128)(2,1)} %bitcast.26), custom_call_target="tpu_custom_call" | custom-call | flops 2415919104 | bytes 3145728 | tf_op jit(solution)/shard_map/rows_kept/pallas_call | solution.py:273
  119.5 8.4 %rows_rest.1 = (bf16[384,768]{1,0:T(8,128)(2,1)S(1)}, bf16[384,768]{1,0:T(8,128)(2,1)S(1)}) custom-call(s32[1]{0:T(128)} %bitcast.t_ref, bf16[384,2048]{1,0:T(8,128)(2,1)S(1)} %get-tuple-element.61.refs_0_, bf16[384,2048]{1,0:T(8,128)(2,1)S(1)} %get-tuple-element.62.refs_1_, bf16[3072,2048]{1,0:T(8,128)(2,1)} %bitcast.22, bf16[3072,2048]{1,0:T(8,128)(2,1)} %bitcast.27, ...), custom_call_target="tpu_custom_call" | custom-call | flops 4831838208 | bytes 6291456 | tf_op jit(solution)/shard_map/rows_rest/pallas_call | solution.py:273
  128.5 1.5 collective-permute-start.32
  130.3 1.3 fusion.3
  131.8 1.6 collective-permute-start.26
  134.5 8.6 %collective-permute-done.31 = bf16[384,768]{1,0:T(8,128)(2,1)S(1)} collective-permute-done((bf16[384,768]{1,0:T(8,128)(2,1)S(1)}, bf16[384,768]{1,0:T(8,128)(2,1)S(1)}, u32[]{:S(2)}, u32[]{:S(2)}) %collective-permute-start.31) | collective-permute-done | bytes 589856 | tf_op jit(solution)/shard_map/ppermute | solution.py:22
  143.7 2.6 %collective-permute-start.33 = (bf16[96,768]{1,0:T(8,128)(2,1)S(1)}, bf16[96,768]{1,0:T(8,128)(2,1)S(1)}, u32[]{:S(2)}, u32[]{:S(2)}) collective-permute-start(bf16[96,768]{1,0:T(8,128)(2,1)S(1)} %get-tuple-element.73), channel_id=1, source_target_pairs={{0,1},{1,0},{2,3},{3,2},{4,5},{5,4},{6,7},{7,6},{8,9},{9,8},{10,11... | collective-permute-start | bytes 442376 | tf_op jit(solution)/shard_map/ppermute | solution.py:22
  146.4 0.9 collective-permute-start.34
  147.9 3.1 %collective-permute-done.33 = bf16[96,768]{1,0:T(8,128)(2,1)S(1)} collective-permute-done((bf16[96,768]{1,0:T(8,128)(2,1)S(1)}, bf16[96,768]{1,0:T(8,128)(2,1)S(1)}, u32[]{:S(2)}, u32[]{:S(2)}) %collective-permute-start.33) | collective-permute-done | bytes 147488 | tf_op jit(solution)/shard_map/ppermute | solution.py:22
  151.1 1.7 collective-permute-start.28
  153.9 1.9 %collective-permute-done.35 = bf16[96,768]{1,0:T(8,128)(2,1)S(1)} collective-permute-done((bf16[96,768]{1,0:T(8,128)(2,1)S(1)}, bf16[96,768]{1,0:T(8,128)(2,1)S(1)}, u32[]{:S(2)}, u32[]{:S(2)}) %collective-permute-start.35) | collective-permute-done | bytes 147488 | tf_op jit(solution)/shard_map/ppermute | solution.py:22
  156.4 1.5 collective-permute-start.36
  158.0 1.9 %collective-permute-done.41 = f32[2,128]{1,0:T(2,128)S(1)} collective-permute-done((f32[2,128]{1,0:T(2,128)S(1)}, f32[2,128]{1,0:T(2,128)S(1)}, u32[]{:S(2)}, u32[]{:S(2)}) %collective-permute-start.41) | collective-permute-done | bytes 1056 | tf_op jit(solution)/shard_map/ppermute | solution.py:22
  159.8 0.8 collective-permute-start.37
  161.9 0.9 assemble.2
  162.8 4.8 %collective-permute-done.37.refs_2_ = bf16[128,768]{1,0:T(8,128)(2,1)S(1)} collective-permute-done((bf16[128,768]{1,0:T(8,128)(2,1)S(1)}, bf16[128,768]{1,0:T(8,128)(2,1)S(1)}, u32[]{:S(2)}, u32[]{:S(2)}) %collective-permute-start.37) | collective-permute-done | bytes 196640 | tf_op jit(solution)/shard_map/ppermute | solution.py:22
  167.6 0.9 assemble.3
  (99 shorter events, 17.7 us)
Async XLA Ops:
  0.6 2.7 %copy-start = (bf16[128,3072]{1,0:T(8,128)(2,1)S(1)}, bf16[128,3072]{1,0:T(8,128)(2,1)}, u32[]{:S(2)}) copy-start(bf16[128,3072]{1,0:T(8,128)(2,1)} %param.7) | copy-start | bytes 2359300
  0.6 6.5 %copy-start.4 = (f32[128,2]{0,1:T(2,128)S(1)}, f32[128,2]{0,1:T(2,128)}, u32[]{:S(2)}) copy-start(f32[128,2]{0,1:T(2,128)} %param.9) | copy-start | bytes 3076
  0.7 6.8 %copy-start.2 = (bf16[128,3072]{1,0:T(8,128)(2,1)S(1)}, bf16[128,3072]{1,0:T(8,128)(2,1)}, u32[]{:S(2)}) copy-start(bf16[128,3072]{1,0:T(8,128)(2,1)} %param.13) | copy-start | bytes 2359300
  3.6 6.8 %collective-permute-start = (bf16[96,768]{1,0:T(8,128)(2,1)S(1)}, bf16[96,768]{1,0:T(8,128)(2,1)S(1)}, u32[]{:S(2)}, u32[]{:S(2)}) collective-permute-start(bf16[96,768]{1,0:T(8,128)(2,1)S(1)} %get-tuple-element.83), channel_id=1, source_target_pairs={{0,1},{1,0},{2,3},{3,2},{4,5},{5,4},{6,7},{7,6},{8,9},{9,8},{10,11... | collective-permute-start | bytes 442376 | tf_op jit(solution)/shard_map/ppermute | solution.py:22
  5.3 11.0 %collective-permute-start.1 = (bf16[96,768]{1,0:T(8,128)(2,1)S(1)}, bf16[96,768]{1,0:T(8,128)(2,1)S(1)}, u32[]{:S(2)}, u32[]{:S(2)}) collective-permute-start(bf16[96,768]{1,0:T(8,128)(2,1)S(1)} %get-tuple-element.82), channel_id=1, source_target_pairs={{0,2},{1,3},{2,0},{3,1},{4,6},{5,7},{6,4},{7,5},{8,10},{9,11},{10,... | collective-permute-start | bytes 442376 | tf_op jit(solution)/shard_map/ppermute | solution.py:22
  5.6 14.4 %collective-permute-start.2 = (bf16[96,768]{1,0:T(8,128)(2,1)S(1)}, bf16[96,768]{1,0:T(8,128)(2,1)S(1)}, u32[]{:S(2)}, u32[]{:S(2)}) collective-permute-start(bf16[96,768]{1,0:T(8,128)(2,1)S(1)} %get-tuple-element.81), channel_id=1, source_target_pairs={{0,3},{1,2},{2,1},{3,0},{4,7},{5,6},{6,5},{7,4},{8,11},{9,10},{10,... | collective-permute-start | bytes 442376 | tf_op jit(solution)/shard_map/ppermute | solution.py:22
  7.3 54.8 %copy-start.3 = (f32[384]{0:T(512)}, f32[384]{0:T(512)S(1)}, u32[]{:S(2)}) copy-start(f32[384]{0:T(512)S(1)} %add_reduce_fusion) | copy-start | bytes 4612
  20.0 11.0 %collective-permute-start.7 = (bf16[288,768]{1,0:T(8,128)(2,1)S(1)}, bf16[288,768]{1,0:T(8,128)(2,1)S(1)}, u32[]{:S(2)}, u32[]{:S(2)}) collective-permute-start(bf16[288,768]{1,0:T(8,128)(2,1)S(1)} %constant_dynamic-update-slice_fusion.refs_0_), channel_id=1, source_target_pairs={{0,8},{4,12},{8,0},{12,4},{1,9},{5,13},{9,1},{13,5},{2,10},{6,14},... | collective-permute-start | bytes 1327112 | tf_op jit(solution)/shard_map/ppermute | solution.py:22
  21.6 12.6 %collective-permute-start.6 = (bf16[288,768]{1,0:T(8,128)(2,1)S(1)}, bf16[288,768]{1,0:T(8,128)(2,1)S(1)}, u32[]{:S(2)}, u32[]{:S(2)}) collective-permute-start(bf16[288,768]{1,0:T(8,128)(2,1)S(1)} %constant_dynamic-update-slice_fusion.refs_0_), channel_id=1, source_target_pairs={{0,4},{4,0},{8,12},{12,8},{1,5},{5,1},{9,13},{13,9},{2,6},{6,2},{1... | collective-permute-start | bytes 1327112 | tf_op jit(solution)/shard_map/ppermute | solution.py:22
  23.1 6.8 %collective-permute-start.3 = (bf16[96,768]{1,0:T(8,128)(2,1)S(1)}, bf16[96,768]{1,0:T(8,128)(2,1)S(1)}, u32[]{:S(2)}, u32[]{:S(2)}) collective-permute-start(bf16[96,768]{1,0:T(8,128)(2,1)S(1)} %get-tuple-element.80), channel_id=1, source_target_pairs={{0,1},{1,0},{2,3},{3,2},{4,5},{5,4},{6,7},{7,6},{8,9},{9,8},{10,11... | collective-permute-start | bytes 442376 | tf_op jit(solution)/shard_map/ppermute | solution.py:22
  23.2 10.9 %collective-permute-start.4 = (bf16[96,768]{1,0:T(8,128)(2,1)S(1)}, bf16[96,768]{1,0:T(8,128)(2,1)S(1)}, u32[]{:S(2)}, u32[]{:S(2)}) collective-permute-start(bf16[96,768]{1,0:T(8,128)(2,1)S(1)} %get-tuple-element.79), channel_id=1, source_target_pairs={{0,2},{1,3},{2,0},{3,1},{4,6},{5,7},{6,4},{7,5},{8,10},{9,11},{10,... | collective-permute-start | bytes 442376 | tf_op jit(solution)/shard_map/ppermute | solution.py:22
  25.4 12.5 %collective-permute-start.5 = (bf16[96,768]{1,0:T(8,128)(2,1)S(1)}, bf16[96,768]{1,0:T(8,128)(2,1)S(1)}, u32[]{:S(2)}, u32[]{:S(2)}) collective-permute-start(bf16[96,768]{1,0:T(8,128)(2,1)S(1)} %get-tuple-element.78), channel_id=1, source_target_pairs={{0,3},{1,2},{2,1},{3,0},{4,7},{5,6},{6,5},{7,4},{8,11},{9,10},{10,... | collective-permute-start | bytes 442376 | tf_op jit(solution)/shard_map/ppermute | solution.py:22
  31.0 6.9 %collective-permute-start.8 = (bf16[288,384]{1,0:T(8,128)(2,1)S(1)}, bf16[288,384]{1,0:T(8,128)(2,1)S(1)}, u32[]{:S(2)}, u32[]{:S(2)}) collective-permute-start(bf16[288,384]{1,0:T(8,128)(2,1)S(1)} %slice.109), channel_id=1, source_target_pairs={{0,4},{4,0},{8,12},{12,8},{1,5},{5,1},{9,13},{13,9},{2,6},{6,2},{1... | collective-permute-start | bytes 663560 | tf_op jit(solution)/shard_map/ppermute | solution.py:22
  34.2 6.0 %collective-permute-start.9 = (bf16[288,384]{1,0:T(8,128)(2,1)S(1)}, bf16[288,384]{1,0:T(8,128)(2,1)S(1)}, u32[]{:S(2)}, u32[]{:S(2)}) collective-permute-start(bf16[288,384]{1,0:T(8,128)(2,1)S(1)} %slice.110), channel_id=1, source_target_pairs={{0,8},{4,12},{8,0},{12,4},{1,9},{5,13},{9,1},{13,5},{2,10},{6,14},... | collective-permute-start | bytes 663560 | tf_op jit(solution)/shard_map/ppermute | solution.py:22
  40.3 10.2 %collective-permute-start.12 = (bf16[288,768]{1,0:T(8,128)(2,1)S(1)}, bf16[288,768]{1,0:T(8,128)(2,1)S(1)}, u32[]{:S(2)}, u32[]{:S(2)}) collective-permute-start(bf16[288,768]{1,0:T(8,128)(2,1)S(1)} %constant_dynamic-update-slice_fusion.3.refs_0_), channel_id=1, source_target_pairs={{0,4},{4,0},{8,12},{12,8},{1,5},{5,1},{9,13},{13,9},{2,6},{6,2},{1... | collective-permute-start | bytes 1327112 | tf_op jit(solution)/shard_map/ppermute | solution.py:22
  40.8 9.7 %collective-permute-start.13 = (bf16[288,768]{1,0:T(8,128)(2,1)S(1)}, bf16[288,768]{1,0:T(8,128)(2,1)S(1)}, u32[]{:S(2)}, u32[]{:S(2)}) collective-permute-start(bf16[288,768]{1,0:T(8,128)(2,1)S(1)} %constant_dynamic-update-slice_fusion.3.refs_0_), channel_id=1, source_target_pairs={{0,8},{4,12},{8,0},{12,4},{1,9},{5,13},{9,1},{13,5},{2,10},{6,14},... | collective-permute-start | bytes 1327112 | tf_op jit(solution)/shard_map/ppermute | solution.py:22
  49.9 12.3 %collective-permute-start.10 = (bf16[384,1024]{1,0:T(8,128)(2,1)S(1)}, bf16[384,1024]{1,0:T(8,128)(2,1)S(1)}, u32[]{:S(2)}, u32[]{:S(2)}) collective-permute-start(bf16[384,1024]{1,0:T(8,128)(2,1)S(1)} %get-tuple-element.39), channel_id=1, source_target_pairs={{0,16},{16,0},{1,17},{17,1},{2,18},{18,2},{3,19},{19,3},{4,20},{20... | collective-permute-start | bytes 2359304 | tf_op jit(solution)/shard_map/ppermute | solution.py:22
  50.0 12.2 %collective-permute-start.11 = (bf16[384,1024]{1,0:T(8,128)(2,1)S(1)}, bf16[384,1024]{1,0:T(8,128)(2,1)S(1)}, u32[]{:S(2)}, u32[]{:S(2)}) collective-permute-start(bf16[384,1024]{1,0:T(8,128)(2,1)S(1)} %get-tuple-element.40), channel_id=1, source_target_pairs={{0,16},{16,0},{1,17},{17,1},{2,18},{18,2},{3,19},{19,3},{4,20},{20... | collective-permute-start | bytes 2359304 | tf_op jit(solution)/shard_map/ppermute | solution.py:22
  59.1 3.1 %collective-permute-start.14 = (bf16[384,1024]{1,0:T(8,128)(2,1)S(1)}, bf16[384,1024]{1,0:T(8,128)(2,1)S(1)}, u32[]{:S(2)}, u32[]{:S(2)}) collective-permute-start(bf16[384,1024]{1,0:T(8,128)(2,1)S(1)} %get-tuple-element.45), channel_id=1, source_target_pairs={{0,16},{16,0},{1,17},{17,1},{2,18},{18,2},{3,19},{19,3},{4,20},{20... | collective-permute-start | bytes 2359304 | tf_op jit(solution)/shard_map/ppermute | solution.py:22
  59.2 3.3 %collective-permute-start.15 = (bf16[384,1024]{1,0:T(8,128)(2,1)S(1)}, bf16[384,1024]{1,0:T(8,128)(2,1)S(1)}, u32[]{:S(2)}, u32[]{:S(2)}) collective-permute-start(bf16[384,1024]{1,0:T(8,128)(2,1)S(1)} %get-tuple-element.46), channel_id=1, source_target_pairs={{0,16},{16,0},{1,17},{17,1},{2,18},{18,2},{3,19},{19,3},{4,20},{20... | collective-permute-start | bytes 2359304 | tf_op jit(solution)/shard_map/ppermute | solution.py:22
  59.7 13.9 %collective-permute-start.18 = (bf16[288,768]{1,0:T(8,128)(2,1)S(1)}, bf16[288,768]{1,0:T(8,128)(2,1)S(1)}, u32[]{:S(2)}, u32[]{:S(2)}) collective-permute-start(bf16[288,768]{1,0:T(8,128)(2,1)S(1)} %constant_dynamic-update-slice_fusion.3.refs_0_), channel_id=1, source_target_pairs={{0,12},{4,8},{8,4},{12,0},{1,13},{5,9},{9,5},{13,1},{2,14},{6,10},... | collective-permute-start | bytes 1327112 | tf_op jit(solution)/shard_map/ppermute | solution.py:22
  62.6 7.6 %slice-start = ((f32[384]{0:T(512)}), f32[96]{0:T(128)S(1)}, s32[]{:S(2)}) async-start(f32[384]{0:T(512)} %copy-done.3), calls=%async_computation | async-start | bytes 1024 | tf_op jit(solution)/shard_map/slice | solution.py:351
  67.1 12.0 %collective-permute-start.16 = (bf16[384,384]{1,0:T(8,128)(2,1)S(1)}, bf16[384,384]{1,0:T(8,128)(2,1)S(1)}, u32[]{:S(2)}, u32[]{:S(2)}) collective-permute-start(bf16[384,384]{1,0:T(8,128)(2,1)S(1)} %get-tuple-element.48), channel_id=1, source_target_pairs={{0,4},{4,0},{8,12},{12,8},{1,5},{5,1},{9,13},{13,9},{2,6},{6,2},{1... | collective-permute-start | bytes 884744 | tf_op jit(solution)/shard_map/ppermute | solution.py:22
  68.6 10.5 %collective-permute-start.17 = (bf16[384,384]{1,0:T(8,128)(2,1)S(1)}, bf16[384,384]{1,0:T(8,128)(2,1)S(1)}, u32[]{:S(2)}, u32[]{:S(2)}) collective-permute-start(bf16[384,384]{1,0:T(8,128)(2,1)S(1)} %get-tuple-element.49), channel_id=1, source_target_pairs={{0,8},{4,12},{8,0},{12,4},{1,9},{5,13},{9,1},{13,5},{2,10},{6,14},... | collective-permute-start | bytes 884744 | tf_op jit(solution)/shard_map/ppermute | solution.py:22
  78.7 15.7 %collective-permute-start.19 = (bf16[384,1024]{1,0:T(8,128)(2,1)S(1)}, bf16[384,1024]{1,0:T(8,128)(2,1)S(1)}, u32[]{:S(2)}, u32[]{:S(2)}) collective-permute-start(bf16[384,1024]{1,0:T(8,128)(2,1)S(1)} %get-tuple-element.53), channel_id=1, source_target_pairs={{0,16},{16,0},{1,17},{17,1},{2,18},{18,2},{3,19},{19,3},{4,20},{20... | collective-permute-start | bytes 2359304 | tf_op jit(solution)/shard_map/ppermute | solution.py:22
  84.2 10.2 %collective-permute-start.20 = (bf16[384,1024]{1,0:T(8,128)(2,1)S(1)}, bf16[384,1024]{1,0:T(8,128)(2,1)S(1)}, u32[]{:S(2)}, u32[]{:S(2)}) collective-permute-start(bf16[384,1024]{1,0:T(8,128)(2,1)S(1)} %get-tuple-element.56), channel_id=1, source_target_pairs={{0,16},{16,0},{1,17},{17,1},{2,18},{18,2},{3,19},{19,3},{4,20},{20... | collective-permute-start | bytes 2359304 | tf_op jit(solution)/shard_map/ppermute | solution.py:22
  91.2 16.2 %collective-permute-start.21 = (bf16[384,768]{1,0:T(8,128)(2,1)S(1)}, bf16[384,768]{1,0:T(8,128)(2,1)S(1)}, u32[]{:S(2)}, u32[]{:S(2)}) collective-permute-start(bf16[384,768]{1,0:T(8,128)(2,1)S(1)} %get-tuple-element.59), channel_id=1, source_target_pairs={{0,4},{4,0},{8,12},{12,8},{1,5},{5,1},{9,13},{13,9},{2,6},{6,2},{1... | collective-permute-start | bytes 1769480 | tf_op jit(solution)/shard_map/ppermute | solution.py:22
  92.8 16.2 %collective-permute-start.22 = (bf16[384,768]{1,0:T(8,128)(2,1)S(1)}, bf16[384,768]{1,0:T(8,128)(2,1)S(1)}, u32[]{:S(2)}, u32[]{:S(2)}) collective-permute-start(bf16[384,768]{1,0:T(8,128)(2,1)S(1)} %get-tuple-element.60), channel_id=1, source_target_pairs={{0,8},{4,12},{8,0},{12,4},{1,9},{5,13},{9,1},{13,5},{2,10},{6,14},... | collective-permute-start | bytes 1769480 | tf_op jit(solution)/shard_map/ppermute | solution.py:22
  102.1 17.3 %collective-permute-start.29 = (bf16[384,384]{1,0:T(8,128)(2,1)S(1)}, bf16[384,384]{1,0:T(8,128)(2,1)S(1)}, u32[]{:S(2)}, u32[]{:S(2)}) collective-permute-start(bf16[384,384]{1,0:T(8,128)(2,1)S(1)} %get-tuple-element.57), channel_id=1, source_target_pairs={{0,4},{4,0},{8,12},{12,8},{1,5},{5,1},{9,13},{13,9},{2,6},{6,2},{1... | collective-permute-start | bytes 884744 | tf_op jit(solution)/shard_map/ppermute | solution.py:22
  102.6 16.8 %collective-permute-start.30 = (bf16[384,384]{1,0:T(8,128)(2,1)S(1)}, bf16[384,384]{1,0:T(8,128)(2,1)S(1)}, u32[]{:S(2)}, u32[]{:S(2)}) collective-permute-start(bf16[384,384]{1,0:T(8,128)(2,1)S(1)} %get-tuple-element.64), channel_id=1, source_target_pairs={{0,8},{4,12},{8,0},{12,4},{1,9},{5,13},{9,1},{13,5},{2,10},{6,14},... | collective-permute-start | bytes 884744 | tf_op jit(solution)/shard_map/ppermute | solution.py:22
  109.2 20.8 %collective-permute-start.23 = (bf16[96,768]{1,0:T(8,128)(2,1)S(1)}, bf16[96,768]{1,0:T(8,128)(2,1)S(1)}, u32[]{:S(2)}, u32[]{:S(2)}) collective-permute-start(bf16[96,768]{1,0:T(8,128)(2,1)S(1)} %get-tuple-element.77), channel_id=1, source_target_pairs={{0,1},{1,0},{2,3},{3,2},{4,5},{5,4},{6,7},{7,6},{8,9},{9,8},{10,11... | collective-permute-start | bytes 442376 | tf_op jit(solution)/shard_map/ppermute | solution.py:22
  112.3 17.7 %collective-permute-start.24 = (bf16[96,768]{1,0:T(8,128)(2,1)S(1)}, bf16[96,768]{1,0:T(8,128)(2,1)S(1)}, u32[]{:S(2)}, u32[]{:S(2)}) collective-permute-start(bf16[96,768]{1,0:T(8,128)(2,1)S(1)} %get-tuple-element.76), channel_id=1, source_target_pairs={{0,2},{1,3},{2,0},{3,1},{4,6},{5,7},{6,4},{7,5},{8,10},{9,11},{10,... | collective-permute-start | bytes 442376 | tf_op jit(solution)/shard_map/ppermute | solution.py:22
  113.0 17.0 %collective-permute-start.25 = (bf16[96,768]{1,0:T(8,128)(2,1)S(1)}, bf16[96,768]{1,0:T(8,128)(2,1)S(1)}, u32[]{:S(2)}, u32[]{:S(2)}) collective-permute-start(bf16[96,768]{1,0:T(8,128)(2,1)S(1)} %get-tuple-element.75), channel_id=1, source_target_pairs={{0,3},{1,2},{2,1},{3,0},{4,7},{5,6},{6,5},{7,4},{8,11},{9,10},{10,... | collective-permute-start | bytes 442376 | tf_op jit(solution)/shard_map/ppermute | solution.py:22
  127.9 15.2 %collective-permute-start.31 = (bf16[384,768]{1,0:T(8,128)(2,1)S(1)}, bf16[384,768]{1,0:T(8,128)(2,1)S(1)}, u32[]{:S(2)}, u32[]{:S(2)}) collective-permute-start(bf16[384,768]{1,0:T(8,128)(2,1)S(1)} %get-tuple-element.65), channel_id=1, source_target_pairs={{0,4},{4,0},{8,12},{12,8},{1,5},{5,1},{9,13},{13,9},{2,6},{6,2},{1... | collective-permute-start | bytes 1769480 | tf_op jit(solution)/shard_map/ppermute | solution.py:22
  128.5 14.9 %collective-permute-start.32 = (bf16[384,768]{1,0:T(8,128)(2,1)S(1)}, bf16[384,768]{1,0:T(8,128)(2,1)S(1)}, u32[]{:S(2)}, u32[]{:S(2)}) collective-permute-start(bf16[384,768]{1,0:T(8,128)(2,1)S(1)} %get-tuple-element.66), channel_id=1, source_target_pairs={{0,8},{4,12},{8,0},{12,4},{1,9},{5,13},{9,1},{13,5},{2,10},{6,14},... | collective-permute-start | bytes 1769480 | tf_op jit(solution)/shard_map/ppermute | solution.py:22
  131.7 2.2 %collective-permute-start.39 = (f32[2,128]{1,0:T(2,128)S(1)}, f32[2,128]{1,0:T(2,128)S(1)}, u32[]{:S(2)}, u32[]{:S(2)}) collective-permute-start(f32[2,128]{1,0:T(2,128)S(1)} %pad_maximum_fusion.6), channel_id=1, source_target_pairs={{0,16},{16,0},{1,17},{17,1},{2,18},{18,2},{3,19},{19,3},{4,20},{20... | collective-permute-start | bytes 3080 | tf_op jit(solution)/shard_map/ppermute | solution.py:22
  131.8 28.9 %collective-permute-start.26 = (bf16[128,768]{1,0:T(8,128)(2,1)S(1)}, bf16[128,768]{1,0:T(8,128)(2,1)S(1)}, u32[]{:S(2)}, u32[]{:S(2)}) collective-permute-start(bf16[128,768]{1,0:T(8,128)(2,1)S(1)} %get-tuple-element.69.refs_0_), channel_id=1, source_target_pairs={{0,4},{4,0},{8,12},{12,8},{1,5},{5,1},{9,13},{13,9},{2,6},{6,2},{1... | collective-permute-start | bytes 589832 | tf_op jit(solution)/shard_map/ppermute | solution.py:22
  133.4 28.5 %collective-permute-start.27 = (bf16[128,768]{1,0:T(8,128)(2,1)S(1)}, bf16[128,768]{1,0:T(8,128)(2,1)S(1)}, u32[]{:S(2)}, u32[]{:S(2)}) collective-permute-start(bf16[128,768]{1,0:T(8,128)(2,1)S(1)} %get-tuple-element.69.refs_0_), channel_id=1, source_target_pairs={{0,8},{4,12},{8,0},{12,4},{1,9},{5,13},{9,1},{13,5},{2,10},{6,14},... | collective-permute-start | bytes 589832 | tf_op jit(solution)/shard_map/ppermute | solution.py:22
  133.9 13.4 %collective-permute-start.40 = (f32[2,128]{1,0:T(2,128)S(1)}, f32[2,128]{1,0:T(2,128)S(1)}, u32[]{:S(2)}, u32[]{:S(2)}) collective-permute-start(f32[2,128]{1,0:T(2,128)S(1)} %fusion.25), channel_id=1, source_target_pairs={{0,4},{4,0},{8,12},{12,8},{1,5},{5,1},{9,13},{13,9},{2,6},{6,2},{1... | collective-permute-start | bytes 3080 | tf_op jit(solution)/shard_map/ppermute | solution.py:22
  143.7 7.3 %collective-permute-start.33 = (bf16[96,768]{1,0:T(8,128)(2,1)S(1)}, bf16[96,768]{1,0:T(8,128)(2,1)S(1)}, u32[]{:S(2)}, u32[]{:S(2)}) collective-permute-start(bf16[96,768]{1,0:T(8,128)(2,1)S(1)} %get-tuple-element.73), channel_id=1, source_target_pairs={{0,1},{1,0},{2,3},{3,2},{4,5},{5,4},{6,7},{7,6},{8,9},{9,8},{10,11... | collective-permute-start | bytes 442376 | tf_op jit(solution)/shard_map/ppermute | solution.py:22
  146.4 6.9 %collective-permute-start.34 = (bf16[96,768]{1,0:T(8,128)(2,1)S(1)}, bf16[96,768]{1,0:T(8,128)(2,1)S(1)}, u32[]{:S(2)}, u32[]{:S(2)}) collective-permute-start(bf16[96,768]{1,0:T(8,128)(2,1)S(1)} %get-tuple-element.72), channel_id=1, source_target_pairs={{0,2},{1,3},{2,0},{3,1},{4,6},{5,7},{6,4},{7,5},{8,10},{9,11},{10,... | collective-permute-start | bytes 442376 | tf_op jit(solution)/shard_map/ppermute | solution.py:22
  147.3 8.5 %collective-permute-start.35 = (bf16[96,768]{1,0:T(8,128)(2,1)S(1)}, bf16[96,768]{1,0:T(8,128)(2,1)S(1)}, u32[]{:S(2)}, u32[]{:S(2)}) collective-permute-start(bf16[96,768]{1,0:T(8,128)(2,1)S(1)} %get-tuple-element.71), channel_id=1, source_target_pairs={{0,3},{1,2},{2,1},{3,0},{4,7},{5,6},{6,5},{7,4},{8,11},{9,10},{10,... | collective-permute-start | bytes 442376 | tf_op jit(solution)/shard_map/ppermute | solution.py:22
  151.1 10.8 %collective-permute-start.28 = (bf16[128,768]{1,0:T(8,128)(2,1)S(1)}, bf16[128,768]{1,0:T(8,128)(2,1)S(1)}, u32[]{:S(2)}, u32[]{:S(2)}) collective-permute-start(bf16[128,768]{1,0:T(8,128)(2,1)S(1)} %get-tuple-element.69.refs_0_), channel_id=1, source_target_pairs={{0,12},{4,8},{8,4},{12,0},{1,13},{5,9},{9,5},{13,1},{2,14},{6,10},... | collective-permute-start | bytes 589832 | tf_op jit(solution)/shard_map/ppermute | solution.py:22
  153.3 6.6 %collective-permute-start.41 = (f32[2,128]{1,0:T(2,128)S(1)}, f32[2,128]{1,0:T(2,128)S(1)}, u32[]{:S(2)}, u32[]{:S(2)}) collective-permute-start(f32[2,128]{1,0:T(2,128)S(1)} %fusion.32), channel_id=1, source_target_pairs={{0,8},{4,12},{8,0},{12,4},{1,9},{5,13},{9,1},{13,5},{2,10},{6,14},... | collective-permute-start | bytes 3080 | tf_op jit(solution)/shard_map/ppermute | solution.py:22
  156.4 6.4 %collective-permute-start.36 = (bf16[128,768]{1,0:T(8,128)(2,1)S(1)}, bf16[128,768]{1,0:T(8,128)(2,1)S(1)}, u32[]{:S(2)}, u32[]{:S(2)}) collective-permute-start(bf16[128,768]{1,0:T(8,128)(2,1)S(1)} %fusion.2.refs_0_), channel_id=1, source_target_pairs={{0,4},{4,0},{8,12},{12,8},{1,5},{5,1},{9,13},{13,9},{2,6},{6,2},{1... | collective-permute-start | bytes 589832 | tf_op jit(solution)/shard_map/ppermute | solution.py:22
  159.8 7.8 %collective-permute-start.37 = (bf16[128,768]{1,0:T(8,128)(2,1)S(1)}, bf16[128,768]{1,0:T(8,128)(2,1)S(1)}, u32[]{:S(2)}, u32[]{:S(2)}) collective-permute-start(bf16[128,768]{1,0:T(8,128)(2,1)S(1)} %fusion.2.refs_0_), channel_id=1, source_target_pairs={{0,8},{4,12},{8,0},{12,4},{1,9},{5,13},{9,1},{13,5},{2,10},{6,14},... | collective-permute-start | bytes 589832 | tf_op jit(solution)/shard_map/ppermute | solution.py:22
  160.7 7.0 %collective-permute-start.38 = (bf16[128,768]{1,0:T(8,128)(2,1)S(1)}, bf16[128,768]{1,0:T(8,128)(2,1)S(1)}, u32[]{:S(2)}, u32[]{:S(2)}) collective-permute-start(bf16[128,768]{1,0:T(8,128)(2,1)S(1)} %fusion.2.refs_0_), channel_id=1, source_target_pairs={{0,12},{4,8},{8,4},{12,0},{1,13},{5,9},{9,5},{13,1},{2,14},{6,10},... | collective-permute-start | bytes 589832 | tf_op jit(solution)/shard_map/ppermute | solution.py:22
  161.9 6.7 %copy-start.1 = (bf16[128,3072]{1,0:T(8,128)(2,1)S(1)}, bf16[128,3072]{1,0:T(8,128)(2,1)}, u32[]{:S(2)}) copy-start(bf16[128,3072]{1,0:T(8,128)(2,1)} %param.7) | copy-start | bytes 2359300

commit v3 on v0

v3 whole, which is shorter than its diff:
```python
import jax
import jax.numpy as jnp
from jax import lax
from jax.experimental import pallas as pl
from jax.experimental.pallas import tpu as pltpu
from jax.sharding import PartitionSpec as P

BF = jnp.bfloat16
F32 = jnp.float32
MIB = 1024 * 1024


def slot_index(expert_ids, experts):
    hit_table = (expert_ids[:, :, None] == jnp.arange(experts, dtype=jnp.int32)).astype(jnp.int32)
    per_row = jnp.sum(hit_table, axis=1)
    before = jnp.cumsum(per_row, axis=0) - per_row
    return jnp.sum(hit_table * before[:, None, :], axis=2)


def exchange(array, axis, bit):
    size = lax.axis_size(axis)
    return lax.ppermute(array, axis, [(i, i ^ bit) for i in range(size)])


def dot_nn(a, b):
    return jnp.dot(a, b, preferred_element_type=F32)


def dot_nt(a, b):
    return lax.dot_general(a, b, (((1,), (1,)), ((), ())), preferred_element_type=F32)


def params(mib):
    return pltpu.CompilerParams(vmem_limit_bytes=mib * MIB)


VMEM = pl.BlockSpec(memory_space=pltpu.VMEM)
HBM = pl.BlockSpec(memory_space=pltpu.HBM)
SMEM = pl.BlockSpec(memory_space=pltpu.SMEM)


def sds(shape, dtype):
    return jax.ShapeDtypeStruct(shape, dtype)


def call(kernel, t, ins, outs, scratch, flops, mib, name, far=0):
    return pl.pallas_call(
        kernel,
        in_specs=[SMEM] + [VMEM] * (len(ins) - far) + [HBM] * far,
        out_specs=[VMEM] * len(outs),
        out_shape=outs,
        scratch_shapes=scratch,
        compiler_params=params(mib),
        cost_estimate=pl.CostEstimate(flops=flops, bytes_accessed=MIB, transcendentals=0),
        name=name,
    )(t, *ins)


def fetch(matrix):
    def kernel(source, held, sem):
        copy = pltpu.make_async_copy(source, held, sem)
        copy.start()
        copy.wait()

    return pl.pallas_call(
        kernel,
        in_specs=[HBM],
        out_specs=VMEM,
        out_shape=pltpu.VMEM(matrix.shape, matrix.dtype),
        scratch_shapes=[pltpu.SemaphoreType.DMA],
        compiler_params=params(LIMIT),
        cost_estimate=pl.CostEstimate(
            flops=0, bytes_accessed=2 * matrix.size, transcendentals=0
        ),
        name="fetch",
    )(matrix)


def lay_out(t, own, parts, rows_ref):
    cap = own.shape[0]
    n, _, quarter = rows_ref.shape
    for q in range(n):
        rows_ref[q, :cap, :] = own[:, q * quarter : (q + 1) * quarter]
    for j in range(n):
        at = cap
        for piece in parts[j]:
            rows_ref[t ^ j, at : at + piece.shape[0], :] = piece[...]
            at += piece.shape[0]


def split_parts(refs, counts):
    parts, at = [], 0
    for c in counts:
        parts.append(refs[at : at + c])
        at += c
    return parts, refs[at:]


BLOCK = 256


def pre_acts(t, own, parts, gate_mat, up_mat, start, stop):
    depth = gate_mat.shape[0]
    n = len(parts)
    quarter = depth // n
    rows = own.shape[0] + sum(p.shape[0] for p in parts[0])
    counts = [len(p) for p in parts]

    def kernel(t_ref, own_ref, *refs):
        pieces, refs = split_parts(refs, counts)
        gate_w, up_w, gate_o, up_o, gate_s, up_s, rows_ref = refs
        lay_out(t_ref[0], own_ref, pieces, rows_ref)

        @pl.loop(0, (stop - start) // BLOCK)
        def _(i):
            off = pl.multiple_of(i * BLOCK, BLOCK)
            for w, out, send in ((gate_w, gate_o, gate_s), (up_w, up_o, up_s)):
                total = None
                for q in range(n):
                    part = dot_nn(
                        rows_ref[q], w[q * quarter : (q + 1) * quarter, pl.ds(start + off, BLOCK)]
                    )
                    total = part if total is None else total + part
                out[:, pl.ds(off, BLOCK)] = total
                send[:, pl.ds(off, BLOCK)] = total.astype(BF)

    shape = (rows, stop - start)
    return call(
        kernel,
        t,
        [own] + [x for p in parts for x in p] + [gate_mat, up_mat],
        [sds(shape, F32)] * 2 + [sds(shape, BF)] * 2,
        [pltpu.VMEM((n, rows, quarter), BF)],
        4 * rows * depth * (stop - start),
        LIMIT,
        "pre_acts",
    )


def grad_hiddens(t, own, parts, down_mat, start, stop):
    depth = down_mat.shape[1]
    n = len(parts)
    quarter = depth // n
    rows = own.shape[0] + sum(p.shape[0] for p in parts[0])
    counts = [len(p) for p in parts]

    steps = (stop - start) // BLOCK

    def kernel(t_ref, own_ref, *refs):
        pieces, refs = split_parts(refs, counts)
        down_w, out, send, rows_ref, held, sems = refs
        copies = [
            pltpu.make_async_copy(
                down_w.at[pl.ds(start + i * BLOCK, BLOCK)], held.at[i], sems.at[i]
            )
            for i in range(steps)
        ]
        for copy in copies:
            copy.start()
        lay_out(t_ref[0], own_ref, pieces, rows_ref)
        for i in range(steps):
            copies[i].wait()
            total = None
            for q in range(n):
                part = dot_nt(rows_ref[q], held[i, :, q * quarter : (q + 1) * quarter])
                total = part if total is None else total + part
            out[:, i * BLOCK : (i + 1) * BLOCK] = total
            send[:, i * BLOCK : (i + 1) * BLOCK] = total.astype(BF)

    shape = (rows, stop - start)
    return call(
        kernel,
        t,
        [own] + [x for p in parts for x in p] + [down_mat],
        [sds(shape, F32), sds(shape, BF)],
        [
            pltpu.VMEM((n, rows, quarter), BF),
            pltpu.VMEM((steps, BLOCK, depth), BF),
            pltpu.SemaphoreType.DMA((steps,)),
        ],
        2 * rows * depth * (stop - start),
        12,
        "grad_hidden",
        far=1,
    )


STRIP = 32
LIMIT = 8


def strips(rows, body):
    @pl.loop(0, rows // STRIP)
    def _(i):
        body(pl.ds(pl.multiple_of(i * STRIP, STRIP), STRIP))


def hidden_strips(ins, acts):
    (hidden_ref,) = acts

    def body(here):
        at = 0
        for g in range(0, len(ins), 4):
            gate_o, up_o, gate_r, up_r = ins[g : g + 4]
            cols = slice(at, at + gate_o.shape[1])
            gate = gate_o[here, :] + gate_r[here, :].astype(F32)
            up = up_o[here, :] + up_r[here, :].astype(F32)
            hidden_ref[here, cols] = (gate * jax.nn.sigmoid(gate) * up).astype(BF)
            at += gate_o.shape[1]

    strips(hidden_ref.shape[0], body)


def grad_strips(ins, acts):
    gg_ref, gu_ref = acts

    def body(here):
        at = 0
        for g in range(0, len(ins), 6):
            gate_o, up_o, gate_r, up_r, gh_o, gh_r = ins[g : g + 6]
            cols = slice(at, at + gate_o.shape[1])
            gate = gate_o[here, :] + gate_r[here, :].astype(F32)
            up = up_o[here, :] + up_r[here, :].astype(F32)
            grad = gh_o[here, :] + gh_r[here, :].astype(F32)
            s = jax.nn.sigmoid(gate)
            gg_ref[here, cols] = (grad * up * (s * (1.0 + gate * (1.0 - s)))).astype(BF)
            gu_ref[here, cols] = (grad * (gate * s)).astype(BF)
            at += gate_o.shape[1]

    strips(gg_ref.shape[0], body)


class Stream:
    def __init__(self, mats, n, nn, pieces):
        self.mats, self.nn = len(mats), nn
        self.hidden, depth = mats[0].shape if nn else mats[0].shape[::-1]
        self.quarter = depth // n
        self.width = self.quarter if nn else BLOCK
        self.each = self.quarter // self.width
        chunk = (self.hidden, self.width) if nn else (self.width, self.hidden)
        count = pieces * self.each * self.mats
        self.scratch = [pltpu.VMEM((count,) + chunk, BF), pltpu.SemaphoreType.DMA((count,))]
        self.mib = 2 + 2 * count * self.hidden * self.width // MIB

    def start(self, weights, bases, held, sems):
        self.held, self.copies = held, []
        for base in bases:
            for c in range(self.each):
                cut = pl.ds(pl.multiple_of(base + c * self.width, BLOCK), self.width)
                for w in weights:
                    source = w.at[:, cut] if self.nn else w.at[cut]
                    k = len(self.copies)
                    self.copies.append(pltpu.make_async_copy(source, held.at[k], sems.at[k]))
                    self.copies[-1].start()

    def products(self, piece, acts):
        for c in range(self.each):
            total = None
            for m in range(self.mats):
                k = (piece * self.each + c) * self.mats + m
                self.copies[k].wait()
                dot = dot_nn if self.nn else dot_nt
                part = dot(acts[m][...], self.held[k])
                total = part if total is None else total + part
            yield slice(c * self.width, (c + 1) * self.width), total


def first_piece(t, n, make, nn, ins, mats, name):
    stream = Stream(mats, n, nn, 1)
    rows = ins[0].shape[0]
    half, quarter, hidden = rows // 2, stream.quarter, stream.hidden

    def kernel(t_ref, *refs):
        parts, refs = refs[: len(ins)], refs[len(ins) :]
        weights, refs = refs[: len(mats)], refs[len(mats) :]
        halves, acts, scratch = refs[:2], refs[2 : 2 + len(mats)], refs[2 + len(mats) :]
        stream.start(weights, [(t_ref[0] ^ 3) * quarter], *scratch)
        make(parts, acts)
        for cols, total in stream.products(0, acts):
            halves[0][:, cols] = total[:half].astype(BF)
            halves[1][:, cols] = total[half:].astype(BF)

    return call(
        kernel,
        t,
        list(ins) + list(mats),
        [sds((half, quarter), BF)] * 2 + [sds((rows, hidden), BF)] * len(mats),
        stream.scratch,
        2 * rows * quarter * hidden * len(mats),
        stream.mib + 4,
        name,
        far=len(mats),
    )


def pieces(t, n, nn, acts, mats, order, name):
    stream = Stream(mats, n, nn, len(order))
    rows, quarter = acts[0].shape[0], stream.quarter

    def kernel(t_ref, *refs):
        ins, refs = refs[: len(acts)], refs[len(acts) :]
        weights, refs = refs[: len(mats)], refs[len(mats) :]
        outs, scratch = refs[: len(order)], refs[len(order) :]
        stream.start(weights, [(t_ref[0] ^ j) * quarter for j in order], *scratch)
        for k, out in enumerate(outs):
            for cols, total in stream.products(k, ins):
                out[:, cols] = total

    return call(
        kernel,
        t,
        list(acts) + list(mats),
        [sds((rows, quarter), F32)] * len(order),
        stream.scratch,
        2 * rows * quarter * len(order) * stream.hidden * len(mats),
        stream.mib + 4,
        name,
        far=len(mats),
    )


def add_diagonal(t, to_x, to_y, top, low):
    half = top.shape[0]

    def kernel(t_ref, x_ref, y_ref, top_ref, low_ref, x_out, y_out):
        x_out[:half, :] = x_ref[:half, :].astype(BF)
        x_out[half:, :] = (x_ref[half:, :] + low_ref[...].astype(F32)).astype(BF)
        y_out[:half, :] = (y_ref[:half, :] + top_ref[...].astype(F32)).astype(BF)
        y_out[half:, :] = y_ref[half:, :].astype(BF)

    return call(
        kernel, t, [to_x, to_y, top, low], [sds(to_x.shape, BF)] * 2, [], to_x.size, LIMIT, "add"
    )


def assemble(t, parts):
    rows, width = parts[0].shape

    def kernel(t_ref, *refs):
        for j, part in enumerate(refs[:-1]):
            refs[-1][:, pl.ds(pl.multiple_of((t_ref[0] ^ j) * width, 128), width)] = part[...]

    (out,) = call(
        kernel, t, parts, [sds((rows, width * len(parts)), parts[0].dtype)], [], 0, LIMIT, "assemble"
    )
    return out


def after(value, *others):
    return lax.optimization_barrier((value,) + others)[0]


def local(tokens, expert_ids, gate_values, w_gate, w_up, w_down, cotangent):
    tok_rows, depth = tokens.shape
    groups = lax.axis_size("expert")
    n = lax.axis_size("tensor")
    z = lax.axis_index("expert")
    t = lax.axis_index("tensor")
    t_arr = t.astype(jnp.int32).reshape(1)
    experts = groups
    cap = min(tok_rows, 3 * tok_rows // experts)
    quarter = depth // n
    gate_mat, up_mat, down_mat = (
        pltpu.with_memory_space_constraint(w[0], pltpu.HBM) for w in (w_gate, w_up, w_down)
    )
    gate_held, up_held = fetch(gate_mat), fetch(up_mat)
    hidden_here = gate_mat.shape[1]

    slot_of = slot_index(expert_ids, experts)
    order = (expert_ids ^ z) * cap + slot_of
    cells = jnp.arange(experts * cap, dtype=jnp.int32)
    pick = [order[:, k][None, :] == cells[:, None] for k in range(2)]
    spread = jnp.logical_or(pick[0], pick[1]).astype(BF)
    slot_gate = jnp.sum(
        jnp.where(pick[0], gate_values[:, 0][None, :], 0.0)
        + jnp.where(pick[1], gate_values[:, 1][None, :], 0.0),
        axis=1,
        keepdims=True,
    )

    def outgoing(source, scale):
        part = lax.dynamic_slice(source, (0, t * quarter), (tok_rows, quarter))
        out = dot_nn(spread[cap:], part)
        own = dot_nn(spread[:cap], source)
        if scale is not None:
            out, own = out * scale[cap:], own * scale[:cap]
        return own.astype(BF), out.astype(BF)

    def over_z(out):
        return [exchange(out[(k - 1) * cap : k * cap], "expert", k) for k in range(1, groups)]

    tok_own, tok_out = outgoing(tokens, None)
    cot_own, cot_out = outgoing(cotangent, slot_gate)
    tok_part = jnp.concatenate(over_z(tok_out), axis=0)
    tok_x, tok_y = exchange(tok_part, "tensor", 1), exchange(tok_part, "tensor", 2)
    cot_pieces = over_z(after(cot_out, tok_part))
    split = tok_part.shape[0] // 2
    tok_d = [exchange(tok_y[:split], "tensor", 1), exchange(tok_x[split:], "tensor", 2)]
    tok_d[0], tok_d[1], *cot_pieces = lax.optimization_barrier((*tok_d, *cot_pieces))
    tok_parts = [[tok_part], [tok_x], [tok_y], tok_d]
    cot_part = jnp.concatenate(cot_pieces, axis=0)
    cot_parts = [[cot_part]] + [[exchange(cot_part, "tensor", j)] for j in range(1, n)]

    turn = after(t_arr, cot_part)
    pres = []
    for start in range(0, hidden_here, hidden_here // 2):
        if start:
            turn = after(t_arr, cot_parts[1][0], cot_parts[2][0])
        gate_o, up_o, gate_s, up_s = pre_acts(
            turn, tok_own, tok_parts, gate_held, up_held, start, start + hidden_here // 2
        )
        pres.append([gate_o, up_o, exchange(gate_s, "wide", 1), exchange(up_s, "wide", 1)])

    def sum_back(arrived, keep, *others):
        total = keep
        for piece in arrived:
            total = total + piece.astype(F32)
        total = total.astype(BF)
        back = [total[:cap]] + [
            exchange(total[k * cap : (k + 1) * cap], "expert", k) for k in range(1, groups)
        ]
        back = lax.optimization_barrier((*back, *others))[:groups]
        return jnp.concatenate(back, axis=0)

    def gathered(part):
        return assemble(t_arr, [part] + [exchange(part, "tensor", j) for j in range(1, n)])

    gather = [(order[:, k][:, None] == cells[None, :]).astype(BF) for k in range(2)]

    d_top, d_low, hidden = first_piece(
        t_arr, n, hidden_strips, True, sum(pres, []), [down_mat], "project_first"
    )
    added = [exchange(d_top, "tensor", 1), exchange(d_low, "tensor", 2)]
    to_x, to_y = pieces(t_arr, n, True, [hidden], [down_mat], (1, 2), "project_send")
    grads = []
    turn = after(t_arr, to_x)
    for start in range(0, hidden_here, hidden_here // 2):
        if start:
            to_x, to_y = add_diagonal(t_arr, to_x, to_y, *added)
            turn = after(t_arr, to_x)
        gh_o, gh_s = grad_hiddens(
            turn, cot_own, cot_parts, down_mat, start, start + hidden_here // 2
        )
        grads.append([gh_o, exchange(gh_s, "wide", 1)])
    (keep,) = pieces(after(t_arr, gh_s), n, True, [hidden], [down_mat], (0,), "project_keep")

    e_top, e_low, grad_g, grad_u = first_piece(
        after(t_arr, keep), n, grad_strips, False,
        sum([p + g for p, g in zip(pres, grads)], []), [gate_mat, up_mat], "rows_first",
    )
    gadded = [exchange(e_top, "tensor", 1), exchange(e_low, "tensor", 2)]
    from_x, from_y = exchange(to_x, "tensor", 1), exchange(to_y, "tensor", 2)
    gto_x, gto_y = pieces(
        t_arr, n, False, [grad_g, grad_u], [gate_mat, up_mat], (1, 2), "rows_send",
    )
    gto_x, gto_y = add_diagonal(t_arr, gto_x, gto_y, *gadded)
    (gkeep,) = pieces(
        after(t_arr, gto_x), n, False, [grad_g, grad_u], [gate_mat, up_mat], (0,), "rows_keep"
    )
    returned = sum_back((from_x, from_y), after(keep, gto_x), gkeep)
    chosen = [dot_nn(g, returned) for g in gather]
    layer_part = (gate_values[:, 0:1] * chosen[0] + gate_values[:, 1:2] * chosen[1]).astype(BF)
    layer_out = gathered(layer_part)
    cot_here = lax.dynamic_slice(cotangent, (0, t * quarter), (tok_rows, quarter)).astype(F32)
    gate_grad = jnp.stack([jnp.sum(cot_here * c, axis=1) for c in chosen], axis=0)
    for axis, bit in (("wide", 1), ("tensor", 1), ("tensor", 2)):
        gate_grad = gate_grad + exchange(gate_grad, axis, bit)

    greturned = sum_back((exchange(gto_x, "tensor", 1), exchange(gto_y, "tensor", 2)), gkeep)
    grad_part = (dot_nn(gather[0], greturned) + dot_nn(gather[1], greturned)).astype(BF)
    token_grad = gathered(grad_part)
    return (layer_out, token_grad, gate_grad.T)


def plain_local(tokens, expert_ids, gate_values, w_gate, w_up, w_down, cotangent):
    tok_rows, depth = tokens.shape
    groups = lax.axis_size("expert")
    experts = groups * w_gate.shape[0]
    cap = min(tok_rows, 3 * tok_rows // experts)
    total_rows = groups * cap
    gate_mat, up_mat, down_mat = w_gate[0], w_up[0], w_down[0]
    order = expert_ids * cap + slot_index(expert_ids, experts)
    cells = jnp.arange(experts * cap, dtype=jnp.int32)
    pick = [order[:, k][None, :] == cells[:, None] for k in range(2)]
    gather = [(order[:, k][:, None] == cells[None, :]).astype(BF) for k in range(2)]

    def to_owners(rows):
        out = rows.astype(BF).reshape(groups, cap, depth)
        out = lax.all_to_all(out, "expert", split_axis=0, concat_axis=0, tiled=True)
        return out.reshape(total_rows, depth)

    def send_back(rows):
        share = lax.psum_scatter(rows, "tensor", scatter_dimension=0, tiled=True).astype(BF)
        return to_owners(lax.all_gather(share, "tensor", axis=0, tiled=True))

    spread = jnp.logical_or(pick[0], pick[1]).astype(BF)
    arrived = to_owners(dot_nn(spread, tokens))
    gate_pre, up_pre = lax.psum((dot_nn(arrived, gate_mat), dot_nn(arrived, up_mat)), "wide")
    s = jax.nn.sigmoid(gate_pre)
    returned = send_back(dot_nn((gate_pre * s * up_pre).astype(BF), down_mat))
    chosen = [dot_nn(g, returned) for g in gather]
    layer_out = (gate_values[:, 0:1] * chosen[0] + gate_values[:, 1:2] * chosen[1]).astype(BF)
    upstream = cotangent.astype(F32)
    gate_grad = lax.psum(
        jnp.stack([jnp.sum(upstream * c, axis=1) for c in chosen], axis=1), "wide"
    )
    slot_gate = jnp.sum(
        jnp.where(pick[0], gate_values[:, 0][None, :], 0.0)
        + jnp.where(pick[1], gate_values[:, 1][None, :], 0.0),
        axis=1,
        keepdims=True,
    )
    grad_arrived = to_owners(dot_nn(spread, cotangent) * slot_gate)
    grad_hidden = lax.psum(dot_nt(grad_arrived, down_mat), "wide")
    grad_gate = (grad_hidden * up_pre * (s * (1.0 + gate_pre * (1.0 - s)))).astype(BF)
    grad_up = (grad_hidden * (gate_pre * s)).astype(BF)
    back = send_back(dot_nt(grad_gate, gate_mat) + dot_nt(grad_up, up_mat))
    token_grad = (dot_nn(gather[0], back) + dot_nn(gather[1], back)).astype(BF)
    return (layer_out, token_grad, gate_grad)


def solution(mesh):
    in_specs = (
        P("expert", "wide"),
        P("expert", None),
        P("expert", None),
        P("expert", "wide", "tensor"),
        P("expert", "wide", "tensor"),
        P("expert", "tensor", "wide"),
        P("expert", "wide"),
    )
    out_specs = (P("expert", "wide"), P("expert", "wide"), P("expert", None))
    laid_out = mesh.shape["tensor"] == 4 and mesh.shape["expert"] == 4 and mesh.shape["wide"] == 2
    return jax.shard_map(
        local if laid_out else plain_local,
        mesh=mesh,
        in_specs=in_specs,
        out_specs=out_specs,
        check_vma=False,
    )
```

time: 477 us -> 165 us (0.35)
  waiting for transfers between devices: 338 us -> 36 us
  matrix products: 83.2 us -> 2.48 us
  Pallas kernels: 0 us -> 77 us
  starting transfers between devices: 25.4 us -> 42.3 us
  between operations: 13.8 us -> 1.19 us
    all_to_all x4 -> x0, waiting for transfers between devices: 136 us -> none  [the longest x2 77.8 us: to_owners(): lax.all_to_all(buffer, 'expert', split_axis=0, concat_axis=0, tiled=True)]
    reduce_scatter x2 -> x0, waiting for transfers between devices: 86.4 us -> none  [send_back(): lax.psum_scatter(project(pieces), 'tensor', scatter_dimension=0, tiled=True)]
    dot_general x12 -> x8, matrix products: 83.2 us -> 2.48 us  [dot_nn(): return jnp.dot(a, b, preferred_element_type=F32)]
    pallas_call x0 -> x16, Pallas kernels: none -> 77 us  [the longest x14 67.7 us: call(): pl.pallas_call(kernel, in_specs=[SMEM] + [VMEM] * (len(ins) - far) + [HBM...]
    all_gather x2 -> x0, waiting for transfers between devices: 72.3 us -> none  [send_back(): entire = lax.all_gather(shares, 'tensor', axis=0, tiled=True)]
    psum x1 -> x0, waiting for transfers between devices: 43.3 us -> none  [local(): lax.psum((jnp.dot(arrived, gate_mat, preferred_element_type=jnp.float32),...]
    ppermute x0 -> x42, starting transfers between devices: none -> 42.3 us  [exchange(): return lax.ppermute(array, axis, [(i, i ^ bit) for i in range(size)])]
    ppermute x0 -> x42, waiting for transfers between devices: none -> 36 us  [exchange(): return lax.ppermute(array, axis, [(i, i ^ bit) for i in range(size)])]
  transfers between devices with their start and end apart: 9 -> 42, of which waited for: 9 -> 17; matrix products, arithmetic and copies ran while one was open for 13% -> 2% of each run, Pallas kernels for 0% -> 47%
where the time goes in v3:
time: 165 us; the launch traced here: 163 us
  Pallas kernels  77 us (47%)
  starting transfers between devices  42.3 us (26%)
  waiting for transfers between devices  36 us (22%)
  other arithmetic  3.55 us (2%)
  matrix products  2.48 us (2%)
    pallas_call x14, Pallas kernels, call(): pl.pallas_call(kernel, in_specs=[SMEM] + [VMEM] * (len(ins) - far) + [HBM...  67.7 us
    ppermute x42, starting transfers between devices, exchange(): return lax.ppermute(array, axis, [(i, i ^ bit) for i in range(size)])  42.3 us
    ppermute x42, waiting for transfers between devices, exchange(): return lax.ppermute(array, axis, [(i, i ^ bit) for i in range(size)])  36 us
    pallas_call x2, Pallas kernels, fetch(): pl.pallas_call(kernel, in_specs=[HBM], out_specs=VMEM, out_shape=pltpu.VM...  9.25 us
  transfers between devices with their start and end apart: 42, of which 17 were waited for; matrix products, arithmetic and copies ran while one was open for 2% of the time, Pallas kernels for 47%

profile of v3, /device:TPU:16, one launch (start us, length us, event | category | flops | bytes accessed | tf_op | source)
XLA Modules:
  0.0 163.2 jit_solution(14405524179845576614)
XLA Ops:
  3.6 1.6 %collective-permute-start = (bf16[96,768]{1,0:T(8,128)(2,1)S(1)}, bf16[96,768]{1,0:T(8,128)(2,1)S(1)}, u32[]{:S(2)}, u32[]{:S(2)}) collective-permute-start(bf16[96,768]{1,0:T(8,128)(2,1)S(1)} %get-tuple-element.117), channel_id=1, source_target_pairs={{0,1},{1,0},{2,3},{3,2},{4,5},{5,4},{6,7},{7,6},{8,9},{9,8},{10,11... | collective-permute-start | bytes 442376 | tf_op jit(solution)/shard_map/ppermute | solution.py:22
  5.5 1.6 collective-permute-start.2
  7.3 4.6 %fetch.2.refs_5_ = bf16[3072,2048]{1,0:T(8,128)(2,1)S(1)} custom-call(bf16[3072,2048]{1,0:T(8,128)(2,1)} %bitcast.27), custom_call_target="tpu_custom_call" | custom-call | bytes 12582912 | tf_op jit(solution)/shard_map/fetch/pallas_call | solution.py:65
  12.0 4.7 %fetch.3.refs_6_ = bf16[3072,2048]{1,0:T(8,128)(2,1)S(1)} custom-call(bf16[3072,2048]{1,0:T(8,128)(2,1)} %bitcast.31), custom_call_target="tpu_custom_call" | custom-call | bytes 12582912 | tf_op jit(solution)/shard_map/fetch/pallas_call | solution.py:65
  16.7 3.2 %collective-permute-done.2 = bf16[96,768]{1,0:T(8,128)(2,1)S(1)} collective-permute-done((bf16[96,768]{1,0:T(8,128)(2,1)S(1)}, bf16[96,768]{1,0:T(8,128)(2,1)S(1)}, u32[]{:S(2)}, u32[]{:S(2)}) %collective-permute-start.2) | collective-permute-done | bytes 147488 | tf_op jit(solution)/shard_map/ppermute | solution.py:22
  19.9 1.6 collective-permute-start.3
  21.5 1.5 collective-permute-start.5
  23.4 1.9 %collective-permute-start.8 = (bf16[96,768]{1,0:T(8,128)(2,1)S(1)}, bf16[96,768]{1,0:T(8,128)(2,1)S(1)}, u32[]{:S(2)}, u32[]{:S(2)}) collective-permute-start(bf16[96,768]{1,0:T(8,128)(2,1)S(1)} %get-tuple-element.113), channel_id=1, source_target_pairs={{0,2},{1,3},{2,0},{3,1},{4,6},{5,7},{6,4},{7,5},{8,10},{9,11},{10,... | collective-permute-start | bytes 442376 | tf_op jit(solution)/shard_map/ppermute | solution.py:22
  25.3 1.6 collective-permute-start.9
  26.9 4.1 %collective-permute-done.3.refs_2_ = bf16[288,768]{1,0:T(8,128)(2,1)S(1)} collective-permute-done((bf16[288,768]{1,0:T(8,128)(2,1)S(1)}, bf16[288,768]{1,0:T(8,128)(2,1)S(1)}, u32[]{:S(2)}, u32[]{:S(2)}) %collective-permute-start.3) | collective-permute-done | bytes 442400 | tf_op jit(solution)/shard_map/ppermute | solution.py:22
  31.0 1.6 collective-permute-start.4
  32.7 1.4 collective-permute-start.6
  34.5 3.7 %collective-permute-done.9 = bf16[96,768]{1,0:T(8,128)(2,1)S(1)} collective-permute-done((bf16[96,768]{1,0:T(8,128)(2,1)S(1)}, bf16[96,768]{1,0:T(8,128)(2,1)S(1)}, u32[]{:S(2)}, u32[]{:S(2)}) %collective-permute-start.9) | collective-permute-done | bytes 147488 | tf_op jit(solution)/shard_map/ppermute | solution.py:22
  38.8 1.6 collective-permute-start.12
  40.7 5.8 %pre_acts.2 = (f32[384,1024]{1,0:T(8,128)S(1)}, f32[384,1024]{1,0:T(8,128)S(1)}, bf16[384,1024]{1,0:T(8,128)(2,1)S(1)}, bf16[384,1024]{1,0:T(8,128)(2,1)S(1)}) custom-call(s32[1]{0:T(128)} %bitcast.t_ref, bf16[96,3072]{1,0:T(8,128)(2,1)S(1)} %convolution_convert_fusion.own_ref, bf16[288,768]{1,0:T(8,128)(2,1)S(1)} %constant_dynamic-update-slice_fusion.refs_0_, ...), custom_call_target="tpu_custom_call" | custom-call | flops 4831838208 | bytes 1048576 | tf_op jit(solution)/shard_map/pre_acts/pallas_call | solution.py:47
  47.2 2.3 %collective-permute-done.12.refs_1_ = bf16[288,768]{1,0:T(8,128)(2,1)S(1)} collective-permute-done((bf16[288,768]{1,0:T(8,128)(2,1)S(1)}, bf16[288,768]{1,0:T(8,128)(2,1)S(1)}, u32[]{:S(2)}, u32[]{:S(2)}) %collective-permute-start.12) | collective-permute-done | bytes 442400 | tf_op jit(solution)/shard_map/ppermute | solution.py:22
  49.7 5.8 %pre_acts.3 = (f32[384,1024]{1,0:T(8,128)S(1)}, f32[384,1024]{1,0:T(8,128)S(1)}, bf16[384,1024]{1,0:T(8,128)(2,1)S(1)}, bf16[384,1024]{1,0:T(8,128)(2,1)S(1)}) custom-call(s32[1]{0:T(128)} %bitcast.t_ref, bf16[96,3072]{1,0:T(8,128)(2,1)S(1)} %convolution_convert_fusion.own_ref, bf16[288,768]{1,0:T(8,128)(2,1)S(1)} %constant_dynamic-update-slice_fusion.refs_0_, ...), custom_call_target="tpu_custom_call" | custom-call | flops 4831838208 | bytes 1048576 | tf_op jit(solution)/shard_map/pre_acts/pallas_call | solution.py:47
  56.2 1.5 collective-permute-start.18
  58.0 1.1 collective-permute-done.15.refs_7_.refs_9_
  59.1 3.3 %project_first.1 = (bf16[192,768]{1,0:T(8,128)(2,1)S(1)}, bf16[192,768]{1,0:T(8,128)(2,1)S(1)}, bf16[384,2048]{1,0:T(8,128)(2,1)S(1)}) custom-call(s32[1]{0:T(128)} %bitcast.t_ref, f32[384,1024]{1,0:T(8,128)S(1)} %get-tuple-element.59.refs_0_, f32[384,1024]{1,0:T(8,128)S(1)} %get-tuple-element.60.refs_1_, ...), custom_call_target="tpu_custom_call" | custom-call | flops 1207959552 | bytes 1048576 | tf_op jit(solution)/shard_map/project_first/pallas_call | solution.py:47
  62.4 1.6 collective-permute-start.16
  64.5 5.5 %project_send.1 = (f32[384,768]{1,0:T(8,128)S(1)}, f32[384,768]{1,0:T(8,128)S(1)}) custom-call(s32[1]{0:T(128)} %bitcast.t_ref, bf16[384,2048]{1,0:T(8,128)(2,1)S(1)} %get-tuple-element.68.refs_0_, bf16[2048,3072]{1,0:T(8,128)(2,1)} %bitcast.23), custom_call_target="tpu_custom_call" | custom-call | flops 2415919104 | bytes 1048576 | tf_op jit(solution)/shard_map/project_send/pallas_call | solution.py:47
  70.1 7.0 %grad_hidden.3 = (f32[384,1024]{1,0:T(8,128)S(1)}, bf16[384,1024]{1,0:T(8,128)(2,1)S(1)}) custom-call(s32[1]{0:T(128)} %bitcast.t_ref, bf16[96,3072]{1,0:T(8,128)(2,1)S(1)} %fusion.own_ref, bf16[288,768]{1,0:T(8,128)(2,1)S(1)} %constant_dynamic-update-slice_fusion.3.refs_0_, bf16[288,768]{1,0:T(8,128)(2,1)S(1)} %collective-permute-done.12.refs_1_, ...), custom_call_target="tpu_custom_call" | custom-call | flops 2415919104 | bytes 1048576 | tf_op jit(solution)/shard_map/grad_hidden/pallas_call | solution.py:47
  77.4 7.0 %grad_hidden.2 = (f32[384,1024]{1,0:T(8,128)S(1)}, bf16[384,1024]{1,0:T(8,128)(2,1)S(1)}) custom-call(s32[1]{0:T(128)} %bitcast.t_ref, bf16[96,3072]{1,0:T(8,128)(2,1)S(1)} %fusion.own_ref, bf16[288,768]{1,0:T(8,128)(2,1)S(1)} %constant_dynamic-update-slice_fusion.3.refs_0_, bf16[288,768]{1,0:T(8,128)(2,1)S(1)} %collective-permute-done.12.refs_1_, ...), custom_call_target="tpu_custom_call" | custom-call | flops 2415919104 | bytes 1048576 | tf_op jit(solution)/shard_map/grad_hidden/pallas_call | solution.py:47
  85.0 1.5 collective-permute-start.23
  86.5 3.3 %project_keep.1 = f32[384,768]{1,0:T(8,128)S(1)} custom-call(s32[1]{0:T(128)} %bitcast.t_ref, bf16[384,2048]{1,0:T(8,128)(2,1)S(1)} %get-tuple-element.68.refs_0_, bf16[2048,3072]{1,0:T(8,128)(2,1)} %bitcast.26), custom_call_target="tpu_custom_call" | custom-call | flops 1207959552 | bytes 1048576 | tf_op jit(solution)/shard_map/project_keep/pallas_call | solution.py:47
  90.4 7.4 %rows_first.1 = (bf16[192,768]{1,0:T(8,128)(2,1)S(1)}, bf16[192,768]{1,0:T(8,128)(2,1)S(1)}, bf16[384,2048]{1,0:T(8,128)(2,1)S(1)}, bf16[384,2048]{1,0:T(8,128)(2,1)S(1)}) custom-call(s32[1]{0:T(128)} %bitcast.t_ref, f32[384,1024]{1,0:T(8,128)S(1)} %get-tuple-element.59.refs_0_, f32[384,1024]{1,0:T(8,128)S(1)} %get-tuple-element.60.refs_1_, ...), custom_call_target="tpu_custom_call" | custom-call | flops 2415919104 | bytes 1048576 | tf_op jit(solution)/shard_map/rows_first/pallas_call | solution.py:47
  97.8 1.4 collective-permute-start.21
  99.9 13.4 %rows_send.1 = (f32[384,768]{1,0:T(8,128)S(1)}, f32[384,768]{1,0:T(8,128)S(1)}) custom-call(s32[1]{0:T(128)} %bitcast.t_ref, bf16[384,2048]{1,0:T(8,128)(2,1)S(1)} %get-tuple-element.82.refs_0_, bf16[384,2048]{1,0:T(8,128)(2,1)S(1)} %get-tuple-element.83.refs_1_, bf16[3072,2048]{1,0:T(8,128)(2,1)} %bitcast.29, bf16[3072,2048]{1,0:T(8,128)(2,1)} %bitcast.33), custom_call_target="tpu_custom_call" | custom-call | flops 4831838208 | bytes 1048576 | tf_op jit(solution)/shard_map/rows_send/pallas_call | solution.py:47
  113.5 1.6 collective-permute-start.31
  115.4 1.0 collective-permute-start.26
  116.4 2.5 %collective-permute-start.27 = (bf16[96,768]{1,0:T(8,128)(2,1)S(1)}, bf16[96,768]{1,0:T(8,128)(2,1)S(1)}, u32[]{:S(2)}, u32[]{:S(2)}) collective-permute-start(bf16[96,768]{1,0:T(8,128)(2,1)S(1)} %get-tuple-element.108), channel_id=1, source_target_pairs={{0,3},{1,2},{2,1},{3,0},{4,7},{5,6},{6,5},{7,4},{8,11},{9,10},{10,... | collective-permute-start | bytes 442376 | tf_op jit(solution)/shard_map/ppermute | solution.py:22
  119.4 6.9 %rows_keep.1 = f32[384,768]{1,0:T(8,128)S(1)} custom-call(s32[1]{0:T(128)} %bitcast.t_ref, bf16[384,2048]{1,0:T(8,128)(2,1)S(1)} %get-tuple-element.82.refs_0_, bf16[384,2048]{1,0:T(8,128)(2,1)S(1)} %get-tuple-element.83.refs_1_, bf16[3072,2048]{1,0:T(8,128)(2,1)} %bitcast.30, bf16[3072,2048]{1,0:T(8,128)(2,1)} %bitcast.34), custom_call_target="tpu_custom_call" | custom-call | flops 2415919104 | bytes 1048576 | tf_op jit(solution)/shard_map/rows_keep/pallas_call | solution.py:47
  126.6 3.7 %collective-permute-done.27 = bf16[96,768]{1,0:T(8,128)(2,1)S(1)} collective-permute-done((bf16[96,768]{1,0:T(8,128)(2,1)S(1)}, bf16[96,768]{1,0:T(8,128)(2,1)S(1)}, u32[]{:S(2)}, u32[]{:S(2)}) %collective-permute-start.27) | collective-permute-done | bytes 147488 | tf_op jit(solution)/shard_map/ppermute | solution.py:22
  131.8 1.4 collective-permute-start.29
  134.3 1.8 %collective-permute-start.34 = (bf16[96,768]{1,0:T(8,128)(2,1)S(1)}, bf16[96,768]{1,0:T(8,128)(2,1)S(1)}, u32[]{:S(2)}, u32[]{:S(2)}) collective-permute-start(bf16[96,768]{1,0:T(8,128)(2,1)S(1)} %get-tuple-element.105), channel_id=1, source_target_pairs={{0,2},{1,3},{2,0},{3,1},{4,6},{5,7},{6,4},{7,5},{8,10},{9,11},{10,... | collective-permute-start | bytes 442376 | tf_op jit(solution)/shard_map/ppermute | solution.py:22
  136.1 2.5 %collective-permute-done.40 = f32[2,128]{1,0:T(2,128)S(1)} collective-permute-done((f32[2,128]{1,0:T(2,128)S(1)}, f32[2,128]{1,0:T(2,128)S(1)}, u32[]{:S(2)}, u32[]{:S(2)}) %collective-permute-start.40) | collective-permute-done | bytes 1056 | tf_op jit(solution)/shard_map/ppermute | solution.py:22
  139.0 2.1 %collective-permute-done.33 = bf16[96,768]{1,0:T(8,128)(2,1)S(1)} collective-permute-done((bf16[96,768]{1,0:T(8,128)(2,1)S(1)}, bf16[96,768]{1,0:T(8,128)(2,1)S(1)}, u32[]{:S(2)}, u32[]{:S(2)}) %collective-permute-start.33) | collective-permute-done | bytes 147488 | tf_op jit(solution)/shard_map/ppermute | solution.py:22
  141.0 1.5 collective-permute-start.30
  142.5 3.3 %collective-permute-done.34 = bf16[96,768]{1,0:T(8,128)(2,1)S(1)} collective-permute-done((bf16[96,768]{1,0:T(8,128)(2,1)S(1)}, bf16[96,768]{1,0:T(8,128)(2,1)S(1)}, u32[]{:S(2)}, u32[]{:S(2)}) %collective-permute-start.34) | collective-permute-done | bytes 147488 | tf_op jit(solution)/shard_map/ppermute | solution.py:22
  145.8 2.1 %collective-permute-start.41 = (f32[2,128]{1,0:T(2,128)S(1)}, f32[2,128]{1,0:T(2,128)S(1)}, u32[]{:S(2)}, u32[]{:S(2)}) collective-permute-start(f32[2,128]{1,0:T(2,128)S(1)} %fusion.32), channel_id=1, source_target_pairs={{0,8},{4,12},{8,0},{12,4},{1,9},{5,13},{9,1},{13,5},{2,10},{6,14},... | collective-permute-start | bytes 3080 | tf_op jit(solution)/shard_map/ppermute | solution.py:22
  147.9 2.4 %collective-permute-done.35 = bf16[96,768]{1,0:T(8,128)(2,1)S(1)} collective-permute-done((bf16[96,768]{1,0:T(8,128)(2,1)S(1)}, bf16[96,768]{1,0:T(8,128)(2,1)S(1)}, u32[]{:S(2)}, u32[]{:S(2)}) %collective-permute-start.35) | collective-permute-done | bytes 147488 | tf_op jit(solution)/shard_map/ppermute | solution.py:22
  151.0 1.4 collective-permute-start.36
  153.1 1.5 collective-permute-start.38
  155.1 0.9 assemble.2
  156.1 2.8 %collective-permute-done.36.refs_1_ = bf16[128,768]{1,0:T(8,128)(2,1)S(1)} collective-permute-done((bf16[128,768]{1,0:T(8,128)(2,1)S(1)}, bf16[128,768]{1,0:T(8,128)(2,1)S(1)}, u32[]{:S(2)}, u32[]{:S(2)}) %collective-permute-start.36) | collective-permute-done | bytes 196640 | tf_op jit(solution)/shard_map/ppermute | solution.py:22
  158.8 3.4 %collective-permute-done.37.refs_2_ = bf16[128,768]{1,0:T(8,128)(2,1)S(1)} collective-permute-done((bf16[128,768]{1,0:T(8,128)(2,1)S(1)}, bf16[128,768]{1,0:T(8,128)(2,1)S(1)}, u32[]{:S(2)}, u32[]{:S(2)}) %collective-permute-start.37) | collective-permute-done | bytes 196640 | tf_op jit(solution)/shard_map/ppermute | solution.py:22
  162.2 0.9 assemble.3
  (107 shorter events, 15.9 us)
Async XLA Ops:
  0.6 2.6 %copy-start = (bf16[128,3072]{1,0:T(8,128)(2,1)S(1)}, bf16[128,3072]{1,0:T(8,128)(2,1)}, u32[]{:S(2)}) copy-start(bf16[128,3072]{1,0:T(8,128)(2,1)} %param.7) | copy-start | bytes 2359300
  0.6 6.5 %copy-start.3 = (f32[128,2]{0,1:T(2,128)S(1)}, f32[128,2]{0,1:T(2,128)}, u32[]{:S(2)}) copy-start(f32[128,2]{0,1:T(2,128)} %param.9) | copy-start | bytes 3076
  3.6 13.1 %collective-permute-start = (bf16[96,768]{1,0:T(8,128)(2,1)S(1)}, bf16[96,768]{1,0:T(8,128)(2,1)S(1)}, u32[]{:S(2)}, u32[]{:S(2)}) collective-permute-start(bf16[96,768]{1,0:T(8,128)(2,1)S(1)} %get-tuple-element.117), channel_id=1, source_target_pairs={{0,1},{1,0},{2,3},{3,2},{4,5},{5,4},{6,7},{7,6},{8,9},{9,8},{10,11... | collective-permute-start | bytes 442376 | tf_op jit(solution)/shard_map/ppermute | solution.py:22
  5.2 11.5 %collective-permute-start.1 = (bf16[96,768]{1,0:T(8,128)(2,1)S(1)}, bf16[96,768]{1,0:T(8,128)(2,1)S(1)}, u32[]{:S(2)}, u32[]{:S(2)}) collective-permute-start(bf16[96,768]{1,0:T(8,128)(2,1)S(1)} %get-tuple-element.116), channel_id=1, source_target_pairs={{0,2},{1,3},{2,0},{3,1},{4,6},{5,7},{6,4},{7,5},{8,10},{9,11},{10,... | collective-permute-start | bytes 442376 | tf_op jit(solution)/shard_map/ppermute | solution.py:22
  5.5 14.4 %collective-permute-start.2 = (bf16[96,768]{1,0:T(8,128)(2,1)S(1)}, bf16[96,768]{1,0:T(8,128)(2,1)S(1)}, u32[]{:S(2)}, u32[]{:S(2)}) collective-permute-start(bf16[96,768]{1,0:T(8,128)(2,1)S(1)} %get-tuple-element.115), channel_id=1, source_target_pairs={{0,3},{1,2},{2,1},{3,0},{4,7},{5,6},{6,5},{7,4},{8,11},{9,10},{10,... | collective-permute-start | bytes 442376 | tf_op jit(solution)/shard_map/ppermute | solution.py:22
  11.9 11.1 %copy-start.2 = (bf16[128,3072]{1,0:T(8,128)(2,1)S(1)}, bf16[128,3072]{1,0:T(8,128)(2,1)}, u32[]{:S(2)}) copy-start(bf16[128,3072]{1,0:T(8,128)(2,1)} %param.13) | copy-start | bytes 2359300
  19.9 11.0 %collective-permute-start.3 = (bf16[288,768]{1,0:T(8,128)(2,1)S(1)}, bf16[288,768]{1,0:T(8,128)(2,1)S(1)}, u32[]{:S(2)}, u32[]{:S(2)}) collective-permute-start(bf16[288,768]{1,0:T(8,128)(2,1)S(1)} %constant_dynamic-update-slice_fusion.refs_0_), channel_id=1, source_target_pairs={{0,8},{4,12},{8,0},{12,4},{1,9},{5,13},{9,1},{13,5},{2,10},{6,14},... | collective-permute-start | bytes 1327112 | tf_op jit(solution)/shard_map/ppermute | solution.py:22
  21.5 11.2 %collective-permute-start.5 = (bf16[288,768]{1,0:T(8,128)(2,1)S(1)}, bf16[288,768]{1,0:T(8,128)(2,1)S(1)}, u32[]{:S(2)}, u32[]{:S(2)}) collective-permute-start(bf16[288,768]{1,0:T(8,128)(2,1)S(1)} %constant_dynamic-update-slice_fusion.refs_0_), channel_id=1, source_target_pairs={{0,4},{4,0},{8,12},{12,8},{1,5},{5,1},{9,13},{13,9},{2,6},{6,2},{1... | collective-permute-start | bytes 1327112 | tf_op jit(solution)/shard_map/ppermute | solution.py:22
  23.3 11.1 %collective-permute-start.7 = (bf16[96,768]{1,0:T(8,128)(2,1)S(1)}, bf16[96,768]{1,0:T(8,128)(2,1)S(1)}, u32[]{:S(2)}, u32[]{:S(2)}) collective-permute-start(bf16[96,768]{1,0:T(8,128)(2,1)S(1)} %get-tuple-element.114), channel_id=1, source_target_pairs={{0,1},{1,0},{2,3},{3,2},{4,5},{5,4},{6,7},{7,6},{8,9},{9,8},{10,11... | collective-permute-start | bytes 442376 | tf_op jit(solution)/shard_map/ppermute | solution.py:22
  23.4 11.1 %collective-permute-start.8 = (bf16[96,768]{1,0:T(8,128)(2,1)S(1)}, bf16[96,768]{1,0:T(8,128)(2,1)S(1)}, u32[]{:S(2)}, u32[]{:S(2)}) collective-permute-start(bf16[96,768]{1,0:T(8,128)(2,1)S(1)} %get-tuple-element.113), channel_id=1, source_target_pairs={{0,2},{1,3},{2,0},{3,1},{4,6},{5,7},{6,4},{7,5},{8,10},{9,11},{10,... | collective-permute-start | bytes 442376 | tf_op jit(solution)/shard_map/ppermute | solution.py:22
  25.3 12.8 %collective-permute-start.9 = (bf16[96,768]{1,0:T(8,128)(2,1)S(1)}, bf16[96,768]{1,0:T(8,128)(2,1)S(1)}, u32[]{:S(2)}, u32[]{:S(2)}) collective-permute-start(bf16[96,768]{1,0:T(8,128)(2,1)S(1)} %get-tuple-element.112), channel_id=1, source_target_pairs={{0,3},{1,2},{2,1},{3,0},{4,7},{5,6},{6,5},{7,4},{8,11},{9,10},{10,... | collective-permute-start | bytes 442376 | tf_op jit(solution)/shard_map/ppermute | solution.py:22
  31.0 7.2 %collective-permute-start.4 = (bf16[144,768]{1,0:T(8,128)(2,1)S(1)}, bf16[144,768]{1,0:T(8,128)(2,1)S(1)}, u32[]{:S(2)}, u32[]{:S(2)}) collective-permute-start(bf16[144,768]{1,0:T(8,128)(2,1)S(1)} %slice.108), channel_id=1, source_target_pairs={{0,4},{4,0},{8,12},{12,8},{1,5},{5,1},{9,13},{13,9},{2,6},{6,2},{1... | collective-permute-start | bytes 663560 | tf_op jit(solution)/shard_map/ppermute | solution.py:22
  32.7 6.0 %collective-permute-start.6 = (bf16[144,768]{1,0:T(8,128)(2,1)S(1)}, bf16[144,768]{1,0:T(8,128)(2,1)S(1)}, u32[]{:S(2)}, u32[]{:S(2)}) collective-permute-start(bf16[144,768]{1,0:T(8,128)(2,1)S(1)} %slice.109), channel_id=1, source_target_pairs={{0,8},{4,12},{8,0},{12,4},{1,9},{5,13},{9,1},{13,5},{2,10},{6,14},... | collective-permute-start | bytes 663560 | tf_op jit(solution)/shard_map/ppermute | solution.py:22
  38.8 10.7 %collective-permute-start.12 = (bf16[288,768]{1,0:T(8,128)(2,1)S(1)}, bf16[288,768]{1,0:T(8,128)(2,1)S(1)}, u32[]{:S(2)}, u32[]{:S(2)}) collective-permute-start(bf16[288,768]{1,0:T(8,128)(2,1)S(1)} %constant_dynamic-update-slice_fusion.3.refs_0_), channel_id=1, source_target_pairs={{0,4},{4,0},{8,12},{12,8},{1,5},{5,1},{9,13},{13,9},{2,6},{6,2},{1... | collective-permute-start | bytes 1327112 | tf_op jit(solution)/shard_map/ppermute | solution.py:22
  40.4 9.4 %collective-permute-start.13 = (bf16[288,768]{1,0:T(8,128)(2,1)S(1)}, bf16[288,768]{1,0:T(8,128)(2,1)S(1)}, u32[]{:S(2)}, u32[]{:S(2)}) collective-permute-start(bf16[288,768]{1,0:T(8,128)(2,1)S(1)} %constant_dynamic-update-slice_fusion.3.refs_0_), channel_id=1, source_target_pairs={{0,8},{4,12},{8,0},{12,4},{1,9},{5,13},{9,1},{13,5},{2,10},{6,14},... | collective-permute-start | bytes 1327112 | tf_op jit(solution)/shard_map/ppermute | solution.py:22
  46.6 11.4 %collective-permute-start.10 = (bf16[384,1024]{1,0:T(8,128)(2,1)S(1)}, bf16[384,1024]{1,0:T(8,128)(2,1)S(1)}, u32[]{:S(2)}, u32[]{:S(2)}) collective-permute-start(bf16[384,1024]{1,0:T(8,128)(2,1)S(1)} %get-tuple-element.61), channel_id=1, source_target_pairs={{0,16},{16,0},{1,17},{17,1},{2,18},{18,2},{3,19},{19,3},{4,20},{20... | collective-permute-start | bytes 2359304 | tf_op jit(solution)/shard_map/ppermute | solution.py:22
  46.7 11.3 %collective-permute-start.11 = (bf16[384,1024]{1,0:T(8,128)(2,1)S(1)}, bf16[384,1024]{1,0:T(8,128)(2,1)S(1)}, u32[]{:S(2)}, u32[]{:S(2)}) collective-permute-start(bf16[384,1024]{1,0:T(8,128)(2,1)S(1)} %get-tuple-element.62), channel_id=1, source_target_pairs={{0,16},{16,0},{1,17},{17,1},{2,18},{18,2},{3,19},{19,3},{4,20},{20... | collective-permute-start | bytes 2359304 | tf_op jit(solution)/shard_map/ppermute | solution.py:22
  55.6 2.4 %collective-permute-start.14 = (bf16[384,1024]{1,0:T(8,128)(2,1)S(1)}, bf16[384,1024]{1,0:T(8,128)(2,1)S(1)}, u32[]{:S(2)}, u32[]{:S(2)}) collective-permute-start(bf16[384,1024]{1,0:T(8,128)(2,1)S(1)} %get-tuple-element.66), channel_id=1, source_target_pairs={{0,16},{16,0},{1,17},{17,1},{2,18},{18,2},{3,19},{19,3},{4,20},{20... | collective-permute-start | bytes 2359304 | tf_op jit(solution)/shard_map/ppermute | solution.py:22
  55.7 3.4 %collective-permute-start.15 = (bf16[384,1024]{1,0:T(8,128)(2,1)S(1)}, bf16[384,1024]{1,0:T(8,128)(2,1)S(1)}, u32[]{:S(2)}, u32[]{:S(2)}) collective-permute-start(bf16[384,1024]{1,0:T(8,128)(2,1)S(1)} %get-tuple-element.67), channel_id=1, source_target_pairs={{0,16},{16,0},{1,17},{17,1},{2,18},{18,2},{3,19},{19,3},{4,20},{20... | collective-permute-start | bytes 2359304 | tf_op jit(solution)/shard_map/ppermute | solution.py:22
  56.2 14.0 %collective-permute-start.18 = (bf16[288,768]{1,0:T(8,128)(2,1)S(1)}, bf16[288,768]{1,0:T(8,128)(2,1)S(1)}, u32[]{:S(2)}, u32[]{:S(2)}) collective-permute-start(bf16[288,768]{1,0:T(8,128)(2,1)S(1)} %constant_dynamic-update-slice_fusion.3.refs_0_), channel_id=1, source_target_pairs={{0,12},{4,8},{8,4},{12,0},{1,13},{5,9},{9,5},{13,1},{2,14},{6,10},... | collective-permute-start | bytes 1327112 | tf_op jit(solution)/shard_map/ppermute | solution.py:22
  62.4 14.9 %collective-permute-start.16 = (bf16[192,768]{1,0:T(8,128)(2,1)S(1)}, bf16[192,768]{1,0:T(8,128)(2,1)S(1)}, u32[]{:S(2)}, u32[]{:S(2)}) collective-permute-start(bf16[192,768]{1,0:T(8,128)(2,1)S(1)} %get-tuple-element.71), channel_id=1, source_target_pairs={{0,4},{4,0},{8,12},{12,8},{1,5},{5,1},{9,13},{13,9},{2,6},{6,2},{1... | collective-permute-start | bytes 884744 | tf_op jit(solution)/shard_map/ppermute | solution.py:22
  63.9 13.3 %collective-permute-start.17 = (bf16[192,768]{1,0:T(8,128)(2,1)S(1)}, bf16[192,768]{1,0:T(8,128)(2,1)S(1)}, u32[]{:S(2)}, u32[]{:S(2)}) collective-permute-start(bf16[192,768]{1,0:T(8,128)(2,1)S(1)} %get-tuple-element.72), channel_id=1, source_target_pairs={{0,8},{4,12},{8,0},{12,4},{1,9},{5,13},{9,1},{13,5},{2,10},{6,14},... | collective-permute-start | bytes 884744 | tf_op jit(solution)/shard_map/ppermute | solution.py:22
  77.2 13.3 %collective-permute-start.19 = (bf16[384,1024]{1,0:T(8,128)(2,1)S(1)}, bf16[384,1024]{1,0:T(8,128)(2,1)S(1)}, u32[]{:S(2)}, u32[]{:S(2)}) collective-permute-start(bf16[384,1024]{1,0:T(8,128)(2,1)S(1)} %get-tuple-element.80), channel_id=1, source_target_pairs={{0,16},{16,0},{1,17},{17,1},{2,18},{18,2},{3,19},{19,3},{4,20},{20... | collective-permute-start | bytes 2359304 | tf_op jit(solution)/shard_map/ppermute | solution.py:22
  84.5 5.9 %collective-permute-start.20 = (bf16[384,1024]{1,0:T(8,128)(2,1)S(1)}, bf16[384,1024]{1,0:T(8,128)(2,1)S(1)}, u32[]{:S(2)}, u32[]{:S(2)}) collective-permute-start(bf16[384,1024]{1,0:T(8,128)(2,1)S(1)} %get-tuple-element.75), channel_id=1, source_target_pairs={{0,16},{16,0},{1,17},{17,1},{2,18},{18,2},{3,19},{19,3},{4,20},{20... | collective-permute-start | bytes 2359304 | tf_op jit(solution)/shard_map/ppermute | solution.py:22
  85.0 30.1 %collective-permute-start.23 = (bf16[384,768]{1,0:T(8,128)(2,1)S(1)}, bf16[384,768]{1,0:T(8,128)(2,1)S(1)}, u32[]{:S(2)}, u32[]{:S(2)}) collective-permute-start(bf16[384,768]{1,0:T(8,128)(2,1)S(1)} %get-tuple-element.73), channel_id=1, source_target_pairs={{0,4},{4,0},{8,12},{12,8},{1,5},{5,1},{9,13},{13,9},{2,6},{6,2},{1... | collective-permute-start | bytes 1769480 | tf_op jit(solution)/shard_map/ppermute | solution.py:22
  89.8 25.3 %collective-permute-start.24 = (bf16[384,768]{1,0:T(8,128)(2,1)S(1)}, bf16[384,768]{1,0:T(8,128)(2,1)S(1)}, u32[]{:S(2)}, u32[]{:S(2)}) collective-permute-start(bf16[384,768]{1,0:T(8,128)(2,1)S(1)} %get-tuple-element.90), channel_id=1, source_target_pairs={{0,8},{4,12},{8,0},{12,4},{1,9},{5,13},{9,1},{13,5},{2,10},{6,14},... | collective-permute-start | bytes 1769480 | tf_op jit(solution)/shard_map/ppermute | solution.py:22
  97.8 15.5 %collective-permute-start.21 = (bf16[192,768]{1,0:T(8,128)(2,1)S(1)}, bf16[192,768]{1,0:T(8,128)(2,1)S(1)}, u32[]{:S(2)}, u32[]{:S(2)}) collective-permute-start(bf16[192,768]{1,0:T(8,128)(2,1)S(1)} %get-tuple-element.86), channel_id=1, source_target_pairs={{0,4},{4,0},{8,12},{12,8},{1,5},{5,1},{9,13},{13,9},{2,6},{6,2},{1... | collective-permute-start | bytes 884744 | tf_op jit(solution)/shard_map/ppermute | solution.py:22
  99.3 14.1 %collective-permute-start.22 = (bf16[192,768]{1,0:T(8,128)(2,1)S(1)}, bf16[192,768]{1,0:T(8,128)(2,1)S(1)}, u32[]{:S(2)}, u32[]{:S(2)}) collective-permute-start(bf16[192,768]{1,0:T(8,128)(2,1)S(1)} %get-tuple-element.87), channel_id=1, source_target_pairs={{0,8},{4,12},{8,0},{12,4},{1,9},{5,13},{9,1},{13,5},{2,10},{6,14},... | collective-permute-start | bytes 884744 | tf_op jit(solution)/shard_map/ppermute | solution.py:22
  113.5 20.3 %collective-permute-start.31 = (bf16[384,768]{1,0:T(8,128)(2,1)S(1)}, bf16[384,768]{1,0:T(8,128)(2,1)S(1)}, u32[]{:S(2)}, u32[]{:S(2)}) collective-permute-start(bf16[384,768]{1,0:T(8,128)(2,1)S(1)} %get-tuple-element.88), channel_id=1, source_target_pairs={{0,4},{4,0},{8,12},{12,8},{1,5},{5,1},{9,13},{13,9},{2,6},{6,2},{1... | collective-permute-start | bytes 1769480 | tf_op jit(solution)/shard_map/ppermute | solution.py:22
  115.4 11.0 %collective-permute-start.25 = (bf16[96,768]{1,0:T(8,128)(2,1)S(1)}, bf16[96,768]{1,0:T(8,128)(2,1)S(1)}, u32[]{:S(2)}, u32[]{:S(2)}) collective-permute-start(bf16[96,768]{1,0:T(8,128)(2,1)S(1)} %get-tuple-element.110), channel_id=1, source_target_pairs={{0,1},{1,0},{2,3},{3,2},{4,5},{5,4},{6,7},{7,6},{8,9},{9,8},{10,11... | collective-permute-start | bytes 442376 | tf_op jit(solution)/shard_map/ppermute | solution.py:22
  115.4 11.2 %collective-permute-start.26 = (bf16[96,768]{1,0:T(8,128)(2,1)S(1)}, bf16[96,768]{1,0:T(8,128)(2,1)S(1)}, u32[]{:S(2)}, u32[]{:S(2)}) collective-permute-start(bf16[96,768]{1,0:T(8,128)(2,1)S(1)} %get-tuple-element.109), channel_id=1, source_target_pairs={{0,2},{1,3},{2,0},{3,1},{4,6},{5,7},{6,4},{7,5},{8,10},{9,11},{10,... | collective-permute-start | bytes 442376 | tf_op jit(solution)/shard_map/ppermute | solution.py:22
  116.4 13.9 %collective-permute-start.27 = (bf16[96,768]{1,0:T(8,128)(2,1)S(1)}, bf16[96,768]{1,0:T(8,128)(2,1)S(1)}, u32[]{:S(2)}, u32[]{:S(2)}) collective-permute-start(bf16[96,768]{1,0:T(8,128)(2,1)S(1)} %get-tuple-element.108), channel_id=1, source_target_pairs={{0,3},{1,2},{2,1},{3,0},{4,7},{5,6},{6,5},{7,4},{8,11},{9,10},{10,... | collective-permute-start | bytes 442376 | tf_op jit(solution)/shard_map/ppermute | solution.py:22
  118.9 15.0 %collective-permute-start.32 = (bf16[384,768]{1,0:T(8,128)(2,1)S(1)}, bf16[384,768]{1,0:T(8,128)(2,1)S(1)}, u32[]{:S(2)}, u32[]{:S(2)}) collective-permute-start(bf16[384,768]{1,0:T(8,128)(2,1)S(1)} %get-tuple-element.96), channel_id=1, source_target_pairs={{0,8},{4,12},{8,0},{12,4},{1,9},{5,13},{9,1},{13,5},{2,10},{6,14},... | collective-permute-start | bytes 1769480 | tf_op jit(solution)/shard_map/ppermute | solution.py:22
  131.1 2.0 %collective-permute-start.39 = (f32[2,128]{1,0:T(2,128)S(1)}, f32[2,128]{1,0:T(2,128)S(1)}, u32[]{:S(2)}, u32[]{:S(2)}) collective-permute-start(f32[2,128]{1,0:T(2,128)S(1)} %pad_maximum_fusion), channel_id=1, source_target_pairs={{0,16},{16,0},{1,17},{17,1},{2,18},{18,2},{3,19},{19,3},{4,20},{20... | collective-permute-start | bytes 3080 | tf_op jit(solution)/shard_map/ppermute | solution.py:22
  131.2 21.9 %collective-permute-start.28 = (bf16[128,768]{1,0:T(8,128)(2,1)S(1)}, bf16[128,768]{1,0:T(8,128)(2,1)S(1)}, u32[]{:S(2)}, u32[]{:S(2)}) collective-permute-start(bf16[128,768]{1,0:T(8,128)(2,1)S(1)} %get-tuple-element.103.refs_0_), channel_id=1, source_target_pairs={{0,4},{4,0},{8,12},{12,8},{1,5},{5,1},{9,13},{13,9},{2,6},{6,2},{1... | collective-permute-start | bytes 589832 | tf_op jit(solution)/shard_map/ppermute | solution.py:22
  131.8 23.3 %collective-permute-start.29 = (bf16[128,768]{1,0:T(8,128)(2,1)S(1)}, bf16[128,768]{1,0:T(8,128)(2,1)S(1)}, u32[]{:S(2)}, u32[]{:S(2)}) collective-permute-start(bf16[128,768]{1,0:T(8,128)(2,1)S(1)} %get-tuple-element.103.refs_0_), channel_id=1, source_target_pairs={{0,8},{4,12},{8,0},{12,4},{1,9},{5,13},{9,1},{13,5},{2,10},{6,14},... | collective-permute-start | bytes 589832 | tf_op jit(solution)/shard_map/ppermute | solution.py:22
  133.2 5.4 %collective-permute-start.40 = (f32[2,128]{1,0:T(2,128)S(1)}, f32[2,128]{1,0:T(2,128)S(1)}, u32[]{:S(2)}, u32[]{:S(2)}) collective-permute-start(f32[2,128]{1,0:T(2,128)S(1)} %fusion.21), channel_id=1, source_target_pairs={{0,4},{4,0},{8,12},{12,8},{1,5},{5,1},{9,13},{13,9},{2,6},{6,2},{1... | collective-permute-start | bytes 3080 | tf_op jit(solution)/shard_map/ppermute | solution.py:22
  134.2 6.8 %collective-permute-start.33 = (bf16[96,768]{1,0:T(8,128)(2,1)S(1)}, bf16[96,768]{1,0:T(8,128)(2,1)S(1)}, u32[]{:S(2)}, u32[]{:S(2)}) collective-permute-start(bf16[96,768]{1,0:T(8,128)(2,1)S(1)} %get-tuple-element.106), channel_id=1, source_target_pairs={{0,1},{1,0},{2,3},{3,2},{4,5},{5,4},{6,7},{7,6},{8,9},{9,8},{10,11... | collective-permute-start | bytes 442376 | tf_op jit(solution)/shard_map/ppermute | solution.py:22
  134.3 11.6 %collective-permute-start.34 = (bf16[96,768]{1,0:T(8,128)(2,1)S(1)}, bf16[96,768]{1,0:T(8,128)(2,1)S(1)}, u32[]{:S(2)}, u32[]{:S(2)}) collective-permute-start(bf16[96,768]{1,0:T(8,128)(2,1)S(1)} %get-tuple-element.105), channel_id=1, source_target_pairs={{0,2},{1,3},{2,0},{3,1},{4,6},{5,7},{6,4},{7,5},{8,10},{9,11},{10,... | collective-permute-start | bytes 442376 | tf_op jit(solution)/shard_map/ppermute | solution.py:22
  138.6 11.7 %collective-permute-start.35 = (bf16[96,768]{1,0:T(8,128)(2,1)S(1)}, bf16[96,768]{1,0:T(8,128)(2,1)S(1)}, u32[]{:S(2)}, u32[]{:S(2)}) collective-permute-start(bf16[96,768]{1,0:T(8,128)(2,1)S(1)} %get-tuple-element.104), channel_id=1, source_target_pairs={{0,3},{1,2},{2,1},{3,0},{4,7},{5,6},{6,5},{7,4},{8,11},{9,10},{10,... | collective-permute-start | bytes 442376 | tf_op jit(solution)/shard_map/ppermute | solution.py:22
  141.0 14.1 %collective-permute-start.30 = (bf16[128,768]{1,0:T(8,128)(2,1)S(1)}, bf16[128,768]{1,0:T(8,128)(2,1)S(1)}, u32[]{:S(2)}, u32[]{:S(2)}) collective-permute-start(bf16[128,768]{1,0:T(8,128)(2,1)S(1)} %get-tuple-element.103.refs_0_), channel_id=1, source_target_pairs={{0,12},{4,8},{8,4},{12,0},{1,13},{5,9},{9,5},{13,1},{2,14},{6,10},... | collective-permute-start | bytes 589832 | tf_op jit(solution)/shard_map/ppermute | solution.py:22
  145.8 6.6 %collective-permute-start.41 = (f32[2,128]{1,0:T(2,128)S(1)}, f32[2,128]{1,0:T(2,128)S(1)}, u32[]{:S(2)}, u32[]{:S(2)}) collective-permute-start(f32[2,128]{1,0:T(2,128)S(1)} %fusion.32), channel_id=1, source_target_pairs={{0,8},{4,12},{8,0},{12,4},{1,9},{5,13},{9,1},{13,5},{2,10},{6,14},... | collective-permute-start | bytes 3080 | tf_op jit(solution)/shard_map/ppermute | solution.py:22
  151.0 7.9 %collective-permute-start.36 = (bf16[128,768]{1,0:T(8,128)(2,1)S(1)}, bf16[128,768]{1,0:T(8,128)(2,1)S(1)}, u32[]{:S(2)}, u32[]{:S(2)}) collective-permute-start(bf16[128,768]{1,0:T(8,128)(2,1)S(1)} %fusion.2.refs_0_), channel_id=1, source_target_pairs={{0,4},{4,0},{8,12},{12,8},{1,5},{5,1},{9,13},{13,9},{2,6},{6,2},{1... | collective-permute-start | bytes 589832 | tf_op jit(solution)/shard_map/ppermute | solution.py:22
  152.4 9.8 %collective-permute-start.37 = (bf16[128,768]{1,0:T(8,128)(2,1)S(1)}, bf16[128,768]{1,0:T(8,128)(2,1)S(1)}, u32[]{:S(2)}, u32[]{:S(2)}) collective-permute-start(bf16[128,768]{1,0:T(8,128)(2,1)S(1)} %fusion.2.refs_0_), channel_id=1, source_target_pairs={{0,8},{4,12},{8,0},{12,4},{1,9},{5,13},{9,1},{13,5},{2,10},{6,14},... | collective-permute-start | bytes 589832 | tf_op jit(solution)/shard_map/ppermute | solution.py:22
  153.1 9.2 %collective-permute-start.38 = (bf16[128,768]{1,0:T(8,128)(2,1)S(1)}, bf16[128,768]{1,0:T(8,128)(2,1)S(1)}, u32[]{:S(2)}, u32[]{:S(2)}) collective-permute-start(bf16[128,768]{1,0:T(8,128)(2,1)S(1)} %fusion.2.refs_0_), channel_id=1, source_target_pairs={{0,12},{4,8},{8,4},{12,0},{1,13},{5,9},{9,5},{13,1},{2,14},{6,10},... | collective-permute-start | bytes 589832 | tf_op jit(solution)/shard_map/ppermute | solution.py:22
  155.1 8.1 %copy-start.1 = (bf16[128,3072]{1,0:T(8,128)(2,1)S(1)}, bf16[128,3072]{1,0:T(8,128)(2,1)}, u32[]{:S(2)}) copy-start(bf16[128,3072]{1,0:T(8,128)(2,1)} %param.7) | copy-start | bytes 2359300

commit v4 on v3

--- a/solution.py
+++ b/solution.py
@@ -144,14 +144,15 @@
     rows = own.shape[0] + sum(p.shape[0] for p in parts[0])
     counts = [len(p) for p in parts]
 
-    steps = (stop - start) // BLOCK
+    block = 2 * BLOCK
+    steps = (stop - start) // block
 
     def kernel(t_ref, own_ref, *refs):
         pieces, refs = split_parts(refs, counts)
         down_w, out, send, rows_ref, held, sems = refs
         copies = [
             pltpu.make_async_copy(
-                down_w.at[pl.ds(start + i * BLOCK, BLOCK)], held.at[i], sems.at[i]
+                down_w.at[pl.ds(start + i * block, block)], held.at[i], sems.at[i]
             )
             for i in range(steps)
         ]
@@ -164,8 +165,8 @@
             for q in range(n):
                 part = dot_nt(rows_ref[q], held[i, :, q * quarter : (q + 1) * quarter])
                 total = part if total is None else total + part
-            out[:, i * BLOCK : (i + 1) * BLOCK] = total
-            send[:, i * BLOCK : (i + 1) * BLOCK] = total.astype(BF)
+            out[:, i * block : (i + 1) * block] = total
+            send[:, i * block : (i + 1) * block] = total.astype(BF)
 
     shape = (rows, stop - start)
     return call(
@@ -175,7 +176,7 @@
         [sds(shape, F32), sds(shape, BF)],
         [
             pltpu.VMEM((n, rows, quarter), BF),
-            pltpu.VMEM((steps, BLOCK, depth), BF),
+            pltpu.VMEM((steps, block, depth), BF),
             pltpu.SemaphoreType.DMA((steps,)),
         ],
         2 * rows * depth * (stop - start),
@@ -235,8 +236,7 @@
         self.mats, self.nn = len(mats), nn
         self.hidden, depth = mats[0].shape if nn else mats[0].shape[::-1]
         self.quarter = depth // n
-        self.width = self.quarter if nn else BLOCK
-        self.each = self.quarter // self.width
+        self.width, self.each = self.quarter, 1
         chunk = (self.hidden, self.width) if nn else (self.width, self.hidden)
         count = pieces * self.each * self.mats
         self.scratch = [pltpu.VMEM((count,) + chunk, BF), pltpu.SemaphoreType.DMA((count,))]
@@ -363,7 +363,6 @@
     gate_mat, up_mat, down_mat = (
         pltpu.with_memory_space_constraint(w[0], pltpu.HBM) for w in (w_gate, w_up, w_down)
     )
-    gate_held, up_held = fetch(gate_mat), fetch(up_mat)
     hidden_here = gate_mat.shape[1]
 
     slot_of = slot_index(expert_ids, experts)
@@ -391,14 +390,17 @@
 
     tok_own, tok_out = outgoing(tokens, None)
     cot_own, cot_out = outgoing(cotangent, slot_gate)
-    tok_part = jnp.concatenate(over_z(tok_out), axis=0)
-    tok_x, tok_y = exchange(tok_part, "tensor", 1), exchange(tok_part, "tensor", 2)
-    cot_pieces = over_z(after(cot_out, tok_part))
-    split = tok_part.shape[0] // 2
-    tok_d = [exchange(tok_y[:split], "tensor", 1), exchange(tok_x[split:], "tensor", 2)]
-    tok_d[0], tok_d[1], *cot_pieces = lax.optimization_barrier((*tok_d, *cot_pieces))
-    tok_parts = [[tok_part], [tok_x], [tok_y], tok_d]
-    cot_part = jnp.concatenate(cot_pieces, axis=0)
+    tok_pieces = over_z(tok_out)
+    tok_parts = [tok_pieces] + [
+        [exchange(piece, "tensor", j) for piece in tok_pieces] for j in range(1, n)
+    ]
+    gate_mat, up_mat, *tok_pieces = lax.optimization_barrier((gate_mat, up_mat, *tok_pieces))
+    gate_held, up_held = fetch(gate_mat), fetch(up_mat)
+    cot_pieces = over_z(after(cot_out, *tok_pieces))
+    far = [x for parts in tok_parts[1:] for x in parts]
+    held = lax.optimization_barrier((*far, *cot_pieces))
+    tok_parts[1:] = [list(held[k : k + n - 1]) for k in range(0, len(far), n - 1)]
+    cot_part = jnp.concatenate(held[len(far) :], axis=0)
     cot_parts = [[cot_part]] + [[exchange(cot_part, "tensor", j)] for j in range(1, n)]
 
     turn = after(t_arr, cot_part)

time: 165 us -> 172 us (1.042)
  Pallas kernels: 77 us -> 66.4 us
  starting transfers between devices: 42.3 us -> 50.8 us
  waiting for transfers between devices: 36 us -> 43 us
    pallas_call x14, Pallas kernels: 67.7 us -> 57.2 us  [call(): pl.pallas_call(kernel, in_specs=[SMEM] + [VMEM] * (len(ins) - far) + [HBM...]
    ppermute x42 -> x47, starting transfers between devices: 42.3 us -> 50.8 us  [exchange(): return lax.ppermute(array, axis, [(i, i ^ bit) for i in range(size)])]
    ppermute x42 -> x47, waiting for transfers between devices: 36 us -> 43 us  [exchange(): return lax.ppermute(array, axis, [(i, i ^ bit) for i in range(size)])]
  transfers between devices with their start and end apart: 42 -> 47, of which waited for: 17 -> 15; matrix products, arithmetic and copies ran while one was open for 2% -> 2% of each run, Pallas kernels for 47% -> 39%
where the time goes in v4:
time: 172 us; the launch traced here: 170 us
  Pallas kernels  66.4 us (39%)
  starting transfers between devices  50.8 us (30%)
  waiting for transfers between devices  43 us (25%)
  other arithmetic  3.55 us (2%)
  matrix products  3.42 us (2%)
    pallas_call x14, Pallas kernels, call(): pl.pallas_call(kernel, in_specs=[SMEM] + [VMEM] * (len(ins) - far) + [HBM...  57.2 us
    ppermute x47, starting transfers between devices, exchange(): return lax.ppermute(array, axis, [(i, i ^ bit) for i in range(size)])  50.8 us
    ppermute x47, waiting for transfers between devices, exchange(): return lax.ppermute(array, axis, [(i, i ^ bit) for i in range(size)])  43 us
    pallas_call x2, Pallas kernels, fetch(): pl.pallas_call(kernel, in_specs=[HBM], out_specs=VMEM, out_shape=pltpu.VM...  9.17 us
  transfers between devices with their start and end apart: 47, of which 15 were waited for; matrix products, arithmetic and copies ran while one was open for 2% of the time, Pallas kernels for 39%

profile of v4, /device:TPU:16, one launch (start us, length us, event | category | flops | bytes accessed | tf_op | source)
XLA Modules:
  0.0 169.7 jit_solution(3847213420855104138)
XLA Ops:
  4.2 1.2 fusion.1
  5.5 1.7 collective-permute-start.12
  7.9 3.1 %collective-permute-start.4 = (bf16[96,768]{1,0:T(8,128)(2,1)S(1)}, bf16[96,768]{1,0:T(8,128)(2,1)S(1)}, u32[]{:S(2)}, u32[]{:S(2)}) collective-permute-start(bf16[96,768]{1,0:T(8,128)(2,1)S(1)} %get-tuple-element.131), channel_id=1, source_target_pairs={{0,3},{1,2},{2,1},{3,0},{4,7},{5,6},{6,5},{7,4},{8,11},{9,10},{10,... | collective-permute-start | bytes 442376 | tf_op jit(solution)/shard_map/ppermute | solution.py:22
  11.0 1.2 collective-permute-start.13
  13.8 2.4 %collective-permute-done.refs_0_ = bf16[96,768]{1,0:T(8,128)(2,1)S(1)} collective-permute-done((bf16[96,768]{1,0:T(8,128)(2,1)S(1)}, bf16[96,768]{1,0:T(8,128)(2,1)S(1)}, u32[]{:S(2)}, u32[]{:S(2)}) %collective-permute-start) | collective-permute-done | bytes 147488 | tf_op jit(solution)/shard_map/ppermute | solution.py:22
  16.2 1.5 collective-permute-start.1
  18.6 2.5 %collective-permute-start.10 = (bf16[96,768]{1,0:T(8,128)(2,1)S(1)}, bf16[96,768]{1,0:T(8,128)(2,1)S(1)}, u32[]{:S(2)}, u32[]{:S(2)}) collective-permute-start(bf16[96,768]{1,0:T(8,128)(2,1)S(1)} %collective-permute-done.2.refs_1_), channel_id=1, source_target_pairs={{0,12},{4,8},{8,4},{12,0},{1,13},{5,9},{9,5},{13,1},{2,14},{6,10},... | collective-permute-start | bytes 442376 | tf_op jit(solution)/shard_map/ppermute | solution.py:22
  21.0 10.5 %collective-permute-done.4.refs_2_ = bf16[96,768]{1,0:T(8,128)(2,1)S(1)} collective-permute-done((bf16[96,768]{1,0:T(8,128)(2,1)S(1)}, bf16[96,768]{1,0:T(8,128)(2,1)S(1)}, u32[]{:S(2)}, u32[]{:S(2)}) %collective-permute-start.4) | collective-permute-done | bytes 147488 | tf_op jit(solution)/shard_map/ppermute | solution.py:22
  31.6 2.4 %collective-permute-start.11 = (bf16[96,768]{1,0:T(8,128)(2,1)S(1)}, bf16[96,768]{1,0:T(8,128)(2,1)S(1)}, u32[]{:S(2)}, u32[]{:S(2)}) collective-permute-start(bf16[96,768]{1,0:T(8,128)(2,1)S(1)} %collective-permute-done.4.refs_2_), channel_id=1, source_target_pairs={{0,12},{4,8},{8,4},{12,0},{1,13},{5,9},{9,5},{13,1},{2,14},{6,10},... | collective-permute-start | bytes 442376 | tf_op jit(solution)/shard_map/ppermute | solution.py:22
  34.5 1.6 collective-permute-done.14
  36.1 1.5 collective-permute-start.5
  37.6 1.5 collective-permute-start.6
  39.7 1.5 collective-permute-start.8
  42.3 4.6 %fetch.2.refs_12_ = bf16[3072,2048]{1,0:T(8,128)(2,1)S(1)} custom-call(bf16[3072,2048]{1,0:T(8,128)(2,1)} %bitcast.27), custom_call_target="tpu_custom_call" | custom-call | bytes 12582912 | tf_op jit(solution)/shard_map/fetch/pallas_call | solution.py:65
  46.9 4.6 %fetch.3.refs_13_ = bf16[3072,2048]{1,0:T(8,128)(2,1)S(1)} custom-call(bf16[3072,2048]{1,0:T(8,128)(2,1)} %bitcast.31), custom_call_target="tpu_custom_call" | custom-call | bytes 12582912 | tf_op jit(solution)/shard_map/fetch/pallas_call | solution.py:65
  51.6 1.2 collective-permute-start.17
  52.9 1.5 collective-permute-start.18
  54.4 6.0 %pre_acts.2 = (f32[384,1024]{1,0:T(8,128)S(1)}, f32[384,1024]{1,0:T(8,128)S(1)}, bf16[384,1024]{1,0:T(8,128)(2,1)S(1)}, bf16[384,1024]{1,0:T(8,128)(2,1)S(1)}) custom-call(s32[1]{0:T(128)} %bitcast.t_ref, bf16[96,3072]{1,0:T(8,128)(2,1)S(1)} %convolution_convert_fusion.own_ref, bf16[96,768]{1,0:T(8,128)(2,1)S(1)} %collective-permute-done.refs_0_, ...), custom_call_target="tpu_custom_call" | custom-call | flops 4831838208 | bytes 1048576 | tf_op jit(solution)/shard_map/pre_acts/pallas_call | solution.py:47
  61.3 5.8 %pre_acts.3 = (f32[384,1024]{1,0:T(8,128)S(1)}, f32[384,1024]{1,0:T(8,128)S(1)}, bf16[384,1024]{1,0:T(8,128)(2,1)S(1)}, bf16[384,1024]{1,0:T(8,128)(2,1)S(1)}) custom-call(s32[1]{0:T(128)} %bitcast.t_ref, bf16[96,3072]{1,0:T(8,128)(2,1)S(1)} %convolution_convert_fusion.own_ref, bf16[96,768]{1,0:T(8,128)(2,1)S(1)} %collective-permute-done.refs_0_, ...), custom_call_target="tpu_custom_call" | custom-call | flops 4831838208 | bytes 1048576 | tf_op jit(solution)/shard_map/pre_acts/pallas_call | solution.py:47
  67.8 2.7 %collective-permute-start.23 = (bf16[288,768]{1,0:T(8,128)(2,1)S(1)}, bf16[288,768]{1,0:T(8,128)(2,1)S(1)}, u32[]{:S(2)}, u32[]{:S(2)}) collective-permute-start(bf16[288,768]{1,0:T(8,128)(2,1)S(1)} %constant_dynamic-update-slice_fusion.refs_0_), channel_id=1, source_target_pairs={{0,12},{4,8},{8,4},{12,0},{1,13},{5,9},{9,5},{13,1},{2,14},{6,10},... | collective-permute-start | bytes 1327112 | tf_op jit(solution)/shard_map/ppermute | solution.py:22
  70.9 3.6 %project_first.1 = (bf16[192,768]{1,0:T(8,128)(2,1)S(1)}, bf16[192,768]{1,0:T(8,128)(2,1)S(1)}, bf16[384,2048]{1,0:T(8,128)(2,1)S(1)}) custom-call(s32[1]{0:T(128)} %bitcast.t_ref, f32[384,1024]{1,0:T(8,128)S(1)} %get-tuple-element.75.refs_0_, f32[384,1024]{1,0:T(8,128)S(1)} %get-tuple-element.76.refs_1_, ...), custom_call_target="tpu_custom_call" | custom-call | flops 1207959552 | bytes 1048576 | tf_op jit(solution)/shard_map/project_first/pallas_call | solution.py:47
  74.5 1.2 collective-permute-start.21
  75.7 1.7 collective-permute-start.22
  77.4 5.5 %project_send.1 = (f32[384,768]{1,0:T(8,128)S(1)}, f32[384,768]{1,0:T(8,128)S(1)}) custom-call(s32[1]{0:T(128)} %bitcast.t_ref, bf16[384,2048]{1,0:T(8,128)(2,1)S(1)} %get-tuple-element.84.refs_0_, bf16[2048,3072]{1,0:T(8,128)(2,1)} %bitcast.23), custom_call_target="tpu_custom_call" | custom-call | flops 2415919104 | bytes 1048576 | tf_op jit(solution)/shard_map/project_send/pallas_call | solution.py:47
  82.9 4.7 %grad_hidden.3 = (f32[384,1024]{1,0:T(8,128)S(1)}, bf16[384,1024]{1,0:T(8,128)(2,1)S(1)}) custom-call(s32[1]{0:T(128)} %bitcast.t_ref, bf16[96,3072]{1,0:T(8,128)(2,1)S(1)} %fusion.own_ref, bf16[288,768]{1,0:T(8,128)(2,1)S(1)} %constant_dynamic-update-slice_fusion.refs_0_, bf16[288,768]{1,0:T(8,128)(2,1)S(1)} %collective-permute-done.17.refs_1_, ...), custom_call_target="tpu_custom_call" | custom-call | flops 2415919104 | bytes 1048576 | tf_op jit(solution)/shard_map/grad_hidden/pallas_call | solution.py:47
  87.9 4.7 %grad_hidden.2 = (f32[384,1024]{1,0:T(8,128)S(1)}, bf16[384,1024]{1,0:T(8,128)(2,1)S(1)}) custom-call(s32[1]{0:T(128)} %bitcast.t_ref, bf16[96,3072]{1,0:T(8,128)(2,1)S(1)} %fusion.own_ref, bf16[288,768]{1,0:T(8,128)(2,1)S(1)} %constant_dynamic-update-slice_fusion.refs_0_, bf16[288,768]{1,0:T(8,128)(2,1)S(1)} %collective-permute-done.17.refs_1_, ...), custom_call_target="tpu_custom_call" | custom-call | flops 2415919104 | bytes 1048576 | tf_op jit(solution)/shard_map/grad_hidden/pallas_call | solution.py:47
  94.1 3.3 %project_keep.1 = f32[384,768]{1,0:T(8,128)S(1)} custom-call(s32[1]{0:T(128)} %bitcast.t_ref, bf16[384,2048]{1,0:T(8,128)(2,1)S(1)} %get-tuple-element.84.refs_0_, bf16[2048,3072]{1,0:T(8,128)(2,1)} %bitcast.26), custom_call_target="tpu_custom_call" | custom-call | flops 1207959552 | bytes 1048576 | tf_op jit(solution)/shard_map/project_keep/pallas_call | solution.py:47
  97.4 1.5 collective-permute-start.29
  98.9 5.6 %rows_first.1 = (bf16[192,768]{1,0:T(8,128)(2,1)S(1)}, bf16[192,768]{1,0:T(8,128)(2,1)S(1)}, bf16[384,2048]{1,0:T(8,128)(2,1)S(1)}, bf16[384,2048]{1,0:T(8,128)(2,1)S(1)}) custom-call(s32[1]{0:T(128)} %bitcast.t_ref, f32[384,1024]{1,0:T(8,128)S(1)} %get-tuple-element.75.refs_0_, f32[384,1024]{1,0:T(8,128)S(1)} %copy-done.3, ...), custom_call_target="tpu_custom_call" | custom-call | flops 2415919104 | bytes 1048576 | tf_op jit(solution)/shard_map/rows_first/pallas_call | solution.py:47
  105.1 1.2 collective-permute-start.27
  106.3 10.2 %rows_send.1 = (f32[384,768]{1,0:T(8,128)S(1)}, f32[384,768]{1,0:T(8,128)S(1)}) custom-call(s32[1]{0:T(128)} %bitcast.t_ref, bf16[384,2048]{1,0:T(8,128)(2,1)S(1)} %get-tuple-element.98.refs_0_, bf16[384,2048]{1,0:T(8,128)(2,1)S(1)} %get-tuple-element.99.refs_1_, bf16[3072,2048]{1,0:T(8,128)(2,1)} %bitcast.29, bf16[3072,2048]{1,0:T(8,128)(2,1)} %bitcast.33), custom_call_target="tpu_custom_call" | custom-call | flops 4831838208 | bytes 1048576 | tf_op jit(solution)/shard_map/rows_send/pallas_call | solution.py:47
  116.5 2.7 %collective-permute-done.27.low_ref = bf16[192,768]{1,0:T(8,128)(2,1)S(1)} collective-permute-done((bf16[192,768]{1,0:T(8,128)(2,1)S(1)}, bf16[192,768]{1,0:T(8,128)(2,1)S(1)}, u32[]{:S(2)}, u32[]{:S(2)}) %collective-permute-start.27) | collective-permute-done | bytes 294944 | tf_op jit(solution)/shard_map/ppermute | solution.py:22
  120.4 1.3 collective-permute-start.30
  121.7 2.2 %collective-permute-start.32 = (bf16[96,768]{1,0:T(8,128)(2,1)S(1)}, bf16[96,768]{1,0:T(8,128)(2,1)S(1)}, u32[]{:S(2)}, u32[]{:S(2)}) collective-permute-start(bf16[96,768]{1,0:T(8,128)(2,1)S(1)} %get-tuple-element.124), channel_id=1, source_target_pairs={{0,3},{1,2},{2,1},{3,0},{4,7},{5,6},{6,5},{7,4},{8,11},{9,10},{10,... | collective-permute-start | bytes 442376 | tf_op jit(solution)/shard_map/ppermute | solution.py:22
  125.1 5.5 %rows_keep.1 = f32[384,768]{1,0:T(8,128)S(1)} custom-call(s32[1]{0:T(128)} %bitcast.t_ref, bf16[384,2048]{1,0:T(8,128)(2,1)S(1)} %get-tuple-element.98.refs_0_, bf16[384,2048]{1,0:T(8,128)(2,1)S(1)} %get-tuple-element.99.refs_1_, bf16[3072,2048]{1,0:T(8,128)(2,1)} %bitcast.30, bf16[3072,2048]{1,0:T(8,128)(2,1)} %bitcast.34), custom_call_target="tpu_custom_call" | custom-call | flops 2415919104 | bytes 1048576 | tf_op jit(solution)/shard_map/rows_keep/pallas_call | solution.py:47
  131.8 3.7 %collective-permute-done.32 = bf16[96,768]{1,0:T(8,128)(2,1)S(1)} collective-permute-done((bf16[96,768]{1,0:T(8,128)(2,1)S(1)}, bf16[96,768]{1,0:T(8,128)(2,1)S(1)}, u32[]{:S(2)}, u32[]{:S(2)}) %collective-permute-start.32) | collective-permute-done | bytes 147488 | tf_op jit(solution)/shard_map/ppermute | solution.py:22
  136.4 1.7 %collective-permute-start.33 = (bf16[128,768]{1,0:T(8,128)(2,1)S(1)}, bf16[128,768]{1,0:T(8,128)(2,1)S(1)}, u32[]{:S(2)}, u32[]{:S(2)}) collective-permute-start(bf16[128,768]{1,0:T(8,128)(2,1)S(1)} %get-tuple-element.119.refs_0_), channel_id=1, source_target_pairs={{0,4},{4,0},{8,12},{12,8},{1,5},{5,1},{9,13},{13,9},{2,6},{6,2},{1... | collective-permute-start | bytes 589832 | tf_op jit(solution)/shard_map/ppermute | solution.py:22
  138.2 1.4 collective-permute-start.34
  140.5 1.9 %collective-permute-start.39 = (bf16[96,768]{1,0:T(8,128)(2,1)S(1)}, bf16[96,768]{1,0:T(8,128)(2,1)S(1)}, u32[]{:S(2)}, u32[]{:S(2)}) collective-permute-start(bf16[96,768]{1,0:T(8,128)(2,1)S(1)} %get-tuple-element.121), channel_id=1, source_target_pairs={{0,2},{1,3},{2,0},{3,1},{4,6},{5,7},{6,4},{7,5},{8,10},{9,11},{10,... | collective-permute-start | bytes 442376 | tf_op jit(solution)/shard_map/ppermute | solution.py:22
  142.4 1.4 collective-permute-done.45
  144.2 3.1 %collective-permute-done.38 = bf16[96,768]{1,0:T(8,128)(2,1)S(1)} collective-permute-done((bf16[96,768]{1,0:T(8,128)(2,1)S(1)}, bf16[96,768]{1,0:T(8,128)(2,1)S(1)}, u32[]{:S(2)}, u32[]{:S(2)}) %collective-permute-start.38) | collective-permute-done | bytes 147488 | tf_op jit(solution)/shard_map/ppermute | solution.py:22
  147.2 1.6 collective-permute-start.35
  148.9 3.9 %collective-permute-done.39 = bf16[96,768]{1,0:T(8,128)(2,1)S(1)} collective-permute-done((bf16[96,768]{1,0:T(8,128)(2,1)S(1)}, bf16[96,768]{1,0:T(8,128)(2,1)S(1)}, u32[]{:S(2)}, u32[]{:S(2)}) %collective-permute-start.39) | collective-permute-done | bytes 147488 | tf_op jit(solution)/shard_map/ppermute | solution.py:22
  152.7 3.8 %collective-permute-done.40 = bf16[96,768]{1,0:T(8,128)(2,1)S(1)} collective-permute-done((bf16[96,768]{1,0:T(8,128)(2,1)S(1)}, bf16[96,768]{1,0:T(8,128)(2,1)S(1)}, u32[]{:S(2)}, u32[]{:S(2)}) %collective-permute-start.40) | collective-permute-done | bytes 147488 | tf_op jit(solution)/shard_map/ppermute | solution.py:22
  157.2 1.7 collective-permute-start.41
  159.5 1.3 collective-permute-start.43
  162.3 2.4 %collective-permute-done.41.refs_1_ = bf16[128,768]{1,0:T(8,128)(2,1)S(1)} collective-permute-done((bf16[128,768]{1,0:T(8,128)(2,1)S(1)}, bf16[128,768]{1,0:T(8,128)(2,1)S(1)}, u32[]{:S(2)}, u32[]{:S(2)}) %collective-permute-start.41) | collective-permute-done | bytes 196640 | tf_op jit(solution)/shard_map/ppermute | solution.py:22
  164.7 4.0 %collective-permute-done.42.refs_2_ = bf16[128,768]{1,0:T(8,128)(2,1)S(1)} collective-permute-done((bf16[128,768]{1,0:T(8,128)(2,1)S(1)}, bf16[128,768]{1,0:T(8,128)(2,1)S(1)}, u32[]{:S(2)}, u32[]{:S(2)}) %collective-permute-start.42) | collective-permute-done | bytes 196640 | tf_op jit(solution)/shard_map/ppermute | solution.py:22
  (118 shorter events, 22.5 us)
Async XLA Ops:
  5.5 7.8 %collective-permute-start.12 = (bf16[96,768]{1,0:T(8,128)(2,1)S(1)}, bf16[96,768]{1,0:T(8,128)(2,1)S(1)}, u32[]{:S(2)}, u32[]{:S(2)}) collective-permute-start(bf16[96,768]{1,0:T(8,128)(2,1)S(1)} %get-tuple-element.130), channel_id=1, source_target_pairs={{0,1},{1,0},{2,3},{3,2},{4,5},{5,4},{6,7},{7,6},{8,9},{9,8},{10,11... | collective-permute-start | bytes 442376 | tf_op jit(solution)/shard_map/ppermute | solution.py:22
  7.4 8.7 %collective-permute-start = (bf16[96,768]{1,0:T(8,128)(2,1)S(1)}, bf16[96,768]{1,0:T(8,128)(2,1)S(1)}, u32[]{:S(2)}, u32[]{:S(2)}) collective-permute-start(bf16[96,768]{1,0:T(8,128)(2,1)S(1)} %get-tuple-element.133), channel_id=1, source_target_pairs={{0,1},{1,0},{2,3},{3,2},{4,5},{5,4},{6,7},{7,6},{8,9},{9,8},{10,11... | collective-permute-start | bytes 442376 | tf_op jit(solution)/shard_map/ppermute | solution.py:22
  7.9 10.6 %collective-permute-start.2 = (bf16[96,768]{1,0:T(8,128)(2,1)S(1)}, bf16[96,768]{1,0:T(8,128)(2,1)S(1)}, u32[]{:S(2)}, u32[]{:S(2)}) collective-permute-start(bf16[96,768]{1,0:T(8,128)(2,1)S(1)} %get-tuple-element.132), channel_id=1, source_target_pairs={{0,2},{1,3},{2,0},{3,1},{4,6},{5,7},{6,4},{7,5},{8,10},{9,11},{10,... | collective-permute-start | bytes 442376 | tf_op jit(solution)/shard_map/ppermute | solution.py:22
  7.9 23.6 %collective-permute-start.4 = (bf16[96,768]{1,0:T(8,128)(2,1)S(1)}, bf16[96,768]{1,0:T(8,128)(2,1)S(1)}, u32[]{:S(2)}, u32[]{:S(2)}) collective-permute-start(bf16[96,768]{1,0:T(8,128)(2,1)S(1)} %get-tuple-element.131), channel_id=1, source_target_pairs={{0,3},{1,2},{2,1},{3,0},{4,7},{5,6},{6,5},{7,4},{8,11},{9,10},{10,... | collective-permute-start | bytes 442376 | tf_op jit(solution)/shard_map/ppermute | solution.py:22
  11.0 23.0 %collective-permute-start.13 = (bf16[96,768]{1,0:T(8,128)(2,1)S(1)}, bf16[96,768]{1,0:T(8,128)(2,1)S(1)}, u32[]{:S(2)}, u32[]{:S(2)}) collective-permute-start(bf16[96,768]{1,0:T(8,128)(2,1)S(1)} %get-tuple-element.129), channel_id=1, source_target_pairs={{0,2},{1,3},{2,0},{3,1},{4,6},{5,7},{6,4},{7,5},{8,10},{9,11},{10,... | collective-permute-start | bytes 442376 | tf_op jit(solution)/shard_map/ppermute | solution.py:22
  13.3 22.8 %collective-permute-start.14 = (bf16[96,768]{1,0:T(8,128)(2,1)S(1)}, bf16[96,768]{1,0:T(8,128)(2,1)S(1)}, u32[]{:S(2)}, u32[]{:S(2)}) collective-permute-start(bf16[96,768]{1,0:T(8,128)(2,1)S(1)} %get-tuple-element.128), channel_id=1, source_target_pairs={{0,3},{1,2},{2,1},{3,0},{4,7},{5,6},{6,5},{7,4},{8,11},{9,10},{10,... | collective-permute-start | bytes 442376 | tf_op jit(solution)/shard_map/ppermute | solution.py:22
  16.2 21.5 %collective-permute-start.1 = (bf16[96,768]{1,0:T(8,128)(2,1)S(1)}, bf16[96,768]{1,0:T(8,128)(2,1)S(1)}, u32[]{:S(2)}, u32[]{:S(2)}) collective-permute-start(bf16[96,768]{1,0:T(8,128)(2,1)S(1)} %collective-permute-done.refs_0_), channel_id=1, source_target_pairs={{0,4},{4,0},{8,12},{12,8},{1,5},{5,1},{9,13},{13,9},{2,6},{6,2},{1... | collective-permute-start | bytes 442376 | tf_op jit(solution)/shard_map/ppermute | solution.py:22
  18.6 20.6 %collective-permute-start.10 = (bf16[96,768]{1,0:T(8,128)(2,1)S(1)}, bf16[96,768]{1,0:T(8,128)(2,1)S(1)}, u32[]{:S(2)}, u32[]{:S(2)}) collective-permute-start(bf16[96,768]{1,0:T(8,128)(2,1)S(1)} %collective-permute-done.2.refs_1_), channel_id=1, source_target_pairs={{0,12},{4,8},{8,4},{12,0},{1,13},{5,9},{9,5},{13,1},{2,14},{6,10},... | collective-permute-start | bytes 442376 | tf_op jit(solution)/shard_map/ppermute | solution.py:22
  31.6 8.1 %collective-permute-start.11 = (bf16[96,768]{1,0:T(8,128)(2,1)S(1)}, bf16[96,768]{1,0:T(8,128)(2,1)S(1)}, u32[]{:S(2)}, u32[]{:S(2)}) collective-permute-start(bf16[96,768]{1,0:T(8,128)(2,1)S(1)} %collective-permute-done.4.refs_2_), channel_id=1, source_target_pairs={{0,12},{4,8},{8,4},{12,0},{1,13},{5,9},{9,5},{13,1},{2,14},{6,10},... | collective-permute-start | bytes 442376 | tf_op jit(solution)/shard_map/ppermute | solution.py:22
  34.0 7.2 %collective-permute-start.3 = (bf16[96,768]{1,0:T(8,128)(2,1)S(1)}, bf16[96,768]{1,0:T(8,128)(2,1)S(1)}, u32[]{:S(2)}, u32[]{:S(2)}) collective-permute-start(bf16[96,768]{1,0:T(8,128)(2,1)S(1)} %collective-permute-done.2.refs_1_), channel_id=1, source_target_pairs={{0,4},{4,0},{8,12},{12,8},{1,5},{5,1},{9,13},{13,9},{2,6},{6,2},{1... | collective-permute-start | bytes 442376 | tf_op jit(solution)/shard_map/ppermute | solution.py:22
  36.1 15.4 %collective-permute-start.5 = (bf16[96,768]{1,0:T(8,128)(2,1)S(1)}, bf16[96,768]{1,0:T(8,128)(2,1)S(1)}, u32[]{:S(2)}, u32[]{:S(2)}) collective-permute-start(bf16[96,768]{1,0:T(8,128)(2,1)S(1)} %collective-permute-done.4.refs_2_), channel_id=1, source_target_pairs={{0,4},{4,0},{8,12},{12,8},{1,5},{5,1},{9,13},{13,9},{2,6},{6,2},{1... | collective-permute-start | bytes 442376 | tf_op jit(solution)/shard_map/ppermute | solution.py:22
  37.6 13.9 %collective-permute-start.6 = (bf16[96,768]{1,0:T(8,128)(2,1)S(1)}, bf16[96,768]{1,0:T(8,128)(2,1)S(1)}, u32[]{:S(2)}, u32[]{:S(2)}) collective-permute-start(bf16[96,768]{1,0:T(8,128)(2,1)S(1)} %collective-permute-done.refs_0_), channel_id=1, source_target_pairs={{0,8},{4,12},{8,0},{12,4},{1,9},{5,13},{9,1},{13,5},{2,10},{6,14},... | collective-permute-start | bytes 442376 | tf_op jit(solution)/shard_map/ppermute | solution.py:22
  39.2 12.4 %collective-permute-start.7 = (bf16[96,768]{1,0:T(8,128)(2,1)S(1)}, bf16[96,768]{1,0:T(8,128)(2,1)S(1)}, u32[]{:S(2)}, u32[]{:S(2)}) collective-permute-start(bf16[96,768]{1,0:T(8,128)(2,1)S(1)} %collective-permute-done.2.refs_1_), channel_id=1, source_target_pairs={{0,8},{4,12},{8,0},{12,4},{1,9},{5,13},{9,1},{13,5},{2,10},{6,14},... | collective-permute-start | bytes 442376 | tf_op jit(solution)/shard_map/ppermute | solution.py:22
  39.7 11.9 %collective-permute-start.8 = (bf16[96,768]{1,0:T(8,128)(2,1)S(1)}, bf16[96,768]{1,0:T(8,128)(2,1)S(1)}, u32[]{:S(2)}, u32[]{:S(2)}) collective-permute-start(bf16[96,768]{1,0:T(8,128)(2,1)S(1)} %collective-permute-done.4.refs_2_), channel_id=1, source_target_pairs={{0,8},{4,12},{8,0},{12,4},{1,9},{5,13},{9,1},{13,5},{2,10},{6,14},... | collective-permute-start | bytes 442376 | tf_op jit(solution)/shard_map/ppermute | solution.py:22
  41.2 10.4 %collective-permute-start.9 = (bf16[96,768]{1,0:T(8,128)(2,1)S(1)}, bf16[96,768]{1,0:T(8,128)(2,1)S(1)}, u32[]{:S(2)}, u32[]{:S(2)}) collective-permute-start(bf16[96,768]{1,0:T(8,128)(2,1)S(1)} %collective-permute-done.refs_0_), channel_id=1, source_target_pairs={{0,12},{4,8},{8,4},{12,0},{1,13},{5,9},{9,5},{13,1},{2,14},{6,10},... | collective-permute-start | bytes 442376 | tf_op jit(solution)/shard_map/ppermute | solution.py:22
  51.6 9.4 %collective-permute-start.17 = (bf16[288,768]{1,0:T(8,128)(2,1)S(1)}, bf16[288,768]{1,0:T(8,128)(2,1)S(1)}, u32[]{:S(2)}, u32[]{:S(2)}) collective-permute-start(bf16[288,768]{1,0:T(8,128)(2,1)S(1)} %constant_dynamic-update-slice_fusion.refs_0_), channel_id=1, source_target_pairs={{0,4},{4,0},{8,12},{12,8},{1,5},{5,1},{9,13},{13,9},{2,6},{6,2},{1... | collective-permute-start | bytes 1327112 | tf_op jit(solution)/shard_map/ppermute | solution.py:22
  52.9 8.5 %collective-permute-start.18 = (bf16[288,768]{1,0:T(8,128)(2,1)S(1)}, bf16[288,768]{1,0:T(8,128)(2,1)S(1)}, u32[]{:S(2)}, u32[]{:S(2)}) collective-permute-start(bf16[288,768]{1,0:T(8,128)(2,1)S(1)} %constant_dynamic-update-slice_fusion.refs_0_), channel_id=1, source_target_pairs={{0,8},{4,12},{8,0},{12,4},{1,9},{5,13},{9,1},{13,5},{2,10},{6,14},... | collective-permute-start | bytes 1327112 | tf_op jit(solution)/shard_map/ppermute | solution.py:22
  60.4 10.5 %copy-start.2 = (f32[384,1024]{1,0:T(8,128)}, f32[384,1024]{1,0:T(8,128)S(1)}, u32[]{:S(2)}) copy-start(f32[384,1024]{1,0:T(8,128)S(1)} %get-tuple-element.76.refs_1_) | copy-start | bytes 4718596
  60.4 10.4 %collective-permute-start.15 = (bf16[384,1024]{1,0:T(8,128)(2,1)S(1)}, bf16[384,1024]{1,0:T(8,128)(2,1)S(1)}, u32[]{:S(2)}, u32[]{:S(2)}) collective-permute-start(bf16[384,1024]{1,0:T(8,128)(2,1)S(1)} %get-tuple-element.77), channel_id=1, source_target_pairs={{0,16},{16,0},{1,17},{17,1},{2,18},{18,2},{3,19},{19,3},{4,20},{20... | collective-permute-start | bytes 2359304 | tf_op jit(solution)/shard_map/ppermute | solution.py:22
  60.5 10.3 %collective-permute-start.16 = (bf16[384,1024]{1,0:T(8,128)(2,1)S(1)}, bf16[384,1024]{1,0:T(8,128)(2,1)S(1)}, u32[]{:S(2)}, u32[]{:S(2)}) collective-permute-start(bf16[384,1024]{1,0:T(8,128)(2,1)S(1)} %get-tuple-element.78), channel_id=1, source_target_pairs={{0,16},{16,0},{1,17},{17,1},{2,18},{18,2},{3,19},{19,3},{4,20},{20... | collective-permute-start | bytes 2359304 | tf_op jit(solution)/shard_map/ppermute | solution.py:22
  67.2 3.7 %collective-permute-start.19 = (bf16[384,1024]{1,0:T(8,128)(2,1)S(1)}, bf16[384,1024]{1,0:T(8,128)(2,1)S(1)}, u32[]{:S(2)}, u32[]{:S(2)}) collective-permute-start(bf16[384,1024]{1,0:T(8,128)(2,1)S(1)} %get-tuple-element.82), channel_id=1, source_target_pairs={{0,16},{16,0},{1,17},{17,1},{2,18},{18,2},{3,19},{19,3},{4,20},{20... | collective-permute-start | bytes 2359304 | tf_op jit(solution)/shard_map/ppermute | solution.py:22
  67.3 3.6 %collective-permute-start.20 = (bf16[384,1024]{1,0:T(8,128)(2,1)S(1)}, bf16[384,1024]{1,0:T(8,128)(2,1)S(1)}, u32[]{:S(2)}, u32[]{:S(2)}) collective-permute-start(bf16[384,1024]{1,0:T(8,128)(2,1)S(1)} %get-tuple-element.83), channel_id=1, source_target_pairs={{0,16},{16,0},{1,17},{17,1},{2,18},{18,2},{3,19},{19,3},{4,20},{20... | collective-permute-start | bytes 2359304 | tf_op jit(solution)/shard_map/ppermute | solution.py:22
  67.8 15.1 %collective-permute-start.23 = (bf16[288,768]{1,0:T(8,128)(2,1)S(1)}, bf16[288,768]{1,0:T(8,128)(2,1)S(1)}, u32[]{:S(2)}, u32[]{:S(2)}) collective-permute-start(bf16[288,768]{1,0:T(8,128)(2,1)S(1)} %constant_dynamic-update-slice_fusion.refs_0_), channel_id=1, source_target_pairs={{0,12},{4,8},{8,4},{12,0},{1,13},{5,9},{9,5},{13,1},{2,14},{6,10},... | collective-permute-start | bytes 1327112 | tf_op jit(solution)/shard_map/ppermute | solution.py:22
  74.5 13.2 %collective-permute-start.21 = (bf16[192,768]{1,0:T(8,128)(2,1)S(1)}, bf16[192,768]{1,0:T(8,128)(2,1)S(1)}, u32[]{:S(2)}, u32[]{:S(2)}) collective-permute-start(bf16[192,768]{1,0:T(8,128)(2,1)S(1)} %get-tuple-element.87), channel_id=1, source_target_pairs={{0,4},{4,0},{8,12},{12,8},{1,5},{5,1},{9,13},{13,9},{2,6},{6,2},{1... | collective-permute-start | bytes 884744 | tf_op jit(solution)/shard_map/ppermute | solution.py:22
  75.7 12.0 %collective-permute-start.22 = (bf16[192,768]{1,0:T(8,128)(2,1)S(1)}, bf16[192,768]{1,0:T(8,128)(2,1)S(1)}, u32[]{:S(2)}, u32[]{:S(2)}) collective-permute-start(bf16[192,768]{1,0:T(8,128)(2,1)S(1)} %get-tuple-element.88), channel_id=1, source_target_pairs={{0,8},{4,12},{8,0},{12,4},{1,9},{5,13},{9,1},{13,5},{2,10},{6,14},... | collective-permute-start | bytes 884744 | tf_op jit(solution)/shard_map/ppermute | solution.py:22
  87.6 11.3 %collective-permute-start.24 = (bf16[384,1024]{1,0:T(8,128)(2,1)S(1)}, bf16[384,1024]{1,0:T(8,128)(2,1)S(1)}, u32[]{:S(2)}, u32[]{:S(2)}) collective-permute-start(bf16[384,1024]{1,0:T(8,128)(2,1)S(1)} %get-tuple-element.96), channel_id=1, source_target_pairs={{0,16},{16,0},{1,17},{17,1},{2,18},{18,2},{3,19},{19,3},{4,20},{20... | collective-permute-start | bytes 2359304 | tf_op jit(solution)/shard_map/ppermute | solution.py:22
  92.7 6.2 %collective-permute-start.25 = (bf16[384,1024]{1,0:T(8,128)(2,1)S(1)}, bf16[384,1024]{1,0:T(8,128)(2,1)S(1)}, u32[]{:S(2)}, u32[]{:S(2)}) collective-permute-start(bf16[384,1024]{1,0:T(8,128)(2,1)S(1)} %get-tuple-element.91), channel_id=1, source_target_pairs={{0,16},{16,0},{1,17},{17,1},{2,18},{18,2},{3,19},{19,3},{4,20},{20... | collective-permute-start | bytes 2359304 | tf_op jit(solution)/shard_map/ppermute | solution.py:22
  93.2 27.0 %collective-permute-start.28 = (bf16[384,768]{1,0:T(8,128)(2,1)S(1)}, bf16[384,768]{1,0:T(8,128)(2,1)S(1)}, u32[]{:S(2)}, u32[]{:S(2)}) collective-permute-start(bf16[384,768]{1,0:T(8,128)(2,1)S(1)} %get-tuple-element.89), channel_id=1, source_target_pairs={{0,4},{4,0},{8,12},{12,8},{1,5},{5,1},{9,13},{13,9},{2,6},{6,2},{1... | collective-permute-start | bytes 1769480 | tf_op jit(solution)/shard_map/ppermute | solution.py:22
  97.4 22.8 %collective-permute-start.29 = (bf16[384,768]{1,0:T(8,128)(2,1)S(1)}, bf16[384,768]{1,0:T(8,128)(2,1)S(1)}, u32[]{:S(2)}, u32[]{:S(2)}) collective-permute-start(bf16[384,768]{1,0:T(8,128)(2,1)S(1)} %get-tuple-element.106), channel_id=1, source_target_pairs={{0,8},{4,12},{8,0},{12,4},{1,9},{5,13},{9,1},{13,5},{2,10},{6,14},... | collective-permute-start | bytes 1769480 | tf_op jit(solution)/shard_map/ppermute | solution.py:22
  104.5 12.0 %collective-permute-start.26 = (bf16[192,768]{1,0:T(8,128)(2,1)S(1)}, bf16[192,768]{1,0:T(8,128)(2,1)S(1)}, u32[]{:S(2)}, u32[]{:S(2)}) collective-permute-start(bf16[192,768]{1,0:T(8,128)(2,1)S(1)} %get-tuple-element.102), channel_id=1, source_target_pairs={{0,4},{4,0},{8,12},{12,8},{1,5},{5,1},{9,13},{13,9},{2,6},{6,2},{1... | collective-permute-start | bytes 884744 | tf_op jit(solution)/shard_map/ppermute | solution.py:22
  105.1 14.1 %collective-permute-start.27 = (bf16[192,768]{1,0:T(8,128)(2,1)S(1)}, bf16[192,768]{1,0:T(8,128)(2,1)S(1)}, u32[]{:S(2)}, u32[]{:S(2)}) collective-permute-start(bf16[192,768]{1,0:T(8,128)(2,1)S(1)} %get-tuple-element.103), channel_id=1, source_target_pairs={{0,8},{4,12},{8,0},{12,4},{1,9},{5,13},{9,1},{13,5},{2,10},{6,14},... | collective-permute-start | bytes 884744 | tf_op jit(solution)/shard_map/ppermute | solution.py:22
  119.3 20.8 %collective-permute-start.36 = (bf16[384,768]{1,0:T(8,128)(2,1)S(1)}, bf16[384,768]{1,0:T(8,128)(2,1)S(1)}, u32[]{:S(2)}, u32[]{:S(2)}) collective-permute-start(bf16[384,768]{1,0:T(8,128)(2,1)S(1)} %get-tuple-element.104), channel_id=1, source_target_pairs={{0,4},{4,0},{8,12},{12,8},{1,5},{5,1},{9,13},{13,9},{2,6},{6,2},{1... | collective-permute-start | bytes 1769480 | tf_op jit(solution)/shard_map/ppermute | solution.py:22
  120.4 10.2 %collective-permute-start.30 = (bf16[96,768]{1,0:T(8,128)(2,1)S(1)}, bf16[96,768]{1,0:T(8,128)(2,1)S(1)}, u32[]{:S(2)}, u32[]{:S(2)}) collective-permute-start(bf16[96,768]{1,0:T(8,128)(2,1)S(1)} %get-tuple-element.126), channel_id=1, source_target_pairs={{0,1},{1,0},{2,3},{3,2},{4,5},{5,4},{6,7},{7,6},{8,9},{9,8},{10,11... | collective-permute-start | bytes 442376 | tf_op jit(solution)/shard_map/ppermute | solution.py:22
  121.7 10.1 %collective-permute-start.31 = (bf16[96,768]{1,0:T(8,128)(2,1)S(1)}, bf16[96,768]{1,0:T(8,128)(2,1)S(1)}, u32[]{:S(2)}, u32[]{:S(2)}) collective-permute-start(bf16[96,768]{1,0:T(8,128)(2,1)S(1)} %get-tuple-element.125), channel_id=1, source_target_pairs={{0,2},{1,3},{2,0},{3,1},{4,6},{5,7},{6,4},{7,5},{8,10},{9,11},{10,... | collective-permute-start | bytes 442376 | tf_op jit(solution)/shard_map/ppermute | solution.py:22
  121.7 13.8 %collective-permute-start.32 = (bf16[96,768]{1,0:T(8,128)(2,1)S(1)}, bf16[96,768]{1,0:T(8,128)(2,1)S(1)}, u32[]{:S(2)}, u32[]{:S(2)}) collective-permute-start(bf16[96,768]{1,0:T(8,128)(2,1)S(1)} %get-tuple-element.124), channel_id=1, source_target_pairs={{0,3},{1,2},{2,1},{3,0},{4,7},{5,6},{6,5},{7,4},{8,11},{9,10},{10,... | collective-permute-start | bytes 442376 | tf_op jit(solution)/shard_map/ppermute | solution.py:22
  124.0 16.1 %collective-permute-start.37 = (bf16[384,768]{1,0:T(8,128)(2,1)S(1)}, bf16[384,768]{1,0:T(8,128)(2,1)S(1)}, u32[]{:S(2)}, u32[]{:S(2)}) collective-permute-start(bf16[384,768]{1,0:T(8,128)(2,1)S(1)} %get-tuple-element.112), channel_id=1, source_target_pairs={{0,8},{4,12},{8,0},{12,4},{1,9},{5,13},{9,1},{13,5},{2,10},{6,14},... | collective-permute-start | bytes 1769480 | tf_op jit(solution)/shard_map/ppermute | solution.py:22
  136.3 3.2 %collective-permute-start.44 = (f32[2,128]{1,0:T(2,128)S(1)}, f32[2,128]{1,0:T(2,128)S(1)}, u32[]{:S(2)}, u32[]{:S(2)}) collective-permute-start(f32[2,128]{1,0:T(2,128)S(1)} %pad_maximum_fusion), channel_id=1, source_target_pairs={{0,16},{16,0},{1,17},{17,1},{2,18},{18,2},{3,19},{19,3},{4,20},{20... | collective-permute-start | bytes 3080 | tf_op jit(solution)/shard_map/ppermute | solution.py:22
  136.4 23.1 %collective-permute-start.33 = (bf16[128,768]{1,0:T(8,128)(2,1)S(1)}, bf16[128,768]{1,0:T(8,128)(2,1)S(1)}, u32[]{:S(2)}, u32[]{:S(2)}) collective-permute-start(bf16[128,768]{1,0:T(8,128)(2,1)S(1)} %get-tuple-element.119.refs_0_), channel_id=1, source_target_pairs={{0,4},{4,0},{8,12},{12,8},{1,5},{5,1},{9,13},{13,9},{2,6},{6,2},{1... | collective-permute-start | bytes 589832 | tf_op jit(solution)/shard_map/ppermute | solution.py:22
  138.2 23.2 %collective-permute-start.34 = (bf16[128,768]{1,0:T(8,128)(2,1)S(1)}, bf16[128,768]{1,0:T(8,128)(2,1)S(1)}, u32[]{:S(2)}, u32[]{:S(2)}) collective-permute-start(bf16[128,768]{1,0:T(8,128)(2,1)S(1)} %get-tuple-element.119.refs_0_), channel_id=1, source_target_pairs={{0,8},{4,12},{8,0},{12,4},{1,9},{5,13},{9,1},{13,5},{2,10},{6,14},... | collective-permute-start | bytes 589832 | tf_op jit(solution)/shard_map/ppermute | solution.py:22
  139.6 4.2 %collective-permute-start.45 = (f32[2,128]{1,0:T(2,128)S(1)}, f32[2,128]{1,0:T(2,128)S(1)}, u32[]{:S(2)}, u32[]{:S(2)}) collective-permute-start(f32[2,128]{1,0:T(2,128)S(1)} %fusion.21), channel_id=1, source_target_pairs={{0,4},{4,0},{8,12},{12,8},{1,5},{5,1},{9,13},{13,9},{2,6},{6,2},{1... | collective-permute-start | bytes 3080 | tf_op jit(solution)/shard_map/ppermute | solution.py:22
  140.4 6.8 %collective-permute-start.38 = (bf16[96,768]{1,0:T(8,128)(2,1)S(1)}, bf16[96,768]{1,0:T(8,128)(2,1)S(1)}, u32[]{:S(2)}, u32[]{:S(2)}) collective-permute-start(bf16[96,768]{1,0:T(8,128)(2,1)S(1)} %get-tuple-element.122), channel_id=1, source_target_pairs={{0,1},{1,0},{2,3},{3,2},{4,5},{5,4},{6,7},{7,6},{8,9},{9,8},{10,11... | collective-permute-start | bytes 442376 | tf_op jit(solution)/shard_map/ppermute | solution.py:22
  140.5 12.3 %collective-permute-start.39 = (bf16[96,768]{1,0:T(8,128)(2,1)S(1)}, bf16[96,768]{1,0:T(8,128)(2,1)S(1)}, u32[]{:S(2)}, u32[]{:S(2)}) collective-permute-start(bf16[96,768]{1,0:T(8,128)(2,1)S(1)} %get-tuple-element.121), channel_id=1, source_target_pairs={{0,2},{1,3},{2,0},{3,1},{4,6},{5,7},{6,4},{7,5},{8,10},{9,11},{10,... | collective-permute-start | bytes 442376 | tf_op jit(solution)/shard_map/ppermute | solution.py:22
  143.8 12.7 %collective-permute-start.40 = (bf16[96,768]{1,0:T(8,128)(2,1)S(1)}, bf16[96,768]{1,0:T(8,128)(2,1)S(1)}, u32[]{:S(2)}, u32[]{:S(2)}) collective-permute-start(bf16[96,768]{1,0:T(8,128)(2,1)S(1)} %get-tuple-element.120), channel_id=1, source_target_pairs={{0,3},{1,2},{2,1},{3,0},{4,7},{5,6},{6,5},{7,4},{8,11},{9,10},{10,... | collective-permute-start | bytes 442376 | tf_op jit(solution)/shard_map/ppermute | solution.py:22
  147.2 14.1 %collective-permute-start.35 = (bf16[128,768]{1,0:T(8,128)(2,1)S(1)}, bf16[128,768]{1,0:T(8,128)(2,1)S(1)}, u32[]{:S(2)}, u32[]{:S(2)}) collective-permute-start(bf16[128,768]{1,0:T(8,128)(2,1)S(1)} %get-tuple-element.119.refs_0_), channel_id=1, source_target_pairs={{0,12},{4,8},{8,4},{12,0},{1,13},{5,9},{9,5},{13,1},{2,14},{6,10},... | collective-permute-start | bytes 589832 | tf_op jit(solution)/shard_map/ppermute | solution.py:22
  152.7 6.1 %collective-permute-start.46 = (f32[2,128]{1,0:T(2,128)S(1)}, f32[2,128]{1,0:T(2,128)S(1)}, u32[]{:S(2)}, u32[]{:S(2)}) collective-permute-start(f32[2,128]{1,0:T(2,128)S(1)} %fusion.32), channel_id=1, source_target_pairs={{0,8},{4,12},{8,0},{12,4},{1,9},{5,13},{9,1},{13,5},{2,10},{6,14},... | collective-permute-start | bytes 3080 | tf_op jit(solution)/shard_map/ppermute | solution.py:22
  157.2 7.5 %collective-permute-start.41 = (bf16[128,768]{1,0:T(8,128)(2,1)S(1)}, bf16[128,768]{1,0:T(8,128)(2,1)S(1)}, u32[]{:S(2)}, u32[]{:S(2)}) collective-permute-start(bf16[128,768]{1,0:T(8,128)(2,1)S(1)} %fusion.2.refs_0_), channel_id=1, source_target_pairs={{0,4},{4,0},{8,12},{12,8},{1,5},{5,1},{9,13},{13,9},{2,6},{6,2},{1... | collective-permute-start | bytes 589832 | tf_op jit(solution)/shard_map/ppermute | solution.py:22
  158.9 9.9 %collective-permute-start.42 = (bf16[128,768]{1,0:T(8,128)(2,1)S(1)}, bf16[128,768]{1,0:T(8,128)(2,1)S(1)}, u32[]{:S(2)}, u32[]{:S(2)}) collective-permute-start(bf16[128,768]{1,0:T(8,128)(2,1)S(1)} %fusion.2.refs_0_), channel_id=1, source_target_pairs={{0,8},{4,12},{8,0},{12,4},{1,9},{5,13},{9,1},{13,5},{2,10},{6,14},... | collective-permute-start | bytes 589832 | tf_op jit(solution)/shard_map/ppermute | solution.py:22
  159.5 9.3 %collective-permute-start.43 = (bf16[128,768]{1,0:T(8,128)(2,1)S(1)}, bf16[128,768]{1,0:T(8,128)(2,1)S(1)}, u32[]{:S(2)}, u32[]{:S(2)}) collective-permute-start(bf16[128,768]{1,0:T(8,128)(2,1)S(1)} %fusion.2.refs_0_), channel_id=1, source_target_pairs={{0,12},{4,8},{8,4},{12,0},{1,13},{5,9},{9,5},{13,1},{2,14},{6,10},... | collective-permute-start | bytes 589832 | tf_op jit(solution)/shard_map/ppermute | solution.py:22
  (6 other events, 41.0 us)

commit v5 on v4

--- a/solution.py
+++ b/solution.py
@@ -108,13 +108,13 @@
 
     def kernel(t_ref, own_ref, *refs):
         pieces, refs = split_parts(refs, counts)
-        gate_w, up_w, gate_o, up_o, gate_s, up_s, rows_ref = refs
+        gate_w, up_w, gate_o, up_o, send, rows_ref = refs
         lay_out(t_ref[0], own_ref, pieces, rows_ref)
 
         @pl.loop(0, (stop - start) // BLOCK)
         def _(i):
             off = pl.multiple_of(i * BLOCK, BLOCK)
-            for w, out, send in ((gate_w, gate_o, gate_s), (up_w, up_o, up_s)):
+            for w, out, at in ((gate_w, gate_o, 0), (up_w, up_o, stop - start)):
                 total = None
                 for q in range(n):
                     part = dot_nn(
@@ -122,14 +122,14 @@
                     )
                     total = part if total is None else total + part
                 out[:, pl.ds(off, BLOCK)] = total
-                send[:, pl.ds(off, BLOCK)] = total.astype(BF)
+                send[:, pl.ds(at + off, BLOCK)] = total.astype(BF)
 
     shape = (rows, stop - start)
     return call(
         kernel,
         t,
         [own] + [x for p in parts for x in p] + [gate_mat, up_mat],
-        [sds(shape, F32)] * 2 + [sds(shape, BF)] * 2,
+        [sds(shape, F32)] * 2 + [sds((rows, 2 * (stop - start)), BF)],
         [pltpu.VMEM((n, rows, quarter), BF)],
         4 * rows * depth * (stop - start),
         LIMIT,
@@ -201,11 +201,12 @@
 
     def body(here):
         at = 0
-        for g in range(0, len(ins), 4):
-            gate_o, up_o, gate_r, up_r = ins[g : g + 4]
-            cols = slice(at, at + gate_o.shape[1])
-            gate = gate_o[here, :] + gate_r[here, :].astype(F32)
-            up = up_o[here, :] + up_r[here, :].astype(F32)
+        for g in range(0, len(ins), 3):
+            gate_o, up_o, both_r = ins[g : g + 3]
+            width = gate_o.shape[1]
+            cols = slice(at, at + width)
+            gate = gate_o[here, :] + both_r[here, :width].astype(F32)
+            up = up_o[here, :] + both_r[here, width:].astype(F32)
             hidden_ref[here, cols] = (gate * jax.nn.sigmoid(gate) * up).astype(BF)
             at += gate_o.shape[1]
 
@@ -217,11 +218,12 @@
 
     def body(here):
         at = 0
-        for g in range(0, len(ins), 6):
-            gate_o, up_o, gate_r, up_r, gh_o, gh_r = ins[g : g + 6]
-            cols = slice(at, at + gate_o.shape[1])
-            gate = gate_o[here, :] + gate_r[here, :].astype(F32)
-            up = up_o[here, :] + up_r[here, :].astype(F32)
+        for g in range(0, len(ins), 5):
+            gate_o, up_o, both_r, gh_o, gh_r = ins[g : g + 5]
+            width = gate_o.shape[1]
+            cols = slice(at, at + width)
+            gate = gate_o[here, :] + both_r[here, :width].astype(F32)
+            up = up_o[here, :] + both_r[here, width:].astype(F32)
             grad = gh_o[here, :] + gh_r[here, :].astype(F32)
             s = jax.nn.sigmoid(gate)
             gg_ref[here, cols] = (grad * up * (s * (1.0 + gate * (1.0 - s)))).astype(BF)
@@ -390,17 +392,21 @@
 
     tok_own, tok_out = outgoing(tokens, None)
     cot_own, cot_out = outgoing(cotangent, slot_gate)
-    tok_pieces = over_z(tok_out)
-    tok_parts = [tok_pieces] + [
-        [exchange(piece, "tensor", j) for piece in tok_pieces] for j in range(1, n)
+    tok_z = over_z(tok_out)
+    first, rest = tok_z[0], tok_z[1:]
+    first_far = [exchange(first, "tensor", j) for j in range(1, n)]
+    gate_held = fetch(after(gate_mat, first))
+    up_held = fetch(after(up_mat, gate_held, *first_far))
+    rest = jnp.concatenate(after(tuple(rest), up_held), axis=0)
+    rest_x, rest_y = exchange(rest, "tensor", 1), exchange(rest, "tensor", 2)
+    cot_z = over_z(after(cot_out, rest))
+    split = rest.shape[0] // 2
+    rest_d = [exchange(rest_y[:split], "tensor", 1), exchange(rest_x[split:], "tensor", 2)]
+    rest_d[0], rest_d[1], *cot_z = lax.optimization_barrier((*rest_d, *cot_z))
+    tok_parts = [
+        [first, rest], [first_far[0], rest_x], [first_far[1], rest_y], [first_far[2], *rest_d]
     ]
-    gate_mat, up_mat, *tok_pieces = lax.optimization_barrier((gate_mat, up_mat, *tok_pieces))
-    gate_held, up_held = fetch(gate_mat), fetch(up_mat)
-    cot_pieces = over_z(after(cot_out, *tok_pieces))
-    far = [x for parts in tok_parts[1:] for x in parts]
-    held = lax.optimization_barrier((*far, *cot_pieces))
-    tok_parts[1:] = [list(held[k : k + n - 1]) for k in range(0, len(far), n - 1)]
-    cot_part = jnp.concatenate(held[len(far) :], axis=0)
+    cot_part = jnp.concatenate(cot_z, axis=0)
     cot_parts = [[cot_part]] + [[exchange(cot_part, "tensor", j)] for j in range(1, n)]
 
     turn = after(t_arr, cot_part)
@@ -408,21 +414,21 @@
     for start in range(0, hidden_here, hidden_here // 2):
         if start:
             turn = after(t_arr, cot_parts[1][0], cot_parts[2][0])
-        gate_o, up_o, gate_s, up_s = pre_acts(
+        gate_o, up_o, sent = pre_acts(
             turn, tok_own, tok_parts, gate_held, up_held, start, start + hidden_here // 2
         )
-        pres.append([gate_o, up_o, exchange(gate_s, "wide", 1), exchange(up_s, "wide", 1)])
-
-    def sum_back(arrived, keep, *others):
+        pres.append([gate_o, up_o, exchange(sent, "wide", 1)])
+
+    def summed(arrived, keep):
         total = keep
         for piece in arrived:
             total = total + piece.astype(F32)
-        total = total.astype(BF)
-        back = [total[:cap]] + [
+        return total.astype(BF)
+
+    def to_tokens(total):
+        return [total[:cap]] + [
             exchange(total[k * cap : (k + 1) * cap], "expert", k) for k in range(1, groups)
         ]
-        back = lax.optimization_barrier((*back, *others))[:groups]
-        return jnp.concatenate(back, axis=0)
 
     def gathered(part):
         return assemble(t_arr, [part] + [exchange(part, "tensor", j) for j in range(1, n)])
@@ -459,7 +465,10 @@
     (gkeep,) = pieces(
         after(t_arr, gto_x), n, False, [grad_g, grad_u], [gate_mat, up_mat], (0,), "rows_keep"
     )
-    returned = sum_back((from_x, from_y), after(keep, gto_x), gkeep)
+    gtotal = summed((exchange(gto_x, "tensor", 1), exchange(gto_y, "tensor", 2)), gkeep)
+    returned = to_tokens(summed((from_x, from_y), after(keep, gto_x)))
+    greturned = to_tokens(gtotal)
+    returned = jnp.concatenate(after(tuple(returned), greturned[1]), axis=0)
     chosen = [dot_nn(g, returned) for g in gather]
     layer_part = (gate_values[:, 0:1] * chosen[0] + gate_values[:, 1:2] * chosen[1]).astype(BF)
     layer_out = gathered(layer_part)
@@ -468,7 +477,7 @@
     for axis, bit in (("wide", 1), ("tensor", 1), ("tensor", 2)):
         gate_grad = gate_grad + exchange(gate_grad, axis, bit)
 
-    greturned = sum_back((exchange(gto_x, "tensor", 1), exchange(gto_y, "tensor", 2)), gkeep)
+    greturned = jnp.concatenate(greturned, axis=0)
     grad_part = (dot_nn(gather[0], greturned) + dot_nn(gather[1], greturned)).astype(BF)
     token_grad = gathered(grad_part)
     return (layer_out, token_grad, gate_grad.T)

time: 172 us -> 164 us (0.953)
  starting transfers between devices: 50.8 us -> 44.8 us
    ppermute x47 -> x43, starting transfers between devices: 50.8 us -> 44.8 us  [exchange(): return lax.ppermute(array, axis, [(i, i ^ bit) for i in range(size)])]
    ppermute x47 -> x43, waiting for transfers between devices: 43 us -> 44.5 us  [exchange(): return lax.ppermute(array, axis, [(i, i ^ bit) for i in range(size)])]
  transfers between devices with their start and end apart: 47 -> 43, of which waited for: 15 -> 19; matrix products, arithmetic and copies ran while one was open for 2% -> 2% of each run, Pallas kernels for 39% -> 40%
where the time goes in v5:
time: 164 us; the launch traced here: 163 us
  Pallas kernels  66.3 us (40%)
  starting transfers between devices  44.8 us (27%)
  waiting for transfers between devices  44.5 us (27%)
  other arithmetic  3.55 us (2%)
  matrix products  2.47 us (2%)
    pallas_call x14, Pallas kernels, call(): pl.pallas_call(kernel, in_specs=[SMEM] + [VMEM] * (len(ins) - far) + [HBM...  57 us
    ppermute x43, starting transfers between devices, exchange(): return lax.ppermute(array, axis, [(i, i ^ bit) for i in range(size)])  44.8 us
    ppermute x43, waiting for transfers between devices, exchange(): return lax.ppermute(array, axis, [(i, i ^ bit) for i in range(size)])  44.5 us
    pallas_call x2, Pallas kernels, fetch(): pl.pallas_call(kernel, in_specs=[HBM], out_specs=VMEM, out_shape=pltpu.VM...  9.25 us
  transfers between devices with their start and end apart: 43, of which 19 were waited for; matrix products, arithmetic and copies ran while one was open for 2% of the time, Pallas kernels for 40%

profile of v5, /device:TPU:16, one launch (start us, length us, event | category | flops | bytes accessed | tf_op | source)
XLA Modules:
  0.0 163.3 jit_solution(14616199823268950445)
XLA Ops:
  3.6 1.6 %collective-permute-start.2 = (bf16[96,768]{1,0:T(8,128)(2,1)S(1)}, bf16[96,768]{1,0:T(8,128)(2,1)S(1)}, u32[]{:S(2)}, u32[]{:S(2)}) collective-permute-start(bf16[96,768]{1,0:T(8,128)(2,1)S(1)} %get-tuple-element.111), channel_id=1, source_target_pairs={{0,1},{1,0},{2,3},{3,2},{4,5},{5,4},{6,7},{7,6},{8,9},{9,8},{10,11... | collective-permute-start | bytes 442376 | tf_op jit(solution)/shard_map/ppermute | solution.py:22
  5.5 1.6 collective-permute-start.1
  7.1 3.2 %collective-permute-done.2.refs_0_ = bf16[96,768]{1,0:T(8,128)(2,1)S(1)} collective-permute-done((bf16[96,768]{1,0:T(8,128)(2,1)S(1)}, bf16[96,768]{1,0:T(8,128)(2,1)S(1)}, u32[]{:S(2)}, u32[]{:S(2)}) %collective-permute-start.2) | collective-permute-done | bytes 147488 | tf_op jit(solution)/shard_map/ppermute | solution.py:22
  10.4 1.5 collective-permute-start.3
  11.9 1.5 collective-permute-start.4
  14.1 4.6 %fetch.2.refs_9_ = bf16[3072,2048]{1,0:T(8,128)(2,1)S(1)} custom-call(bf16[3072,2048]{1,0:T(8,128)(2,1)} %bitcast.25), custom_call_target="tpu_custom_call" | custom-call | bytes 12582912 | tf_op jit(solution)/shard_map/fetch/pallas_call | solution.py:65
  19.6 4.7 %fetch.3.refs_10_ = bf16[3072,2048]{1,0:T(8,128)(2,1)S(1)} custom-call(bf16[3072,2048]{1,0:T(8,128)(2,1)} %bitcast.29), custom_call_target="tpu_custom_call" | custom-call | bytes 12582912 | tf_op jit(solution)/shard_map/fetch/pallas_call | solution.py:65
  25.4 1.1 collective-permute-start.8
  26.9 2.4 %collective-permute-start.10 = (bf16[96,768]{1,0:T(8,128)(2,1)S(1)}, bf16[96,768]{1,0:T(8,128)(2,1)S(1)}, u32[]{:S(2)}, u32[]{:S(2)}) collective-permute-start(bf16[96,768]{1,0:T(8,128)(2,1)S(1)} %get-tuple-element.110), channel_id=1, source_target_pairs={{0,1},{1,0},{2,3},{3,2},{4,5},{5,4},{6,7},{7,6},{8,9},{9,8},{10,11... | collective-permute-start | bytes 442376 | tf_op jit(solution)/shard_map/ppermute | solution.py:22
  29.3 1.5 collective-permute-start.12
  32.2 1.5 collective-permute-done.8.refs_3_
  33.8 1.1 collective-permute-start.9
  35.2 2.8 %collective-permute-done.11 = bf16[96,768]{1,0:T(8,128)(2,1)S(1)} collective-permute-done((bf16[96,768]{1,0:T(8,128)(2,1)S(1)}, bf16[96,768]{1,0:T(8,128)(2,1)S(1)}, u32[]{:S(2)}, u32[]{:S(2)}) %collective-permute-start.11) | collective-permute-done | bytes 147488 | tf_op jit(solution)/shard_map/ppermute | solution.py:22
  38.0 3.6 %collective-permute-done.12 = bf16[96,768]{1,0:T(8,128)(2,1)S(1)} collective-permute-done((bf16[96,768]{1,0:T(8,128)(2,1)S(1)}, bf16[96,768]{1,0:T(8,128)(2,1)S(1)}, u32[]{:S(2)}, u32[]{:S(2)}) %collective-permute-start.12) | collective-permute-done | bytes 147488 | tf_op jit(solution)/shard_map/ppermute | solution.py:22
  42.8 1.5 collective-permute-start.15
  44.2 6.1 %pre_acts.2 = (f32[384,1024]{1,0:T(8,128)S(1)}, f32[384,1024]{1,0:T(8,128)S(1)}, bf16[384,2048]{1,0:T(8,128)(2,1)S(1)}) custom-call(s32[1]{0:T(128)} %bitcast.t_ref, bf16[96,3072]{1,0:T(8,128)(2,1)S(1)} %convolution_convert_fusion.own_ref, bf16[96,768]{1,0:T(8,128)(2,1)S(1)} %collective-permute-done.2.refs_0_, ...), custom_call_target="tpu_custom_call" | custom-call | flops 4831838208 | bytes 1048576 | tf_op jit(solution)/shard_map/pre_acts/pallas_call | solution.py:47
  52.1 5.9 %pre_acts.3 = (f32[384,1024]{1,0:T(8,128)S(1)}, f32[384,1024]{1,0:T(8,128)S(1)}, bf16[384,2048]{1,0:T(8,128)(2,1)S(1)}) custom-call(s32[1]{0:T(128)} %bitcast.t_ref, bf16[96,3072]{1,0:T(8,128)(2,1)S(1)} %convolution_convert_fusion.own_ref, bf16[96,768]{1,0:T(8,128)(2,1)S(1)} %collective-permute-done.2.refs_0_, ...), custom_call_target="tpu_custom_call" | custom-call | flops 4831838208 | bytes 1048576 | tf_op jit(solution)/shard_map/pre_acts/pallas_call | solution.py:47
  58.1 1.6 collective-permute-start.19
  60.0 1.5 collective-permute-done.16.refs_5_.refs_7_
  61.5 3.3 %project_first.1 = (bf16[192,768]{1,0:T(8,128)(2,1)S(1)}, bf16[192,768]{1,0:T(8,128)(2,1)S(1)}, bf16[384,2048]{1,0:T(8,128)(2,1)S(1)}) custom-call(s32[1]{0:T(128)} %bitcast.t_ref, f32[384,1024]{1,0:T(8,128)S(1)} %get-tuple-element.61.refs_0_, f32[384,1024]{1,0:T(8,128)S(1)} %get-tuple-element.62.refs_1_, ...), custom_call_target="tpu_custom_call" | custom-call | flops 1207959552 | bytes 1048576 | tf_op jit(solution)/shard_map/project_first/pallas_call | solution.py:47
  66.9 5.5 %project_send.1 = (f32[384,768]{1,0:T(8,128)S(1)}, f32[384,768]{1,0:T(8,128)S(1)}) custom-call(s32[1]{0:T(128)} %bitcast.t_ref, bf16[384,2048]{1,0:T(8,128)(2,1)S(1)} %get-tuple-element.68.refs_0_, bf16[2048,3072]{1,0:T(8,128)(2,1)} %bitcast.21), custom_call_target="tpu_custom_call" | custom-call | flops 2415919104 | bytes 1048576 | tf_op jit(solution)/shard_map/project_send/pallas_call | solution.py:47
  72.4 4.7 %grad_hidden.3 = (f32[384,1024]{1,0:T(8,128)S(1)}, bf16[384,1024]{1,0:T(8,128)(2,1)S(1)}) custom-call(s32[1]{0:T(128)} %bitcast.t_ref, bf16[96,3072]{1,0:T(8,128)(2,1)S(1)} %fusion.own_ref, bf16[288,768]{1,0:T(8,128)(2,1)S(1)} %constant_dynamic-update-slice_fusion.2.refs_0_, bf16[288,768]{1,0:T(8,128)(2,1)S(1)} %collective-permute-done.14.refs_1_, ...), custom_call_target="tpu_custom_call" | custom-call | flops 2415919104 | bytes 1048576 | tf_op jit(solution)/shard_map/grad_hidden/pallas_call | solution.py:47
  78.3 4.7 %grad_hidden.2 = (f32[384,1024]{1,0:T(8,128)S(1)}, bf16[384,1024]{1,0:T(8,128)(2,1)S(1)}) custom-call(s32[1]{0:T(128)} %bitcast.t_ref, bf16[96,3072]{1,0:T(8,128)(2,1)S(1)} %fusion.own_ref, bf16[288,768]{1,0:T(8,128)(2,1)S(1)} %constant_dynamic-update-slice_fusion.2.refs_0_, bf16[288,768]{1,0:T(8,128)(2,1)S(1)} %collective-permute-done.14.refs_1_, ...), custom_call_target="tpu_custom_call" | custom-call | flops 2415919104 | bytes 1048576 | tf_op jit(solution)/shard_map/grad_hidden/pallas_call | solution.py:47
  83.2 1.2 collective-permute-start.24
  84.4 3.3 %project_keep.1 = f32[384,768]{1,0:T(8,128)S(1)} custom-call(s32[1]{0:T(128)} %bitcast.t_ref, bf16[384,2048]{1,0:T(8,128)(2,1)S(1)} %get-tuple-element.68.refs_0_, bf16[2048,3072]{1,0:T(8,128)(2,1)} %bitcast.24), custom_call_target="tpu_custom_call" | custom-call | flops 1207959552 | bytes 1048576 | tf_op jit(solution)/shard_map/project_keep/pallas_call | solution.py:47
  88.4 5.5 %rows_first.1 = (bf16[192,768]{1,0:T(8,128)(2,1)S(1)}, bf16[192,768]{1,0:T(8,128)(2,1)S(1)}, bf16[384,2048]{1,0:T(8,128)(2,1)S(1)}, bf16[384,2048]{1,0:T(8,128)(2,1)S(1)}) custom-call(s32[1]{0:T(128)} %bitcast.t_ref, f32[384,1024]{1,0:T(8,128)S(1)} %get-tuple-element.61.refs_0_, f32[384,1024]{1,0:T(8,128)S(1)} %get-tuple-element.62.refs_1_, ...), custom_call_target="tpu_custom_call" | custom-call | flops 2415919104 | bytes 1048576 | tf_op jit(solution)/shard_map/rows_first/pallas_call | solution.py:47
  93.9 1.7 %collective-permute-start.22 = (bf16[192,768]{1,0:T(8,128)(2,1)S(1)}, bf16[192,768]{1,0:T(8,128)(2,1)S(1)}, u32[]{:S(2)}, u32[]{:S(2)}) collective-permute-start(bf16[192,768]{1,0:T(8,128)(2,1)S(1)} %get-tuple-element.86), channel_id=1, source_target_pairs={{0,4},{4,0},{8,12},{12,8},{1,5},{5,1},{9,13},{13,9},{2,6},{6,2},{1... | collective-permute-start | bytes 884744 | tf_op jit(solution)/shard_map/ppermute | solution.py:22
  96.3 10.2 %rows_send.1 = (f32[384,768]{1,0:T(8,128)S(1)}, f32[384,768]{1,0:T(8,128)S(1)}) custom-call(s32[1]{0:T(128)} %bitcast.t_ref, bf16[384,2048]{1,0:T(8,128)(2,1)S(1)} %get-tuple-element.82.refs_0_, bf16[384,2048]{1,0:T(8,128)(2,1)S(1)} %get-tuple-element.83.refs_1_, bf16[3072,2048]{1,0:T(8,128)(2,1)} %bitcast.27, bf16[3072,2048]{1,0:T(8,128)(2,1)} %bitcast.31), custom_call_target="tpu_custom_call" | custom-call | flops 4831838208 | bytes 1048576 | tf_op jit(solution)/shard_map/rows_send/pallas_call | solution.py:47
  106.5 2.6 %collective-permute-done.23.low_ref = bf16[192,768]{1,0:T(8,128)(2,1)S(1)} collective-permute-done((bf16[192,768]{1,0:T(8,128)(2,1)S(1)}, bf16[192,768]{1,0:T(8,128)(2,1)S(1)}, u32[]{:S(2)}, u32[]{:S(2)}) %collective-permute-start.23) | collective-permute-done | bytes 294944 | tf_op jit(solution)/shard_map/ppermute | solution.py:22
  109.3 1.3 collective-permute-start.29
  110.6 1.4 collective-permute-start.30
  112.3 2.2 %collective-permute-start.27 = (bf16[96,768]{1,0:T(8,128)(2,1)S(1)}, bf16[96,768]{1,0:T(8,128)(2,1)S(1)}, u32[]{:S(2)}, u32[]{:S(2)}) collective-permute-start(bf16[96,768]{1,0:T(8,128)(2,1)S(1)} %get-tuple-element.105), channel_id=1, source_target_pairs={{0,2},{1,3},{2,0},{3,1},{4,6},{5,7},{6,4},{7,5},{8,10},{9,11},{10,... | collective-permute-start | bytes 442376 | tf_op jit(solution)/shard_map/ppermute | solution.py:22
  114.5 1.3 collective-permute-start.28
  115.8 5.5 %rows_keep.1 = f32[384,768]{1,0:T(8,128)S(1)} custom-call(s32[1]{0:T(128)} %bitcast.t_ref, bf16[384,2048]{1,0:T(8,128)(2,1)S(1)} %get-tuple-element.82.refs_0_, bf16[384,2048]{1,0:T(8,128)(2,1)S(1)} %get-tuple-element.83.refs_1_, bf16[3072,2048]{1,0:T(8,128)(2,1)} %bitcast.28, bf16[3072,2048]{1,0:T(8,128)(2,1)} %bitcast.32), custom_call_target="tpu_custom_call" | custom-call | flops 2415919104 | bytes 1048576 | tf_op jit(solution)/shard_map/rows_keep/pallas_call | solution.py:47
  121.3 2.2 %collective-permute-done.29 = bf16[384,768]{1,0:T(8,128)(2,1)S(1)} collective-permute-done((bf16[384,768]{1,0:T(8,128)(2,1)S(1)}, bf16[384,768]{1,0:T(8,128)(2,1)S(1)}, u32[]{:S(2)}, u32[]{:S(2)}) %collective-permute-start.29) | collective-permute-done | bytes 589856 | tf_op jit(solution)/shard_map/ppermute | solution.py:22
  123.5 1.4 collective-permute-done.30
  125.2 2.2 %collective-permute-start.35 = (bf16[96,768]{1,0:T(8,128)(2,1)S(1)}, bf16[96,768]{1,0:T(8,128)(2,1)S(1)}, u32[]{:S(2)}, u32[]{:S(2)}) collective-permute-start(bf16[96,768]{1,0:T(8,128)(2,1)S(1)} %get-tuple-element.102), channel_id=1, source_target_pairs={{0,2},{1,3},{2,0},{3,1},{4,6},{5,7},{6,4},{7,5},{8,10},{9,11},{10,... | collective-permute-start | bytes 442376 | tf_op jit(solution)/shard_map/ppermute | solution.py:22
  127.4 1.3 collective-permute-start.36
  128.7 3.3 %collective-permute-done.31 = bf16[96,768]{1,0:T(8,128)(2,1)S(1)} collective-permute-done((bf16[96,768]{1,0:T(8,128)(2,1)S(1)}, bf16[96,768]{1,0:T(8,128)(2,1)S(1)}, u32[]{:S(2)}, u32[]{:S(2)}) %collective-permute-start.31) | collective-permute-done | bytes 147488 | tf_op jit(solution)/shard_map/ppermute | solution.py:22
  132.9 3.5 %collective-permute-done.35 = bf16[96,768]{1,0:T(8,128)(2,1)S(1)} collective-permute-done((bf16[96,768]{1,0:T(8,128)(2,1)S(1)}, bf16[96,768]{1,0:T(8,128)(2,1)S(1)}, u32[]{:S(2)}, u32[]{:S(2)}) %collective-permute-start.35) | collective-permute-done | bytes 147488 | tf_op jit(solution)/shard_map/ppermute | solution.py:22
  136.4 3.7 %collective-permute-done.36 = bf16[96,768]{1,0:T(8,128)(2,1)S(1)} collective-permute-done((bf16[96,768]{1,0:T(8,128)(2,1)S(1)}, bf16[96,768]{1,0:T(8,128)(2,1)S(1)}, u32[]{:S(2)}, u32[]{:S(2)}) %collective-permute-start.36) | collective-permute-done | bytes 147488 | tf_op jit(solution)/shard_map/ppermute | solution.py:22
  141.2 1.7 %collective-permute-start.37 = (bf16[128,768]{1,0:T(8,128)(2,1)S(1)}, bf16[128,768]{1,0:T(8,128)(2,1)S(1)}, u32[]{:S(2)}, u32[]{:S(2)}) collective-permute-start(bf16[128,768]{1,0:T(8,128)(2,1)S(1)} %fusion.2.refs_0_), channel_id=1, source_target_pairs={{0,4},{4,0},{8,12},{12,8},{1,5},{5,1},{9,13},{13,9},{2,6},{6,2},{1... | collective-permute-start | bytes 589832 | tf_op jit(solution)/shard_map/ppermute | solution.py:22
  142.9 1.2 collective-permute-done.41
  144.2 1.1 collective-permute-start.42
  147.3 1.5 collective-permute-start.32
  149.8 1.1 collective-permute-start.34
  151.4 6.7 %collective-permute-done.38.refs_2_ = bf16[128,768]{1,0:T(8,128)(2,1)S(1)} collective-permute-done((bf16[128,768]{1,0:T(8,128)(2,1)S(1)}, bf16[128,768]{1,0:T(8,128)(2,1)S(1)}, u32[]{:S(2)}, u32[]{:S(2)}) %collective-permute-start.38) | collective-permute-done | bytes 196640 | tf_op jit(solution)/shard_map/ppermute | solution.py:22
  159.0 3.3 %collective-permute-done.33.refs_2_ = bf16[128,768]{1,0:T(8,128)(2,1)S(1)} collective-permute-done((bf16[128,768]{1,0:T(8,128)(2,1)S(1)}, bf16[128,768]{1,0:T(8,128)(2,1)S(1)}, u32[]{:S(2)}, u32[]{:S(2)}) %collective-permute-start.33) | collective-permute-done | bytes 196640 | tf_op jit(solution)/shard_map/ppermute | solution.py:22
  (104 shorter events, 24.0 us)
Async XLA Ops:
  0.6 2.6 %copy-start = (bf16[128,3072]{1,0:T(8,128)(2,1)S(1)}, bf16[128,3072]{1,0:T(8,128)(2,1)}, u32[]{:S(2)}) copy-start(bf16[128,3072]{1,0:T(8,128)(2,1)} %param.7) | copy-start | bytes 2359300
  0.6 13.2 %copy-start.3 = (f32[128,2]{0,1:T(2,128)S(1)}, f32[128,2]{0,1:T(2,128)}, u32[]{:S(2)}) copy-start(f32[128,2]{0,1:T(2,128)} %param.9) | copy-start | bytes 3076
  3.6 6.8 %collective-permute-start.2 = (bf16[96,768]{1,0:T(8,128)(2,1)S(1)}, bf16[96,768]{1,0:T(8,128)(2,1)S(1)}, u32[]{:S(2)}, u32[]{:S(2)}) collective-permute-start(bf16[96,768]{1,0:T(8,128)(2,1)S(1)} %get-tuple-element.111), channel_id=1, source_target_pairs={{0,1},{1,0},{2,3},{3,2},{4,5},{5,4},{6,7},{7,6},{8,9},{9,8},{10,11... | collective-permute-start | bytes 442376 | tf_op jit(solution)/shard_map/ppermute | solution.py:22
  5.2 19.1 %collective-permute-start = (bf16[96,768]{1,0:T(8,128)(2,1)S(1)}, bf16[96,768]{1,0:T(8,128)(2,1)S(1)}, u32[]{:S(2)}, u32[]{:S(2)}) collective-permute-start(bf16[96,768]{1,0:T(8,128)(2,1)S(1)} %get-tuple-element.113), channel_id=1, source_target_pairs={{0,2},{1,3},{2,0},{3,1},{4,6},{5,7},{6,4},{7,5},{8,10},{9,11},{10,... | collective-permute-start | bytes 442376 | tf_op jit(solution)/shard_map/ppermute | solution.py:22
  5.5 18.8 %collective-permute-start.1 = (bf16[96,768]{1,0:T(8,128)(2,1)S(1)}, bf16[96,768]{1,0:T(8,128)(2,1)S(1)}, u32[]{:S(2)}, u32[]{:S(2)}) collective-permute-start(bf16[96,768]{1,0:T(8,128)(2,1)S(1)} %get-tuple-element.112), channel_id=1, source_target_pairs={{0,3},{1,2},{2,1},{3,0},{4,7},{5,6},{6,5},{7,4},{8,11},{9,10},{10,... | collective-permute-start | bytes 442376 | tf_op jit(solution)/shard_map/ppermute | solution.py:22
  10.4 8.3 %collective-permute-start.3 = (bf16[96,768]{1,0:T(8,128)(2,1)S(1)}, bf16[96,768]{1,0:T(8,128)(2,1)S(1)}, u32[]{:S(2)}, u32[]{:S(2)}) collective-permute-start(bf16[96,768]{1,0:T(8,128)(2,1)S(1)} %collective-permute-done.2.refs_0_), channel_id=1, source_target_pairs={{0,4},{4,0},{8,12},{12,8},{1,5},{5,1},{9,13},{13,9},{2,6},{6,2},{1... | collective-permute-start | bytes 442376 | tf_op jit(solution)/shard_map/ppermute | solution.py:22
  11.9 7.8 %collective-permute-start.4 = (bf16[96,768]{1,0:T(8,128)(2,1)S(1)}, bf16[96,768]{1,0:T(8,128)(2,1)S(1)}, u32[]{:S(2)}, u32[]{:S(2)}) collective-permute-start(bf16[96,768]{1,0:T(8,128)(2,1)S(1)} %collective-permute-done.2.refs_0_), channel_id=1, source_target_pairs={{0,8},{4,12},{8,0},{12,4},{1,9},{5,13},{9,1},{13,5},{2,10},{6,14},... | collective-permute-start | bytes 442376 | tf_op jit(solution)/shard_map/ppermute | solution.py:22
  13.4 6.3 %collective-permute-start.5 = (bf16[96,768]{1,0:T(8,128)(2,1)S(1)}, bf16[96,768]{1,0:T(8,128)(2,1)S(1)}, u32[]{:S(2)}, u32[]{:S(2)}) collective-permute-start(bf16[96,768]{1,0:T(8,128)(2,1)S(1)} %collective-permute-done.2.refs_0_), channel_id=1, source_target_pairs={{0,12},{4,8},{8,4},{12,0},{1,13},{5,9},{9,5},{13,1},{2,14},{6,10},... | collective-permute-start | bytes 442376 | tf_op jit(solution)/shard_map/ppermute | solution.py:22
  19.6 6.9 %copy-start.2 = (bf16[128,3072]{1,0:T(8,128)(2,1)S(1)}, bf16[128,3072]{1,0:T(8,128)(2,1)}, u32[]{:S(2)}) copy-start(bf16[128,3072]{1,0:T(8,128)(2,1)} %param.13) | copy-start | bytes 2359300
  24.4 6.8 %collective-permute-start.6 = (bf16[192,768]{1,0:T(8,128)(2,1)S(1)}, bf16[192,768]{1,0:T(8,128)(2,1)S(1)}, u32[]{:S(2)}, u32[]{:S(2)}) collective-permute-start(bf16[192,768]{1,0:T(8,128)(2,1)S(1)} %constant_dynamic-update-slice_fusion.refs_1_), channel_id=1, source_target_pairs={{0,8},{4,12},{8,0},{12,4},{1,9},{5,13},{9,1},{13,5},{2,10},{6,14},... | collective-permute-start | bytes 884744 | tf_op jit(solution)/shard_map/ppermute | solution.py:22
  25.4 8.3 %collective-permute-start.8 = (bf16[192,768]{1,0:T(8,128)(2,1)S(1)}, bf16[192,768]{1,0:T(8,128)(2,1)S(1)}, u32[]{:S(2)}, u32[]{:S(2)}) collective-permute-start(bf16[192,768]{1,0:T(8,128)(2,1)S(1)} %constant_dynamic-update-slice_fusion.refs_1_), channel_id=1, source_target_pairs={{0,4},{4,0},{8,12},{12,8},{1,5},{5,1},{9,13},{13,9},{2,6},{6,2},{1... | collective-permute-start | bytes 884744 | tf_op jit(solution)/shard_map/ppermute | solution.py:22
  26.9 8.3 %collective-permute-start.10 = (bf16[96,768]{1,0:T(8,128)(2,1)S(1)}, bf16[96,768]{1,0:T(8,128)(2,1)S(1)}, u32[]{:S(2)}, u32[]{:S(2)}) collective-permute-start(bf16[96,768]{1,0:T(8,128)(2,1)S(1)} %get-tuple-element.110), channel_id=1, source_target_pairs={{0,1},{1,0},{2,3},{3,2},{4,5},{5,4},{6,7},{7,6},{8,9},{9,8},{10,11... | collective-permute-start | bytes 442376 | tf_op jit(solution)/shard_map/ppermute | solution.py:22
  29.3 8.7 %collective-permute-start.11 = (bf16[96,768]{1,0:T(8,128)(2,1)S(1)}, bf16[96,768]{1,0:T(8,128)(2,1)S(1)}, u32[]{:S(2)}, u32[]{:S(2)}) collective-permute-start(bf16[96,768]{1,0:T(8,128)(2,1)S(1)} %get-tuple-element.109), channel_id=1, source_target_pairs={{0,2},{1,3},{2,0},{3,1},{4,6},{5,7},{6,4},{7,5},{8,10},{9,11},{10,... | collective-permute-start | bytes 442376 | tf_op jit(solution)/shard_map/ppermute | solution.py:22
  29.3 12.4 %collective-permute-start.12 = (bf16[96,768]{1,0:T(8,128)(2,1)S(1)}, bf16[96,768]{1,0:T(8,128)(2,1)S(1)}, u32[]{:S(2)}, u32[]{:S(2)}) collective-permute-start(bf16[96,768]{1,0:T(8,128)(2,1)S(1)} %get-tuple-element.108), channel_id=1, source_target_pairs={{0,3},{1,2},{2,1},{3,0},{4,7},{5,6},{6,5},{7,4},{8,11},{9,10},{10,... | collective-permute-start | bytes 442376 | tf_op jit(solution)/shard_map/ppermute | solution.py:22
  31.2 10.5 %collective-permute-start.7 = (bf16[96,768]{1,0:T(8,128)(2,1)S(1)}, bf16[96,768]{1,0:T(8,128)(2,1)S(1)}, u32[]{:S(2)}, u32[]{:S(2)}) collective-permute-start(bf16[96,768]{1,0:T(8,128)(2,1)S(1)} %slice.108), channel_id=1, source_target_pairs={{0,4},{4,0},{8,12},{12,8},{1,5},{5,1},{9,13},{13,9},{2,6},{6,2},{1... | collective-permute-start | bytes 442376 | tf_op jit(solution)/shard_map/ppermute | solution.py:22
  33.8 7.9 %collective-permute-start.9 = (bf16[96,768]{1,0:T(8,128)(2,1)S(1)}, bf16[96,768]{1,0:T(8,128)(2,1)S(1)}, u32[]{:S(2)}, u32[]{:S(2)}) collective-permute-start(bf16[96,768]{1,0:T(8,128)(2,1)S(1)} %slice.109), channel_id=1, source_target_pairs={{0,8},{4,12},{8,0},{12,4},{1,9},{5,13},{9,1},{13,5},{2,10},{6,14},... | collective-permute-start | bytes 442376 | tf_op jit(solution)/shard_map/ppermute | solution.py:22
  41.7 9.7 %collective-permute-start.14 = (bf16[288,768]{1,0:T(8,128)(2,1)S(1)}, bf16[288,768]{1,0:T(8,128)(2,1)S(1)}, u32[]{:S(2)}, u32[]{:S(2)}) collective-permute-start(bf16[288,768]{1,0:T(8,128)(2,1)S(1)} %constant_dynamic-update-slice_fusion.2.refs_0_), channel_id=1, source_target_pairs={{0,4},{4,0},{8,12},{12,8},{1,5},{5,1},{9,13},{13,9},{2,6},{6,2},{1... | collective-permute-start | bytes 1327112 | tf_op jit(solution)/shard_map/ppermute | solution.py:22
  42.8 9.3 %collective-permute-start.15 = (bf16[288,768]{1,0:T(8,128)(2,1)S(1)}, bf16[288,768]{1,0:T(8,128)(2,1)S(1)}, u32[]{:S(2)}, u32[]{:S(2)}) collective-permute-start(bf16[288,768]{1,0:T(8,128)(2,1)S(1)} %constant_dynamic-update-slice_fusion.2.refs_0_), channel_id=1, source_target_pairs={{0,8},{4,12},{8,0},{12,4},{1,9},{5,13},{9,1},{13,5},{2,10},{6,14},... | collective-permute-start | bytes 1327112 | tf_op jit(solution)/shard_map/ppermute | solution.py:22
  50.3 9.7 %collective-permute-start.13 = (bf16[384,2048]{1,0:T(8,128)(2,1)S(1)}, bf16[384,2048]{1,0:T(8,128)(2,1)S(1)}, u32[]{:S(2)}, u32[]{:S(2)}) collective-permute-start(bf16[384,2048]{1,0:T(8,128)(2,1)S(1)} %get-tuple-element.63), channel_id=1, source_target_pairs={{0,16},{16,0},{1,17},{17,1},{2,18},{18,2},{3,19},{19,3},{4,20},{20... | collective-permute-start | bytes 4718600 | tf_op jit(solution)/shard_map/ppermute | solution.py:22
  58.0 3.5 %collective-permute-start.16 = (bf16[384,2048]{1,0:T(8,128)(2,1)S(1)}, bf16[384,2048]{1,0:T(8,128)(2,1)S(1)}, u32[]{:S(2)}, u32[]{:S(2)}) collective-permute-start(bf16[384,2048]{1,0:T(8,128)(2,1)S(1)} %get-tuple-element.67), channel_id=1, source_target_pairs={{0,16},{16,0},{1,17},{17,1},{2,18},{18,2},{3,19},{19,3},{4,20},{20... | collective-permute-start | bytes 4718600 | tf_op jit(solution)/shard_map/ppermute | solution.py:22
  58.1 14.3 %collective-permute-start.19 = (bf16[288,768]{1,0:T(8,128)(2,1)S(1)}, bf16[288,768]{1,0:T(8,128)(2,1)S(1)}, u32[]{:S(2)}, u32[]{:S(2)}) collective-permute-start(bf16[288,768]{1,0:T(8,128)(2,1)S(1)} %constant_dynamic-update-slice_fusion.2.refs_0_), channel_id=1, source_target_pairs={{0,12},{4,8},{8,4},{12,0},{1,13},{5,9},{9,5},{13,1},{2,14},{6,10},... | collective-permute-start | bytes 1327112 | tf_op jit(solution)/shard_map/ppermute | solution.py:22
  64.8 13.4 %collective-permute-start.17 = (bf16[192,768]{1,0:T(8,128)(2,1)S(1)}, bf16[192,768]{1,0:T(8,128)(2,1)S(1)}, u32[]{:S(2)}, u32[]{:S(2)}) collective-permute-start(bf16[192,768]{1,0:T(8,128)(2,1)S(1)} %get-tuple-element.71), channel_id=1, source_target_pairs={{0,4},{4,0},{8,12},{12,8},{1,5},{5,1},{9,13},{13,9},{2,6},{6,2},{1... | collective-permute-start | bytes 884744 | tf_op jit(solution)/shard_map/ppermute | solution.py:22
  65.9 12.3 %collective-permute-start.18 = (bf16[192,768]{1,0:T(8,128)(2,1)S(1)}, bf16[192,768]{1,0:T(8,128)(2,1)S(1)}, u32[]{:S(2)}, u32[]{:S(2)}) collective-permute-start(bf16[192,768]{1,0:T(8,128)(2,1)S(1)} %get-tuple-element.72), channel_id=1, source_target_pairs={{0,8},{4,12},{8,0},{12,4},{1,9},{5,13},{9,1},{13,5},{2,10},{6,14},... | collective-permute-start | bytes 884744 | tf_op jit(solution)/shard_map/ppermute | solution.py:22
  77.2 11.2 %collective-permute-start.20 = (bf16[384,1024]{1,0:T(8,128)(2,1)S(1)}, bf16[384,1024]{1,0:T(8,128)(2,1)S(1)}, u32[]{:S(2)}, u32[]{:S(2)}) collective-permute-start(bf16[384,1024]{1,0:T(8,128)(2,1)S(1)} %get-tuple-element.80), channel_id=1, source_target_pairs={{0,16},{16,0},{1,17},{17,1},{2,18},{18,2},{3,19},{19,3},{4,20},{20... | collective-permute-start | bytes 2359304 | tf_op jit(solution)/shard_map/ppermute | solution.py:22
  83.1 5.3 %collective-permute-start.21 = (bf16[384,1024]{1,0:T(8,128)(2,1)S(1)}, bf16[384,1024]{1,0:T(8,128)(2,1)S(1)}, u32[]{:S(2)}, u32[]{:S(2)}) collective-permute-start(bf16[384,1024]{1,0:T(8,128)(2,1)S(1)} %get-tuple-element.75), channel_id=1, source_target_pairs={{0,16},{16,0},{1,17},{17,1},{2,18},{18,2},{3,19},{19,3},{4,20},{20... | collective-permute-start | bytes 2359304 | tf_op jit(solution)/shard_map/ppermute | solution.py:22
  83.2 28.8 %collective-permute-start.24 = (bf16[384,768]{1,0:T(8,128)(2,1)S(1)}, bf16[384,768]{1,0:T(8,128)(2,1)S(1)}, u32[]{:S(2)}, u32[]{:S(2)}) collective-permute-start(bf16[384,768]{1,0:T(8,128)(2,1)S(1)} %get-tuple-element.73), channel_id=1, source_target_pairs={{0,4},{4,0},{8,12},{12,8},{1,5},{5,1},{9,13},{13,9},{2,6},{6,2},{1... | collective-permute-start | bytes 1769480 | tf_op jit(solution)/shard_map/ppermute | solution.py:22
  87.7 24.3 %collective-permute-start.25 = (bf16[384,768]{1,0:T(8,128)(2,1)S(1)}, bf16[384,768]{1,0:T(8,128)(2,1)S(1)}, u32[]{:S(2)}, u32[]{:S(2)}) collective-permute-start(bf16[384,768]{1,0:T(8,128)(2,1)S(1)} %get-tuple-element.90), channel_id=1, source_target_pairs={{0,8},{4,12},{8,0},{12,4},{1,9},{5,13},{9,1},{13,5},{2,10},{6,14},... | collective-permute-start | bytes 1769480 | tf_op jit(solution)/shard_map/ppermute | solution.py:22
  93.9 12.6 %collective-permute-start.22 = (bf16[192,768]{1,0:T(8,128)(2,1)S(1)}, bf16[192,768]{1,0:T(8,128)(2,1)S(1)}, u32[]{:S(2)}, u32[]{:S(2)}) collective-permute-start(bf16[192,768]{1,0:T(8,128)(2,1)S(1)} %get-tuple-element.86), channel_id=1, source_target_pairs={{0,4},{4,0},{8,12},{12,8},{1,5},{5,1},{9,13},{13,9},{2,6},{6,2},{1... | collective-permute-start | bytes 884744 | tf_op jit(solution)/shard_map/ppermute | solution.py:22
  95.7 13.5 %collective-permute-start.23 = (bf16[192,768]{1,0:T(8,128)(2,1)S(1)}, bf16[192,768]{1,0:T(8,128)(2,1)S(1)}, u32[]{:S(2)}, u32[]{:S(2)}) collective-permute-start(bf16[192,768]{1,0:T(8,128)(2,1)S(1)} %get-tuple-element.87), channel_id=1, source_target_pairs={{0,8},{4,12},{8,0},{12,4},{1,9},{5,13},{9,1},{13,5},{2,10},{6,14},... | collective-permute-start | bytes 884744 | tf_op jit(solution)/shard_map/ppermute | solution.py:22
  109.3 14.2 %collective-permute-start.29 = (bf16[384,768]{1,0:T(8,128)(2,1)S(1)}, bf16[384,768]{1,0:T(8,128)(2,1)S(1)}, u32[]{:S(2)}, u32[]{:S(2)}) collective-permute-start(bf16[384,768]{1,0:T(8,128)(2,1)S(1)} %get-tuple-element.88), channel_id=1, source_target_pairs={{0,4},{4,0},{8,12},{12,8},{1,5},{5,1},{9,13},{13,9},{2,6},{6,2},{1... | collective-permute-start | bytes 1769480 | tf_op jit(solution)/shard_map/ppermute | solution.py:22
  110.6 14.3 %collective-permute-start.30 = (bf16[384,768]{1,0:T(8,128)(2,1)S(1)}, bf16[384,768]{1,0:T(8,128)(2,1)S(1)}, u32[]{:S(2)}, u32[]{:S(2)}) collective-permute-start(bf16[384,768]{1,0:T(8,128)(2,1)S(1)} %get-tuple-element.92), channel_id=1, source_target_pairs={{0,8},{4,12},{8,0},{12,4},{1,9},{5,13},{9,1},{13,5},{2,10},{6,14},... | collective-permute-start | bytes 1769480 | tf_op jit(solution)/shard_map/ppermute | solution.py:22
  112.2 15.2 %collective-permute-start.26 = (bf16[96,768]{1,0:T(8,128)(2,1)S(1)}, bf16[96,768]{1,0:T(8,128)(2,1)S(1)}, u32[]{:S(2)}, u32[]{:S(2)}) collective-permute-start(bf16[96,768]{1,0:T(8,128)(2,1)S(1)} %get-tuple-element.106), channel_id=1, source_target_pairs={{0,1},{1,0},{2,3},{3,2},{4,5},{5,4},{6,7},{7,6},{8,9},{9,8},{10,11... | collective-permute-start | bytes 442376 | tf_op jit(solution)/shard_map/ppermute | solution.py:22
  112.3 16.4 %collective-permute-start.27 = (bf16[96,768]{1,0:T(8,128)(2,1)S(1)}, bf16[96,768]{1,0:T(8,128)(2,1)S(1)}, u32[]{:S(2)}, u32[]{:S(2)}) collective-permute-start(bf16[96,768]{1,0:T(8,128)(2,1)S(1)} %get-tuple-element.105), channel_id=1, source_target_pairs={{0,2},{1,3},{2,0},{3,1},{4,6},{5,7},{6,4},{7,5},{8,10},{9,11},{10,... | collective-permute-start | bytes 442376 | tf_op jit(solution)/shard_map/ppermute | solution.py:22
  114.5 14.2 %collective-permute-start.28 = (bf16[96,768]{1,0:T(8,128)(2,1)S(1)}, bf16[96,768]{1,0:T(8,128)(2,1)S(1)}, u32[]{:S(2)}, u32[]{:S(2)}) collective-permute-start(bf16[96,768]{1,0:T(8,128)(2,1)S(1)} %get-tuple-element.104), channel_id=1, source_target_pairs={{0,3},{1,2},{2,1},{3,0},{4,7},{5,6},{6,5},{7,4},{8,11},{9,10},{10,... | collective-permute-start | bytes 442376 | tf_op jit(solution)/shard_map/ppermute | solution.py:22
  125.2 6.9 %collective-permute-start.31 = (bf16[96,768]{1,0:T(8,128)(2,1)S(1)}, bf16[96,768]{1,0:T(8,128)(2,1)S(1)}, u32[]{:S(2)}, u32[]{:S(2)}) collective-permute-start(bf16[96,768]{1,0:T(8,128)(2,1)S(1)} %get-tuple-element.103), channel_id=1, source_target_pairs={{0,1},{1,0},{2,3},{3,2},{4,5},{5,4},{6,7},{7,6},{8,9},{9,8},{10,11... | collective-permute-start | bytes 442376 | tf_op jit(solution)/shard_map/ppermute | solution.py:22
  125.2 11.2 %collective-permute-start.35 = (bf16[96,768]{1,0:T(8,128)(2,1)S(1)}, bf16[96,768]{1,0:T(8,128)(2,1)S(1)}, u32[]{:S(2)}, u32[]{:S(2)}) collective-permute-start(bf16[96,768]{1,0:T(8,128)(2,1)S(1)} %get-tuple-element.102), channel_id=1, source_target_pairs={{0,2},{1,3},{2,0},{3,1},{4,6},{5,7},{6,4},{7,5},{8,10},{9,11},{10,... | collective-permute-start | bytes 442376 | tf_op jit(solution)/shard_map/ppermute | solution.py:22
  127.4 12.7 %collective-permute-start.36 = (bf16[96,768]{1,0:T(8,128)(2,1)S(1)}, bf16[96,768]{1,0:T(8,128)(2,1)S(1)}, u32[]{:S(2)}, u32[]{:S(2)}) collective-permute-start(bf16[96,768]{1,0:T(8,128)(2,1)S(1)} %get-tuple-element.101), channel_id=1, source_target_pairs={{0,3},{1,2},{2,1},{3,0},{4,7},{5,6},{6,5},{7,4},{8,11},{9,10},{10,... | collective-permute-start | bytes 442376 | tf_op jit(solution)/shard_map/ppermute | solution.py:22
  132.8 7.6 %collective-permute-start.40 = (f32[2,128]{1,0:T(2,128)S(1)}, f32[2,128]{1,0:T(2,128)S(1)}, u32[]{:S(2)}, u32[]{:S(2)}) collective-permute-start(f32[2,128]{1,0:T(2,128)S(1)} %pad_maximum_fusion.3), channel_id=1, source_target_pairs={{0,16},{16,0},{1,17},{17,1},{2,18},{18,2},{3,19},{19,3},{4,20},{20... | collective-permute-start | bytes 3080 | tf_op jit(solution)/shard_map/ppermute | solution.py:22
  140.5 3.7 %collective-permute-start.41 = (f32[2,128]{1,0:T(2,128)S(1)}, f32[2,128]{1,0:T(2,128)S(1)}, u32[]{:S(2)}, u32[]{:S(2)}) collective-permute-start(f32[2,128]{1,0:T(2,128)S(1)} %fusion.23), channel_id=1, source_target_pairs={{0,4},{4,0},{8,12},{12,8},{1,5},{5,1},{9,13},{13,9},{2,6},{6,2},{1... | collective-permute-start | bytes 3080 | tf_op jit(solution)/shard_map/ppermute | solution.py:22
  141.2 8.6 %collective-permute-start.37 = (bf16[128,768]{1,0:T(8,128)(2,1)S(1)}, bf16[128,768]{1,0:T(8,128)(2,1)S(1)}, u32[]{:S(2)}, u32[]{:S(2)}) collective-permute-start(bf16[128,768]{1,0:T(8,128)(2,1)S(1)} %fusion.2.refs_0_), channel_id=1, source_target_pairs={{0,4},{4,0},{8,12},{12,8},{1,5},{5,1},{9,13},{13,9},{2,6},{6,2},{1... | collective-permute-start | bytes 589832 | tf_op jit(solution)/shard_map/ppermute | solution.py:22
  144.2 4.6 %collective-permute-start.42 = (f32[2,128]{1,0:T(2,128)S(1)}, f32[2,128]{1,0:T(2,128)S(1)}, u32[]{:S(2)}, u32[]{:S(2)}) collective-permute-start(f32[2,128]{1,0:T(2,128)S(1)} %fusion.32), channel_id=1, source_target_pairs={{0,8},{4,12},{8,0},{12,4},{1,9},{5,13},{9,1},{13,5},{2,10},{6,14},... | collective-permute-start | bytes 3080 | tf_op jit(solution)/shard_map/ppermute | solution.py:22
  145.3 12.8 %collective-permute-start.38 = (bf16[128,768]{1,0:T(8,128)(2,1)S(1)}, bf16[128,768]{1,0:T(8,128)(2,1)S(1)}, u32[]{:S(2)}, u32[]{:S(2)}) collective-permute-start(bf16[128,768]{1,0:T(8,128)(2,1)S(1)} %fusion.2.refs_0_), channel_id=1, source_target_pairs={{0,8},{4,12},{8,0},{12,4},{1,9},{5,13},{9,1},{13,5},{2,10},{6,14},... | collective-permute-start | bytes 589832 | tf_op jit(solution)/shard_map/ppermute | solution.py:22
  146.3 11.8 %collective-permute-start.39 = (bf16[128,768]{1,0:T(8,128)(2,1)S(1)}, bf16[128,768]{1,0:T(8,128)(2,1)S(1)}, u32[]{:S(2)}, u32[]{:S(2)}) collective-permute-start(bf16[128,768]{1,0:T(8,128)(2,1)S(1)} %fusion.2.refs_0_), channel_id=1, source_target_pairs={{0,12},{4,8},{8,4},{12,0},{1,13},{5,9},{9,5},{13,1},{2,14},{6,10},... | collective-permute-start | bytes 589832 | tf_op jit(solution)/shard_map/ppermute | solution.py:22
  147.3 11.7 %collective-permute-start.32 = (bf16[128,768]{1,0:T(8,128)(2,1)S(1)}, bf16[128,768]{1,0:T(8,128)(2,1)S(1)}, u32[]{:S(2)}, u32[]{:S(2)}) collective-permute-start(bf16[128,768]{1,0:T(8,128)(2,1)S(1)} %get-tuple-element.99.refs_0_), channel_id=1, source_target_pairs={{0,4},{4,0},{8,12},{12,8},{1,5},{5,1},{9,13},{13,9},{2,6},{6,2},{1... | collective-permute-start | bytes 589832 | tf_op jit(solution)/shard_map/ppermute | solution.py:22
  148.8 13.5 %collective-permute-start.33 = (bf16[128,768]{1,0:T(8,128)(2,1)S(1)}, bf16[128,768]{1,0:T(8,128)(2,1)S(1)}, u32[]{:S(2)}, u32[]{:S(2)}) collective-permute-start(bf16[128,768]{1,0:T(8,128)(2,1)S(1)} %get-tuple-element.99.refs_0_), channel_id=1, source_target_pairs={{0,8},{4,12},{8,0},{12,4},{1,9},{5,13},{9,1},{13,5},{2,10},{6,14},... | collective-permute-start | bytes 589832 | tf_op jit(solution)/shard_map/ppermute | solution.py:22
  149.8 12.5 %collective-permute-start.34 = (bf16[128,768]{1,0:T(8,128)(2,1)S(1)}, bf16[128,768]{1,0:T(8,128)(2,1)S(1)}, u32[]{:S(2)}, u32[]{:S(2)}) collective-permute-start(bf16[128,768]{1,0:T(8,128)(2,1)S(1)} %get-tuple-element.99.refs_0_), channel_id=1, source_target_pairs={{0,12},{4,8},{8,4},{12,0},{1,13},{5,9},{9,5},{13,1},{2,14},{6,10},... | collective-permute-start | bytes 589832 | tf_op jit(solution)/shard_map/ppermute | solution.py:22
  158.1 5.2 %copy-start.1 = (bf16[128,3072]{1,0:T(8,128)(2,1)S(1)}, bf16[128,3072]{1,0:T(8,128)(2,1)}, u32[]{:S(2)}) copy-start(bf16[128,3072]{1,0:T(8,128)(2,1)} %param.7) | copy-start | bytes 2359300

commit v6 on v5

--- a/solution.py
+++ b/solution.py
@@ -99,41 +99,51 @@
 BLOCK = 256
 
 
-def pre_acts(t, own, parts, gate_mat, up_mat, start, stop):
-    depth = gate_mat.shape[0]
+def pre_acts(t, own, parts, gate_held, up_mat, start, stop):
+    depth = up_mat.shape[0]
     n = len(parts)
     quarter = depth // n
     rows = own.shape[0] + sum(p.shape[0] for p in parts[0])
     counts = [len(p) for p in parts]
+    width = stop - start
 
     def kernel(t_ref, own_ref, *refs):
         pieces, refs = split_parts(refs, counts)
-        gate_w, up_w, gate_o, up_o, send, rows_ref = refs
+        gate_w, up_w, gate_o, up_o, send, rows_ref, up_held, sem = refs
+        copy = pltpu.make_async_copy(up_w.at[:, pl.ds(start, width)], up_held, sem)
+        copy.start()
         lay_out(t_ref[0], own_ref, pieces, rows_ref)
-
-        @pl.loop(0, (stop - start) // BLOCK)
-        def _(i):
-            off = pl.multiple_of(i * BLOCK, BLOCK)
-            for w, out, at in ((gate_w, gate_o, 0), (up_w, up_o, stop - start)):
+        for w, base, out, at in ((gate_w, start, gate_o, 0), (up_held, 0, up_o, width)):
+            if at:
+                copy.wait()
+
+            @pl.loop(0, width // BLOCK)
+            def _(i):
+                off = pl.multiple_of(i * BLOCK, BLOCK)
                 total = None
                 for q in range(n):
                     part = dot_nn(
-                        rows_ref[q], w[q * quarter : (q + 1) * quarter, pl.ds(start + off, BLOCK)]
+                        rows_ref[q], w[q * quarter : (q + 1) * quarter, pl.ds(base + off, BLOCK)]
                     )
                     total = part if total is None else total + part
                 out[:, pl.ds(off, BLOCK)] = total
                 send[:, pl.ds(at + off, BLOCK)] = total.astype(BF)
 
-    shape = (rows, stop - start)
+    shape = (rows, width)
     return call(
         kernel,
         t,
-        [own] + [x for p in parts for x in p] + [gate_mat, up_mat],
-        [sds(shape, F32)] * 2 + [sds((rows, 2 * (stop - start)), BF)],
-        [pltpu.VMEM((n, rows, quarter), BF)],
-        4 * rows * depth * (stop - start),
-        LIMIT,
+        [own] + [x for p in parts for x in p] + [gate_held, up_mat],
+        [sds(shape, F32)] * 2 + [sds((rows, 2 * width), BF)],
+        [
+            pltpu.VMEM((n, rows, quarter), BF),
+            pltpu.VMEM((depth, width), BF),
+            pltpu.SemaphoreType.DMA,
+        ],
+        4 * rows * depth * width,
+        14,
         "pre_acts",
+        far=1,
     )
 
 
@@ -144,29 +154,30 @@
     rows = own.shape[0] + sum(p.shape[0] for p in parts[0])
     counts = [len(p) for p in parts]
 
-    block = 2 * BLOCK
-    steps = (stop - start) // block
+    steps = (stop - start) // BLOCK
 
     def kernel(t_ref, own_ref, *refs):
         pieces, refs = split_parts(refs, counts)
         down_w, out, send, rows_ref, held, sems = refs
-        copies = [
-            pltpu.make_async_copy(
-                down_w.at[pl.ds(start + i * block, block)], held.at[i], sems.at[i]
-            )
-            for i in range(steps)
-        ]
-        for copy in copies:
-            copy.start()
+
+        def copy(i):
+            source = down_w.at[pl.ds(start + i * BLOCK, BLOCK)]
+            return pltpu.make_async_copy(source, held.at[i], sems.at[i])
+
+        for i in range(steps):
+            copy(i).start()
         lay_out(t_ref[0], own_ref, pieces, rows_ref)
-        for i in range(steps):
-            copies[i].wait()
+
+        @pl.loop(0, steps)
+        def _(i):
+            copy(i).wait()
             total = None
             for q in range(n):
                 part = dot_nt(rows_ref[q], held[i, :, q * quarter : (q + 1) * quarter])
                 total = part if total is None else total + part
-            out[:, i * block : (i + 1) * block] = total
-            send[:, i * block : (i + 1) * block] = total.astype(BF)
+            off = pl.multiple_of(i * BLOCK, BLOCK)
+            out[:, pl.ds(off, BLOCK)] = total
+            send[:, pl.ds(off, BLOCK)] = total.astype(BF)
 
     shape = (rows, stop - start)
     return call(
@@ -176,7 +187,7 @@
         [sds(shape, F32), sds(shape, BF)],
         [
             pltpu.VMEM((n, rows, quarter), BF),
-            pltpu.VMEM((steps, block, depth), BF),
+            pltpu.VMEM((steps, BLOCK, depth), BF),
             pltpu.SemaphoreType.DMA((steps,)),
         ],
         2 * rows * depth * (stop - start),
@@ -238,33 +249,48 @@
         self.mats, self.nn = len(mats), nn
         self.hidden, depth = mats[0].shape if nn else mats[0].shape[::-1]
         self.quarter = depth // n
-        self.width, self.each = self.quarter, 1
-        chunk = (self.hidden, self.width) if nn else (self.width, self.hidden)
-        count = pieces * self.each * self.mats
-        self.scratch = [pltpu.VMEM((count,) + chunk, BF), pltpu.SemaphoreType.DMA((count,))]
-        self.mib = 2 + 2 * count * self.hidden * self.width // MIB
+        self.blocks = self.quarter // BLOCK
+        self.each = 1 if nn else self.blocks
+        chunk = (self.hidden, self.quarter) if nn else (BLOCK, self.hidden)
+        self.count = pieces * self.each
+        total = self.count * self.mats
+        self.scratch = [pltpu.VMEM((total,) + chunk, BF), pltpu.SemaphoreType.DMA((total,))]
+        self.mib = 2 + 2 * pieces * self.mats * self.hidden * self.quarter // MIB
+
+    def copy(self, chunk, m):
+        base = self.bases[0]
+        for k in range(1, len(self.bases)):
+            base = jnp.where(chunk >= k * self.each, self.bases[k], base)
+        width = self.quarter if self.nn else BLOCK
+        cut = pl.ds(pl.multiple_of(base + chunk % self.each * width, BLOCK), width)
+        source = self.weights[m].at[:, cut] if self.nn else self.weights[m].at[cut]
+        slot = chunk * self.mats + m
+        return pltpu.make_async_copy(source, self.held.at[slot], self.sems.at[slot])
 
     def start(self, weights, bases, held, sems):
-        self.held, self.copies = held, []
-        for base in bases:
-            for c in range(self.each):
-                cut = pl.ds(pl.multiple_of(base + c * self.width, BLOCK), self.width)
-                for w in weights:
-                    source = w.at[:, cut] if self.nn else w.at[cut]
-                    k = len(self.copies)
-                    self.copies.append(pltpu.make_async_copy(source, held.at[k], sems.at[k]))
-                    self.copies[-1].start()
-
-    def products(self, piece, acts):
-        for c in range(self.each):
-            total = None
+        self.weights, self.bases, self.held, self.sems = weights, bases, held, sems
+        for chunk in range(self.count):
             for m in range(self.mats):
-                k = (piece * self.each + c) * self.mats + m
-                self.copies[k].wait()
-                dot = dot_nn if self.nn else dot_nt
-                part = dot(acts[m][...], self.held[k])
-                total = part if total is None else total + part
-            yield slice(c * self.width, (c + 1) * self.width), total
+                self.copy(chunk, m).start()
+
+    def products(self, acts, store):
+        @pl.loop(0, len(self.bases) * self.blocks)
+        def _(i):
+            piece, off = i // self.blocks, pl.multiple_of(i % self.blocks * BLOCK, BLOCK)
+            if self.nn:
+
+                @pl.when(off == 0)
+                def _():
+                    self.copy(piece, 0).wait()
+
+                total = dot_nn(acts[0][...], self.held[piece, :, pl.ds(off, BLOCK)])
+            else:
+                total = None
+                for m in range(self.mats):
+                    self.copy(i, m).wait()
+                    part = dot_nt(acts[m][...], self.held[i * self.mats + m])
+                    total = part if total is None else total + part
+            store(piece, pl.ds(off, BLOCK), total)
 
 
 def first_piece(t, n, make, nn, ins, mats, name):
@@ -278,9 +304,12 @@
         halves, acts, scratch = refs[:2], refs[2 : 2 + len(mats)], refs[2 + len(mats) :]
         stream.start(weights, [(t_ref[0] ^ 3) * quarter], *scratch)
         make(parts, acts)
-        for cols, total in stream.products(0, acts):
+
+        def store(piece, cols, total):
             halves[0][:, cols] = total[:half].astype(BF)
             halves[1][:, cols] = total[half:].astype(BF)
+
+        stream.products(acts, store)
 
     return call(
         kernel,
@@ -302,36 +331,39 @@
     def kernel(t_ref, *refs):
         ins, refs = refs[: len(acts)], refs[len(acts) :]
         weights, refs = refs[: len(mats)], refs[len(mats) :]
-        outs, scratch = refs[: len(order)], refs[len(order) :]
+        out, scratch = refs[0], refs[1:]
         stream.start(weights, [(t_ref[0] ^ j) * quarter for j in order], *scratch)
-        for k, out in enumerate(outs):
-            for cols, total in stream.products(k, ins):
-                out[:, cols] = total
-
-    return call(
+
+        def store(piece, cols, total):
+            out[piece, :, cols] = total
+
+        stream.products(ins, store)
+
+    (out,) = call(
         kernel,
         t,
         list(acts) + list(mats),
-        [sds((rows, quarter), F32)] * len(order),
+        [sds((len(order), rows, quarter), F32)],
         stream.scratch,
         2 * rows * quarter * len(order) * stream.hidden * len(mats),
         stream.mib + 4,
         name,
         far=len(mats),
     )
-
-
-def add_diagonal(t, to_x, to_y, top, low):
+    return out
+
+
+def add_diagonal(t, both, top, low):
     half = top.shape[0]
 
-    def kernel(t_ref, x_ref, y_ref, top_ref, low_ref, x_out, y_out):
-        x_out[:half, :] = x_ref[:half, :].astype(BF)
-        x_out[half:, :] = (x_ref[half:, :] + low_ref[...].astype(F32)).astype(BF)
-        y_out[:half, :] = (y_ref[:half, :] + top_ref[...].astype(F32)).astype(BF)
-        y_out[half:, :] = y_ref[half:, :].astype(BF)
+    def kernel(t_ref, both_ref, top_ref, low_ref, x_out, y_out):
+        x_out[:half, :] = both_ref[0, :half, :].astype(BF)
+        x_out[half:, :] = (both_ref[0, half:, :] + low_ref[...].astype(F32)).astype(BF)
+        y_out[:half, :] = (both_ref[1, :half, :] + top_ref[...].astype(F32)).astype(BF)
+        y_out[half:, :] = both_ref[1, half:, :].astype(BF)
 
     return call(
-        kernel, t, [to_x, to_y, top, low], [sds(to_x.shape, BF)] * 2, [], to_x.size, LIMIT, "add"
+        kernel, t, [both, top, low], [sds(both.shape[1:], BF)] * 2, [], both.size, LIMIT, "add"
     )
 
 
@@ -395,27 +427,22 @@
     tok_z = over_z(tok_out)
     first, rest = tok_z[0], tok_z[1:]
     first_far = [exchange(first, "tensor", j) for j in range(1, n)]
-    gate_held = fetch(after(gate_mat, first))
-    up_held = fetch(after(up_mat, gate_held, *first_far))
-    rest = jnp.concatenate(after(tuple(rest), up_held), axis=0)
+    gate_held = fetch(gate_mat)
+    rest = jnp.concatenate(after(tuple(rest), gate_held, *first_far), axis=0)
     rest_x, rest_y = exchange(rest, "tensor", 1), exchange(rest, "tensor", 2)
     cot_z = over_z(after(cot_out, rest))
     split = rest.shape[0] // 2
     rest_d = [exchange(rest_y[:split], "tensor", 1), exchange(rest_x[split:], "tensor", 2)]
-    rest_d[0], rest_d[1], *cot_z = lax.optimization_barrier((*rest_d, *cot_z))
     tok_parts = [
         [first, rest], [first_far[0], rest_x], [first_far[1], rest_y], [first_far[2], *rest_d]
     ]
-    cot_part = jnp.concatenate(cot_z, axis=0)
+    cot_part = jnp.concatenate(after(tuple(cot_z), *rest_d), axis=0)
     cot_parts = [[cot_part]] + [[exchange(cot_part, "tensor", j)] for j in range(1, n)]
-
-    turn = after(t_arr, cot_part)
     pres = []
-    for start in range(0, hidden_here, hidden_here // 2):
-        if start:
-            turn = after(t_arr, cot_parts[1][0], cot_parts[2][0])
+    half = hidden_here // 2
+    for start, turn in ((0, (cot_part,)), (half, (cot_parts[1][0], cot_parts[2][0]))):
         gate_o, up_o, sent = pre_acts(
-            turn, tok_own, tok_parts, gate_held, up_held, start, start + hidden_here // 2
+            after(t_arr, *turn), tok_own, tok_parts, gate_held, up_mat, start, start + half
         )
         pres.append([gate_o, up_o, exchange(sent, "wide", 1)])
 
@@ -430,8 +457,8 @@
             exchange(total[k * cap : (k + 1) * cap], "expert", k) for k in range(1, groups)
         ]
 
-    def gathered(part):
-        return assemble(t_arr, [part] + [exchange(part, "tensor", j) for j in range(1, n)])
+    def around(part):
+        return [part] + [exchange(part, "tensor", j) for j in range(1, n)]
 
     gather = [(order[:, k][:, None] == cells[None, :]).astype(BF) for k in range(2)]
 
@@ -439,18 +466,18 @@
         t_arr, n, hidden_strips, True, sum(pres, []), [down_mat], "project_first"
     )
     added = [exchange(d_top, "tensor", 1), exchange(d_low, "tensor", 2)]
-    to_x, to_y = pieces(t_arr, n, True, [hidden], [down_mat], (1, 2), "project_send")
+    both = pieces(t_arr, n, True, [hidden], [down_mat], (1, 2), "project_send")
     grads = []
-    turn = after(t_arr, to_x)
+    turn = after(t_arr, both)
     for start in range(0, hidden_here, hidden_here // 2):
         if start:
-            to_x, to_y = add_diagonal(t_arr, to_x, to_y, *added)
+            to_x, to_y = add_diagonal(t_arr, both, *added)
             turn = after(t_arr, to_x)
         gh_o, gh_s = grad_hiddens(
             turn, cot_own, cot_parts, down_mat, start, start + hidden_here // 2
         )
         grads.append([gh_o, exchange(gh_s, "wide", 1)])
-    (keep,) = pieces(after(t_arr, gh_s), n, True, [hidden], [down_mat], (0,), "project_keep")
+    keep = pieces(after(t_arr, gh_s), n, True, [hidden], [down_mat], (0,), "project_keep")[0]
 
     e_top, e_low, grad_g, grad_u = first_piece(
         after(t_arr, keep), n, grad_strips, False,
@@ -458,28 +485,30 @@
     )
     gadded = [exchange(e_top, "tensor", 1), exchange(e_low, "tensor", 2)]
     from_x, from_y = exchange(to_x, "tensor", 1), exchange(to_y, "tensor", 2)
-    gto_x, gto_y = pieces(
+    gboth = pieces(
         t_arr, n, False, [grad_g, grad_u], [gate_mat, up_mat], (1, 2), "rows_send",
     )
-    gto_x, gto_y = add_diagonal(t_arr, gto_x, gto_y, *gadded)
-    (gkeep,) = pieces(
+    gto_x, gto_y = add_diagonal(t_arr, gboth, *gadded)
+    gkeep = pieces(
         after(t_arr, gto_x), n, False, [grad_g, grad_u], [gate_mat, up_mat], (0,), "rows_keep"
-    )
+    )[0]
     gtotal = summed((exchange(gto_x, "tensor", 1), exchange(gto_y, "tensor", 2)), gkeep)
     returned = to_tokens(summed((from_x, from_y), after(keep, gto_x)))
     greturned = to_tokens(gtotal)
     returned = jnp.concatenate(after(tuple(returned), greturned[1]), axis=0)
     chosen = [dot_nn(g, returned) for g in gather]
     layer_part = (gate_values[:, 0:1] * chosen[0] + gate_values[:, 1:2] * chosen[1]).astype(BF)
-    layer_out = gathered(layer_part)
+    layer_parts = around(layer_part)
+    layer_out = assemble(t_arr, layer_parts)
+    greturned = jnp.concatenate(tuple(greturned), axis=0)
     cot_here = lax.dynamic_slice(cotangent, (0, t * quarter), (tok_rows, quarter)).astype(F32)
     gate_grad = jnp.stack([jnp.sum(cot_here * c, axis=1) for c in chosen], axis=0)
+    gate_grad = after(gate_grad, layer_parts[1], layer_parts[2])
     for axis, bit in (("wide", 1), ("tensor", 1), ("tensor", 2)):
         gate_grad = gate_grad + exchange(gate_grad, axis, bit)
 
-    greturned = jnp.concatenate(greturned, axis=0)
     grad_part = (dot_nn(gather[0], greturned) + dot_nn(gather[1], greturned)).astype(BF)
-    token_grad = gathered(grad_part)
+    token_grad = assemble(t_arr, around(grad_part))
     return (layer_out, token_grad, gate_grad.T)
 
 

time: 164 us -> 153 us (0.933)
  waiting for transfers between devices: 44.5 us -> 38.9 us
  Pallas kernels: 66.3 us -> 61.7 us
    ppermute x43, waiting for transfers between devices: 44.5 us -> 38.9 us  [exchange(): return lax.ppermute(array, axis, [(i, i ^ bit) for i in range(size)])]
    pallas_call x2 -> x1, Pallas kernels: 9.25 us -> 4.66 us  [fetch(): pl.pallas_call(kernel, in_specs=[HBM], out_specs=VMEM, out_shape=pltpu.VM...]
  transfers between devices with their start and end apart: 43 -> 43, of which waited for: 19 -> 18; matrix products, arithmetic and copies ran while one was open for 2% -> 2% of each run, Pallas kernels for 40% -> 40%
where the time goes in v6:
time: 153 us
  Pallas kernels  61.7 us (40%)
  starting transfers between devices  44.6 us (29%)
  waiting for transfers between devices  38.9 us (25%)
  other arithmetic  3.53 us (2%)
  matrix products  2.48 us (2%)
    pallas_call x14, Pallas kernels, call(): pl.pallas_call(kernel, in_specs=[SMEM] + [VMEM] * (len(ins) - far) + [HBM...  57 us
    ppermute x43, starting transfers between devices, exchange(): return lax.ppermute(array, axis, [(i, i ^ bit) for i in range(size)])  44.6 us
    ppermute x43, waiting for transfers between devices, exchange(): return lax.ppermute(array, axis, [(i, i ^ bit) for i in range(size)])  38.9 us
    pallas_call x1, Pallas kernels, fetch(): pl.pallas_call(kernel, in_specs=[HBM], out_specs=VMEM, out_shape=pltpu.VM...  4.66 us
  transfers between devices with their start and end apart: 43, of which 18 were waited for; matrix products, arithmetic and copies ran while one was open for 2% of the time, Pallas kernels for 40%

profile of v6, /device:TPU:16, one launch (start us, length us, event | category | flops | bytes accessed | tf_op | source)
XLA Modules:
  0.0 152.8 jit_solution(14722865137515066226)
XLA Ops:
  3.6 1.6 %collective-permute-start.2 = (bf16[96,768]{1,0:T(8,128)(2,1)S(1)}, bf16[96,768]{1,0:T(8,128)(2,1)S(1)}, u32[]{:S(2)}, u32[]{:S(2)}) collective-permute-start(bf16[96,768]{1,0:T(8,128)(2,1)S(1)} %get-tuple-element.97), channel_id=1, source_target_pairs={{0,1},{1,0},{2,3},{3,2},{4,5},{5,4},{6,7},{7,6},{8,9},{9,8},{10,11... | collective-permute-start | bytes 442376 | tf_op jit(solution)/shard_map/ppermute | solution.py:22
  5.5 1.6 %collective-permute-start.1 = (bf16[96,768]{1,0:T(8,128)(2,1)S(1)}, bf16[96,768]{1,0:T(8,128)(2,1)S(1)}, u32[]{:S(2)}, u32[]{:S(2)}) collective-permute-start(bf16[96,768]{1,0:T(8,128)(2,1)S(1)} %get-tuple-element.98), channel_id=1, source_target_pairs={{0,3},{1,2},{2,1},{3,0},{4,7},{5,6},{6,5},{7,4},{8,11},{9,10},{10,... | collective-permute-start | bytes 442376 | tf_op jit(solution)/shard_map/ppermute | solution.py:22
  7.1 3.2 %collective-permute-done.2.refs_0_ = bf16[96,768]{1,0:T(8,128)(2,1)S(1)} collective-permute-done((bf16[96,768]{1,0:T(8,128)(2,1)S(1)}, bf16[96,768]{1,0:T(8,128)(2,1)S(1)}, u32[]{:S(2)}, u32[]{:S(2)}) %collective-permute-start.2) | collective-permute-done | bytes 147488 | tf_op jit(solution)/shard_map/ppermute | solution.py:22
  10.4 1.5 collective-permute-start.3
  11.9 1.5 collective-permute-start.4
  13.9 4.7 %fetch.1.refs_9_ = bf16[3072,2048]{1,0:T(8,128)(2,1)S(1)} custom-call(bf16[3072,2048]{1,0:T(8,128)(2,1)} %bitcast.38), custom_call_target="tpu_custom_call" | custom-call | bytes 12582912 | tf_op jit(solution)/shard_map/fetch/pallas_call | solution.py:65
  18.8 1.2 collective-permute-done.1
  20.0 1.6 %collective-permute-start.9 = (bf16[192,768]{1,0:T(8,128)(2,1)S(1)}, bf16[192,768]{1,0:T(8,128)(2,1)S(1)}, u32[]{:S(2)}, u32[]{:S(2)}) collective-permute-start(bf16[192,768]{1,0:T(8,128)(2,1)S(1)} %constant_dynamic-update-slice_fusion.refs_1_), channel_id=1, source_target_pairs={{0,8},{4,12},{8,0},{12,4},{1,9},{5,13},{9,1},{13,5},{2,10},{6,14},... | collective-permute-start | bytes 884744 | tf_op jit(solution)/shard_map/ppermute | solution.py:22
  21.6 1.5 collective-permute-start.11
  23.4 1.3 collective-permute-start.6
  25.4 1.6 %collective-permute-start.8 = (bf16[96,768]{1,0:T(8,128)(2,1)S(1)}, bf16[96,768]{1,0:T(8,128)(2,1)S(1)}, u32[]{:S(2)}, u32[]{:S(2)}) collective-permute-start(bf16[96,768]{1,0:T(8,128)(2,1)S(1)} %get-tuple-element.94), channel_id=1, source_target_pairs={{0,3},{1,2},{2,1},{3,0},{4,7},{5,6},{6,5},{7,4},{8,11},{9,10},{10,... | collective-permute-start | bytes 442376 | tf_op jit(solution)/shard_map/ppermute | solution.py:22
  27.9 1.6 %collective-permute-start.10 = (bf16[96,768]{1,0:T(8,128)(2,1)S(1)}, bf16[96,768]{1,0:T(8,128)(2,1)S(1)}, u32[]{:S(2)}, u32[]{:S(2)}) collective-permute-start(bf16[96,768]{1,0:T(8,128)(2,1)S(1)} %slice.108), channel_id=1, source_target_pairs={{0,4},{4,0},{8,12},{12,8},{1,5},{5,1},{9,13},{13,9},{2,6},{6,2},{1... | collective-permute-start | bytes 442376 | tf_op jit(solution)/shard_map/ppermute | solution.py:22
  29.6 1.4 collective-permute-start.12
  31.3 3.0 %collective-permute-done.7 = bf16[96,768]{1,0:T(8,128)(2,1)S(1)} collective-permute-done((bf16[96,768]{1,0:T(8,128)(2,1)S(1)}, bf16[96,768]{1,0:T(8,128)(2,1)S(1)}, u32[]{:S(2)}, u32[]{:S(2)}) %collective-permute-start.7) | collective-permute-done | bytes 147488 | tf_op jit(solution)/shard_map/ppermute | solution.py:22
  34.4 3.8 %collective-permute-done.8 = bf16[96,768]{1,0:T(8,128)(2,1)S(1)} collective-permute-done((bf16[96,768]{1,0:T(8,128)(2,1)S(1)}, bf16[96,768]{1,0:T(8,128)(2,1)S(1)}, u32[]{:S(2)}, u32[]{:S(2)}) %collective-permute-start.8) | collective-permute-done | bytes 147488 | tf_op jit(solution)/shard_map/ppermute | solution.py:22
  39.6 6.8 %pre_acts.2 = (f32[384,1024]{1,0:T(8,128)S(1)}, f32[384,1024]{1,0:T(8,128)S(1)}, bf16[384,2048]{1,0:T(8,128)(2,1)S(1)}) custom-call(s32[1]{0:T(128)} %bitcast.t_ref, bf16[96,3072]{1,0:T(8,128)(2,1)S(1)} %convolution_convert_fusion.own_ref, bf16[96,768]{1,0:T(8,128)(2,1)S(1)} %collective-permute-done.2.refs_0_, ...), custom_call_target="tpu_custom_call" | custom-call | flops 4831838208 | bytes 1048576 | tf_op jit(solution)/shard_map/pre_acts/pallas_call | solution.py:47
  46.4 3.2 %collective-permute-done.14.refs_1_ = bf16[288,768]{1,0:T(8,128)(2,1)S(1)} collective-permute-done((bf16[288,768]{1,0:T(8,128)(2,1)S(1)}, bf16[288,768]{1,0:T(8,128)(2,1)S(1)}, u32[]{:S(2)}, u32[]{:S(2)}) %collective-permute-start.14) | collective-permute-done | bytes 442400 | tf_op jit(solution)/shard_map/ppermute | solution.py:22
  49.7 6.6 %pre_acts.3 = (f32[384,1024]{1,0:T(8,128)S(1)}, f32[384,1024]{1,0:T(8,128)S(1)}, bf16[384,2048]{1,0:T(8,128)(2,1)S(1)}) custom-call(s32[1]{0:T(128)} %bitcast.t_ref, bf16[96,3072]{1,0:T(8,128)(2,1)S(1)} %convolution_convert_fusion.own_ref, bf16[96,768]{1,0:T(8,128)(2,1)S(1)} %collective-permute-done.2.refs_0_, ...), custom_call_target="tpu_custom_call" | custom-call | flops 4831838208 | bytes 1048576 | tf_op jit(solution)/shard_map/pre_acts/pallas_call | solution.py:47
  56.4 1.6 %collective-permute-start.19 = (bf16[288,768]{1,0:T(8,128)(2,1)S(1)}, bf16[288,768]{1,0:T(8,128)(2,1)S(1)}, u32[]{:S(2)}, u32[]{:S(2)}) collective-permute-start(bf16[288,768]{1,0:T(8,128)(2,1)S(1)} %constant_dynamic-update-slice_fusion.2.refs_0_), channel_id=1, source_target_pairs={{0,12},{4,8},{8,4},{12,0},{1,13},{5,9},{9,5},{13,1},{2,14},{6,10},... | collective-permute-start | bytes 1327112 | tf_op jit(solution)/shard_map/ppermute | solution.py:22
  58.2 1.5 collective-permute-done.16.refs_5_.refs_7_
  59.7 3.7 %project_first.1 = (bf16[192,768]{1,0:T(8,128)(2,1)S(1)}, bf16[192,768]{1,0:T(8,128)(2,1)S(1)}, bf16[384,2048]{1,0:T(8,128)(2,1)S(1)}) custom-call(s32[1]{0:T(128)} %bitcast.t_ref, f32[384,1024]{1,0:T(8,128)S(1)} %get-tuple-element.50.refs_0_, f32[384,1024]{1,0:T(8,128)S(1)} %get-tuple-element.51.refs_1_, ...), custom_call_target="tpu_custom_call" | custom-call | flops 1207959552 | bytes 1048576 | tf_op jit(solution)/shard_map/project_first/pallas_call | solution.py:47
  63.4 1.7 %collective-permute-start.17 = (bf16[192,768]{1,0:T(8,128)(2,1)S(1)}, bf16[192,768]{1,0:T(8,128)(2,1)S(1)}, u32[]{:S(2)}, u32[]{:S(2)}) collective-permute-start(bf16[192,768]{1,0:T(8,128)(2,1)S(1)} %get-tuple-element.58), channel_id=1, source_target_pairs={{0,4},{4,0},{8,12},{12,8},{1,5},{5,1},{9,13},{13,9},{2,6},{6,2},{1... | collective-permute-start | bytes 884744 | tf_op jit(solution)/shard_map/ppermute | solution.py:22
  65.5 5.4 %project_send.1.both_ref = f32[2,384,768]{2,1,0:T(8,128)S(1)} custom-call(s32[1]{0:T(128)} %bitcast.t_ref, bf16[384,2048]{1,0:T(8,128)(2,1)S(1)} %get-tuple-element.57.refs_0_, bf16[2048,3072]{1,0:T(8,128)(2,1)} %bitcast.29), custom_call_target="tpu_custom_call" | custom-call | flops 2415919104 | bytes 1048576 | tf_op jit(solution)/shard_map/project_send/pallas_call | solution.py:47
  71.0 4.7 %grad_hidden.3 = (f32[384,1024]{1,0:T(8,128)S(1)}, bf16[384,1024]{1,0:T(8,128)(2,1)S(1)}) custom-call(s32[1]{0:T(128)} %bitcast.t_ref, bf16[96,3072]{1,0:T(8,128)(2,1)S(1)} %fusion.own_ref, bf16[288,768]{1,0:T(8,128)(2,1)S(1)} %constant_dynamic-update-slice_fusion.2.refs_0_, bf16[288,768]{1,0:T(8,128)(2,1)S(1)} %collective-permute-done.14.refs_1_, ...), custom_call_target="tpu_custom_call" | custom-call | flops 2415919104 | bytes 1048576 | tf_op jit(solution)/shard_map/grad_hidden/pallas_call | solution.py:47
  76.3 4.7 %grad_hidden.2 = (f32[384,1024]{1,0:T(8,128)S(1)}, bf16[384,1024]{1,0:T(8,128)(2,1)S(1)}) custom-call(s32[1]{0:T(128)} %bitcast.t_ref, bf16[96,3072]{1,0:T(8,128)(2,1)S(1)} %fusion.own_ref, bf16[288,768]{1,0:T(8,128)(2,1)S(1)} %constant_dynamic-update-slice_fusion.2.refs_0_, bf16[288,768]{1,0:T(8,128)(2,1)S(1)} %collective-permute-done.14.refs_1_, ...), custom_call_target="tpu_custom_call" | custom-call | flops 2415919104 | bytes 1048576 | tf_op jit(solution)/shard_map/grad_hidden/pallas_call | solution.py:47
  81.2 1.6 %collective-permute-start.24 = (bf16[384,768]{1,0:T(8,128)(2,1)S(1)}, bf16[384,768]{1,0:T(8,128)(2,1)S(1)}, u32[]{:S(2)}, u32[]{:S(2)}) collective-permute-start(bf16[384,768]{1,0:T(8,128)(2,1)S(1)} %get-tuple-element.60), channel_id=1, source_target_pairs={{0,4},{4,0},{8,12},{12,8},{1,5},{5,1},{9,13},{13,9},{2,6},{6,2},{1... | collective-permute-start | bytes 1769480 | tf_op jit(solution)/shard_map/ppermute | solution.py:22
  82.8 3.6 %project_keep.1 = f32[1,384,768]{2,1,0:T(8,128)S(1)} custom-call(s32[1]{0:T(128)} %bitcast.t_ref, bf16[384,2048]{1,0:T(8,128)(2,1)S(1)} %get-tuple-element.57.refs_0_, bf16[2048,3072]{1,0:T(8,128)(2,1)} %bitcast.32), custom_call_target="tpu_custom_call" | custom-call | flops 1207959552 | bytes 1048576 | tf_op jit(solution)/shard_map/project_keep/pallas_call | solution.py:47
  87.2 5.6 %rows_first.1 = (bf16[192,768]{1,0:T(8,128)(2,1)S(1)}, bf16[192,768]{1,0:T(8,128)(2,1)S(1)}, bf16[384,2048]{1,0:T(8,128)(2,1)S(1)}, bf16[384,2048]{1,0:T(8,128)(2,1)S(1)}) custom-call(s32[1]{0:T(128)} %bitcast.t_ref, f32[384,1024]{1,0:T(8,128)S(1)} %get-tuple-element.50.refs_0_, f32[384,1024]{1,0:T(8,128)S(1)} %get-tuple-element.51.refs_1_, ...), custom_call_target="tpu_custom_call" | custom-call | flops 2415919104 | bytes 1048576 | tf_op jit(solution)/shard_map/rows_first/pallas_call | solution.py:47
  92.7 1.5 collective-permute-start.22
  94.6 8.6 %rows_send.1.both_ref = f32[2,384,768]{2,1,0:T(8,128)S(1)} custom-call(s32[1]{0:T(128)} %bitcast.t_ref, bf16[384,2048]{1,0:T(8,128)(2,1)S(1)} %get-tuple-element.69.refs_0_, bf16[384,2048]{1,0:T(8,128)(2,1)S(1)} %get-tuple-element.70.refs_1_, bf16[3072,2048]{1,0:T(8,128)(2,1)} %bitcast.40, bf16[3072,2048]{1,0:T(8,128)(2,1)} %bitcast.36), custom_call_target="tpu_custom_call" | custom-call | flops 4831838208 | bytes 1048576 | tf_op jit(solution)/shard_map/rows_send/pallas_call | solution.py:47
  103.2 5.1 %collective-permute-done.23.low_ref = bf16[192,768]{1,0:T(8,128)(2,1)S(1)} collective-permute-done((bf16[192,768]{1,0:T(8,128)(2,1)S(1)}, bf16[192,768]{1,0:T(8,128)(2,1)S(1)}, u32[]{:S(2)}, u32[]{:S(2)}) %collective-permute-start.23) | collective-permute-done | bytes 294944 | tf_op jit(solution)/shard_map/ppermute | solution.py:22
  108.9 1.3 collective-permute-start.30
  110.5 1.0 collective-permute-start.27
  111.5 2.5 %collective-permute-start.28 = (bf16[96,768]{1,0:T(8,128)(2,1)S(1)}, bf16[96,768]{1,0:T(8,128)(2,1)S(1)}, u32[]{:S(2)}, u32[]{:S(2)}) collective-permute-start(bf16[96,768]{1,0:T(8,128)(2,1)S(1)} %get-tuple-element.90), channel_id=1, source_target_pairs={{0,3},{1,2},{2,1},{3,0},{4,7},{5,6},{6,5},{7,4},{8,11},{9,10},{10,... | collective-permute-start | bytes 442376 | tf_op jit(solution)/shard_map/ppermute | solution.py:22
  113.9 5.2 %rows_keep.1 = f32[1,384,768]{2,1,0:T(8,128)S(1)} custom-call(s32[1]{0:T(128)} %bitcast.t_ref, bf16[384,2048]{1,0:T(8,128)(2,1)S(1)} %get-tuple-element.69.refs_0_, bf16[384,2048]{1,0:T(8,128)(2,1)S(1)} %get-tuple-element.70.refs_1_, bf16[3072,2048]{1,0:T(8,128)(2,1)} %bitcast.41, bf16[3072,2048]{1,0:T(8,128)(2,1)} %bitcast.37), custom_call_target="tpu_custom_call" | custom-call | flops 2415919104 | bytes 1048576 | tf_op jit(solution)/shard_map/rows_keep/pallas_call | solution.py:47
  119.2 3.9 %collective-permute-done.29 = bf16[384,768]{1,0:T(8,128)(2,1)S(1)} collective-permute-done((bf16[384,768]{1,0:T(8,128)(2,1)S(1)}, bf16[384,768]{1,0:T(8,128)(2,1)S(1)}, u32[]{:S(2)}, u32[]{:S(2)}) %collective-permute-start.29) | collective-permute-done | bytes 589856 | tf_op jit(solution)/shard_map/ppermute | solution.py:22
  123.5 1.0 collective-permute-start.35
  124.5 2.5 %collective-permute-start.36 = (bf16[96,768]{1,0:T(8,128)(2,1)S(1)}, bf16[96,768]{1,0:T(8,128)(2,1)S(1)}, u32[]{:S(2)}, u32[]{:S(2)}) collective-permute-start(bf16[96,768]{1,0:T(8,128)(2,1)S(1)} %get-tuple-element.87), channel_id=1, source_target_pairs={{0,3},{1,2},{2,1},{3,0},{4,7},{5,6},{6,5},{7,4},{8,11},{9,10},{10,... | collective-permute-start | bytes 442376 | tf_op jit(solution)/shard_map/ppermute | solution.py:22
  127.0 3.3 %collective-permute-done.31 = bf16[96,768]{1,0:T(8,128)(2,1)S(1)} collective-permute-done((bf16[96,768]{1,0:T(8,128)(2,1)S(1)}, bf16[96,768]{1,0:T(8,128)(2,1)S(1)}, u32[]{:S(2)}, u32[]{:S(2)}) %collective-permute-start.31) | collective-permute-done | bytes 147488 | tf_op jit(solution)/shard_map/ppermute | solution.py:22
  131.1 1.7 %collective-permute-start.32 = (bf16[128,768]{1,0:T(8,128)(2,1)S(1)}, bf16[128,768]{1,0:T(8,128)(2,1)S(1)}, u32[]{:S(2)}, u32[]{:S(2)}) collective-permute-start(bf16[128,768]{1,0:T(8,128)(2,1)S(1)} %get-tuple-element.85.refs_0_), channel_id=1, source_target_pairs={{0,4},{4,0},{8,12},{12,8},{1,5},{5,1},{9,13},{13,9},{2,6},{6,2},{1... | collective-permute-start | bytes 589832 | tf_op jit(solution)/shard_map/ppermute | solution.py:22
  133.4 1.2 collective-permute-start.34
  134.6 3.4 %collective-permute-done.36 = bf16[96,768]{1,0:T(8,128)(2,1)S(1)} collective-permute-done((bf16[96,768]{1,0:T(8,128)(2,1)S(1)}, bf16[96,768]{1,0:T(8,128)(2,1)S(1)}, u32[]{:S(2)}, u32[]{:S(2)}) %collective-permute-start.36) | collective-permute-done | bytes 147488 | tf_op jit(solution)/shard_map/ppermute | solution.py:22
  138.7 1.6 %collective-permute-start.37 = (bf16[128,768]{1,0:T(8,128)(2,1)S(1)}, bf16[128,768]{1,0:T(8,128)(2,1)S(1)}, u32[]{:S(2)}, u32[]{:S(2)}) collective-permute-start(bf16[128,768]{1,0:T(8,128)(2,1)S(1)} %fusion.4.refs_0_), channel_id=1, source_target_pairs={{0,4},{4,0},{8,12},{12,8},{1,5},{5,1},{9,13},{13,9},{2,6},{6,2},{1... | collective-permute-start | bytes 589832 | tf_op jit(solution)/shard_map/ppermute | solution.py:22
  141.2 1.1 collective-permute-start.39
  142.3 1.1 collective-permute-done.40
  143.5 1.5 collective-permute-start.41
  145.0 3.7 %collective-permute-done.41 = f32[2,128]{1,0:T(2,128)S(1)} collective-permute-done((f32[2,128]{1,0:T(2,128)S(1)}, f32[2,128]{1,0:T(2,128)S(1)}, u32[]{:S(2)}, u32[]{:S(2)}) %collective-permute-start.41) | collective-permute-done | bytes 1056 | tf_op jit(solution)/shard_map/ppermute | solution.py:22
  148.7 1.0 collective-permute-start.42
  (103 shorter events, 18.0 us)
Async XLA Ops:
  0.6 2.6 %copy-start = (bf16[128,3072]{1,0:T(8,128)(2,1)S(1)}, bf16[128,3072]{1,0:T(8,128)(2,1)}, u32[]{:S(2)}) copy-start(bf16[128,3072]{1,0:T(8,128)(2,1)} %param.7) | copy-start | bytes 2359300
  0.6 13.2 %copy-start.3 = (f32[128,2]{0,1:T(2,128)S(1)}, f32[128,2]{0,1:T(2,128)}, u32[]{:S(2)}) copy-start(f32[128,2]{0,1:T(2,128)} %param.9) | copy-start | bytes 3076
  3.6 6.8 %collective-permute-start.2 = (bf16[96,768]{1,0:T(8,128)(2,1)S(1)}, bf16[96,768]{1,0:T(8,128)(2,1)S(1)}, u32[]{:S(2)}, u32[]{:S(2)}) collective-permute-start(bf16[96,768]{1,0:T(8,128)(2,1)S(1)} %get-tuple-element.97), channel_id=1, source_target_pairs={{0,1},{1,0},{2,3},{3,2},{4,5},{5,4},{6,7},{7,6},{8,9},{9,8},{10,11... | collective-permute-start | bytes 442376 | tf_op jit(solution)/shard_map/ppermute | solution.py:22
  5.2 13.6 %collective-permute-start = (bf16[96,768]{1,0:T(8,128)(2,1)S(1)}, bf16[96,768]{1,0:T(8,128)(2,1)S(1)}, u32[]{:S(2)}, u32[]{:S(2)}) collective-permute-start(bf16[96,768]{1,0:T(8,128)(2,1)S(1)} %get-tuple-element.99), channel_id=1, source_target_pairs={{0,2},{1,3},{2,0},{3,1},{4,6},{5,7},{6,4},{7,5},{8,10},{9,11},{10,... | collective-permute-start | bytes 442376 | tf_op jit(solution)/shard_map/ppermute | solution.py:22
  5.5 14.4 %collective-permute-start.1 = (bf16[96,768]{1,0:T(8,128)(2,1)S(1)}, bf16[96,768]{1,0:T(8,128)(2,1)S(1)}, u32[]{:S(2)}, u32[]{:S(2)}) collective-permute-start(bf16[96,768]{1,0:T(8,128)(2,1)S(1)} %get-tuple-element.98), channel_id=1, source_target_pairs={{0,3},{1,2},{2,1},{3,0},{4,7},{5,6},{6,5},{7,4},{8,11},{9,10},{10,... | collective-permute-start | bytes 442376 | tf_op jit(solution)/shard_map/ppermute | solution.py:22
  10.4 9.6 %collective-permute-start.3 = (bf16[96,768]{1,0:T(8,128)(2,1)S(1)}, bf16[96,768]{1,0:T(8,128)(2,1)S(1)}, u32[]{:S(2)}, u32[]{:S(2)}) collective-permute-start(bf16[96,768]{1,0:T(8,128)(2,1)S(1)} %collective-permute-done.2.refs_0_), channel_id=1, source_target_pairs={{0,4},{4,0},{8,12},{12,8},{1,5},{5,1},{9,13},{13,9},{2,6},{6,2},{1... | collective-permute-start | bytes 442376 | tf_op jit(solution)/shard_map/ppermute | solution.py:22
  11.9 8.1 %collective-permute-start.4 = (bf16[96,768]{1,0:T(8,128)(2,1)S(1)}, bf16[96,768]{1,0:T(8,128)(2,1)S(1)}, u32[]{:S(2)}, u32[]{:S(2)}) collective-permute-start(bf16[96,768]{1,0:T(8,128)(2,1)S(1)} %collective-permute-done.2.refs_0_), channel_id=1, source_target_pairs={{0,8},{4,12},{8,0},{12,4},{1,9},{5,13},{9,1},{13,5},{2,10},{6,14},... | collective-permute-start | bytes 442376 | tf_op jit(solution)/shard_map/ppermute | solution.py:22
  13.4 6.6 %collective-permute-start.5 = (bf16[96,768]{1,0:T(8,128)(2,1)S(1)}, bf16[96,768]{1,0:T(8,128)(2,1)S(1)}, u32[]{:S(2)}, u32[]{:S(2)}) collective-permute-start(bf16[96,768]{1,0:T(8,128)(2,1)S(1)} %collective-permute-done.2.refs_0_), channel_id=1, source_target_pairs={{0,12},{4,8},{8,4},{12,0},{1,13},{5,9},{9,5},{13,1},{2,14},{6,10},... | collective-permute-start | bytes 442376 | tf_op jit(solution)/shard_map/ppermute | solution.py:22
  13.9 9.2 %copy-start.2 = (bf16[128,3072]{1,0:T(8,128)(2,1)S(1)}, bf16[128,3072]{1,0:T(8,128)(2,1)}, u32[]{:S(2)}) copy-start(bf16[128,3072]{1,0:T(8,128)(2,1)} %param.13) | copy-start | bytes 2359300
  20.0 7.9 %collective-permute-start.9 = (bf16[192,768]{1,0:T(8,128)(2,1)S(1)}, bf16[192,768]{1,0:T(8,128)(2,1)S(1)}, u32[]{:S(2)}, u32[]{:S(2)}) collective-permute-start(bf16[192,768]{1,0:T(8,128)(2,1)S(1)} %constant_dynamic-update-slice_fusion.refs_1_), channel_id=1, source_target_pairs={{0,8},{4,12},{8,0},{12,4},{1,9},{5,13},{9,1},{13,5},{2,10},{6,14},... | collective-permute-start | bytes 884744 | tf_op jit(solution)/shard_map/ppermute | solution.py:22
  21.6 8.0 %collective-permute-start.11 = (bf16[192,768]{1,0:T(8,128)(2,1)S(1)}, bf16[192,768]{1,0:T(8,128)(2,1)S(1)}, u32[]{:S(2)}, u32[]{:S(2)}) collective-permute-start(bf16[192,768]{1,0:T(8,128)(2,1)S(1)} %constant_dynamic-update-slice_fusion.refs_1_), channel_id=1, source_target_pairs={{0,4},{4,0},{8,12},{12,8},{1,5},{5,1},{9,13},{13,9},{2,6},{6,2},{1... | collective-permute-start | bytes 884744 | tf_op jit(solution)/shard_map/ppermute | solution.py:22
  23.4 8.0 %collective-permute-start.6 = (bf16[96,768]{1,0:T(8,128)(2,1)S(1)}, bf16[96,768]{1,0:T(8,128)(2,1)S(1)}, u32[]{:S(2)}, u32[]{:S(2)}) collective-permute-start(bf16[96,768]{1,0:T(8,128)(2,1)S(1)} %get-tuple-element.96), channel_id=1, source_target_pairs={{0,1},{1,0},{2,3},{3,2},{4,5},{5,4},{6,7},{7,6},{8,9},{9,8},{10,11... | collective-permute-start | bytes 442376 | tf_op jit(solution)/shard_map/ppermute | solution.py:22
  24.6 9.7 %collective-permute-start.7 = (bf16[96,768]{1,0:T(8,128)(2,1)S(1)}, bf16[96,768]{1,0:T(8,128)(2,1)S(1)}, u32[]{:S(2)}, u32[]{:S(2)}) collective-permute-start(bf16[96,768]{1,0:T(8,128)(2,1)S(1)} %get-tuple-element.95), channel_id=1, source_target_pairs={{0,2},{1,3},{2,0},{3,1},{4,6},{5,7},{6,4},{7,5},{8,10},{9,11},{10,... | collective-permute-start | bytes 442376 | tf_op jit(solution)/shard_map/ppermute | solution.py:22
  25.4 12.9 %collective-permute-start.8 = (bf16[96,768]{1,0:T(8,128)(2,1)S(1)}, bf16[96,768]{1,0:T(8,128)(2,1)S(1)}, u32[]{:S(2)}, u32[]{:S(2)}) collective-permute-start(bf16[96,768]{1,0:T(8,128)(2,1)S(1)} %get-tuple-element.94), channel_id=1, source_target_pairs={{0,3},{1,2},{2,1},{3,0},{4,7},{5,6},{6,5},{7,4},{8,11},{9,10},{10,... | collective-permute-start | bytes 442376 | tf_op jit(solution)/shard_map/ppermute | solution.py:22
  27.9 10.4 %collective-permute-start.10 = (bf16[96,768]{1,0:T(8,128)(2,1)S(1)}, bf16[96,768]{1,0:T(8,128)(2,1)S(1)}, u32[]{:S(2)}, u32[]{:S(2)}) collective-permute-start(bf16[96,768]{1,0:T(8,128)(2,1)S(1)} %slice.108), channel_id=1, source_target_pairs={{0,4},{4,0},{8,12},{12,8},{1,5},{5,1},{9,13},{13,9},{2,6},{6,2},{1... | collective-permute-start | bytes 442376 | tf_op jit(solution)/shard_map/ppermute | solution.py:22
  29.6 8.6 %collective-permute-start.12 = (bf16[96,768]{1,0:T(8,128)(2,1)S(1)}, bf16[96,768]{1,0:T(8,128)(2,1)S(1)}, u32[]{:S(2)}, u32[]{:S(2)}) collective-permute-start(bf16[96,768]{1,0:T(8,128)(2,1)S(1)} %slice.109), channel_id=1, source_target_pairs={{0,8},{4,12},{8,0},{12,4},{1,9},{5,13},{9,1},{13,5},{2,10},{6,14},... | collective-permute-start | bytes 442376 | tf_op jit(solution)/shard_map/ppermute | solution.py:22
  38.3 11.3 %collective-permute-start.14 = (bf16[288,768]{1,0:T(8,128)(2,1)S(1)}, bf16[288,768]{1,0:T(8,128)(2,1)S(1)}, u32[]{:S(2)}, u32[]{:S(2)}) collective-permute-start(bf16[288,768]{1,0:T(8,128)(2,1)S(1)} %constant_dynamic-update-slice_fusion.2.refs_0_), channel_id=1, source_target_pairs={{0,4},{4,0},{8,12},{12,8},{1,5},{5,1},{9,13},{13,9},{2,6},{6,2},{1... | collective-permute-start | bytes 1327112 | tf_op jit(solution)/shard_map/ppermute | solution.py:22
  38.9 10.8 %collective-permute-start.15 = (bf16[288,768]{1,0:T(8,128)(2,1)S(1)}, bf16[288,768]{1,0:T(8,128)(2,1)S(1)}, u32[]{:S(2)}, u32[]{:S(2)}) collective-permute-start(bf16[288,768]{1,0:T(8,128)(2,1)S(1)} %constant_dynamic-update-slice_fusion.2.refs_0_), channel_id=1, source_target_pairs={{0,8},{4,12},{8,0},{12,4},{1,9},{5,13},{9,1},{13,5},{2,10},{6,14},... | collective-permute-start | bytes 1327112 | tf_op jit(solution)/shard_map/ppermute | solution.py:22
  46.3 11.9 %collective-permute-start.13 = (bf16[384,2048]{1,0:T(8,128)(2,1)S(1)}, bf16[384,2048]{1,0:T(8,128)(2,1)S(1)}, u32[]{:S(2)}, u32[]{:S(2)}) collective-permute-start(bf16[384,2048]{1,0:T(8,128)(2,1)S(1)} %get-tuple-element.52), channel_id=1, source_target_pairs={{0,16},{16,0},{1,17},{17,1},{2,18},{18,2},{3,19},{19,3},{4,20},{20... | collective-permute-start | bytes 4718600 | tf_op jit(solution)/shard_map/ppermute | solution.py:22
  56.3 3.5 %collective-permute-start.16 = (bf16[384,2048]{1,0:T(8,128)(2,1)S(1)}, bf16[384,2048]{1,0:T(8,128)(2,1)S(1)}, u32[]{:S(2)}, u32[]{:S(2)}) collective-permute-start(bf16[384,2048]{1,0:T(8,128)(2,1)S(1)} %get-tuple-element.56), channel_id=1, source_target_pairs={{0,16},{16,0},{1,17},{17,1},{2,18},{18,2},{3,19},{19,3},{4,20},{20... | collective-permute-start | bytes 4718600 | tf_op jit(solution)/shard_map/ppermute | solution.py:22
  56.4 14.6 %collective-permute-start.19 = (bf16[288,768]{1,0:T(8,128)(2,1)S(1)}, bf16[288,768]{1,0:T(8,128)(2,1)S(1)}, u32[]{:S(2)}, u32[]{:S(2)}) collective-permute-start(bf16[288,768]{1,0:T(8,128)(2,1)S(1)} %constant_dynamic-update-slice_fusion.2.refs_0_), channel_id=1, source_target_pairs={{0,12},{4,8},{8,4},{12,0},{1,13},{5,9},{9,5},{13,1},{2,14},{6,10},... | collective-permute-start | bytes 1327112 | tf_op jit(solution)/shard_map/ppermute | solution.py:22
  63.4 12.4 %collective-permute-start.17 = (bf16[192,768]{1,0:T(8,128)(2,1)S(1)}, bf16[192,768]{1,0:T(8,128)(2,1)S(1)}, u32[]{:S(2)}, u32[]{:S(2)}) collective-permute-start(bf16[192,768]{1,0:T(8,128)(2,1)S(1)} %get-tuple-element.58), channel_id=1, source_target_pairs={{0,4},{4,0},{8,12},{12,8},{1,5},{5,1},{9,13},{13,9},{2,6},{6,2},{1... | collective-permute-start | bytes 884744 | tf_op jit(solution)/shard_map/ppermute | solution.py:22
  65.1 11.0 %collective-permute-start.18 = (bf16[192,768]{1,0:T(8,128)(2,1)S(1)}, bf16[192,768]{1,0:T(8,128)(2,1)S(1)}, u32[]{:S(2)}, u32[]{:S(2)}) collective-permute-start(bf16[192,768]{1,0:T(8,128)(2,1)S(1)} %get-tuple-element.59), channel_id=1, source_target_pairs={{0,8},{4,12},{8,0},{12,4},{1,9},{5,13},{9,1},{13,5},{2,10},{6,14},... | collective-permute-start | bytes 884744 | tf_op jit(solution)/shard_map/ppermute | solution.py:22
  75.7 11.5 %collective-permute-start.20 = (bf16[384,1024]{1,0:T(8,128)(2,1)S(1)}, bf16[384,1024]{1,0:T(8,128)(2,1)S(1)}, u32[]{:S(2)}, u32[]{:S(2)}) collective-permute-start(bf16[384,1024]{1,0:T(8,128)(2,1)S(1)} %get-tuple-element.67), channel_id=1, source_target_pairs={{0,16},{16,0},{1,17},{17,1},{2,18},{18,2},{3,19},{19,3},{4,20},{20... | collective-permute-start | bytes 2359304 | tf_op jit(solution)/shard_map/ppermute | solution.py:22
  81.0 6.2 %collective-permute-start.21 = (bf16[384,1024]{1,0:T(8,128)(2,1)S(1)}, bf16[384,1024]{1,0:T(8,128)(2,1)S(1)}, u32[]{:S(2)}, u32[]{:S(2)}) collective-permute-start(bf16[384,1024]{1,0:T(8,128)(2,1)S(1)} %get-tuple-element.62), channel_id=1, source_target_pairs={{0,16},{16,0},{1,17},{17,1},{2,18},{18,2},{3,19},{19,3},{4,20},{20... | collective-permute-start | bytes 2359304 | tf_op jit(solution)/shard_map/ppermute | solution.py:22
  81.2 29.0 %collective-permute-start.24 = (bf16[384,768]{1,0:T(8,128)(2,1)S(1)}, bf16[384,768]{1,0:T(8,128)(2,1)S(1)}, u32[]{:S(2)}, u32[]{:S(2)}) collective-permute-start(bf16[384,768]{1,0:T(8,128)(2,1)S(1)} %get-tuple-element.60), channel_id=1, source_target_pairs={{0,4},{4,0},{8,12},{12,8},{1,5},{5,1},{9,13},{13,9},{2,6},{6,2},{1... | collective-permute-start | bytes 1769480 | tf_op jit(solution)/shard_map/ppermute | solution.py:22
  86.5 23.7 %collective-permute-start.25 = (bf16[384,768]{1,0:T(8,128)(2,1)S(1)}, bf16[384,768]{1,0:T(8,128)(2,1)S(1)}, u32[]{:S(2)}, u32[]{:S(2)}) collective-permute-start(bf16[384,768]{1,0:T(8,128)(2,1)S(1)} %get-tuple-element.75), channel_id=1, source_target_pairs={{0,8},{4,12},{8,0},{12,4},{1,9},{5,13},{9,1},{13,5},{2,10},{6,14},... | collective-permute-start | bytes 1769480 | tf_op jit(solution)/shard_map/ppermute | solution.py:22
  92.7 10.5 %collective-permute-start.22 = (bf16[192,768]{1,0:T(8,128)(2,1)S(1)}, bf16[192,768]{1,0:T(8,128)(2,1)S(1)}, u32[]{:S(2)}, u32[]{:S(2)}) collective-permute-start(bf16[192,768]{1,0:T(8,128)(2,1)S(1)} %get-tuple-element.71), channel_id=1, source_target_pairs={{0,4},{4,0},{8,12},{12,8},{1,5},{5,1},{9,13},{13,9},{2,6},{6,2},{1... | collective-permute-start | bytes 884744 | tf_op jit(solution)/shard_map/ppermute | solution.py:22
  94.2 14.1 %collective-permute-start.23 = (bf16[192,768]{1,0:T(8,128)(2,1)S(1)}, bf16[192,768]{1,0:T(8,128)(2,1)S(1)}, u32[]{:S(2)}, u32[]{:S(2)}) collective-permute-start(bf16[192,768]{1,0:T(8,128)(2,1)S(1)} %get-tuple-element.72), channel_id=1, source_target_pairs={{0,8},{4,12},{8,0},{12,4},{1,9},{5,13},{9,1},{13,5},{2,10},{6,14},... | collective-permute-start | bytes 884744 | tf_op jit(solution)/shard_map/ppermute | solution.py:22
  108.4 14.6 %collective-permute-start.29 = (bf16[384,768]{1,0:T(8,128)(2,1)S(1)}, bf16[384,768]{1,0:T(8,128)(2,1)S(1)}, u32[]{:S(2)}, u32[]{:S(2)}) collective-permute-start(bf16[384,768]{1,0:T(8,128)(2,1)S(1)} %get-tuple-element.73), channel_id=1, source_target_pairs={{0,4},{4,0},{8,12},{12,8},{1,5},{5,1},{9,13},{13,9},{2,6},{6,2},{1... | collective-permute-start | bytes 1769480 | tf_op jit(solution)/shard_map/ppermute | solution.py:22
  108.9 14.3 %collective-permute-start.30 = (bf16[384,768]{1,0:T(8,128)(2,1)S(1)}, bf16[384,768]{1,0:T(8,128)(2,1)S(1)}, u32[]{:S(2)}, u32[]{:S(2)}) collective-permute-start(bf16[384,768]{1,0:T(8,128)(2,1)S(1)} %get-tuple-element.77), channel_id=1, source_target_pairs={{0,8},{4,12},{8,0},{12,4},{1,9},{5,13},{9,1},{13,5},{2,10},{6,14},... | collective-permute-start | bytes 1769480 | tf_op jit(solution)/shard_map/ppermute | solution.py:22
  110.4 14.1 %collective-permute-start.26 = (bf16[96,768]{1,0:T(8,128)(2,1)S(1)}, bf16[96,768]{1,0:T(8,128)(2,1)S(1)}, u32[]{:S(2)}, u32[]{:S(2)}) collective-permute-start(bf16[96,768]{1,0:T(8,128)(2,1)S(1)} %get-tuple-element.92), channel_id=1, source_target_pairs={{0,1},{1,0},{2,3},{3,2},{4,5},{5,4},{6,7},{7,6},{8,9},{9,8},{10,11... | collective-permute-start | bytes 442376 | tf_op jit(solution)/shard_map/ppermute | solution.py:22
  110.5 16.5 %collective-permute-start.27 = (bf16[96,768]{1,0:T(8,128)(2,1)S(1)}, bf16[96,768]{1,0:T(8,128)(2,1)S(1)}, u32[]{:S(2)}, u32[]{:S(2)}) collective-permute-start(bf16[96,768]{1,0:T(8,128)(2,1)S(1)} %get-tuple-element.91), channel_id=1, source_target_pairs={{0,2},{1,3},{2,0},{3,1},{4,6},{5,7},{6,4},{7,5},{8,10},{9,11},{10,... | collective-permute-start | bytes 442376 | tf_op jit(solution)/shard_map/ppermute | solution.py:22
  111.5 15.5 %collective-permute-start.28 = (bf16[96,768]{1,0:T(8,128)(2,1)S(1)}, bf16[96,768]{1,0:T(8,128)(2,1)S(1)}, u32[]{:S(2)}, u32[]{:S(2)}) collective-permute-start(bf16[96,768]{1,0:T(8,128)(2,1)S(1)} %get-tuple-element.90), channel_id=1, source_target_pairs={{0,3},{1,2},{2,1},{3,0},{4,7},{5,6},{6,5},{7,4},{8,11},{9,10},{10,... | collective-permute-start | bytes 442376 | tf_op jit(solution)/shard_map/ppermute | solution.py:22
  123.4 6.9 %collective-permute-start.31 = (bf16[96,768]{1,0:T(8,128)(2,1)S(1)}, bf16[96,768]{1,0:T(8,128)(2,1)S(1)}, u32[]{:S(2)}, u32[]{:S(2)}) collective-permute-start(bf16[96,768]{1,0:T(8,128)(2,1)S(1)} %get-tuple-element.89), channel_id=1, source_target_pairs={{0,1},{1,0},{2,3},{3,2},{4,5},{5,4},{6,7},{7,6},{8,9},{9,8},{10,11... | collective-permute-start | bytes 442376 | tf_op jit(solution)/shard_map/ppermute | solution.py:22
  123.5 11.1 %collective-permute-start.35 = (bf16[96,768]{1,0:T(8,128)(2,1)S(1)}, bf16[96,768]{1,0:T(8,128)(2,1)S(1)}, u32[]{:S(2)}, u32[]{:S(2)}) collective-permute-start(bf16[96,768]{1,0:T(8,128)(2,1)S(1)} %get-tuple-element.88), channel_id=1, source_target_pairs={{0,2},{1,3},{2,0},{3,1},{4,6},{5,7},{6,4},{7,5},{8,10},{9,11},{10,... | collective-permute-start | bytes 442376 | tf_op jit(solution)/shard_map/ppermute | solution.py:22
  124.5 13.5 %collective-permute-start.36 = (bf16[96,768]{1,0:T(8,128)(2,1)S(1)}, bf16[96,768]{1,0:T(8,128)(2,1)S(1)}, u32[]{:S(2)}, u32[]{:S(2)}) collective-permute-start(bf16[96,768]{1,0:T(8,128)(2,1)S(1)} %get-tuple-element.87), channel_id=1, source_target_pairs={{0,3},{1,2},{2,1},{3,0},{4,7},{5,6},{6,5},{7,4},{8,11},{9,10},{10,... | collective-permute-start | bytes 442376 | tf_op jit(solution)/shard_map/ppermute | solution.py:22
  131.1 10.1 %collective-permute-start.32 = (bf16[128,768]{1,0:T(8,128)(2,1)S(1)}, bf16[128,768]{1,0:T(8,128)(2,1)S(1)}, u32[]{:S(2)}, u32[]{:S(2)}) collective-permute-start(bf16[128,768]{1,0:T(8,128)(2,1)S(1)} %get-tuple-element.85.refs_0_), channel_id=1, source_target_pairs={{0,4},{4,0},{8,12},{12,8},{1,5},{5,1},{9,13},{13,9},{2,6},{6,2},{1... | collective-permute-start | bytes 589832 | tf_op jit(solution)/shard_map/ppermute | solution.py:22
  132.8 9.4 %collective-permute-start.33 = (bf16[128,768]{1,0:T(8,128)(2,1)S(1)}, bf16[128,768]{1,0:T(8,128)(2,1)S(1)}, u32[]{:S(2)}, u32[]{:S(2)}) collective-permute-start(bf16[128,768]{1,0:T(8,128)(2,1)S(1)} %get-tuple-element.85.refs_0_), channel_id=1, source_target_pairs={{0,8},{4,12},{8,0},{12,4},{1,9},{5,13},{9,1},{13,5},{2,10},{6,14},... | collective-permute-start | bytes 589832 | tf_op jit(solution)/shard_map/ppermute | solution.py:22
  133.4 16.2 %collective-permute-start.34 = (bf16[128,768]{1,0:T(8,128)(2,1)S(1)}, bf16[128,768]{1,0:T(8,128)(2,1)S(1)}, u32[]{:S(2)}, u32[]{:S(2)}) collective-permute-start(bf16[128,768]{1,0:T(8,128)(2,1)S(1)} %get-tuple-element.85.refs_0_), channel_id=1, source_target_pairs={{0,12},{4,8},{8,4},{12,0},{1,13},{5,9},{9,5},{13,1},{2,14},{6,10},... | collective-permute-start | bytes 589832 | tf_op jit(solution)/shard_map/ppermute | solution.py:22
  138.7 11.9 %collective-permute-start.37 = (bf16[128,768]{1,0:T(8,128)(2,1)S(1)}, bf16[128,768]{1,0:T(8,128)(2,1)S(1)}, u32[]{:S(2)}, u32[]{:S(2)}) collective-permute-start(bf16[128,768]{1,0:T(8,128)(2,1)S(1)} %fusion.4.refs_0_), channel_id=1, source_target_pairs={{0,4},{4,0},{8,12},{12,8},{1,5},{5,1},{9,13},{13,9},{2,6},{6,2},{1... | collective-permute-start | bytes 589832 | tf_op jit(solution)/shard_map/ppermute | solution.py:22
  140.3 10.3 %collective-permute-start.38 = (bf16[128,768]{1,0:T(8,128)(2,1)S(1)}, bf16[128,768]{1,0:T(8,128)(2,1)S(1)}, u32[]{:S(2)}, u32[]{:S(2)}) collective-permute-start(bf16[128,768]{1,0:T(8,128)(2,1)S(1)} %fusion.4.refs_0_), channel_id=1, source_target_pairs={{0,8},{4,12},{8,0},{12,4},{1,9},{5,13},{9,1},{13,5},{2,10},{6,14},... | collective-permute-start | bytes 589832 | tf_op jit(solution)/shard_map/ppermute | solution.py:22
  141.2 9.4 %collective-permute-start.39 = (bf16[128,768]{1,0:T(8,128)(2,1)S(1)}, bf16[128,768]{1,0:T(8,128)(2,1)S(1)}, u32[]{:S(2)}, u32[]{:S(2)}) collective-permute-start(bf16[128,768]{1,0:T(8,128)(2,1)S(1)} %fusion.4.refs_0_), channel_id=1, source_target_pairs={{0,12},{4,8},{8,4},{12,0},{1,13},{5,9},{9,5},{13,1},{2,14},{6,10},... | collective-permute-start | bytes 589832 | tf_op jit(solution)/shard_map/ppermute | solution.py:22
  142.3 1.2 collective-permute-start.40
  143.5 5.2 %collective-permute-start.41 = (f32[2,128]{1,0:T(2,128)S(1)}, f32[2,128]{1,0:T(2,128)S(1)}, u32[]{:S(2)}, u32[]{:S(2)}) collective-permute-start(f32[2,128]{1,0:T(2,128)S(1)} %add.49), channel_id=1, source_target_pairs={{0,4},{4,0},{8,12},{12,8},{1,5},{5,1},{9,13},{13,9},{2,6},{6,2},{1... | collective-permute-start | bytes 3080 | tf_op jit(solution)/shard_map/ppermute | solution.py:22
  148.7 3.6 %collective-permute-start.42 = (f32[2,128]{1,0:T(2,128)S(1)}, f32[2,128]{1,0:T(2,128)S(1)}, u32[]{:S(2)}, u32[]{:S(2)}) collective-permute-start(f32[2,128]{1,0:T(2,128)S(1)} %add.50), channel_id=1, source_target_pairs={{0,8},{4,12},{8,0},{12,4},{1,9},{5,13},{9,1},{13,5},{2,10},{6,14},... | collective-permute-start | bytes 3080 | tf_op jit(solution)/shard_map/ppermute | solution.py:22
  149.6 3.2 %copy-start.1 = (bf16[128,3072]{1,0:T(8,128)(2,1)S(1)}, bf16[128,3072]{1,0:T(8,128)(2,1)}, u32[]{:S(2)}) copy-start(bf16[128,3072]{1,0:T(8,128)(2,1)} %param.7) | copy-start | bytes 2359300

commit v7 on v6

--- a/solution.py
+++ b/solution.py
@@ -51,7 +51,7 @@
         out_shape=outs,
         scratch_shapes=scratch,
         compiler_params=params(mib),
-        cost_estimate=pl.CostEstimate(flops=flops, bytes_accessed=MIB, transcendentals=0),
+        cost_estimate=pl.CostEstimate(flops=flops // 2, bytes_accessed=MIB, transcendentals=0),
         name=name,
     )(t, *ins)
 

time: 153 us -> 150 us (0.980)
  waiting for transfers between devices: 38.9 us -> 34.7 us
    ppermute x43, waiting for transfers between devices: 38.9 us -> 34.7 us  [exchange(): return lax.ppermute(array, axis, [(i, i ^ bit) for i in range(size)])]
  transfers between devices with their start and end apart: 43 -> 43, of which waited for: 18 -> 18; matrix products, arithmetic and copies ran while one was open for 2% -> 2% of each run, Pallas kernels for 40% -> 41%
where the time goes in v7:
time: 150 us; the launch traced here: 149 us
  Pallas kernels  61.7 us (41%)
  starting transfers between devices  45.3 us (30%)
  waiting for transfers between devices  34.7 us (23%)
  other arithmetic  3.53 us (2%)
  matrix products  2.49 us (2%)
    pallas_call x14, Pallas kernels, call(): pl.pallas_call(kernel, in_specs=[SMEM] + [VMEM] * (len(ins) - far) + [HBM...  57.1 us
    ppermute x43, starting transfers between devices, exchange(): return lax.ppermute(array, axis, [(i, i ^ bit) for i in range(size)])  45.3 us
    ppermute x43, waiting for transfers between devices, exchange(): return lax.ppermute(array, axis, [(i, i ^ bit) for i in range(size)])  34.7 us
    pallas_call x1, Pallas kernels, fetch(): pl.pallas_call(kernel, in_specs=[HBM], out_specs=VMEM, out_shape=pltpu.VM...  4.66 us
  transfers between devices with their start and end apart: 43, of which 18 were waited for; matrix products, arithmetic and copies ran while one was open for 2% of the time, Pallas kernels for 41%

profile of v7, /device:TPU:16, one launch (start us, length us, event | category | flops | bytes accessed | tf_op | source)
XLA Modules:
  0.0 149.3 jit_solution(4132934292427644975)
XLA Ops:
  3.6 1.6 %collective-permute-start.2 = (bf16[96,768]{1,0:T(8,128)(2,1)S(1)}, bf16[96,768]{1,0:T(8,128)(2,1)S(1)}, u32[]{:S(2)}, u32[]{:S(2)}) collective-permute-start(bf16[96,768]{1,0:T(8,128)(2,1)S(1)} %get-tuple-element.97), channel_id=1, source_target_pairs={{0,1},{1,0},{2,3},{3,2},{4,5},{5,4},{6,7},{7,6},{8,9},{9,8},{10,11... | collective-permute-start | bytes 442376 | tf_op jit(solution)/shard_map/ppermute | solution.py:22
  5.5 1.6 %collective-permute-start.1 = (bf16[96,768]{1,0:T(8,128)(2,1)S(1)}, bf16[96,768]{1,0:T(8,128)(2,1)S(1)}, u32[]{:S(2)}, u32[]{:S(2)}) collective-permute-start(bf16[96,768]{1,0:T(8,128)(2,1)S(1)} %get-tuple-element.98), channel_id=1, source_target_pairs={{0,3},{1,2},{2,1},{3,0},{4,7},{5,6},{6,5},{7,4},{8,11},{9,10},{10,... | collective-permute-start | bytes 442376 | tf_op jit(solution)/shard_map/ppermute | solution.py:22
  7.1 3.2 %collective-permute-done.2.refs_0_ = bf16[96,768]{1,0:T(8,128)(2,1)S(1)} collective-permute-done((bf16[96,768]{1,0:T(8,128)(2,1)S(1)}, bf16[96,768]{1,0:T(8,128)(2,1)S(1)}, u32[]{:S(2)}, u32[]{:S(2)}) %collective-permute-start.2) | collective-permute-done | bytes 147488 | tf_op jit(solution)/shard_map/ppermute | solution.py:22
  10.4 1.5 %collective-permute-start.3 = (bf16[96,768]{1,0:T(8,128)(2,1)S(1)}, bf16[96,768]{1,0:T(8,128)(2,1)S(1)}, u32[]{:S(2)}, u32[]{:S(2)}) collective-permute-start(bf16[96,768]{1,0:T(8,128)(2,1)S(1)} %collective-permute-done.2.refs_0_), channel_id=1, source_target_pairs={{0,4},{4,0},{8,12},{12,8},{1,5},{5,1},{9,13},{13,9},{2,6},{6,2},{1... | collective-permute-start | bytes 442376 | tf_op jit(solution)/shard_map/ppermute | solution.py:22
  11.9 1.5 %collective-permute-start.4 = (bf16[96,768]{1,0:T(8,128)(2,1)S(1)}, bf16[96,768]{1,0:T(8,128)(2,1)S(1)}, u32[]{:S(2)}, u32[]{:S(2)}) collective-permute-start(bf16[96,768]{1,0:T(8,128)(2,1)S(1)} %collective-permute-done.2.refs_0_), channel_id=1, source_target_pairs={{0,8},{4,12},{8,0},{12,4},{1,9},{5,13},{9,1},{13,5},{2,10},{6,14},... | collective-permute-start | bytes 442376 | tf_op jit(solution)/shard_map/ppermute | solution.py:22
  13.9 4.7 %fetch.1.refs_9_ = bf16[3072,2048]{1,0:T(8,128)(2,1)S(1)} custom-call(bf16[3072,2048]{1,0:T(8,128)(2,1)} %bitcast.38), custom_call_target="tpu_custom_call" | custom-call | bytes 12582912 | tf_op jit(solution)/shard_map/fetch/pallas_call | solution.py:65
  18.8 1.2 collective-permute-done.1
  20.0 1.6 %collective-permute-start.9 = (bf16[192,768]{1,0:T(8,128)(2,1)S(1)}, bf16[192,768]{1,0:T(8,128)(2,1)S(1)}, u32[]{:S(2)}, u32[]{:S(2)}) collective-permute-start(bf16[192,768]{1,0:T(8,128)(2,1)S(1)} %constant_dynamic-update-slice_fusion.refs_1_), channel_id=1, source_target_pairs={{0,8},{4,12},{8,0},{12,4},{1,9},{5,13},{9,1},{13,5},{2,10},{6,14},... | collective-permute-start | bytes 884744 | tf_op jit(solution)/shard_map/ppermute | solution.py:22
  21.6 1.5 collective-permute-start.11
  23.4 1.3 collective-permute-start.6
  25.4 1.6 %collective-permute-start.8 = (bf16[96,768]{1,0:T(8,128)(2,1)S(1)}, bf16[96,768]{1,0:T(8,128)(2,1)S(1)}, u32[]{:S(2)}, u32[]{:S(2)}) collective-permute-start(bf16[96,768]{1,0:T(8,128)(2,1)S(1)} %get-tuple-element.94), channel_id=1, source_target_pairs={{0,3},{1,2},{2,1},{3,0},{4,7},{5,6},{6,5},{7,4},{8,11},{9,10},{10,... | collective-permute-start | bytes 442376 | tf_op jit(solution)/shard_map/ppermute | solution.py:22
  27.9 1.6 %collective-permute-start.10 = (bf16[96,768]{1,0:T(8,128)(2,1)S(1)}, bf16[96,768]{1,0:T(8,128)(2,1)S(1)}, u32[]{:S(2)}, u32[]{:S(2)}) collective-permute-start(bf16[96,768]{1,0:T(8,128)(2,1)S(1)} %slice.108), channel_id=1, source_target_pairs={{0,4},{4,0},{8,12},{12,8},{1,5},{5,1},{9,13},{13,9},{2,6},{6,2},{1... | collective-permute-start | bytes 442376 | tf_op jit(solution)/shard_map/ppermute | solution.py:22
  29.6 1.4 collective-permute-start.12
  31.0 3.4 %collective-permute-done.7 = bf16[96,768]{1,0:T(8,128)(2,1)S(1)} collective-permute-done((bf16[96,768]{1,0:T(8,128)(2,1)S(1)}, bf16[96,768]{1,0:T(8,128)(2,1)S(1)}, u32[]{:S(2)}, u32[]{:S(2)}) %collective-permute-start.7) | collective-permute-done | bytes 147488 | tf_op jit(solution)/shard_map/ppermute | solution.py:22
  34.4 3.8 %collective-permute-done.8 = bf16[96,768]{1,0:T(8,128)(2,1)S(1)} collective-permute-done((bf16[96,768]{1,0:T(8,128)(2,1)S(1)}, bf16[96,768]{1,0:T(8,128)(2,1)S(1)}, u32[]{:S(2)}, u32[]{:S(2)}) %collective-permute-start.8) | collective-permute-done | bytes 147488 | tf_op jit(solution)/shard_map/ppermute | solution.py:22
  39.9 6.8 %pre_acts.2 = (f32[384,1024]{1,0:T(8,128)S(1)}, f32[384,1024]{1,0:T(8,128)S(1)}, bf16[384,2048]{1,0:T(8,128)(2,1)S(1)}) custom-call(s32[1]{0:T(128)} %bitcast.t_ref, bf16[96,3072]{1,0:T(8,128)(2,1)S(1)} %convolution_convert_fusion.own_ref, bf16[96,768]{1,0:T(8,128)(2,1)S(1)} %collective-permute-done.2.refs_0_, ...), custom_call_target="tpu_custom_call" | custom-call | flops 2415919104 | bytes 1048576 | tf_op jit(solution)/shard_map/pre_acts/pallas_call | solution.py:47
  46.7 2.9 %collective-permute-done.14.refs_1_ = bf16[288,768]{1,0:T(8,128)(2,1)S(1)} collective-permute-done((bf16[288,768]{1,0:T(8,128)(2,1)S(1)}, bf16[288,768]{1,0:T(8,128)(2,1)S(1)}, u32[]{:S(2)}, u32[]{:S(2)}) %collective-permute-start.14) | collective-permute-done | bytes 442400 | tf_op jit(solution)/shard_map/ppermute | solution.py:22
  49.7 6.6 %pre_acts.3 = (f32[384,1024]{1,0:T(8,128)S(1)}, f32[384,1024]{1,0:T(8,128)S(1)}, bf16[384,2048]{1,0:T(8,128)(2,1)S(1)}) custom-call(s32[1]{0:T(128)} %bitcast.t_ref, bf16[96,3072]{1,0:T(8,128)(2,1)S(1)} %convolution_convert_fusion.own_ref, bf16[96,768]{1,0:T(8,128)(2,1)S(1)} %collective-permute-done.2.refs_0_, ...), custom_call_target="tpu_custom_call" | custom-call | flops 2415919104 | bytes 1048576 | tf_op jit(solution)/shard_map/pre_acts/pallas_call | solution.py:47
  56.3 1.6 %collective-permute-start.19 = (bf16[288,768]{1,0:T(8,128)(2,1)S(1)}, bf16[288,768]{1,0:T(8,128)(2,1)S(1)}, u32[]{:S(2)}, u32[]{:S(2)}) collective-permute-start(bf16[288,768]{1,0:T(8,128)(2,1)S(1)} %constant_dynamic-update-slice_fusion.2.refs_0_), channel_id=1, source_target_pairs={{0,12},{4,8},{8,4},{12,0},{1,13},{5,9},{9,5},{13,1},{2,14},{6,10},... | collective-permute-start | bytes 1327112 | tf_op jit(solution)/shard_map/ppermute | solution.py:22
  57.9 1.8 %collective-permute-done.16.refs_5_.refs_7_ = bf16[384,2048]{1,0:T(8,128)(2,1)S(1)} collective-permute-done((bf16[384,2048]{1,0:T(8,128)(2,1)S(1)}, bf16[384,2048]{1,0:T(8,128)(2,1)S(1)}, u32[]{:S(2)}, u32[]{:S(2)}) %collective-permute-start.16) | collective-permute-done | bytes 1572896 | tf_op jit(solution)/shard_map/ppermute | solution.py:22
  59.7 3.7 %project_first.1 = (bf16[192,768]{1,0:T(8,128)(2,1)S(1)}, bf16[192,768]{1,0:T(8,128)(2,1)S(1)}, bf16[384,2048]{1,0:T(8,128)(2,1)S(1)}) custom-call(s32[1]{0:T(128)} %bitcast.t_ref, f32[384,1024]{1,0:T(8,128)S(1)} %get-tuple-element.50.refs_0_, f32[384,1024]{1,0:T(8,128)S(1)} %get-tuple-element.51.refs_1_, ...), custom_call_target="tpu_custom_call" | custom-call | flops 603979776 | bytes 1048576 | tf_op jit(solution)/shard_map/project_first/pallas_call | solution.py:47
  63.4 1.7 %collective-permute-start.17 = (bf16[192,768]{1,0:T(8,128)(2,1)S(1)}, bf16[192,768]{1,0:T(8,128)(2,1)S(1)}, u32[]{:S(2)}, u32[]{:S(2)}) collective-permute-start(bf16[192,768]{1,0:T(8,128)(2,1)S(1)} %get-tuple-element.58), channel_id=1, source_target_pairs={{0,4},{4,0},{8,12},{12,8},{1,5},{5,1},{9,13},{13,9},{2,6},{6,2},{1... | collective-permute-start | bytes 884744 | tf_op jit(solution)/shard_map/ppermute | solution.py:22
  65.9 5.4 %project_send.1.both_ref = f32[2,384,768]{2,1,0:T(8,128)S(1)} custom-call(s32[1]{0:T(128)} %bitcast.t_ref, bf16[384,2048]{1,0:T(8,128)(2,1)S(1)} %get-tuple-element.57.refs_0_, bf16[2048,3072]{1,0:T(8,128)(2,1)} %bitcast.29), custom_call_target="tpu_custom_call" | custom-call | flops 1207959552 | bytes 1048576 | tf_op jit(solution)/shard_map/project_send/pallas_call | solution.py:47
  71.3 4.7 %grad_hidden.3 = (f32[384,1024]{1,0:T(8,128)S(1)}, bf16[384,1024]{1,0:T(8,128)(2,1)S(1)}) custom-call(s32[1]{0:T(128)} %bitcast.t_ref, bf16[96,3072]{1,0:T(8,128)(2,1)S(1)} %fusion.own_ref, bf16[288,768]{1,0:T(8,128)(2,1)S(1)} %constant_dynamic-update-slice_fusion.2.refs_0_, bf16[288,768]{1,0:T(8,128)(2,1)S(1)} %collective-permute-done.14.refs_1_, ...), custom_call_target="tpu_custom_call" | custom-call | flops 1207959552 | bytes 1048576 | tf_op jit(solution)/shard_map/grad_hidden/pallas_call | solution.py:47
  76.3 4.7 %grad_hidden.2 = (f32[384,1024]{1,0:T(8,128)S(1)}, bf16[384,1024]{1,0:T(8,128)(2,1)S(1)}) custom-call(s32[1]{0:T(128)} %bitcast.t_ref, bf16[96,3072]{1,0:T(8,128)(2,1)S(1)} %fusion.own_ref, bf16[288,768]{1,0:T(8,128)(2,1)S(1)} %constant_dynamic-update-slice_fusion.2.refs_0_, bf16[288,768]{1,0:T(8,128)(2,1)S(1)} %collective-permute-done.14.refs_1_, ...), custom_call_target="tpu_custom_call" | custom-call | flops 1207959552 | bytes 1048576 | tf_op jit(solution)/shard_map/grad_hidden/pallas_call | solution.py:47
  81.5 1.3 collective-permute-start.24
  83.5 3.6 %project_keep.1 = f32[1,384,768]{2,1,0:T(8,128)S(1)} custom-call(s32[1]{0:T(128)} %bitcast.t_ref, bf16[384,2048]{1,0:T(8,128)(2,1)S(1)} %get-tuple-element.57.refs_0_, bf16[2048,3072]{1,0:T(8,128)(2,1)} %bitcast.32), custom_call_target="tpu_custom_call" | custom-call | flops 603979776 | bytes 1048576 | tf_op jit(solution)/shard_map/project_keep/pallas_call | solution.py:47
  87.2 5.6 %rows_first.1 = (bf16[192,768]{1,0:T(8,128)(2,1)S(1)}, bf16[192,768]{1,0:T(8,128)(2,1)S(1)}, bf16[384,2048]{1,0:T(8,128)(2,1)S(1)}, bf16[384,2048]{1,0:T(8,128)(2,1)S(1)}) custom-call(s32[1]{0:T(128)} %bitcast.t_ref, f32[384,1024]{1,0:T(8,128)S(1)} %get-tuple-element.50.refs_0_, f32[384,1024]{1,0:T(8,128)S(1)} %get-tuple-element.51.refs_1_, ...), custom_call_target="tpu_custom_call" | custom-call | flops 1207959552 | bytes 1048576 | tf_op jit(solution)/shard_map/rows_first/pallas_call | solution.py:47
  92.8 1.7 %collective-permute-start.22 = (bf16[192,768]{1,0:T(8,128)(2,1)S(1)}, bf16[192,768]{1,0:T(8,128)(2,1)S(1)}, u32[]{:S(2)}, u32[]{:S(2)}) collective-permute-start(bf16[192,768]{1,0:T(8,128)(2,1)S(1)} %get-tuple-element.71), channel_id=1, source_target_pairs={{0,4},{4,0},{8,12},{12,8},{1,5},{5,1},{9,13},{13,9},{2,6},{6,2},{1... | collective-permute-start | bytes 884744 | tf_op jit(solution)/shard_map/ppermute | solution.py:22
  94.9 8.6 %rows_send.1.both_ref = f32[2,384,768]{2,1,0:T(8,128)S(1)} custom-call(s32[1]{0:T(128)} %bitcast.t_ref, bf16[384,2048]{1,0:T(8,128)(2,1)S(1)} %get-tuple-element.69.refs_0_, bf16[384,2048]{1,0:T(8,128)(2,1)S(1)} %get-tuple-element.70.refs_1_, bf16[3072,2048]{1,0:T(8,128)(2,1)} %bitcast.40, bf16[3072,2048]{1,0:T(8,128)(2,1)} %bitcast.36), custom_call_target="tpu_custom_call" | custom-call | flops 2415919104 | bytes 1048576 | tf_op jit(solution)/shard_map/rows_send/pallas_call | solution.py:47
  103.5 1.0 collective-permute-done.23.low_ref
  105.1 1.6 %collective-permute-start.30 = (bf16[384,768]{1,0:T(8,128)(2,1)S(1)}, bf16[384,768]{1,0:T(8,128)(2,1)S(1)}, u32[]{:S(2)}, u32[]{:S(2)}) collective-permute-start(bf16[384,768]{1,0:T(8,128)(2,1)S(1)} %get-tuple-element.77), channel_id=1, source_target_pairs={{0,8},{4,12},{8,0},{12,4},{1,9},{5,13},{9,1},{13,5},{2,10},{6,14},... | collective-permute-start | bytes 1769480 | tf_op jit(solution)/shard_map/ppermute | solution.py:22
  107.1 1.0 collective-permute-start.27
  108.1 2.5 %collective-permute-start.28 = (bf16[96,768]{1,0:T(8,128)(2,1)S(1)}, bf16[96,768]{1,0:T(8,128)(2,1)S(1)}, u32[]{:S(2)}, u32[]{:S(2)}) collective-permute-start(bf16[96,768]{1,0:T(8,128)(2,1)S(1)} %get-tuple-element.90), channel_id=1, source_target_pairs={{0,3},{1,2},{2,1},{3,0},{4,7},{5,6},{6,5},{7,4},{8,11},{9,10},{10,... | collective-permute-start | bytes 442376 | tf_op jit(solution)/shard_map/ppermute | solution.py:22
  110.6 5.2 %rows_keep.1 = f32[1,384,768]{2,1,0:T(8,128)S(1)} custom-call(s32[1]{0:T(128)} %bitcast.t_ref, bf16[384,2048]{1,0:T(8,128)(2,1)S(1)} %get-tuple-element.69.refs_0_, bf16[384,2048]{1,0:T(8,128)(2,1)S(1)} %get-tuple-element.70.refs_1_, bf16[3072,2048]{1,0:T(8,128)(2,1)} %bitcast.41, bf16[3072,2048]{1,0:T(8,128)(2,1)} %bitcast.37), custom_call_target="tpu_custom_call" | custom-call | flops 1207959552 | bytes 1048576 | tf_op jit(solution)/shard_map/rows_keep/pallas_call | solution.py:47
  115.8 3.6 %collective-permute-done.29 = bf16[384,768]{1,0:T(8,128)(2,1)S(1)} collective-permute-done((bf16[384,768]{1,0:T(8,128)(2,1)S(1)}, bf16[384,768]{1,0:T(8,128)(2,1)S(1)}, u32[]{:S(2)}, u32[]{:S(2)}) %collective-permute-start.29) | collective-permute-done | bytes 589856 | tf_op jit(solution)/shard_map/ppermute | solution.py:22
  120.0 1.0 collective-permute-start.35
  121.0 2.5 %collective-permute-start.36 = (bf16[96,768]{1,0:T(8,128)(2,1)S(1)}, bf16[96,768]{1,0:T(8,128)(2,1)S(1)}, u32[]{:S(2)}, u32[]{:S(2)}) collective-permute-start(bf16[96,768]{1,0:T(8,128)(2,1)S(1)} %get-tuple-element.87), channel_id=1, source_target_pairs={{0,3},{1,2},{2,1},{3,0},{4,7},{5,6},{6,5},{7,4},{8,11},{9,10},{10,... | collective-permute-start | bytes 442376 | tf_op jit(solution)/shard_map/ppermute | solution.py:22
  123.5 3.3 %collective-permute-done.31 = bf16[96,768]{1,0:T(8,128)(2,1)S(1)} collective-permute-done((bf16[96,768]{1,0:T(8,128)(2,1)S(1)}, bf16[96,768]{1,0:T(8,128)(2,1)S(1)}, u32[]{:S(2)}, u32[]{:S(2)}) %collective-permute-start.31) | collective-permute-done | bytes 147488 | tf_op jit(solution)/shard_map/ppermute | solution.py:22
  127.6 1.5 collective-permute-start.32
  129.6 1.6 %collective-permute-start.34 = (bf16[128,768]{1,0:T(8,128)(2,1)S(1)}, bf16[128,768]{1,0:T(8,128)(2,1)S(1)}, u32[]{:S(2)}, u32[]{:S(2)}) collective-permute-start(bf16[128,768]{1,0:T(8,128)(2,1)S(1)} %get-tuple-element.85.refs_0_), channel_id=1, source_target_pairs={{0,12},{4,8},{8,4},{12,0},{1,13},{5,9},{9,5},{13,1},{2,14},{6,10},... | collective-permute-start | bytes 589832 | tf_op jit(solution)/shard_map/ppermute | solution.py:22
  131.2 3.4 %collective-permute-done.36 = bf16[96,768]{1,0:T(8,128)(2,1)S(1)} collective-permute-done((bf16[96,768]{1,0:T(8,128)(2,1)S(1)}, bf16[96,768]{1,0:T(8,128)(2,1)S(1)}, u32[]{:S(2)}, u32[]{:S(2)}) %collective-permute-start.36) | collective-permute-done | bytes 147488 | tf_op jit(solution)/shard_map/ppermute | solution.py:22
  135.3 1.3 collective-permute-start.37
  137.5 1.4 collective-permute-start.39
  138.9 1.1 collective-permute-done.40
  140.1 1.2 collective-permute-start.41
  141.3 3.9 %collective-permute-done.41 = f32[2,128]{1,0:T(2,128)S(1)} collective-permute-done((f32[2,128]{1,0:T(2,128)S(1)}, f32[2,128]{1,0:T(2,128)S(1)}, u32[]{:S(2)}, u32[]{:S(2)}) %collective-permute-start.41) | collective-permute-done | bytes 1056 | tf_op jit(solution)/shard_map/ppermute | solution.py:22
  145.2 1.3 collective-permute-start.42
  (106 shorter events, 17.7 us)
Async XLA Ops:
  0.6 13.2 %copy-start.4 = (f32[128,2]{0,1:T(2,128)S(1)}, f32[128,2]{0,1:T(2,128)}, u32[]{:S(2)}) copy-start(f32[128,2]{0,1:T(2,128)} %param.9) | copy-start | bytes 3076
  3.6 6.8 %collective-permute-start.2 = (bf16[96,768]{1,0:T(8,128)(2,1)S(1)}, bf16[96,768]{1,0:T(8,128)(2,1)S(1)}, u32[]{:S(2)}, u32[]{:S(2)}) collective-permute-start(bf16[96,768]{1,0:T(8,128)(2,1)S(1)} %get-tuple-element.97), channel_id=1, source_target_pairs={{0,1},{1,0},{2,3},{3,2},{4,5},{5,4},{6,7},{7,6},{8,9},{9,8},{10,11... | collective-permute-start | bytes 442376 | tf_op jit(solution)/shard_map/ppermute | solution.py:22
  5.2 13.6 %collective-permute-start = (bf16[96,768]{1,0:T(8,128)(2,1)S(1)}, bf16[96,768]{1,0:T(8,128)(2,1)S(1)}, u32[]{:S(2)}, u32[]{:S(2)}) collective-permute-start(bf16[96,768]{1,0:T(8,128)(2,1)S(1)} %get-tuple-element.99), channel_id=1, source_target_pairs={{0,2},{1,3},{2,0},{3,1},{4,6},{5,7},{6,4},{7,5},{8,10},{9,11},{10,... | collective-permute-start | bytes 442376 | tf_op jit(solution)/shard_map/ppermute | solution.py:22
  5.5 14.4 %collective-permute-start.1 = (bf16[96,768]{1,0:T(8,128)(2,1)S(1)}, bf16[96,768]{1,0:T(8,128)(2,1)S(1)}, u32[]{:S(2)}, u32[]{:S(2)}) collective-permute-start(bf16[96,768]{1,0:T(8,128)(2,1)S(1)} %get-tuple-element.98), channel_id=1, source_target_pairs={{0,3},{1,2},{2,1},{3,0},{4,7},{5,6},{6,5},{7,4},{8,11},{9,10},{10,... | collective-permute-start | bytes 442376 | tf_op jit(solution)/shard_map/ppermute | solution.py:22
  10.4 9.6 %collective-permute-start.3 = (bf16[96,768]{1,0:T(8,128)(2,1)S(1)}, bf16[96,768]{1,0:T(8,128)(2,1)S(1)}, u32[]{:S(2)}, u32[]{:S(2)}) collective-permute-start(bf16[96,768]{1,0:T(8,128)(2,1)S(1)} %collective-permute-done.2.refs_0_), channel_id=1, source_target_pairs={{0,4},{4,0},{8,12},{12,8},{1,5},{5,1},{9,13},{13,9},{2,6},{6,2},{1... | collective-permute-start | bytes 442376 | tf_op jit(solution)/shard_map/ppermute | solution.py:22
  11.9 8.1 %collective-permute-start.4 = (bf16[96,768]{1,0:T(8,128)(2,1)S(1)}, bf16[96,768]{1,0:T(8,128)(2,1)S(1)}, u32[]{:S(2)}, u32[]{:S(2)}) collective-permute-start(bf16[96,768]{1,0:T(8,128)(2,1)S(1)} %collective-permute-done.2.refs_0_), channel_id=1, source_target_pairs={{0,8},{4,12},{8,0},{12,4},{1,9},{5,13},{9,1},{13,5},{2,10},{6,14},... | collective-permute-start | bytes 442376 | tf_op jit(solution)/shard_map/ppermute | solution.py:22
  13.4 6.6 %collective-permute-start.5 = (bf16[96,768]{1,0:T(8,128)(2,1)S(1)}, bf16[96,768]{1,0:T(8,128)(2,1)S(1)}, u32[]{:S(2)}, u32[]{:S(2)}) collective-permute-start(bf16[96,768]{1,0:T(8,128)(2,1)S(1)} %collective-permute-done.2.refs_0_), channel_id=1, source_target_pairs={{0,12},{4,8},{8,4},{12,0},{1,13},{5,9},{9,5},{13,1},{2,14},{6,10},... | collective-permute-start | bytes 442376 | tf_op jit(solution)/shard_map/ppermute | solution.py:22
  13.9 9.2 %copy-start.2 = (bf16[128,3072]{1,0:T(8,128)(2,1)S(1)}, bf16[128,3072]{1,0:T(8,128)(2,1)}, u32[]{:S(2)}) copy-start(bf16[128,3072]{1,0:T(8,128)(2,1)} %param.13) | copy-start | bytes 2359300
  18.7 39.2 %copy-start.3 = (f32[384]{0:T(512)}, f32[384]{0:T(512)S(1)}, u32[]{:S(2)}) copy-start(f32[384]{0:T(512)S(1)} %add_reduce_fusion) | copy-start | bytes 4612
  20.0 7.9 %collective-permute-start.9 = (bf16[192,768]{1,0:T(8,128)(2,1)S(1)}, bf16[192,768]{1,0:T(8,128)(2,1)S(1)}, u32[]{:S(2)}, u32[]{:S(2)}) collective-permute-start(bf16[192,768]{1,0:T(8,128)(2,1)S(1)} %constant_dynamic-update-slice_fusion.refs_1_), channel_id=1, source_target_pairs={{0,8},{4,12},{8,0},{12,4},{1,9},{5,13},{9,1},{13,5},{2,10},{6,14},... | collective-permute-start | bytes 884744 | tf_op jit(solution)/shard_map/ppermute | solution.py:22
  21.6 8.0 %collective-permute-start.11 = (bf16[192,768]{1,0:T(8,128)(2,1)S(1)}, bf16[192,768]{1,0:T(8,128)(2,1)S(1)}, u32[]{:S(2)}, u32[]{:S(2)}) collective-permute-start(bf16[192,768]{1,0:T(8,128)(2,1)S(1)} %constant_dynamic-update-slice_fusion.refs_1_), channel_id=1, source_target_pairs={{0,4},{4,0},{8,12},{12,8},{1,5},{5,1},{9,13},{13,9},{2,6},{6,2},{1... | collective-permute-start | bytes 884744 | tf_op jit(solution)/shard_map/ppermute | solution.py:22
  23.4 7.6 %collective-permute-start.6 = (bf16[96,768]{1,0:T(8,128)(2,1)S(1)}, bf16[96,768]{1,0:T(8,128)(2,1)S(1)}, u32[]{:S(2)}, u32[]{:S(2)}) collective-permute-start(bf16[96,768]{1,0:T(8,128)(2,1)S(1)} %get-tuple-element.96), channel_id=1, source_target_pairs={{0,1},{1,0},{2,3},{3,2},{4,5},{5,4},{6,7},{7,6},{8,9},{9,8},{10,11... | collective-permute-start | bytes 442376 | tf_op jit(solution)/shard_map/ppermute | solution.py:22
  24.6 9.7 %collective-permute-start.7 = (bf16[96,768]{1,0:T(8,128)(2,1)S(1)}, bf16[96,768]{1,0:T(8,128)(2,1)S(1)}, u32[]{:S(2)}, u32[]{:S(2)}) collective-permute-start(bf16[96,768]{1,0:T(8,128)(2,1)S(1)} %get-tuple-element.95), channel_id=1, source_target_pairs={{0,2},{1,3},{2,0},{3,1},{4,6},{5,7},{6,4},{7,5},{8,10},{9,11},{10,... | collective-permute-start | bytes 442376 | tf_op jit(solution)/shard_map/ppermute | solution.py:22
  25.4 12.9 %collective-permute-start.8 = (bf16[96,768]{1,0:T(8,128)(2,1)S(1)}, bf16[96,768]{1,0:T(8,128)(2,1)S(1)}, u32[]{:S(2)}, u32[]{:S(2)}) collective-permute-start(bf16[96,768]{1,0:T(8,128)(2,1)S(1)} %get-tuple-element.94), channel_id=1, source_target_pairs={{0,3},{1,2},{2,1},{3,0},{4,7},{5,6},{6,5},{7,4},{8,11},{9,10},{10,... | collective-permute-start | bytes 442376 | tf_op jit(solution)/shard_map/ppermute | solution.py:22
  27.9 10.4 %collective-permute-start.10 = (bf16[96,768]{1,0:T(8,128)(2,1)S(1)}, bf16[96,768]{1,0:T(8,128)(2,1)S(1)}, u32[]{:S(2)}, u32[]{:S(2)}) collective-permute-start(bf16[96,768]{1,0:T(8,128)(2,1)S(1)} %slice.108), channel_id=1, source_target_pairs={{0,4},{4,0},{8,12},{12,8},{1,5},{5,1},{9,13},{13,9},{2,6},{6,2},{1... | collective-permute-start | bytes 442376 | tf_op jit(solution)/shard_map/ppermute | solution.py:22
  29.6 8.6 %collective-permute-start.12 = (bf16[96,768]{1,0:T(8,128)(2,1)S(1)}, bf16[96,768]{1,0:T(8,128)(2,1)S(1)}, u32[]{:S(2)}, u32[]{:S(2)}) collective-permute-start(bf16[96,768]{1,0:T(8,128)(2,1)S(1)} %slice.109), channel_id=1, source_target_pairs={{0,8},{4,12},{8,0},{12,4},{1,9},{5,13},{9,1},{13,5},{2,10},{6,14},... | collective-permute-start | bytes 442376 | tf_op jit(solution)/shard_map/ppermute | solution.py:22
  38.3 11.3 %collective-permute-start.14 = (bf16[288,768]{1,0:T(8,128)(2,1)S(1)}, bf16[288,768]{1,0:T(8,128)(2,1)S(1)}, u32[]{:S(2)}, u32[]{:S(2)}) collective-permute-start(bf16[288,768]{1,0:T(8,128)(2,1)S(1)} %constant_dynamic-update-slice_fusion.2.refs_0_), channel_id=1, source_target_pairs={{0,4},{4,0},{8,12},{12,8},{1,5},{5,1},{9,13},{13,9},{2,6},{6,2},{1... | collective-permute-start | bytes 1327112 | tf_op jit(solution)/shard_map/ppermute | solution.py:22
  38.9 10.8 %collective-permute-start.15 = (bf16[288,768]{1,0:T(8,128)(2,1)S(1)}, bf16[288,768]{1,0:T(8,128)(2,1)S(1)}, u32[]{:S(2)}, u32[]{:S(2)}) collective-permute-start(bf16[288,768]{1,0:T(8,128)(2,1)S(1)} %constant_dynamic-update-slice_fusion.2.refs_0_), channel_id=1, source_target_pairs={{0,8},{4,12},{8,0},{12,4},{1,9},{5,13},{9,1},{13,5},{2,10},{6,14},... | collective-permute-start | bytes 1327112 | tf_op jit(solution)/shard_map/ppermute | solution.py:22
  46.7 11.3 %collective-permute-start.13 = (bf16[384,2048]{1,0:T(8,128)(2,1)S(1)}, bf16[384,2048]{1,0:T(8,128)(2,1)S(1)}, u32[]{:S(2)}, u32[]{:S(2)}) collective-permute-start(bf16[384,2048]{1,0:T(8,128)(2,1)S(1)} %get-tuple-element.52), channel_id=1, source_target_pairs={{0,16},{16,0},{1,17},{17,1},{2,18},{18,2},{3,19},{19,3},{4,20},{20... | collective-permute-start | bytes 4718600 | tf_op jit(solution)/shard_map/ppermute | solution.py:22
  56.3 3.5 %collective-permute-start.16 = (bf16[384,2048]{1,0:T(8,128)(2,1)S(1)}, bf16[384,2048]{1,0:T(8,128)(2,1)S(1)}, u32[]{:S(2)}, u32[]{:S(2)}) collective-permute-start(bf16[384,2048]{1,0:T(8,128)(2,1)S(1)} %get-tuple-element.56), channel_id=1, source_target_pairs={{0,16},{16,0},{1,17},{17,1},{2,18},{18,2},{3,19},{19,3},{4,20},{20... | collective-permute-start | bytes 4718600 | tf_op jit(solution)/shard_map/ppermute | solution.py:22
  56.3 14.9 %collective-permute-start.19 = (bf16[288,768]{1,0:T(8,128)(2,1)S(1)}, bf16[288,768]{1,0:T(8,128)(2,1)S(1)}, u32[]{:S(2)}, u32[]{:S(2)}) collective-permute-start(bf16[288,768]{1,0:T(8,128)(2,1)S(1)} %constant_dynamic-update-slice_fusion.2.refs_0_), channel_id=1, source_target_pairs={{0,12},{4,8},{8,4},{12,0},{1,13},{5,9},{9,5},{13,1},{2,14},{6,10},... | collective-permute-start | bytes 1327112 | tf_op jit(solution)/shard_map/ppermute | solution.py:22
  59.7 5.8 %slice-start = ((f32[384]{0:T(512)}), f32[96]{0:T(128)S(1)}, s32[]{:S(2)}) async-start(f32[384]{0:T(512)} %copy-done.3), calls=%async_computation | async-start | bytes 1024 | tf_op jit(solution)/shard_map/slice | solution.py:419
  63.4 12.7 %collective-permute-start.17 = (bf16[192,768]{1,0:T(8,128)(2,1)S(1)}, bf16[192,768]{1,0:T(8,128)(2,1)S(1)}, u32[]{:S(2)}, u32[]{:S(2)}) collective-permute-start(bf16[192,768]{1,0:T(8,128)(2,1)S(1)} %get-tuple-element.58), channel_id=1, source_target_pairs={{0,4},{4,0},{8,12},{12,8},{1,5},{5,1},{9,13},{13,9},{2,6},{6,2},{1... | collective-permute-start | bytes 884744 | tf_op jit(solution)/shard_map/ppermute | solution.py:22
  65.2 11.0 %collective-permute-start.18 = (bf16[192,768]{1,0:T(8,128)(2,1)S(1)}, bf16[192,768]{1,0:T(8,128)(2,1)S(1)}, u32[]{:S(2)}, u32[]{:S(2)}) collective-permute-start(bf16[192,768]{1,0:T(8,128)(2,1)S(1)} %get-tuple-element.59), channel_id=1, source_target_pairs={{0,8},{4,12},{8,0},{12,4},{1,9},{5,13},{9,1},{13,5},{2,10},{6,14},... | collective-permute-start | bytes 884744 | tf_op jit(solution)/shard_map/ppermute | solution.py:22
  76.0 11.2 %collective-permute-start.20 = (bf16[384,1024]{1,0:T(8,128)(2,1)S(1)}, bf16[384,1024]{1,0:T(8,128)(2,1)S(1)}, u32[]{:S(2)}, u32[]{:S(2)}) collective-permute-start(bf16[384,1024]{1,0:T(8,128)(2,1)S(1)} %get-tuple-element.67), channel_id=1, source_target_pairs={{0,16},{16,0},{1,17},{17,1},{2,18},{18,2},{3,19},{19,3},{4,20},{20... | collective-permute-start | bytes 2359304 | tf_op jit(solution)/shard_map/ppermute | solution.py:22
  81.0 6.2 %collective-permute-start.21 = (bf16[384,1024]{1,0:T(8,128)(2,1)S(1)}, bf16[384,1024]{1,0:T(8,128)(2,1)S(1)}, u32[]{:S(2)}, u32[]{:S(2)}) collective-permute-start(bf16[384,1024]{1,0:T(8,128)(2,1)S(1)} %get-tuple-element.62), channel_id=1, source_target_pairs={{0,16},{16,0},{1,17},{17,1},{2,18},{18,2},{3,19},{19,3},{4,20},{20... | collective-permute-start | bytes 2359304 | tf_op jit(solution)/shard_map/ppermute | solution.py:22
  81.5 25.2 %collective-permute-start.24 = (bf16[384,768]{1,0:T(8,128)(2,1)S(1)}, bf16[384,768]{1,0:T(8,128)(2,1)S(1)}, u32[]{:S(2)}, u32[]{:S(2)}) collective-permute-start(bf16[384,768]{1,0:T(8,128)(2,1)S(1)} %get-tuple-element.60), channel_id=1, source_target_pairs={{0,4},{4,0},{8,12},{12,8},{1,5},{5,1},{9,13},{13,9},{2,6},{6,2},{1... | collective-permute-start | bytes 1769480 | tf_op jit(solution)/shard_map/ppermute | solution.py:22
  82.8 23.9 %collective-permute-start.25 = (bf16[384,768]{1,0:T(8,128)(2,1)S(1)}, bf16[384,768]{1,0:T(8,128)(2,1)S(1)}, u32[]{:S(2)}, u32[]{:S(2)}) collective-permute-start(bf16[384,768]{1,0:T(8,128)(2,1)S(1)} %get-tuple-element.75), channel_id=1, source_target_pairs={{0,8},{4,12},{8,0},{12,4},{1,9},{5,13},{9,1},{13,5},{2,10},{6,14},... | collective-permute-start | bytes 1769480 | tf_op jit(solution)/shard_map/ppermute | solution.py:22
  92.8 10.7 %collective-permute-start.22 = (bf16[192,768]{1,0:T(8,128)(2,1)S(1)}, bf16[192,768]{1,0:T(8,128)(2,1)S(1)}, u32[]{:S(2)}, u32[]{:S(2)}) collective-permute-start(bf16[192,768]{1,0:T(8,128)(2,1)S(1)} %get-tuple-element.71), channel_id=1, source_target_pairs={{0,4},{4,0},{8,12},{12,8},{1,5},{5,1},{9,13},{13,9},{2,6},{6,2},{1... | collective-permute-start | bytes 884744 | tf_op jit(solution)/shard_map/ppermute | solution.py:22
  94.5 10.0 %collective-permute-start.23 = (bf16[192,768]{1,0:T(8,128)(2,1)S(1)}, bf16[192,768]{1,0:T(8,128)(2,1)S(1)}, u32[]{:S(2)}, u32[]{:S(2)}) collective-permute-start(bf16[192,768]{1,0:T(8,128)(2,1)S(1)} %get-tuple-element.72), channel_id=1, source_target_pairs={{0,8},{4,12},{8,0},{12,4},{1,9},{5,13},{9,1},{13,5},{2,10},{6,14},... | collective-permute-start | bytes 884744 | tf_op jit(solution)/shard_map/ppermute | solution.py:22
  104.7 14.6 %collective-permute-start.29 = (bf16[384,768]{1,0:T(8,128)(2,1)S(1)}, bf16[384,768]{1,0:T(8,128)(2,1)S(1)}, u32[]{:S(2)}, u32[]{:S(2)}) collective-permute-start(bf16[384,768]{1,0:T(8,128)(2,1)S(1)} %get-tuple-element.73), channel_id=1, source_target_pairs={{0,4},{4,0},{8,12},{12,8},{1,5},{5,1},{9,13},{13,9},{2,6},{6,2},{1... | collective-permute-start | bytes 1769480 | tf_op jit(solution)/shard_map/ppermute | solution.py:22
  105.1 14.6 %collective-permute-start.30 = (bf16[384,768]{1,0:T(8,128)(2,1)S(1)}, bf16[384,768]{1,0:T(8,128)(2,1)S(1)}, u32[]{:S(2)}, u32[]{:S(2)}) collective-permute-start(bf16[384,768]{1,0:T(8,128)(2,1)S(1)} %get-tuple-element.77), channel_id=1, source_target_pairs={{0,8},{4,12},{8,0},{12,4},{1,9},{5,13},{9,1},{13,5},{2,10},{6,14},... | collective-permute-start | bytes 1769480 | tf_op jit(solution)/shard_map/ppermute | solution.py:22
  107.0 14.0 %collective-permute-start.26 = (bf16[96,768]{1,0:T(8,128)(2,1)S(1)}, bf16[96,768]{1,0:T(8,128)(2,1)S(1)}, u32[]{:S(2)}, u32[]{:S(2)}) collective-permute-start(bf16[96,768]{1,0:T(8,128)(2,1)S(1)} %get-tuple-element.92), channel_id=1, source_target_pairs={{0,1},{1,0},{2,3},{3,2},{4,5},{5,4},{6,7},{7,6},{8,9},{9,8},{10,11... | collective-permute-start | bytes 442376 | tf_op jit(solution)/shard_map/ppermute | solution.py:22
  107.1 16.4 %collective-permute-start.27 = (bf16[96,768]{1,0:T(8,128)(2,1)S(1)}, bf16[96,768]{1,0:T(8,128)(2,1)S(1)}, u32[]{:S(2)}, u32[]{:S(2)}) collective-permute-start(bf16[96,768]{1,0:T(8,128)(2,1)S(1)} %get-tuple-element.91), channel_id=1, source_target_pairs={{0,2},{1,3},{2,0},{3,1},{4,6},{5,7},{6,4},{7,5},{8,10},{9,11},{10,... | collective-permute-start | bytes 442376 | tf_op jit(solution)/shard_map/ppermute | solution.py:22
  108.1 15.5 %collective-permute-start.28 = (bf16[96,768]{1,0:T(8,128)(2,1)S(1)}, bf16[96,768]{1,0:T(8,128)(2,1)S(1)}, u32[]{:S(2)}, u32[]{:S(2)}) collective-permute-start(bf16[96,768]{1,0:T(8,128)(2,1)S(1)} %get-tuple-element.90), channel_id=1, source_target_pairs={{0,3},{1,2},{2,1},{3,0},{4,7},{5,6},{6,5},{7,4},{8,11},{9,10},{10,... | collective-permute-start | bytes 442376 | tf_op jit(solution)/shard_map/ppermute | solution.py:22
  120.0 6.9 %collective-permute-start.31 = (bf16[96,768]{1,0:T(8,128)(2,1)S(1)}, bf16[96,768]{1,0:T(8,128)(2,1)S(1)}, u32[]{:S(2)}, u32[]{:S(2)}) collective-permute-start(bf16[96,768]{1,0:T(8,128)(2,1)S(1)} %get-tuple-element.89), channel_id=1, source_target_pairs={{0,1},{1,0},{2,3},{3,2},{4,5},{5,4},{6,7},{7,6},{8,9},{9,8},{10,11... | collective-permute-start | bytes 442376 | tf_op jit(solution)/shard_map/ppermute | solution.py:22
  120.0 11.2 %collective-permute-start.35 = (bf16[96,768]{1,0:T(8,128)(2,1)S(1)}, bf16[96,768]{1,0:T(8,128)(2,1)S(1)}, u32[]{:S(2)}, u32[]{:S(2)}) collective-permute-start(bf16[96,768]{1,0:T(8,128)(2,1)S(1)} %get-tuple-element.88), channel_id=1, source_target_pairs={{0,2},{1,3},{2,0},{3,1},{4,6},{5,7},{6,4},{7,5},{8,10},{9,11},{10,... | collective-permute-start | bytes 442376 | tf_op jit(solution)/shard_map/ppermute | solution.py:22
  121.0 13.6 %collective-permute-start.36 = (bf16[96,768]{1,0:T(8,128)(2,1)S(1)}, bf16[96,768]{1,0:T(8,128)(2,1)S(1)}, u32[]{:S(2)}, u32[]{:S(2)}) collective-permute-start(bf16[96,768]{1,0:T(8,128)(2,1)S(1)} %get-tuple-element.87), channel_id=1, source_target_pairs={{0,3},{1,2},{2,1},{3,0},{4,7},{5,6},{6,5},{7,4},{8,11},{9,10},{10,... | collective-permute-start | bytes 442376 | tf_op jit(solution)/shard_map/ppermute | solution.py:22
  127.6 9.8 %collective-permute-start.32 = (bf16[128,768]{1,0:T(8,128)(2,1)S(1)}, bf16[128,768]{1,0:T(8,128)(2,1)S(1)}, u32[]{:S(2)}, u32[]{:S(2)}) collective-permute-start(bf16[128,768]{1,0:T(8,128)(2,1)S(1)} %get-tuple-element.85.refs_0_), channel_id=1, source_target_pairs={{0,4},{4,0},{8,12},{12,8},{1,5},{5,1},{9,13},{13,9},{2,6},{6,2},{1... | collective-permute-start | bytes 589832 | tf_op jit(solution)/shard_map/ppermute | solution.py:22
  129.1 9.7 %collective-permute-start.33 = (bf16[128,768]{1,0:T(8,128)(2,1)S(1)}, bf16[128,768]{1,0:T(8,128)(2,1)S(1)}, u32[]{:S(2)}, u32[]{:S(2)}) collective-permute-start(bf16[128,768]{1,0:T(8,128)(2,1)S(1)} %get-tuple-element.85.refs_0_), channel_id=1, source_target_pairs={{0,8},{4,12},{8,0},{12,4},{1,9},{5,13},{9,1},{13,5},{2,10},{6,14},... | collective-permute-start | bytes 589832 | tf_op jit(solution)/shard_map/ppermute | solution.py:22
  129.6 16.9 %collective-permute-start.34 = (bf16[128,768]{1,0:T(8,128)(2,1)S(1)}, bf16[128,768]{1,0:T(8,128)(2,1)S(1)}, u32[]{:S(2)}, u32[]{:S(2)}) collective-permute-start(bf16[128,768]{1,0:T(8,128)(2,1)S(1)} %get-tuple-element.85.refs_0_), channel_id=1, source_target_pairs={{0,12},{4,8},{8,4},{12,0},{1,13},{5,9},{9,5},{13,1},{2,14},{6,10},... | collective-permute-start | bytes 589832 | tf_op jit(solution)/shard_map/ppermute | solution.py:22
  135.3 12.2 %collective-permute-start.37 = (bf16[128,768]{1,0:T(8,128)(2,1)S(1)}, bf16[128,768]{1,0:T(8,128)(2,1)S(1)}, u32[]{:S(2)}, u32[]{:S(2)}) collective-permute-start(bf16[128,768]{1,0:T(8,128)(2,1)S(1)} %fusion.4.refs_0_), channel_id=1, source_target_pairs={{0,4},{4,0},{8,12},{12,8},{1,5},{5,1},{9,13},{13,9},{2,6},{6,2},{1... | collective-permute-start | bytes 589832 | tf_op jit(solution)/shard_map/ppermute | solution.py:22
  136.5 10.9 %collective-permute-start.38 = (bf16[128,768]{1,0:T(8,128)(2,1)S(1)}, bf16[128,768]{1,0:T(8,128)(2,1)S(1)}, u32[]{:S(2)}, u32[]{:S(2)}) collective-permute-start(bf16[128,768]{1,0:T(8,128)(2,1)S(1)} %fusion.4.refs_0_), channel_id=1, source_target_pairs={{0,8},{4,12},{8,0},{12,4},{1,9},{5,13},{9,1},{13,5},{2,10},{6,14},... | collective-permute-start | bytes 589832 | tf_op jit(solution)/shard_map/ppermute | solution.py:22
  137.5 10.0 %collective-permute-start.39 = (bf16[128,768]{1,0:T(8,128)(2,1)S(1)}, bf16[128,768]{1,0:T(8,128)(2,1)S(1)}, u32[]{:S(2)}, u32[]{:S(2)}) collective-permute-start(bf16[128,768]{1,0:T(8,128)(2,1)S(1)} %fusion.4.refs_0_), channel_id=1, source_target_pairs={{0,12},{4,8},{8,4},{12,0},{1,13},{5,9},{9,5},{13,1},{2,14},{6,10},... | collective-permute-start | bytes 589832 | tf_op jit(solution)/shard_map/ppermute | solution.py:22
  138.9 1.2 collective-permute-start.40
  140.1 5.1 %collective-permute-start.41 = (f32[2,128]{1,0:T(2,128)S(1)}, f32[2,128]{1,0:T(2,128)S(1)}, u32[]{:S(2)}, u32[]{:S(2)}) collective-permute-start(f32[2,128]{1,0:T(2,128)S(1)} %add.49), channel_id=1, source_target_pairs={{0,4},{4,0},{8,12},{12,8},{1,5},{5,1},{9,13},{13,9},{2,6},{6,2},{1... | collective-permute-start | bytes 3080 | tf_op jit(solution)/shard_map/ppermute | solution.py:22
  145.2 3.6 %collective-permute-start.42 = (f32[2,128]{1,0:T(2,128)S(1)}, f32[2,128]{1,0:T(2,128)S(1)}, u32[]{:S(2)}, u32[]{:S(2)}) collective-permute-start(f32[2,128]{1,0:T(2,128)S(1)} %add.50), channel_id=1, source_target_pairs={{0,8},{4,12},{8,0},{12,4},{1,9},{5,13},{9,1},{13,5},{2,10},{6,14},... | collective-permute-start | bytes 3080 | tf_op jit(solution)/shard_map/ppermute | solution.py:22
  146.5 2.8 %copy-start.1 = (bf16[128,3072]{1,0:T(8,128)(2,1)S(1)}, bf16[128,3072]{1,0:T(8,128)(2,1)}, u32[]{:S(2)}) copy-start(bf16[128,3072]{1,0:T(8,128)(2,1)} %param.7) | copy-start | bytes 2359300
  (1 other events, 2.6 us)

commit v8 on v7

--- a/solution.py
+++ b/solution.py
@@ -190,8 +190,8 @@
             pltpu.VMEM((steps, BLOCK, depth), BF),
             pltpu.SemaphoreType.DMA((steps,)),
         ],
-        2 * rows * depth * (stop - start),
-        12,
+        4 * rows * depth * (stop - start),
+        18,
         "grad_hidden",
         far=1,
     )
@@ -226,11 +226,14 @@
 
 def grad_strips(ins, acts):
     gg_ref, gu_ref = acts
+    share = len(ins) // 5
+    ins, grads = ins[: 3 * share], ins[3 * share :]
 
     def body(here):
         at = 0
-        for g in range(0, len(ins), 5):
-            gate_o, up_o, both_r, gh_o, gh_r = ins[g : g + 5]
+        for g in range(share):
+            gate_o, up_o, both_r = ins[3 * g : 3 * g + 3]
+            gh_o, gh_r = grads[2 * g : 2 * g + 2]
             width = gate_o.shape[1]
             cols = slice(at, at + width)
             gate = gate_o[here, :] + both_r[here, :width].astype(F32)
@@ -239,7 +242,7 @@
             s = jax.nn.sigmoid(gate)
             gg_ref[here, cols] = (grad * up * (s * (1.0 + gate * (1.0 - s)))).astype(BF)
             gu_ref[here, cols] = (grad * (gate * s)).astype(BF)
-            at += gate_o.shape[1]
+            at += width
 
     strips(gg_ref.shape[0], body)
 
@@ -293,31 +296,40 @@
             store(piece, pl.ds(off, BLOCK), total)
 
 
-def first_piece(t, n, make, nn, ins, mats, name):
-    stream = Stream(mats, n, nn, 1)
+def first_piece(t, n, make, nn, ins, mats, others, name):
+    stream = Stream(mats, n, nn, 1 + len(others))
     rows = ins[0].shape[0]
     half, quarter, hidden = rows // 2, stream.quarter, stream.hidden
 
     def kernel(t_ref, *refs):
         parts, refs = refs[: len(ins)], refs[len(ins) :]
         weights, refs = refs[: len(mats)], refs[len(mats) :]
-        halves, acts, scratch = refs[:2], refs[2 : 2 + len(mats)], refs[2 + len(mats) :]
-        stream.start(weights, [(t_ref[0] ^ 3) * quarter], *scratch)
+        halves, acts, refs = refs[:2], refs[2 : 2 + len(mats)], refs[2 + len(mats) :]
+        stream.start(weights, [(t_ref[0] ^ j) * quarter for j in (3, *others)], *refs[-2:])
         make(parts, acts)
 
         def store(piece, cols, total):
-            halves[0][:, cols] = total[:half].astype(BF)
-            halves[1][:, cols] = total[half:].astype(BF)
+            @pl.when(piece == 0)
+            def _():
+                halves[0][:, cols] = total[:half].astype(BF)
+                halves[1][:, cols] = total[half:].astype(BF)
+
+            if others:
+
+                @pl.when(piece > 0)
+                def _():
+                    refs[0][piece - 1, :, cols] = total
 
         stream.products(acts, store)
 
+    outs = [sds((half, quarter), BF)] * 2 + [sds((rows, hidden), BF)] * len(mats)
     return call(
         kernel,
         t,
         list(ins) + list(mats),
-        [sds((half, quarter), BF)] * 2 + [sds((rows, hidden), BF)] * len(mats),
+        outs + ([sds((len(others), rows, quarter), F32)] if others else []),
         stream.scratch,
-        2 * rows * quarter * hidden * len(mats),
+        2 * rows * quarter * (1 + len(others)) * hidden * len(mats),
         stream.mib + 4,
         name,
         far=len(mats),
@@ -439,12 +451,15 @@
     cot_part = jnp.concatenate(after(tuple(cot_z), *rest_d), axis=0)
     cot_parts = [[cot_part]] + [[exchange(cot_part, "tensor", j)] for j in range(1, n)]
     pres = []
-    half = hidden_here // 2
-    for start, turn in ((0, (cot_part,)), (half, (cot_parts[1][0], cot_parts[2][0]))):
+    cut = hidden_here * 5 // 8 // BLOCK * BLOCK
+    for start, stop, turn in (
+        (0, cut, (cot_part,)),
+        (cut, hidden_here, (cot_parts[1][0], cot_parts[2][0])),
+    ):
         gate_o, up_o, sent = pre_acts(
-            after(t_arr, *turn), tok_own, tok_parts, gate_held, up_mat, start, start + half
+            after(t_arr, *turn), tok_own, tok_parts, gate_held, up_mat, start, stop
         )
-        pres.append([gate_o, up_o, exchange(sent, "wide", 1)])
+        pres += [gate_o, up_o, exchange(sent, "wide", 1)]
 
     def summed(arrived, keep):
         total = keep
@@ -462,26 +477,23 @@
 
     gather = [(order[:, k][:, None] == cells[None, :]).astype(BF) for k in range(2)]
 
-    d_top, d_low, hidden = first_piece(
-        t_arr, n, hidden_strips, True, sum(pres, []), [down_mat], "project_first"
+    d_top, d_low, hidden, both = first_piece(
+        t_arr, n, hidden_strips, True, pres, [down_mat], (1, 2), "project_send"
     )
     added = [exchange(d_top, "tensor", 1), exchange(d_low, "tensor", 2)]
-    both = pieces(t_arr, n, True, [hidden], [down_mat], (1, 2), "project_send")
     grads = []
     turn = after(t_arr, both)
-    for start in range(0, hidden_here, hidden_here // 2):
+    for start, stop in ((0, cut), (cut, hidden_here)):
         if start:
             to_x, to_y = add_diagonal(t_arr, both, *added)
             turn = after(t_arr, to_x)
-        gh_o, gh_s = grad_hiddens(
-            turn, cot_own, cot_parts, down_mat, start, start + hidden_here // 2
-        )
-        grads.append([gh_o, exchange(gh_s, "wide", 1)])
+        gh_o, gh_s = grad_hiddens(turn, cot_own, cot_parts, down_mat, start, stop)
+        grads += [gh_o, exchange(gh_s, "wide", 1)]
     keep = pieces(after(t_arr, gh_s), n, True, [hidden], [down_mat], (0,), "project_keep")[0]
 
     e_top, e_low, grad_g, grad_u = first_piece(
         after(t_arr, keep), n, grad_strips, False,
-        sum([p + g for p, g in zip(pres, grads)], []), [gate_mat, up_mat], "rows_first",
+        pres + grads, [gate_mat, up_mat], (), "rows_first",
     )
     gadded = [exchange(e_top, "tensor", 1), exchange(e_low, "tensor", 2)]
     from_x, from_y = exchange(to_x, "tensor", 1), exchange(to_y, "tensor", 2)

time: 150 us -> 158 us (1.053)
  waiting for transfers between devices: 34.7 us -> 45.7 us
  Pallas kernels: 61.7 us -> 60 us
    ppermute x43, waiting for transfers between devices: 34.7 us -> 45.7 us  [exchange(): return lax.ppermute(array, axis, [(i, i ^ bit) for i in range(size)])]
    pallas_call x14 -> x13, Pallas kernels: 57.1 us -> 55.3 us  [call(): pl.pallas_call(kernel, in_specs=[SMEM] + [VMEM] * (len(ins) - far) + [HBM...]
  transfers between devices with their start and end apart: 43 -> 43, of which waited for: 18 -> 20; matrix products, arithmetic and copies ran while one was open for 2% -> 2% of each run, Pallas kernels for 41% -> 33%
where the time goes in v8:
time: 158 us; the launch traced here: 157 us
  Pallas kernels  60 us (38%)
  waiting for transfers between devices  45.7 us (29%)
  starting transfers between devices  44.2 us (28%)
  other arithmetic  3.53 us (2%)
  matrix products  2.47 us (2%)
    pallas_call x13, Pallas kernels, call(): pl.pallas_call(kernel, in_specs=[SMEM] + [VMEM] * (len(ins) - far) + [HBM...  55.3 us
    ppermute x43, waiting for transfers between devices, exchange(): return lax.ppermute(array, axis, [(i, i ^ bit) for i in range(size)])  45.7 us
    ppermute x43, starting transfers between devices, exchange(): return lax.ppermute(array, axis, [(i, i ^ bit) for i in range(size)])  44.2 us
    pallas_call x1, Pallas kernels, fetch(): pl.pallas_call(kernel, in_specs=[HBM], out_specs=VMEM, out_shape=pltpu.VM...  4.66 us
  transfers between devices with their start and end apart: 43, of which 20 were waited for; matrix products, arithmetic and copies ran while one was open for 2% of the time, Pallas kernels for 33%

profile of v8, /device:TPU:16, one launch (start us, length us, event | category | flops | bytes accessed | tf_op | source)
XLA Modules:
  0.0 157.5 jit_solution(15130838494599756584)
XLA Ops:
  3.6 1.6 %collective-permute-start.2 = (bf16[96,768]{1,0:T(8,128)(2,1)S(1)}, bf16[96,768]{1,0:T(8,128)(2,1)S(1)}, u32[]{:S(2)}, u32[]{:S(2)}) collective-permute-start(bf16[96,768]{1,0:T(8,128)(2,1)S(1)} %get-tuple-element.99), channel_id=1, source_target_pairs={{0,1},{1,0},{2,3},{3,2},{4,5},{5,4},{6,7},{7,6},{8,9},{9,8},{10,11... | collective-permute-start | bytes 442376 | tf_op jit(solution)/shard_map/ppermute | solution.py:22
  5.5 1.6 collective-permute-start.1
  7.1 3.2 %collective-permute-done.2.refs_0_ = bf16[96,768]{1,0:T(8,128)(2,1)S(1)} collective-permute-done((bf16[96,768]{1,0:T(8,128)(2,1)S(1)}, bf16[96,768]{1,0:T(8,128)(2,1)S(1)}, u32[]{:S(2)}, u32[]{:S(2)}) %collective-permute-start.2) | collective-permute-done | bytes 147488 | tf_op jit(solution)/shard_map/ppermute | solution.py:22
  10.4 1.5 collective-permute-start.3
  11.9 1.5 collective-permute-start.4
  13.9 4.7 %fetch.1.refs_9_ = bf16[3072,2048]{1,0:T(8,128)(2,1)S(1)} custom-call(bf16[3072,2048]{1,0:T(8,128)(2,1)} %bitcast.37), custom_call_target="tpu_custom_call" | custom-call | bytes 12582912 | tf_op jit(solution)/shard_map/fetch/pallas_call | solution.py:65
  18.8 1.2 collective-permute-done.1
  20.0 1.6 %collective-permute-start.9 = (bf16[192,768]{1,0:T(8,128)(2,1)S(1)}, bf16[192,768]{1,0:T(8,128)(2,1)S(1)}, u32[]{:S(2)}, u32[]{:S(2)}) collective-permute-start(bf16[192,768]{1,0:T(8,128)(2,1)S(1)} %constant_dynamic-update-slice_fusion.refs_1_), channel_id=1, source_target_pairs={{0,8},{4,12},{8,0},{12,4},{1,9},{5,13},{9,1},{13,5},{2,10},{6,14},... | collective-permute-start | bytes 884744 | tf_op jit(solution)/shard_map/ppermute | solution.py:22
  21.6 1.5 collective-permute-start.11
  23.4 1.3 collective-permute-start.6
  25.4 1.6 collective-permute-start.8
  27.9 1.6 collective-permute-start.10
  29.6 1.4 collective-permute-start.12
  31.3 3.0 %collective-permute-done.7 = bf16[96,768]{1,0:T(8,128)(2,1)S(1)} collective-permute-done((bf16[96,768]{1,0:T(8,128)(2,1)S(1)}, bf16[96,768]{1,0:T(8,128)(2,1)S(1)}, u32[]{:S(2)}, u32[]{:S(2)}) %collective-permute-start.7) | collective-permute-done | bytes 147488 | tf_op jit(solution)/shard_map/ppermute | solution.py:22
  34.4 3.8 %collective-permute-done.8 = bf16[96,768]{1,0:T(8,128)(2,1)S(1)} collective-permute-done((bf16[96,768]{1,0:T(8,128)(2,1)S(1)}, bf16[96,768]{1,0:T(8,128)(2,1)S(1)}, u32[]{:S(2)}, u32[]{:S(2)}) %collective-permute-start.8) | collective-permute-done | bytes 147488 | tf_op jit(solution)/shard_map/ppermute | solution.py:22
  38.3 8.3 %pre_acts.2 = (f32[384,1280]{1,0:T(8,128)S(1)}, f32[384,1280]{1,0:T(8,128)S(1)}, bf16[384,2560]{1,0:T(8,128)(2,1)S(1)}) custom-call(s32[1]{0:T(128)} %bitcast.t_ref, bf16[96,3072]{1,0:T(8,128)(2,1)S(1)} %convolution_convert_fusion.own_ref, bf16[96,768]{1,0:T(8,128)(2,1)S(1)} %collective-permute-done.2.refs_0_, ...), custom_call_target="tpu_custom_call" | custom-call | flops 3019898880 | bytes 1048576 | tf_op jit(solution)/shard_map/pre_acts/pallas_call | solution.py:47
  47.9 11.3 %collective-permute-done.14.refs_1_ = bf16[288,768]{1,0:T(8,128)(2,1)S(1)} collective-permute-done((bf16[288,768]{1,0:T(8,128)(2,1)S(1)}, bf16[288,768]{1,0:T(8,128)(2,1)S(1)}, u32[]{:S(2)}, u32[]{:S(2)}) %collective-permute-start.14) | collective-permute-done | bytes 442400 | tf_op jit(solution)/shard_map/ppermute | solution.py:22
  59.5 4.9 %pre_acts.3 = (f32[384,768]{1,0:T(8,128)S(1)}, f32[384,768]{1,0:T(8,128)S(1)}, bf16[384,1536]{1,0:T(8,128)(2,1)S(1)}) custom-call(s32[1]{0:T(128)} %bitcast.t_ref, bf16[96,3072]{1,0:T(8,128)(2,1)S(1)} %convolution_convert_fusion.own_ref, bf16[96,768]{1,0:T(8,128)(2,1)S(1)} %collective-permute-done.2.refs_0_, ...), custom_call_target="tpu_custom_call" | custom-call | flops 1811939328 | bytes 1048576 | tf_op jit(solution)/shard_map/pre_acts/pallas_call | solution.py:47
  64.5 1.5 collective-permute-start.19
  66.3 1.0 collective-permute-done.16.refs_5_
  67.3 7.5 %project_send.1 = (bf16[192,768]{1,0:T(8,128)(2,1)S(1)}, bf16[192,768]{1,0:T(8,128)(2,1)S(1)}, bf16[384,2048]{1,0:T(8,128)(2,1)S(1)}, f32[2,384,768]{2,1,0:T(8,128)S(1)}) custom-call(s32[1]{0:T(128)} %bitcast.t_ref, f32[384,1280]{1,0:T(8,128)S(1)} %get-tuple-element.51.refs_0_, f32[384,1280]{1,0:T(8,128)S(1)} %get-tuple-element.52.refs_1_, ...), custom_call_target="tpu_custom_call" | custom-call | flops 1811939328 | bytes 1048576 | tf_op jit(solution)/shard_map/project_send/pallas_call | solution.py:47
  74.8 1.6 collective-permute-start.17
  76.9 1.3 collective-permute-done.19.refs_3_
  78.2 5.5 %grad_hidden.3 = (f32[384,1280]{1,0:T(8,128)S(1)}, bf16[384,1280]{1,0:T(8,128)(2,1)S(1)}) custom-call(s32[1]{0:T(128)} %bitcast.t_ref, bf16[96,3072]{1,0:T(8,128)(2,1)S(1)} %fusion.own_ref, bf16[288,768]{1,0:T(8,128)(2,1)S(1)} %constant_dynamic-update-slice_fusion.2.refs_0_, bf16[288,768]{1,0:T(8,128)(2,1)S(1)} %collective-permute-done.14.refs_1_, ...), custom_call_target="tpu_custom_call" | custom-call | flops 3019898880 | bytes 1048576 | tf_op jit(solution)/shard_map/grad_hidden/pallas_call | solution.py:47
  83.9 1.2 collective-permute-done.18.low_ref
  85.3 3.9 %grad_hidden.2 = (f32[384,768]{1,0:T(8,128)S(1)}, bf16[384,768]{1,0:T(8,128)(2,1)S(1)}) custom-call(s32[1]{0:T(128)} %bitcast.t_ref, bf16[96,3072]{1,0:T(8,128)(2,1)S(1)} %fusion.own_ref, bf16[288,768]{1,0:T(8,128)(2,1)S(1)} %constant_dynamic-update-slice_fusion.2.refs_0_, bf16[288,768]{1,0:T(8,128)(2,1)S(1)} %collective-permute-done.14.refs_1_, ...), custom_call_target="tpu_custom_call" | custom-call | flops 1811939328 | bytes 1048576 | tf_op jit(solution)/shard_map/grad_hidden/pallas_call | solution.py:47
  90.6 3.7 %project_keep.1 = f32[1,384,768]{2,1,0:T(8,128)S(1)} custom-call(s32[1]{0:T(128)} %bitcast.t_ref, bf16[384,2048]{1,0:T(8,128)(2,1)S(1)} %get-tuple-element.65.refs_0_, bf16[2048,3072]{1,0:T(8,128)(2,1)} %bitcast.36), custom_call_target="tpu_custom_call" | custom-call | flops 603979776 | bytes 1048576 | tf_op jit(solution)/shard_map/project_keep/pallas_call | solution.py:47
  94.2 5.6 %rows_first.1 = (bf16[192,768]{1,0:T(8,128)(2,1)S(1)}, bf16[192,768]{1,0:T(8,128)(2,1)S(1)}, bf16[384,2048]{1,0:T(8,128)(2,1)S(1)}, bf16[384,2048]{1,0:T(8,128)(2,1)S(1)}) custom-call(s32[1]{0:T(128)} %bitcast.t_ref, f32[384,1280]{1,0:T(8,128)S(1)} %get-tuple-element.51.refs_0_, f32[384,1280]{1,0:T(8,128)S(1)} %get-tuple-element.52.refs_1_, ...), custom_call_target="tpu_custom_call" | custom-call | flops 1207959552 | bytes 1048576 | tf_op jit(solution)/shard_map/rows_first/pallas_call | solution.py:47
  99.9 1.4 collective-permute-start.22
  101.2 1.5 collective-permute-start.23
  102.7 8.6 %rows_send.1.both_ref = f32[2,384,768]{2,1,0:T(8,128)S(1)} custom-call(s32[1]{0:T(128)} %bitcast.t_ref, bf16[384,2048]{1,0:T(8,128)(2,1)S(1)} %get-tuple-element.71.refs_0_, bf16[384,2048]{1,0:T(8,128)(2,1)S(1)} %get-tuple-element.72.refs_1_, bf16[3072,2048]{1,0:T(8,128)(2,1)} %bitcast.39, bf16[3072,2048]{1,0:T(8,128)(2,1)} %bitcast.31), custom_call_target="tpu_custom_call" | custom-call | flops 2415919104 | bytes 1048576 | tf_op jit(solution)/shard_map/rows_send/pallas_call | solution.py:47
  112.0 1.3 collective-permute-start.29
  114.1 1.7 %collective-permute-start.27 = (bf16[96,768]{1,0:T(8,128)(2,1)S(1)}, bf16[96,768]{1,0:T(8,128)(2,1)S(1)}, u32[]{:S(2)}, u32[]{:S(2)}) collective-permute-start(bf16[96,768]{1,0:T(8,128)(2,1)S(1)} %get-tuple-element.93), channel_id=1, source_target_pairs={{0,2},{1,3},{2,0},{3,1},{4,6},{5,7},{6,4},{7,5},{8,10},{9,11},{10,... | collective-permute-start | bytes 442376 | tf_op jit(solution)/shard_map/ppermute | solution.py:22
  115.8 1.8 %collective-permute-start.28 = (bf16[96,768]{1,0:T(8,128)(2,1)S(1)}, bf16[96,768]{1,0:T(8,128)(2,1)S(1)}, u32[]{:S(2)}, u32[]{:S(2)}) collective-permute-start(bf16[96,768]{1,0:T(8,128)(2,1)S(1)} %get-tuple-element.92), channel_id=1, source_target_pairs={{0,3},{1,2},{2,1},{3,0},{4,7},{5,6},{6,5},{7,4},{8,11},{9,10},{10,... | collective-permute-start | bytes 442376 | tf_op jit(solution)/shard_map/ppermute | solution.py:22
  117.6 5.2 %rows_keep.1 = f32[1,384,768]{2,1,0:T(8,128)S(1)} custom-call(s32[1]{0:T(128)} %bitcast.t_ref, bf16[384,2048]{1,0:T(8,128)(2,1)S(1)} %get-tuple-element.71.refs_0_, bf16[384,2048]{1,0:T(8,128)(2,1)S(1)} %get-tuple-element.72.refs_1_, bf16[3072,2048]{1,0:T(8,128)(2,1)} %bitcast.40, bf16[3072,2048]{1,0:T(8,128)(2,1)} %bitcast.32), custom_call_target="tpu_custom_call" | custom-call | flops 1207959552 | bytes 1048576 | tf_op jit(solution)/shard_map/rows_keep/pallas_call | solution.py:47
  122.8 3.8 %collective-permute-done.29 = bf16[384,768]{1,0:T(8,128)(2,1)S(1)} collective-permute-done((bf16[384,768]{1,0:T(8,128)(2,1)S(1)}, bf16[384,768]{1,0:T(8,128)(2,1)S(1)}, u32[]{:S(2)}, u32[]{:S(2)}) %collective-permute-start.29) | collective-permute-done | bytes 589856 | tf_op jit(solution)/shard_map/ppermute | solution.py:22
  126.6 1.0 collective-permute-done.30
  127.9 1.7 %collective-permute-start.35 = (bf16[96,768]{1,0:T(8,128)(2,1)S(1)}, bf16[96,768]{1,0:T(8,128)(2,1)S(1)}, u32[]{:S(2)}, u32[]{:S(2)}) collective-permute-start(bf16[96,768]{1,0:T(8,128)(2,1)S(1)} %get-tuple-element.90), channel_id=1, source_target_pairs={{0,2},{1,3},{2,0},{3,1},{4,6},{5,7},{6,4},{7,5},{8,10},{9,11},{10,... | collective-permute-start | bytes 442376 | tf_op jit(solution)/shard_map/ppermute | solution.py:22
  129.6 1.8 %collective-permute-start.36 = (bf16[96,768]{1,0:T(8,128)(2,1)S(1)}, bf16[96,768]{1,0:T(8,128)(2,1)S(1)}, u32[]{:S(2)}, u32[]{:S(2)}) collective-permute-start(bf16[96,768]{1,0:T(8,128)(2,1)S(1)} %get-tuple-element.89), channel_id=1, source_target_pairs={{0,3},{1,2},{2,1},{3,0},{4,7},{5,6},{6,5},{7,4},{8,11},{9,10},{10,... | collective-permute-start | bytes 442376 | tf_op jit(solution)/shard_map/ppermute | solution.py:22
  131.4 3.3 %collective-permute-done.31 = bf16[96,768]{1,0:T(8,128)(2,1)S(1)} collective-permute-done((bf16[96,768]{1,0:T(8,128)(2,1)S(1)}, bf16[96,768]{1,0:T(8,128)(2,1)S(1)}, u32[]{:S(2)}, u32[]{:S(2)}) %collective-permute-start.31) | collective-permute-done | bytes 147488 | tf_op jit(solution)/shard_map/ppermute | solution.py:22
  136.8 2.2 %collective-permute-start.34 = (bf16[128,768]{1,0:T(8,128)(2,1)S(1)}, bf16[128,768]{1,0:T(8,128)(2,1)S(1)}, u32[]{:S(2)}, u32[]{:S(2)}) collective-permute-start(bf16[128,768]{1,0:T(8,128)(2,1)S(1)} %get-tuple-element.87.refs_0_), channel_id=1, source_target_pairs={{0,12},{4,8},{8,4},{12,0},{1,13},{5,9},{9,5},{13,1},{2,14},{6,10},... | collective-permute-start | bytes 589832 | tf_op jit(solution)/shard_map/ppermute | solution.py:22
  139.1 3.4 %collective-permute-done.36 = bf16[96,768]{1,0:T(8,128)(2,1)S(1)} collective-permute-done((bf16[96,768]{1,0:T(8,128)(2,1)S(1)}, bf16[96,768]{1,0:T(8,128)(2,1)S(1)}, u32[]{:S(2)}, u32[]{:S(2)}) %collective-permute-start.36) | collective-permute-done | bytes 147488 | tf_op jit(solution)/shard_map/ppermute | solution.py:22
  144.0 1.0 collective-permute-start.38
  144.9 1.7 %collective-permute-start.39 = (bf16[128,768]{1,0:T(8,128)(2,1)S(1)}, bf16[128,768]{1,0:T(8,128)(2,1)S(1)}, u32[]{:S(2)}, u32[]{:S(2)}) collective-permute-start(bf16[128,768]{1,0:T(8,128)(2,1)S(1)} %fusion.4.refs_0_), channel_id=1, source_target_pairs={{0,12},{4,8},{8,4},{12,0},{1,13},{5,9},{9,5},{13,1},{2,14},{6,10},... | collective-permute-start | bytes 589832 | tf_op jit(solution)/shard_map/ppermute | solution.py:22
  146.8 1.1 collective-permute-done.40
  148.7 4.6 %collective-permute-done.41 = f32[2,128]{1,0:T(2,128)S(1)} collective-permute-done((f32[2,128]{1,0:T(2,128)S(1)}, f32[2,128]{1,0:T(2,128)S(1)}, u32[]{:S(2)}, u32[]{:S(2)}) %collective-permute-start.41) | collective-permute-done | bytes 1056 | tf_op jit(solution)/shard_map/ppermute | solution.py:22
  153.3 1.4 collective-permute-start.42
  155.7 0.9 assemble.3
  (102 shorter events, 18.6 us)
Async XLA Ops:
  0.6 2.6 %copy-start = (bf16[128,3072]{1,0:T(8,128)(2,1)S(1)}, bf16[128,3072]{1,0:T(8,128)(2,1)}, u32[]{:S(2)}) copy-start(bf16[128,3072]{1,0:T(8,128)(2,1)} %param.7) | copy-start | bytes 2359300
  0.6 13.2 %copy-start.3 = (f32[128,2]{0,1:T(2,128)S(1)}, f32[128,2]{0,1:T(2,128)}, u32[]{:S(2)}) copy-start(f32[128,2]{0,1:T(2,128)} %param.9) | copy-start | bytes 3076
  3.6 6.8 %collective-permute-start.2 = (bf16[96,768]{1,0:T(8,128)(2,1)S(1)}, bf16[96,768]{1,0:T(8,128)(2,1)S(1)}, u32[]{:S(2)}, u32[]{:S(2)}) collective-permute-start(bf16[96,768]{1,0:T(8,128)(2,1)S(1)} %get-tuple-element.99), channel_id=1, source_target_pairs={{0,1},{1,0},{2,3},{3,2},{4,5},{5,4},{6,7},{7,6},{8,9},{9,8},{10,11... | collective-permute-start | bytes 442376 | tf_op jit(solution)/shard_map/ppermute | solution.py:22
  5.2 13.6 %collective-permute-start = (bf16[96,768]{1,0:T(8,128)(2,1)S(1)}, bf16[96,768]{1,0:T(8,128)(2,1)S(1)}, u32[]{:S(2)}, u32[]{:S(2)}) collective-permute-start(bf16[96,768]{1,0:T(8,128)(2,1)S(1)} %get-tuple-element.101), channel_id=1, source_target_pairs={{0,2},{1,3},{2,0},{3,1},{4,6},{5,7},{6,4},{7,5},{8,10},{9,11},{10,... | collective-permute-start | bytes 442376 | tf_op jit(solution)/shard_map/ppermute | solution.py:22
  5.5 14.4 %collective-permute-start.1 = (bf16[96,768]{1,0:T(8,128)(2,1)S(1)}, bf16[96,768]{1,0:T(8,128)(2,1)S(1)}, u32[]{:S(2)}, u32[]{:S(2)}) collective-permute-start(bf16[96,768]{1,0:T(8,128)(2,1)S(1)} %get-tuple-element.100), channel_id=1, source_target_pairs={{0,3},{1,2},{2,1},{3,0},{4,7},{5,6},{6,5},{7,4},{8,11},{9,10},{10,... | collective-permute-start | bytes 442376 | tf_op jit(solution)/shard_map/ppermute | solution.py:22
  10.4 9.6 %collective-permute-start.3 = (bf16[96,768]{1,0:T(8,128)(2,1)S(1)}, bf16[96,768]{1,0:T(8,128)(2,1)S(1)}, u32[]{:S(2)}, u32[]{:S(2)}) collective-permute-start(bf16[96,768]{1,0:T(8,128)(2,1)S(1)} %collective-permute-done.2.refs_0_), channel_id=1, source_target_pairs={{0,4},{4,0},{8,12},{12,8},{1,5},{5,1},{9,13},{13,9},{2,6},{6,2},{1... | collective-permute-start | bytes 442376 | tf_op jit(solution)/shard_map/ppermute | solution.py:22
  11.9 8.1 %collective-permute-start.4 = (bf16[96,768]{1,0:T(8,128)(2,1)S(1)}, bf16[96,768]{1,0:T(8,128)(2,1)S(1)}, u32[]{:S(2)}, u32[]{:S(2)}) collective-permute-start(bf16[96,768]{1,0:T(8,128)(2,1)S(1)} %collective-permute-done.2.refs_0_), channel_id=1, source_target_pairs={{0,8},{4,12},{8,0},{12,4},{1,9},{5,13},{9,1},{13,5},{2,10},{6,14},... | collective-permute-start | bytes 442376 | tf_op jit(solution)/shard_map/ppermute | solution.py:22
  13.4 6.6 %collective-permute-start.5 = (bf16[96,768]{1,0:T(8,128)(2,1)S(1)}, bf16[96,768]{1,0:T(8,128)(2,1)S(1)}, u32[]{:S(2)}, u32[]{:S(2)}) collective-permute-start(bf16[96,768]{1,0:T(8,128)(2,1)S(1)} %collective-permute-done.2.refs_0_), channel_id=1, source_target_pairs={{0,12},{4,8},{8,4},{12,0},{1,13},{5,9},{9,5},{13,1},{2,14},{6,10},... | collective-permute-start | bytes 442376 | tf_op jit(solution)/shard_map/ppermute | solution.py:22
  13.9 9.2 %copy-start.2 = (bf16[128,3072]{1,0:T(8,128)(2,1)S(1)}, bf16[128,3072]{1,0:T(8,128)(2,1)}, u32[]{:S(2)}) copy-start(bf16[128,3072]{1,0:T(8,128)(2,1)} %param.13) | copy-start | bytes 2359300
  20.0 7.9 %collective-permute-start.9 = (bf16[192,768]{1,0:T(8,128)(2,1)S(1)}, bf16[192,768]{1,0:T(8,128)(2,1)S(1)}, u32[]{:S(2)}, u32[]{:S(2)}) collective-permute-start(bf16[192,768]{1,0:T(8,128)(2,1)S(1)} %constant_dynamic-update-slice_fusion.refs_1_), channel_id=1, source_target_pairs={{0,8},{4,12},{8,0},{12,4},{1,9},{5,13},{9,1},{13,5},{2,10},{6,14},... | collective-permute-start | bytes 884744 | tf_op jit(solution)/shard_map/ppermute | solution.py:22
  21.6 8.0 %collective-permute-start.11 = (bf16[192,768]{1,0:T(8,128)(2,1)S(1)}, bf16[192,768]{1,0:T(8,128)(2,1)S(1)}, u32[]{:S(2)}, u32[]{:S(2)}) collective-permute-start(bf16[192,768]{1,0:T(8,128)(2,1)S(1)} %constant_dynamic-update-slice_fusion.refs_1_), channel_id=1, source_target_pairs={{0,4},{4,0},{8,12},{12,8},{1,5},{5,1},{9,13},{13,9},{2,6},{6,2},{1... | collective-permute-start | bytes 884744 | tf_op jit(solution)/shard_map/ppermute | solution.py:22
  23.4 8.0 %collective-permute-start.6 = (bf16[96,768]{1,0:T(8,128)(2,1)S(1)}, bf16[96,768]{1,0:T(8,128)(2,1)S(1)}, u32[]{:S(2)}, u32[]{:S(2)}) collective-permute-start(bf16[96,768]{1,0:T(8,128)(2,1)S(1)} %get-tuple-element.98), channel_id=1, source_target_pairs={{0,1},{1,0},{2,3},{3,2},{4,5},{5,4},{6,7},{7,6},{8,9},{9,8},{10,11... | collective-permute-start | bytes 442376 | tf_op jit(solution)/shard_map/ppermute | solution.py:22
  24.6 9.7 %collective-permute-start.7 = (bf16[96,768]{1,0:T(8,128)(2,1)S(1)}, bf16[96,768]{1,0:T(8,128)(2,1)S(1)}, u32[]{:S(2)}, u32[]{:S(2)}) collective-permute-start(bf16[96,768]{1,0:T(8,128)(2,1)S(1)} %get-tuple-element.97), channel_id=1, source_target_pairs={{0,2},{1,3},{2,0},{3,1},{4,6},{5,7},{6,4},{7,5},{8,10},{9,11},{10,... | collective-permute-start | bytes 442376 | tf_op jit(solution)/shard_map/ppermute | solution.py:22
  25.4 12.9 %collective-permute-start.8 = (bf16[96,768]{1,0:T(8,128)(2,1)S(1)}, bf16[96,768]{1,0:T(8,128)(2,1)S(1)}, u32[]{:S(2)}, u32[]{:S(2)}) collective-permute-start(bf16[96,768]{1,0:T(8,128)(2,1)S(1)} %get-tuple-element.96), channel_id=1, source_target_pairs={{0,3},{1,2},{2,1},{3,0},{4,7},{5,6},{6,5},{7,4},{8,11},{9,10},{10,... | collective-permute-start | bytes 442376 | tf_op jit(solution)/shard_map/ppermute | solution.py:22
  27.9 10.4 %collective-permute-start.10 = (bf16[96,768]{1,0:T(8,128)(2,1)S(1)}, bf16[96,768]{1,0:T(8,128)(2,1)S(1)}, u32[]{:S(2)}, u32[]{:S(2)}) collective-permute-start(bf16[96,768]{1,0:T(8,128)(2,1)S(1)} %slice.108), channel_id=1, source_target_pairs={{0,4},{4,0},{8,12},{12,8},{1,5},{5,1},{9,13},{13,9},{2,6},{6,2},{1... | collective-permute-start | bytes 442376 | tf_op jit(solution)/shard_map/ppermute | solution.py:22
  29.6 8.6 %collective-permute-start.12 = (bf16[96,768]{1,0:T(8,128)(2,1)S(1)}, bf16[96,768]{1,0:T(8,128)(2,1)S(1)}, u32[]{:S(2)}, u32[]{:S(2)}) collective-permute-start(bf16[96,768]{1,0:T(8,128)(2,1)S(1)} %slice.109), channel_id=1, source_target_pairs={{0,8},{4,12},{8,0},{12,4},{1,9},{5,13},{9,1},{13,5},{2,10},{6,14},... | collective-permute-start | bytes 442376 | tf_op jit(solution)/shard_map/ppermute | solution.py:22
  46.6 20.8 %collective-permute-start.13 = (bf16[384,2560]{1,0:T(8,128)(2,1)S(1)}, bf16[384,2560]{1,0:T(8,128)(2,1)S(1)}, u32[]{:S(2)}, u32[]{:S(2)}) collective-permute-start(bf16[384,2560]{1,0:T(8,128)(2,1)S(1)} %get-tuple-element.53), channel_id=1, source_target_pairs={{0,16},{16,0},{1,17},{17,1},{2,18},{18,2},{3,19},{19,3},{4,20},{20... | collective-permute-start | bytes 5898248 | tf_op jit(solution)/shard_map/ppermute | solution.py:22
  46.7 12.6 %collective-permute-start.14 = (bf16[288,768]{1,0:T(8,128)(2,1)S(1)}, bf16[288,768]{1,0:T(8,128)(2,1)S(1)}, u32[]{:S(2)}, u32[]{:S(2)}) collective-permute-start(bf16[288,768]{1,0:T(8,128)(2,1)S(1)} %constant_dynamic-update-slice_fusion.2.refs_0_), channel_id=1, source_target_pairs={{0,4},{4,0},{8,12},{12,8},{1,5},{5,1},{9,13},{13,9},{2,6},{6,2},{1... | collective-permute-start | bytes 1327112 | tf_op jit(solution)/shard_map/ppermute | solution.py:22
  47.3 12.2 %collective-permute-start.15 = (bf16[288,768]{1,0:T(8,128)(2,1)S(1)}, bf16[288,768]{1,0:T(8,128)(2,1)S(1)}, u32[]{:S(2)}, u32[]{:S(2)}) collective-permute-start(bf16[288,768]{1,0:T(8,128)(2,1)S(1)} %constant_dynamic-update-slice_fusion.2.refs_0_), channel_id=1, source_target_pairs={{0,8},{4,12},{8,0},{12,4},{1,9},{5,13},{9,1},{13,5},{2,10},{6,14},... | collective-permute-start | bytes 1327112 | tf_op jit(solution)/shard_map/ppermute | solution.py:22
  64.4 2.9 %collective-permute-start.16 = (bf16[384,1536]{1,0:T(8,128)(2,1)S(1)}, bf16[384,1536]{1,0:T(8,128)(2,1)S(1)}, u32[]{:S(2)}, u32[]{:S(2)}) collective-permute-start(bf16[384,1536]{1,0:T(8,128)(2,1)S(1)} %get-tuple-element.57), channel_id=1, source_target_pairs={{0,16},{16,0},{1,17},{17,1},{2,18},{18,2},{3,19},{19,3},{4,20},{20... | collective-permute-start | bytes 3538952 | tf_op jit(solution)/shard_map/ppermute | solution.py:22
  64.5 13.7 %collective-permute-start.19 = (bf16[288,768]{1,0:T(8,128)(2,1)S(1)}, bf16[288,768]{1,0:T(8,128)(2,1)S(1)}, u32[]{:S(2)}, u32[]{:S(2)}) collective-permute-start(bf16[288,768]{1,0:T(8,128)(2,1)S(1)} %constant_dynamic-update-slice_fusion.2.refs_0_), channel_id=1, source_target_pairs={{0,12},{4,8},{8,4},{12,0},{1,13},{5,9},{9,5},{13,1},{2,14},{6,10},... | collective-permute-start | bytes 1327112 | tf_op jit(solution)/shard_map/ppermute | solution.py:22
  74.8 9.1 %collective-permute-start.17 = (bf16[192,768]{1,0:T(8,128)(2,1)S(1)}, bf16[192,768]{1,0:T(8,128)(2,1)S(1)}, u32[]{:S(2)}, u32[]{:S(2)}) collective-permute-start(bf16[192,768]{1,0:T(8,128)(2,1)S(1)} %get-tuple-element.59), channel_id=1, source_target_pairs={{0,4},{4,0},{8,12},{12,8},{1,5},{5,1},{9,13},{13,9},{2,6},{6,2},{1... | collective-permute-start | bytes 884744 | tf_op jit(solution)/shard_map/ppermute | solution.py:22
  76.4 8.8 %collective-permute-start.18 = (bf16[192,768]{1,0:T(8,128)(2,1)S(1)}, bf16[192,768]{1,0:T(8,128)(2,1)S(1)}, u32[]{:S(2)}, u32[]{:S(2)}) collective-permute-start(bf16[192,768]{1,0:T(8,128)(2,1)S(1)} %get-tuple-element.60), channel_id=1, source_target_pairs={{0,8},{4,12},{8,0},{12,4},{1,9},{5,13},{9,1},{13,5},{2,10},{6,14},... | collective-permute-start | bytes 884744 | tf_op jit(solution)/shard_map/ppermute | solution.py:22
  83.7 10.5 %collective-permute-start.20 = (bf16[384,1280]{1,0:T(8,128)(2,1)S(1)}, bf16[384,1280]{1,0:T(8,128)(2,1)S(1)}, u32[]{:S(2)}, u32[]{:S(2)}) collective-permute-start(bf16[384,1280]{1,0:T(8,128)(2,1)S(1)} %get-tuple-element.69), channel_id=1, source_target_pairs={{0,16},{16,0},{1,17},{17,1},{2,18},{18,2},{3,19},{19,3},{4,20},{20... | collective-permute-start | bytes 2949128 | tf_op jit(solution)/shard_map/ppermute | solution.py:22
  89.2 5.0 %collective-permute-start.21 = (bf16[384,768]{1,0:T(8,128)(2,1)S(1)}, bf16[384,768]{1,0:T(8,128)(2,1)S(1)}, u32[]{:S(2)}, u32[]{:S(2)}) collective-permute-start(bf16[384,768]{1,0:T(8,128)(2,1)S(1)} %get-tuple-element.63), channel_id=1, source_target_pairs={{0,16},{16,0},{1,17},{17,1},{2,18},{18,2},{3,19},{19,3},{4,20},{20... | collective-permute-start | bytes 1769480 | tf_op jit(solution)/shard_map/ppermute | solution.py:22
  89.3 24.6 %collective-permute-start.24 = (bf16[384,768]{1,0:T(8,128)(2,1)S(1)}, bf16[384,768]{1,0:T(8,128)(2,1)S(1)}, u32[]{:S(2)}, u32[]{:S(2)}) collective-permute-start(bf16[384,768]{1,0:T(8,128)(2,1)S(1)} %get-tuple-element.61), channel_id=1, source_target_pairs={{0,4},{4,0},{8,12},{12,8},{1,5},{5,1},{9,13},{13,9},{2,6},{6,2},{1... | collective-permute-start | bytes 1769480 | tf_op jit(solution)/shard_map/ppermute | solution.py:22
  90.1 23.7 %collective-permute-start.25 = (bf16[384,768]{1,0:T(8,128)(2,1)S(1)}, bf16[384,768]{1,0:T(8,128)(2,1)S(1)}, u32[]{:S(2)}, u32[]{:S(2)}) collective-permute-start(bf16[384,768]{1,0:T(8,128)(2,1)S(1)} %get-tuple-element.77), channel_id=1, source_target_pairs={{0,8},{4,12},{8,0},{12,4},{1,9},{5,13},{9,1},{13,5},{2,10},{6,14},... | collective-permute-start | bytes 1769480 | tf_op jit(solution)/shard_map/ppermute | solution.py:22
  99.9 11.5 %collective-permute-start.22 = (bf16[192,768]{1,0:T(8,128)(2,1)S(1)}, bf16[192,768]{1,0:T(8,128)(2,1)S(1)}, u32[]{:S(2)}, u32[]{:S(2)}) collective-permute-start(bf16[192,768]{1,0:T(8,128)(2,1)S(1)} %get-tuple-element.73), channel_id=1, source_target_pairs={{0,4},{4,0},{8,12},{12,8},{1,5},{5,1},{9,13},{13,9},{2,6},{6,2},{1... | collective-permute-start | bytes 884744 | tf_op jit(solution)/shard_map/ppermute | solution.py:22
  101.2 10.6 %collective-permute-start.23 = (bf16[192,768]{1,0:T(8,128)(2,1)S(1)}, bf16[192,768]{1,0:T(8,128)(2,1)S(1)}, u32[]{:S(2)}, u32[]{:S(2)}) collective-permute-start(bf16[192,768]{1,0:T(8,128)(2,1)S(1)} %get-tuple-element.74), channel_id=1, source_target_pairs={{0,8},{4,12},{8,0},{12,4},{1,9},{5,13},{9,1},{13,5},{2,10},{6,14},... | collective-permute-start | bytes 884744 | tf_op jit(solution)/shard_map/ppermute | solution.py:22
  112.0 14.6 %collective-permute-start.29 = (bf16[384,768]{1,0:T(8,128)(2,1)S(1)}, bf16[384,768]{1,0:T(8,128)(2,1)S(1)}, u32[]{:S(2)}, u32[]{:S(2)}) collective-permute-start(bf16[384,768]{1,0:T(8,128)(2,1)S(1)} %get-tuple-element.75), channel_id=1, source_target_pairs={{0,4},{4,0},{8,12},{12,8},{1,5},{5,1},{9,13},{13,9},{2,6},{6,2},{1... | collective-permute-start | bytes 1769480 | tf_op jit(solution)/shard_map/ppermute | solution.py:22
  113.3 14.3 %collective-permute-start.30 = (bf16[384,768]{1,0:T(8,128)(2,1)S(1)}, bf16[384,768]{1,0:T(8,128)(2,1)S(1)}, u32[]{:S(2)}, u32[]{:S(2)}) collective-permute-start(bf16[384,768]{1,0:T(8,128)(2,1)S(1)} %get-tuple-element.79), channel_id=1, source_target_pairs={{0,8},{4,12},{8,0},{12,4},{1,9},{5,13},{9,1},{13,5},{2,10},{6,14},... | collective-permute-start | bytes 1769480 | tf_op jit(solution)/shard_map/ppermute | solution.py:22
  114.0 15.6 %collective-permute-start.26 = (bf16[96,768]{1,0:T(8,128)(2,1)S(1)}, bf16[96,768]{1,0:T(8,128)(2,1)S(1)}, u32[]{:S(2)}, u32[]{:S(2)}) collective-permute-start(bf16[96,768]{1,0:T(8,128)(2,1)S(1)} %get-tuple-element.94), channel_id=1, source_target_pairs={{0,1},{1,0},{2,3},{3,2},{4,5},{5,4},{6,7},{7,6},{8,9},{9,8},{10,11... | collective-permute-start | bytes 442376 | tf_op jit(solution)/shard_map/ppermute | solution.py:22
  114.1 17.3 %collective-permute-start.27 = (bf16[96,768]{1,0:T(8,128)(2,1)S(1)}, bf16[96,768]{1,0:T(8,128)(2,1)S(1)}, u32[]{:S(2)}, u32[]{:S(2)}) collective-permute-start(bf16[96,768]{1,0:T(8,128)(2,1)S(1)} %get-tuple-element.93), channel_id=1, source_target_pairs={{0,2},{1,3},{2,0},{3,1},{4,6},{5,7},{6,4},{7,5},{8,10},{9,11},{10,... | collective-permute-start | bytes 442376 | tf_op jit(solution)/shard_map/ppermute | solution.py:22
  115.8 15.7 %collective-permute-start.28 = (bf16[96,768]{1,0:T(8,128)(2,1)S(1)}, bf16[96,768]{1,0:T(8,128)(2,1)S(1)}, u32[]{:S(2)}, u32[]{:S(2)}) collective-permute-start(bf16[96,768]{1,0:T(8,128)(2,1)S(1)} %get-tuple-element.92), channel_id=1, source_target_pairs={{0,3},{1,2},{2,1},{3,0},{4,7},{5,6},{6,5},{7,4},{8,11},{9,10},{10,... | collective-permute-start | bytes 442376 | tf_op jit(solution)/shard_map/ppermute | solution.py:22
  127.9 6.9 %collective-permute-start.31 = (bf16[96,768]{1,0:T(8,128)(2,1)S(1)}, bf16[96,768]{1,0:T(8,128)(2,1)S(1)}, u32[]{:S(2)}, u32[]{:S(2)}) collective-permute-start(bf16[96,768]{1,0:T(8,128)(2,1)S(1)} %get-tuple-element.91), channel_id=1, source_target_pairs={{0,1},{1,0},{2,3},{3,2},{4,5},{5,4},{6,7},{7,6},{8,9},{9,8},{10,11... | collective-permute-start | bytes 442376 | tf_op jit(solution)/shard_map/ppermute | solution.py:22
  127.9 11.1 %collective-permute-start.35 = (bf16[96,768]{1,0:T(8,128)(2,1)S(1)}, bf16[96,768]{1,0:T(8,128)(2,1)S(1)}, u32[]{:S(2)}, u32[]{:S(2)}) collective-permute-start(bf16[96,768]{1,0:T(8,128)(2,1)S(1)} %get-tuple-element.90), channel_id=1, source_target_pairs={{0,2},{1,3},{2,0},{3,1},{4,6},{5,7},{6,4},{7,5},{8,10},{9,11},{10,... | collective-permute-start | bytes 442376 | tf_op jit(solution)/shard_map/ppermute | solution.py:22
  129.6 12.9 %collective-permute-start.36 = (bf16[96,768]{1,0:T(8,128)(2,1)S(1)}, bf16[96,768]{1,0:T(8,128)(2,1)S(1)}, u32[]{:S(2)}, u32[]{:S(2)}) collective-permute-start(bf16[96,768]{1,0:T(8,128)(2,1)S(1)} %get-tuple-element.89), channel_id=1, source_target_pairs={{0,3},{1,2},{2,1},{3,0},{4,7},{5,6},{6,5},{7,4},{8,11},{9,10},{10,... | collective-permute-start | bytes 442376 | tf_op jit(solution)/shard_map/ppermute | solution.py:22
  135.5 9.4 %collective-permute-start.32 = (bf16[128,768]{1,0:T(8,128)(2,1)S(1)}, bf16[128,768]{1,0:T(8,128)(2,1)S(1)}, u32[]{:S(2)}, u32[]{:S(2)}) collective-permute-start(bf16[128,768]{1,0:T(8,128)(2,1)S(1)} %get-tuple-element.87.refs_0_), channel_id=1, source_target_pairs={{0,4},{4,0},{8,12},{12,8},{1,5},{5,1},{9,13},{13,9},{2,6},{6,2},{1... | collective-permute-start | bytes 589832 | tf_op jit(solution)/shard_map/ppermute | solution.py:22
  136.4 10.3 %collective-permute-start.33 = (bf16[128,768]{1,0:T(8,128)(2,1)S(1)}, bf16[128,768]{1,0:T(8,128)(2,1)S(1)}, u32[]{:S(2)}, u32[]{:S(2)}) collective-permute-start(bf16[128,768]{1,0:T(8,128)(2,1)S(1)} %get-tuple-element.87.refs_0_), channel_id=1, source_target_pairs={{0,8},{4,12},{8,0},{12,4},{1,9},{5,13},{9,1},{13,5},{2,10},{6,14},... | collective-permute-start | bytes 589832 | tf_op jit(solution)/shard_map/ppermute | solution.py:22
  136.8 17.9 %collective-permute-start.34 = (bf16[128,768]{1,0:T(8,128)(2,1)S(1)}, bf16[128,768]{1,0:T(8,128)(2,1)S(1)}, u32[]{:S(2)}, u32[]{:S(2)}) collective-permute-start(bf16[128,768]{1,0:T(8,128)(2,1)S(1)} %get-tuple-element.87.refs_0_), channel_id=1, source_target_pairs={{0,12},{4,8},{8,4},{12,0},{1,13},{5,9},{9,5},{13,1},{2,14},{6,10},... | collective-permute-start | bytes 589832 | tf_op jit(solution)/shard_map/ppermute | solution.py:22
  143.1 12.6 %collective-permute-start.37 = (bf16[128,768]{1,0:T(8,128)(2,1)S(1)}, bf16[128,768]{1,0:T(8,128)(2,1)S(1)}, u32[]{:S(2)}, u32[]{:S(2)}) collective-permute-start(bf16[128,768]{1,0:T(8,128)(2,1)S(1)} %fusion.4.refs_0_), channel_id=1, source_target_pairs={{0,4},{4,0},{8,12},{12,8},{1,5},{5,1},{9,13},{13,9},{2,6},{6,2},{1... | collective-permute-start | bytes 589832 | tf_op jit(solution)/shard_map/ppermute | solution.py:22
  144.0 11.7 %collective-permute-start.38 = (bf16[128,768]{1,0:T(8,128)(2,1)S(1)}, bf16[128,768]{1,0:T(8,128)(2,1)S(1)}, u32[]{:S(2)}, u32[]{:S(2)}) collective-permute-start(bf16[128,768]{1,0:T(8,128)(2,1)S(1)} %fusion.4.refs_0_), channel_id=1, source_target_pairs={{0,8},{4,12},{8,0},{12,4},{1,9},{5,13},{9,1},{13,5},{2,10},{6,14},... | collective-permute-start | bytes 589832 | tf_op jit(solution)/shard_map/ppermute | solution.py:22
  144.9 10.7 %collective-permute-start.39 = (bf16[128,768]{1,0:T(8,128)(2,1)S(1)}, bf16[128,768]{1,0:T(8,128)(2,1)S(1)}, u32[]{:S(2)}, u32[]{:S(2)}) collective-permute-start(bf16[128,768]{1,0:T(8,128)(2,1)S(1)} %fusion.4.refs_0_), channel_id=1, source_target_pairs={{0,12},{4,8},{8,4},{12,0},{1,13},{5,9},{9,5},{13,1},{2,14},{6,10},... | collective-permute-start | bytes 589832 | tf_op jit(solution)/shard_map/ppermute | solution.py:22
  146.7 1.2 collective-permute-start.40
  147.9 5.4 %collective-permute-start.41 = (f32[2,128]{1,0:T(2,128)S(1)}, f32[2,128]{1,0:T(2,128)S(1)}, u32[]{:S(2)}, u32[]{:S(2)}) collective-permute-start(f32[2,128]{1,0:T(2,128)S(1)} %add.49), channel_id=1, source_target_pairs={{0,4},{4,0},{8,12},{12,8},{1,5},{5,1},{9,13},{13,9},{2,6},{6,2},{1... | collective-permute-start | bytes 3080 | tf_op jit(solution)/shard_map/ppermute | solution.py:22
  153.3 3.6 %collective-permute-start.42 = (f32[2,128]{1,0:T(2,128)S(1)}, f32[2,128]{1,0:T(2,128)S(1)}, u32[]{:S(2)}, u32[]{:S(2)}) collective-permute-start(f32[2,128]{1,0:T(2,128)S(1)} %add.50), channel_id=1, source_target_pairs={{0,8},{4,12},{8,0},{12,4},{1,9},{5,13},{9,1},{13,5},{2,10},{6,14},... | collective-permute-start | bytes 3080 | tf_op jit(solution)/shard_map/ppermute | solution.py:22
  154.7 2.7 %copy-start.1 = (bf16[128,3072]{1,0:T(8,128)(2,1)S(1)}, bf16[128,3072]{1,0:T(8,128)(2,1)}, u32[]{:S(2)}) copy-start(bf16[128,3072]{1,0:T(8,128)(2,1)} %param.7) | copy-start | bytes 2359300

commit v9 on v8

--- a/solution.py
+++ b/solution.py
@@ -451,7 +451,7 @@
     cot_part = jnp.concatenate(after(tuple(cot_z), *rest_d), axis=0)
     cot_parts = [[cot_part]] + [[exchange(cot_part, "tensor", j)] for j in range(1, n)]
     pres = []
-    cut = hidden_here * 5 // 8 // BLOCK * BLOCK
+    cut = hidden_here // 2
     for start, stop, turn in (
         (0, cut, (cot_part,)),
         (cut, hidden_here, (cot_parts[1][0], cot_parts[2][0])),

time: 158 us -> 151 us (0.956)
  waiting for transfers between devices: 45.7 us -> 37.9 us
    ppermute x43, waiting for transfers between devices: 45.7 us -> 37.9 us  [exchange(): return lax.ppermute(array, axis, [(i, i ^ bit) for i in range(size)])]
  transfers between devices with their start and end apart: 43 -> 43, of which waited for: 20 -> 19; matrix products, arithmetic and copies ran while one was open for 2% -> 2% of each run, Pallas kernels for 33% -> 40%
where the time goes in v9:
time: 151 us; the launch traced here: 150 us
  Pallas kernels  60.2 us (40%)
  starting transfers between devices  44.8 us (30%)
  waiting for transfers between devices  37.9 us (25%)
  other arithmetic  3.53 us (2%)
  matrix products  2.47 us (2%)
    pallas_call x13, Pallas kernels, call(): pl.pallas_call(kernel, in_specs=[SMEM] + [VMEM] * (len(ins) - far) + [HBM...  55.5 us
    ppermute x43, starting transfers between devices, exchange(): return lax.ppermute(array, axis, [(i, i ^ bit) for i in range(size)])  44.8 us
    ppermute x43, waiting for transfers between devices, exchange(): return lax.ppermute(array, axis, [(i, i ^ bit) for i in range(size)])  37.9 us
    pallas_call x1, Pallas kernels, fetch(): pl.pallas_call(kernel, in_specs=[HBM], out_specs=VMEM, out_shape=pltpu.VM...  4.66 us
  transfers between devices with their start and end apart: 43, of which 19 were waited for; matrix products, arithmetic and copies ran while one was open for 2% of the time, Pallas kernels for 40%

profile of v9, /device:TPU:16, one launch (start us, length us, event | category | flops | bytes accessed | tf_op | source)
XLA Modules:
  0.0 150.4 jit_solution(6859083788199717391)
XLA Ops:
  3.6 1.6 %collective-permute-start.2 = (bf16[96,768]{1,0:T(8,128)(2,1)S(1)}, bf16[96,768]{1,0:T(8,128)(2,1)S(1)}, u32[]{:S(2)}, u32[]{:S(2)}) collective-permute-start(bf16[96,768]{1,0:T(8,128)(2,1)S(1)} %get-tuple-element.99), channel_id=1, source_target_pairs={{0,1},{1,0},{2,3},{3,2},{4,5},{5,4},{6,7},{7,6},{8,9},{9,8},{10,11... | collective-permute-start | bytes 442376 | tf_op jit(solution)/shard_map/ppermute | solution.py:22
  5.5 1.6 %collective-permute-start.1 = (bf16[96,768]{1,0:T(8,128)(2,1)S(1)}, bf16[96,768]{1,0:T(8,128)(2,1)S(1)}, u32[]{:S(2)}, u32[]{:S(2)}) collective-permute-start(bf16[96,768]{1,0:T(8,128)(2,1)S(1)} %get-tuple-element.100), channel_id=1, source_target_pairs={{0,3},{1,2},{2,1},{3,0},{4,7},{5,6},{6,5},{7,4},{8,11},{9,10},{10,... | collective-permute-start | bytes 442376 | tf_op jit(solution)/shard_map/ppermute | solution.py:22
  7.1 3.2 %collective-permute-done.2.refs_0_ = bf16[96,768]{1,0:T(8,128)(2,1)S(1)} collective-permute-done((bf16[96,768]{1,0:T(8,128)(2,1)S(1)}, bf16[96,768]{1,0:T(8,128)(2,1)S(1)}, u32[]{:S(2)}, u32[]{:S(2)}) %collective-permute-start.2) | collective-permute-done | bytes 147488 | tf_op jit(solution)/shard_map/ppermute | solution.py:22
  10.4 1.5 collective-permute-start.3
  11.9 1.5 %collective-permute-start.4 = (bf16[96,768]{1,0:T(8,128)(2,1)S(1)}, bf16[96,768]{1,0:T(8,128)(2,1)S(1)}, u32[]{:S(2)}, u32[]{:S(2)}) collective-permute-start(bf16[96,768]{1,0:T(8,128)(2,1)S(1)} %collective-permute-done.2.refs_0_), channel_id=1, source_target_pairs={{0,8},{4,12},{8,0},{12,4},{1,9},{5,13},{9,1},{13,5},{2,10},{6,14},... | collective-permute-start | bytes 442376 | tf_op jit(solution)/shard_map/ppermute | solution.py:22
  13.9 4.7 %fetch.1.refs_9_ = bf16[3072,2048]{1,0:T(8,128)(2,1)S(1)} custom-call(bf16[3072,2048]{1,0:T(8,128)(2,1)} %bitcast.37), custom_call_target="tpu_custom_call" | custom-call | bytes 12582912 | tf_op jit(solution)/shard_map/fetch/pallas_call | solution.py:65
  18.8 1.2 collective-permute-done.1
  20.0 1.6 %collective-permute-start.9 = (bf16[192,768]{1,0:T(8,128)(2,1)S(1)}, bf16[192,768]{1,0:T(8,128)(2,1)S(1)}, u32[]{:S(2)}, u32[]{:S(2)}) collective-permute-start(bf16[192,768]{1,0:T(8,128)(2,1)S(1)} %constant_dynamic-update-slice_fusion.refs_1_), channel_id=1, source_target_pairs={{0,8},{4,12},{8,0},{12,4},{1,9},{5,13},{9,1},{13,5},{2,10},{6,14},... | collective-permute-start | bytes 884744 | tf_op jit(solution)/shard_map/ppermute | solution.py:22
  21.6 1.5 collective-permute-start.11
  23.4 1.3 collective-permute-start.6
  25.4 1.6 %collective-permute-start.8 = (bf16[96,768]{1,0:T(8,128)(2,1)S(1)}, bf16[96,768]{1,0:T(8,128)(2,1)S(1)}, u32[]{:S(2)}, u32[]{:S(2)}) collective-permute-start(bf16[96,768]{1,0:T(8,128)(2,1)S(1)} %get-tuple-element.96), channel_id=1, source_target_pairs={{0,3},{1,2},{2,1},{3,0},{4,7},{5,6},{6,5},{7,4},{8,11},{9,10},{10,... | collective-permute-start | bytes 442376 | tf_op jit(solution)/shard_map/ppermute | solution.py:22
  27.9 1.6 %collective-permute-start.10 = (bf16[96,768]{1,0:T(8,128)(2,1)S(1)}, bf16[96,768]{1,0:T(8,128)(2,1)S(1)}, u32[]{:S(2)}, u32[]{:S(2)}) collective-permute-start(bf16[96,768]{1,0:T(8,128)(2,1)S(1)} %slice.108), channel_id=1, source_target_pairs={{0,4},{4,0},{8,12},{12,8},{1,5},{5,1},{9,13},{13,9},{2,6},{6,2},{1... | collective-permute-start | bytes 442376 | tf_op jit(solution)/shard_map/ppermute | solution.py:22
  29.6 1.4 collective-permute-start.12
  31.0 3.4 %collective-permute-done.7 = bf16[96,768]{1,0:T(8,128)(2,1)S(1)} collective-permute-done((bf16[96,768]{1,0:T(8,128)(2,1)S(1)}, bf16[96,768]{1,0:T(8,128)(2,1)S(1)}, u32[]{:S(2)}, u32[]{:S(2)}) %collective-permute-start.7) | collective-permute-done | bytes 147488 | tf_op jit(solution)/shard_map/ppermute | solution.py:22
  34.4 3.8 %collective-permute-done.8 = bf16[96,768]{1,0:T(8,128)(2,1)S(1)} collective-permute-done((bf16[96,768]{1,0:T(8,128)(2,1)S(1)}, bf16[96,768]{1,0:T(8,128)(2,1)S(1)}, u32[]{:S(2)}, u32[]{:S(2)}) %collective-permute-start.8) | collective-permute-done | bytes 147488 | tf_op jit(solution)/shard_map/ppermute | solution.py:22
  39.9 6.8 %pre_acts.2 = (f32[384,1024]{1,0:T(8,128)S(1)}, f32[384,1024]{1,0:T(8,128)S(1)}, bf16[384,2048]{1,0:T(8,128)(2,1)S(1)}) custom-call(s32[1]{0:T(128)} %bitcast.t_ref, bf16[96,3072]{1,0:T(8,128)(2,1)S(1)} %convolution_convert_fusion.own_ref, bf16[96,768]{1,0:T(8,128)(2,1)S(1)} %collective-permute-done.2.refs_0_, ...), custom_call_target="tpu_custom_call" | custom-call | flops 2415919104 | bytes 1048576 | tf_op jit(solution)/shard_map/pre_acts/pallas_call | solution.py:47
  46.7 2.9 %collective-permute-done.14.refs_1_ = bf16[288,768]{1,0:T(8,128)(2,1)S(1)} collective-permute-done((bf16[288,768]{1,0:T(8,128)(2,1)S(1)}, bf16[288,768]{1,0:T(8,128)(2,1)S(1)}, u32[]{:S(2)}, u32[]{:S(2)}) %collective-permute-start.14) | collective-permute-done | bytes 442400 | tf_op jit(solution)/shard_map/ppermute | solution.py:22
  49.7 6.6 %pre_acts.3 = (f32[384,1024]{1,0:T(8,128)S(1)}, f32[384,1024]{1,0:T(8,128)S(1)}, bf16[384,2048]{1,0:T(8,128)(2,1)S(1)}) custom-call(s32[1]{0:T(128)} %bitcast.t_ref, bf16[96,3072]{1,0:T(8,128)(2,1)S(1)} %convolution_convert_fusion.own_ref, bf16[96,768]{1,0:T(8,128)(2,1)S(1)} %collective-permute-done.2.refs_0_, ...), custom_call_target="tpu_custom_call" | custom-call | flops 2415919104 | bytes 1048576 | tf_op jit(solution)/shard_map/pre_acts/pallas_call | solution.py:47
  56.3 1.6 %collective-permute-start.19 = (bf16[288,768]{1,0:T(8,128)(2,1)S(1)}, bf16[288,768]{1,0:T(8,128)(2,1)S(1)}, u32[]{:S(2)}, u32[]{:S(2)}) collective-permute-start(bf16[288,768]{1,0:T(8,128)(2,1)S(1)} %constant_dynamic-update-slice_fusion.2.refs_0_), channel_id=1, source_target_pairs={{0,12},{4,8},{8,4},{12,0},{1,13},{5,9},{9,5},{13,1},{2,14},{6,10},... | collective-permute-start | bytes 1327112 | tf_op jit(solution)/shard_map/ppermute | solution.py:22
  57.9 1.8 %collective-permute-done.16.refs_5_ = bf16[384,2048]{1,0:T(8,128)(2,1)S(1)} collective-permute-done((bf16[384,2048]{1,0:T(8,128)(2,1)S(1)}, bf16[384,2048]{1,0:T(8,128)(2,1)S(1)}, u32[]{:S(2)}, u32[]{:S(2)}) %collective-permute-start.16) | collective-permute-done | bytes 1572896 | tf_op jit(solution)/shard_map/ppermute | solution.py:22
  59.7 7.5 %project_send.1 = (bf16[192,768]{1,0:T(8,128)(2,1)S(1)}, bf16[192,768]{1,0:T(8,128)(2,1)S(1)}, bf16[384,2048]{1,0:T(8,128)(2,1)S(1)}, f32[2,384,768]{2,1,0:T(8,128)S(1)}) custom-call(s32[1]{0:T(128)} %bitcast.t_ref, f32[384,1024]{1,0:T(8,128)S(1)} %get-tuple-element.51.refs_0_, f32[384,1024]{1,0:T(8,128)S(1)} %get-tuple-element.52.refs_1_, ...), custom_call_target="tpu_custom_call" | custom-call | flops 1811939328 | bytes 1048576 | tf_op jit(solution)/shard_map/project_send/pallas_call | solution.py:47
  67.2 1.7 %collective-permute-start.17 = (bf16[192,768]{1,0:T(8,128)(2,1)S(1)}, bf16[192,768]{1,0:T(8,128)(2,1)S(1)}, u32[]{:S(2)}, u32[]{:S(2)}) collective-permute-start(bf16[192,768]{1,0:T(8,128)(2,1)S(1)} %get-tuple-element.59), channel_id=1, source_target_pairs={{0,4},{4,0},{8,12},{12,8},{1,5},{5,1},{9,13},{13,9},{2,6},{6,2},{1... | collective-permute-start | bytes 884744 | tf_op jit(solution)/shard_map/ppermute | solution.py:22
  69.8 4.7 %grad_hidden.3 = (f32[384,1024]{1,0:T(8,128)S(1)}, bf16[384,1024]{1,0:T(8,128)(2,1)S(1)}) custom-call(s32[1]{0:T(128)} %bitcast.t_ref, bf16[96,3072]{1,0:T(8,128)(2,1)S(1)} %fusion.own_ref, bf16[288,768]{1,0:T(8,128)(2,1)S(1)} %constant_dynamic-update-slice_fusion.2.refs_0_, bf16[288,768]{1,0:T(8,128)(2,1)S(1)} %collective-permute-done.14.refs_1_, ...), custom_call_target="tpu_custom_call" | custom-call | flops 2415919104 | bytes 1048576 | tf_op jit(solution)/shard_map/grad_hidden/pallas_call | solution.py:47
  74.6 1.7 %collective-permute-done.17.top_ref = bf16[192,768]{1,0:T(8,128)(2,1)S(1)} collective-permute-done((bf16[192,768]{1,0:T(8,128)(2,1)S(1)}, bf16[192,768]{1,0:T(8,128)(2,1)S(1)}, u32[]{:S(2)}, u32[]{:S(2)}) %collective-permute-start.17) | collective-permute-done | bytes 294944 | tf_op jit(solution)/shard_map/ppermute | solution.py:22
  76.3 1.4 collective-permute-done.18.low_ref
  77.9 4.7 %grad_hidden.2 = (f32[384,1024]{1,0:T(8,128)S(1)}, bf16[384,1024]{1,0:T(8,128)(2,1)S(1)}) custom-call(s32[1]{0:T(128)} %bitcast.t_ref, bf16[96,3072]{1,0:T(8,128)(2,1)S(1)} %fusion.own_ref, bf16[288,768]{1,0:T(8,128)(2,1)S(1)} %constant_dynamic-update-slice_fusion.2.refs_0_, bf16[288,768]{1,0:T(8,128)(2,1)S(1)} %collective-permute-done.14.refs_1_, ...), custom_call_target="tpu_custom_call" | custom-call | flops 2415919104 | bytes 1048576 | tf_op jit(solution)/shard_map/grad_hidden/pallas_call | solution.py:47
  83.5 3.6 %project_keep.1 = f32[1,384,768]{2,1,0:T(8,128)S(1)} custom-call(s32[1]{0:T(128)} %bitcast.t_ref, bf16[384,2048]{1,0:T(8,128)(2,1)S(1)} %get-tuple-element.65.refs_0_, bf16[2048,3072]{1,0:T(8,128)(2,1)} %bitcast.36), custom_call_target="tpu_custom_call" | custom-call | flops 603979776 | bytes 1048576 | tf_op jit(solution)/shard_map/project_keep/pallas_call | solution.py:47
  87.2 5.6 %rows_first.1 = (bf16[192,768]{1,0:T(8,128)(2,1)S(1)}, bf16[192,768]{1,0:T(8,128)(2,1)S(1)}, bf16[384,2048]{1,0:T(8,128)(2,1)S(1)}, bf16[384,2048]{1,0:T(8,128)(2,1)S(1)}) custom-call(s32[1]{0:T(128)} %bitcast.t_ref, f32[384,1024]{1,0:T(8,128)S(1)} %get-tuple-element.51.refs_0_, f32[384,1024]{1,0:T(8,128)S(1)} %get-tuple-element.52.refs_1_, ...), custom_call_target="tpu_custom_call" | custom-call | flops 1207959552 | bytes 1048576 | tf_op jit(solution)/shard_map/rows_first/pallas_call | solution.py:47
  92.8 1.7 %collective-permute-start.22 = (bf16[192,768]{1,0:T(8,128)(2,1)S(1)}, bf16[192,768]{1,0:T(8,128)(2,1)S(1)}, u32[]{:S(2)}, u32[]{:S(2)}) collective-permute-start(bf16[192,768]{1,0:T(8,128)(2,1)S(1)} %get-tuple-element.73), channel_id=1, source_target_pairs={{0,4},{4,0},{8,12},{12,8},{1,5},{5,1},{9,13},{13,9},{2,6},{6,2},{1... | collective-permute-start | bytes 884744 | tf_op jit(solution)/shard_map/ppermute | solution.py:22
  94.5 1.6 %collective-permute-start.23 = (bf16[192,768]{1,0:T(8,128)(2,1)S(1)}, bf16[192,768]{1,0:T(8,128)(2,1)S(1)}, u32[]{:S(2)}, u32[]{:S(2)}) collective-permute-start(bf16[192,768]{1,0:T(8,128)(2,1)S(1)} %get-tuple-element.74), channel_id=1, source_target_pairs={{0,8},{4,12},{8,0},{12,4},{1,9},{5,13},{9,1},{13,5},{2,10},{6,14},... | collective-permute-start | bytes 884744 | tf_op jit(solution)/shard_map/ppermute | solution.py:22
  96.2 8.6 %rows_send.1.both_ref = f32[2,384,768]{2,1,0:T(8,128)S(1)} custom-call(s32[1]{0:T(128)} %bitcast.t_ref, bf16[384,2048]{1,0:T(8,128)(2,1)S(1)} %get-tuple-element.71.refs_0_, bf16[384,2048]{1,0:T(8,128)(2,1)S(1)} %get-tuple-element.72.refs_1_, bf16[3072,2048]{1,0:T(8,128)(2,1)} %bitcast.39, bf16[3072,2048]{1,0:T(8,128)(2,1)} %bitcast.31), custom_call_target="tpu_custom_call" | custom-call | flops 2415919104 | bytes 1048576 | tf_op jit(solution)/shard_map/rows_send/pallas_call | solution.py:47
  105.0 1.7 %collective-permute-start.29 = (bf16[384,768]{1,0:T(8,128)(2,1)S(1)}, bf16[384,768]{1,0:T(8,128)(2,1)S(1)}, u32[]{:S(2)}, u32[]{:S(2)}) collective-permute-start(bf16[384,768]{1,0:T(8,128)(2,1)S(1)} %get-tuple-element.75), channel_id=1, source_target_pairs={{0,4},{4,0},{8,12},{12,8},{1,5},{5,1},{9,13},{13,9},{2,6},{6,2},{1... | collective-permute-start | bytes 1769480 | tf_op jit(solution)/shard_map/ppermute | solution.py:22
  107.4 1.0 collective-permute-start.27
  108.4 2.5 %collective-permute-start.28 = (bf16[96,768]{1,0:T(8,128)(2,1)S(1)}, bf16[96,768]{1,0:T(8,128)(2,1)S(1)}, u32[]{:S(2)}, u32[]{:S(2)}) collective-permute-start(bf16[96,768]{1,0:T(8,128)(2,1)S(1)} %get-tuple-element.92), channel_id=1, source_target_pairs={{0,3},{1,2},{2,1},{3,0},{4,7},{5,6},{6,5},{7,4},{8,11},{9,10},{10,... | collective-permute-start | bytes 442376 | tf_op jit(solution)/shard_map/ppermute | solution.py:22
  110.9 5.2 %rows_keep.1 = f32[1,384,768]{2,1,0:T(8,128)S(1)} custom-call(s32[1]{0:T(128)} %bitcast.t_ref, bf16[384,2048]{1,0:T(8,128)(2,1)S(1)} %get-tuple-element.71.refs_0_, bf16[384,2048]{1,0:T(8,128)(2,1)S(1)} %get-tuple-element.72.refs_1_, bf16[3072,2048]{1,0:T(8,128)(2,1)} %bitcast.40, bf16[3072,2048]{1,0:T(8,128)(2,1)} %bitcast.32), custom_call_target="tpu_custom_call" | custom-call | flops 1207959552 | bytes 1048576 | tf_op jit(solution)/shard_map/rows_keep/pallas_call | solution.py:47
  116.1 3.8 %collective-permute-done.29 = bf16[384,768]{1,0:T(8,128)(2,1)S(1)} collective-permute-done((bf16[384,768]{1,0:T(8,128)(2,1)S(1)}, bf16[384,768]{1,0:T(8,128)(2,1)S(1)}, u32[]{:S(2)}, u32[]{:S(2)}) %collective-permute-start.29) | collective-permute-done | bytes 589856 | tf_op jit(solution)/shard_map/ppermute | solution.py:22
  119.9 1.1 collective-permute-done.30
  121.4 1.0 collective-permute-start.35
  122.4 2.5 %collective-permute-start.36 = (bf16[96,768]{1,0:T(8,128)(2,1)S(1)}, bf16[96,768]{1,0:T(8,128)(2,1)S(1)}, u32[]{:S(2)}, u32[]{:S(2)}) collective-permute-start(bf16[96,768]{1,0:T(8,128)(2,1)S(1)} %get-tuple-element.89), channel_id=1, source_target_pairs={{0,3},{1,2},{2,1},{3,0},{4,7},{5,6},{6,5},{7,4},{8,11},{9,10},{10,... | collective-permute-start | bytes 442376 | tf_op jit(solution)/shard_map/ppermute | solution.py:22
  124.9 3.3 %collective-permute-done.31 = bf16[96,768]{1,0:T(8,128)(2,1)S(1)} collective-permute-done((bf16[96,768]{1,0:T(8,128)(2,1)S(1)}, bf16[96,768]{1,0:T(8,128)(2,1)S(1)}, u32[]{:S(2)}, u32[]{:S(2)}) %collective-permute-start.31) | collective-permute-done | bytes 147488 | tf_op jit(solution)/shard_map/ppermute | solution.py:22
  130.0 2.5 %collective-permute-start.34 = (bf16[128,768]{1,0:T(8,128)(2,1)S(1)}, bf16[128,768]{1,0:T(8,128)(2,1)S(1)}, u32[]{:S(2)}, u32[]{:S(2)}) collective-permute-start(bf16[128,768]{1,0:T(8,128)(2,1)S(1)} %get-tuple-element.87.refs_0_), channel_id=1, source_target_pairs={{0,12},{4,8},{8,4},{12,0},{1,13},{5,9},{9,5},{13,1},{2,14},{6,10},... | collective-permute-start | bytes 589832 | tf_op jit(solution)/shard_map/ppermute | solution.py:22
  132.5 3.2 %collective-permute-done.36 = bf16[96,768]{1,0:T(8,128)(2,1)S(1)} collective-permute-done((bf16[96,768]{1,0:T(8,128)(2,1)S(1)}, bf16[96,768]{1,0:T(8,128)(2,1)S(1)}, u32[]{:S(2)}, u32[]{:S(2)}) %collective-permute-start.36) | collective-permute-done | bytes 147488 | tf_op jit(solution)/shard_map/ppermute | solution.py:22
  138.1 1.9 %collective-permute-start.39 = (bf16[128,768]{1,0:T(8,128)(2,1)S(1)}, bf16[128,768]{1,0:T(8,128)(2,1)S(1)}, u32[]{:S(2)}, u32[]{:S(2)}) collective-permute-start(bf16[128,768]{1,0:T(8,128)(2,1)S(1)} %fusion.4.refs_0_), channel_id=1, source_target_pairs={{0,12},{4,8},{8,4},{12,0},{1,13},{5,9},{9,5},{13,1},{2,14},{6,10},... | collective-permute-start | bytes 589832 | tf_op jit(solution)/shard_map/ppermute | solution.py:22
  140.0 1.1 collective-permute-done.40
  142.0 4.3 %collective-permute-done.41 = f32[2,128]{1,0:T(2,128)S(1)} collective-permute-done((f32[2,128]{1,0:T(2,128)S(1)}, f32[2,128]{1,0:T(2,128)S(1)}, u32[]{:S(2)}, u32[]{:S(2)}) %collective-permute-start.41) | collective-permute-done | bytes 1056 | tf_op jit(solution)/shard_map/ppermute | solution.py:22
  146.3 1.5 %collective-permute-start.42 = (f32[2,128]{1,0:T(2,128)S(1)}, f32[2,128]{1,0:T(2,128)S(1)}, u32[]{:S(2)}, u32[]{:S(2)}) collective-permute-start(f32[2,128]{1,0:T(2,128)S(1)} %add.50), channel_id=1, source_target_pairs={{0,8},{4,12},{8,0},{12,4},{1,9},{5,13},{9,1},{13,5},{2,10},{6,14},... | collective-permute-start | bytes 3080 | tf_op jit(solution)/shard_map/ppermute | solution.py:22
  147.8 0.9 assemble.2
  148.8 0.9 assemble.3
  (105 shorter events, 16.9 us)
Async XLA Ops:
  0.6 2.6 %copy-start = (bf16[128,3072]{1,0:T(8,128)(2,1)S(1)}, bf16[128,3072]{1,0:T(8,128)(2,1)}, u32[]{:S(2)}) copy-start(bf16[128,3072]{1,0:T(8,128)(2,1)} %param.7) | copy-start | bytes 2359300
  0.6 13.2 %copy-start.4 = (f32[128,2]{0,1:T(2,128)S(1)}, f32[128,2]{0,1:T(2,128)}, u32[]{:S(2)}) copy-start(f32[128,2]{0,1:T(2,128)} %param.9) | copy-start | bytes 3076
  3.6 6.8 %collective-permute-start.2 = (bf16[96,768]{1,0:T(8,128)(2,1)S(1)}, bf16[96,768]{1,0:T(8,128)(2,1)S(1)}, u32[]{:S(2)}, u32[]{:S(2)}) collective-permute-start(bf16[96,768]{1,0:T(8,128)(2,1)S(1)} %get-tuple-element.99), channel_id=1, source_target_pairs={{0,1},{1,0},{2,3},{3,2},{4,5},{5,4},{6,7},{7,6},{8,9},{9,8},{10,11... | collective-permute-start | bytes 442376 | tf_op jit(solution)/shard_map/ppermute | solution.py:22
  5.2 13.6 %collective-permute-start = (bf16[96,768]{1,0:T(8,128)(2,1)S(1)}, bf16[96,768]{1,0:T(8,128)(2,1)S(1)}, u32[]{:S(2)}, u32[]{:S(2)}) collective-permute-start(bf16[96,768]{1,0:T(8,128)(2,1)S(1)} %get-tuple-element.101), channel_id=1, source_target_pairs={{0,2},{1,3},{2,0},{3,1},{4,6},{5,7},{6,4},{7,5},{8,10},{9,11},{10,... | collective-permute-start | bytes 442376 | tf_op jit(solution)/shard_map/ppermute | solution.py:22
  5.5 14.4 %collective-permute-start.1 = (bf16[96,768]{1,0:T(8,128)(2,1)S(1)}, bf16[96,768]{1,0:T(8,128)(2,1)S(1)}, u32[]{:S(2)}, u32[]{:S(2)}) collective-permute-start(bf16[96,768]{1,0:T(8,128)(2,1)S(1)} %get-tuple-element.100), channel_id=1, source_target_pairs={{0,3},{1,2},{2,1},{3,0},{4,7},{5,6},{6,5},{7,4},{8,11},{9,10},{10,... | collective-permute-start | bytes 442376 | tf_op jit(solution)/shard_map/ppermute | solution.py:22
  10.4 9.6 %collective-permute-start.3 = (bf16[96,768]{1,0:T(8,128)(2,1)S(1)}, bf16[96,768]{1,0:T(8,128)(2,1)S(1)}, u32[]{:S(2)}, u32[]{:S(2)}) collective-permute-start(bf16[96,768]{1,0:T(8,128)(2,1)S(1)} %collective-permute-done.2.refs_0_), channel_id=1, source_target_pairs={{0,4},{4,0},{8,12},{12,8},{1,5},{5,1},{9,13},{13,9},{2,6},{6,2},{1... | collective-permute-start | bytes 442376 | tf_op jit(solution)/shard_map/ppermute | solution.py:22
  11.9 8.1 %collective-permute-start.4 = (bf16[96,768]{1,0:T(8,128)(2,1)S(1)}, bf16[96,768]{1,0:T(8,128)(2,1)S(1)}, u32[]{:S(2)}, u32[]{:S(2)}) collective-permute-start(bf16[96,768]{1,0:T(8,128)(2,1)S(1)} %collective-permute-done.2.refs_0_), channel_id=1, source_target_pairs={{0,8},{4,12},{8,0},{12,4},{1,9},{5,13},{9,1},{13,5},{2,10},{6,14},... | collective-permute-start | bytes 442376 | tf_op jit(solution)/shard_map/ppermute | solution.py:22
  13.4 6.6 %collective-permute-start.5 = (bf16[96,768]{1,0:T(8,128)(2,1)S(1)}, bf16[96,768]{1,0:T(8,128)(2,1)S(1)}, u32[]{:S(2)}, u32[]{:S(2)}) collective-permute-start(bf16[96,768]{1,0:T(8,128)(2,1)S(1)} %collective-permute-done.2.refs_0_), channel_id=1, source_target_pairs={{0,12},{4,8},{8,4},{12,0},{1,13},{5,9},{9,5},{13,1},{2,14},{6,10},... | collective-permute-start | bytes 442376 | tf_op jit(solution)/shard_map/ppermute | solution.py:22
  13.9 9.2 %copy-start.2 = (bf16[128,3072]{1,0:T(8,128)(2,1)S(1)}, bf16[128,3072]{1,0:T(8,128)(2,1)}, u32[]{:S(2)}) copy-start(bf16[128,3072]{1,0:T(8,128)(2,1)} %param.13) | copy-start | bytes 2359300
  18.7 39.2 %copy-start.3 = (f32[384]{0:T(512)}, f32[384]{0:T(512)S(1)}, u32[]{:S(2)}) copy-start(f32[384]{0:T(512)S(1)} %add_reduce_fusion) | copy-start | bytes 4612
  20.0 7.9 %collective-permute-start.9 = (bf16[192,768]{1,0:T(8,128)(2,1)S(1)}, bf16[192,768]{1,0:T(8,128)(2,1)S(1)}, u32[]{:S(2)}, u32[]{:S(2)}) collective-permute-start(bf16[192,768]{1,0:T(8,128)(2,1)S(1)} %constant_dynamic-update-slice_fusion.refs_1_), channel_id=1, source_target_pairs={{0,8},{4,12},{8,0},{12,4},{1,9},{5,13},{9,1},{13,5},{2,10},{6,14},... | collective-permute-start | bytes 884744 | tf_op jit(solution)/shard_map/ppermute | solution.py:22
  21.6 8.0 %collective-permute-start.11 = (bf16[192,768]{1,0:T(8,128)(2,1)S(1)}, bf16[192,768]{1,0:T(8,128)(2,1)S(1)}, u32[]{:S(2)}, u32[]{:S(2)}) collective-permute-start(bf16[192,768]{1,0:T(8,128)(2,1)S(1)} %constant_dynamic-update-slice_fusion.refs_1_), channel_id=1, source_target_pairs={{0,4},{4,0},{8,12},{12,8},{1,5},{5,1},{9,13},{13,9},{2,6},{6,2},{1... | collective-permute-start | bytes 884744 | tf_op jit(solution)/shard_map/ppermute | solution.py:22
  23.4 7.6 %collective-permute-start.6 = (bf16[96,768]{1,0:T(8,128)(2,1)S(1)}, bf16[96,768]{1,0:T(8,128)(2,1)S(1)}, u32[]{:S(2)}, u32[]{:S(2)}) collective-permute-start(bf16[96,768]{1,0:T(8,128)(2,1)S(1)} %get-tuple-element.98), channel_id=1, source_target_pairs={{0,1},{1,0},{2,3},{3,2},{4,5},{5,4},{6,7},{7,6},{8,9},{9,8},{10,11... | collective-permute-start | bytes 442376 | tf_op jit(solution)/shard_map/ppermute | solution.py:22
  24.6 9.7 %collective-permute-start.7 = (bf16[96,768]{1,0:T(8,128)(2,1)S(1)}, bf16[96,768]{1,0:T(8,128)(2,1)S(1)}, u32[]{:S(2)}, u32[]{:S(2)}) collective-permute-start(bf16[96,768]{1,0:T(8,128)(2,1)S(1)} %get-tuple-element.97), channel_id=1, source_target_pairs={{0,2},{1,3},{2,0},{3,1},{4,6},{5,7},{6,4},{7,5},{8,10},{9,11},{10,... | collective-permute-start | bytes 442376 | tf_op jit(solution)/shard_map/ppermute | solution.py:22
  25.4 12.9 %collective-permute-start.8 = (bf16[96,768]{1,0:T(8,128)(2,1)S(1)}, bf16[96,768]{1,0:T(8,128)(2,1)S(1)}, u32[]{:S(2)}, u32[]{:S(2)}) collective-permute-start(bf16[96,768]{1,0:T(8,128)(2,1)S(1)} %get-tuple-element.96), channel_id=1, source_target_pairs={{0,3},{1,2},{2,1},{3,0},{4,7},{5,6},{6,5},{7,4},{8,11},{9,10},{10,... | collective-permute-start | bytes 442376 | tf_op jit(solution)/shard_map/ppermute | solution.py:22
  27.9 10.4 %collective-permute-start.10 = (bf16[96,768]{1,0:T(8,128)(2,1)S(1)}, bf16[96,768]{1,0:T(8,128)(2,1)S(1)}, u32[]{:S(2)}, u32[]{:S(2)}) collective-permute-start(bf16[96,768]{1,0:T(8,128)(2,1)S(1)} %slice.108), channel_id=1, source_target_pairs={{0,4},{4,0},{8,12},{12,8},{1,5},{5,1},{9,13},{13,9},{2,6},{6,2},{1... | collective-permute-start | bytes 442376 | tf_op jit(solution)/shard_map/ppermute | solution.py:22
  29.6 8.6 %collective-permute-start.12 = (bf16[96,768]{1,0:T(8,128)(2,1)S(1)}, bf16[96,768]{1,0:T(8,128)(2,1)S(1)}, u32[]{:S(2)}, u32[]{:S(2)}) collective-permute-start(bf16[96,768]{1,0:T(8,128)(2,1)S(1)} %slice.109), channel_id=1, source_target_pairs={{0,8},{4,12},{8,0},{12,4},{1,9},{5,13},{9,1},{13,5},{2,10},{6,14},... | collective-permute-start | bytes 442376 | tf_op jit(solution)/shard_map/ppermute | solution.py:22
  38.3 11.3 %collective-permute-start.14 = (bf16[288,768]{1,0:T(8,128)(2,1)S(1)}, bf16[288,768]{1,0:T(8,128)(2,1)S(1)}, u32[]{:S(2)}, u32[]{:S(2)}) collective-permute-start(bf16[288,768]{1,0:T(8,128)(2,1)S(1)} %constant_dynamic-update-slice_fusion.2.refs_0_), channel_id=1, source_target_pairs={{0,4},{4,0},{8,12},{12,8},{1,5},{5,1},{9,13},{13,9},{2,6},{6,2},{1... | collective-permute-start | bytes 1327112 | tf_op jit(solution)/shard_map/ppermute | solution.py:22
  38.9 10.8 %collective-permute-start.15 = (bf16[288,768]{1,0:T(8,128)(2,1)S(1)}, bf16[288,768]{1,0:T(8,128)(2,1)S(1)}, u32[]{:S(2)}, u32[]{:S(2)}) collective-permute-start(bf16[288,768]{1,0:T(8,128)(2,1)S(1)} %constant_dynamic-update-slice_fusion.2.refs_0_), channel_id=1, source_target_pairs={{0,8},{4,12},{8,0},{12,4},{1,9},{5,13},{9,1},{13,5},{2,10},{6,14},... | collective-permute-start | bytes 1327112 | tf_op jit(solution)/shard_map/ppermute | solution.py:22
  46.7 11.3 %collective-permute-start.13 = (bf16[384,2048]{1,0:T(8,128)(2,1)S(1)}, bf16[384,2048]{1,0:T(8,128)(2,1)S(1)}, u32[]{:S(2)}, u32[]{:S(2)}) collective-permute-start(bf16[384,2048]{1,0:T(8,128)(2,1)S(1)} %get-tuple-element.53), channel_id=1, source_target_pairs={{0,16},{16,0},{1,17},{17,1},{2,18},{18,2},{3,19},{19,3},{4,20},{20... | collective-permute-start | bytes 4718600 | tf_op jit(solution)/shard_map/ppermute | solution.py:22
  56.3 3.5 %collective-permute-start.16 = (bf16[384,2048]{1,0:T(8,128)(2,1)S(1)}, bf16[384,2048]{1,0:T(8,128)(2,1)S(1)}, u32[]{:S(2)}, u32[]{:S(2)}) collective-permute-start(bf16[384,2048]{1,0:T(8,128)(2,1)S(1)} %get-tuple-element.57), channel_id=1, source_target_pairs={{0,16},{16,0},{1,17},{17,1},{2,18},{18,2},{3,19},{19,3},{4,20},{20... | collective-permute-start | bytes 4718600 | tf_op jit(solution)/shard_map/ppermute | solution.py:22
  56.3 13.5 %collective-permute-start.19 = (bf16[288,768]{1,0:T(8,128)(2,1)S(1)}, bf16[288,768]{1,0:T(8,128)(2,1)S(1)}, u32[]{:S(2)}, u32[]{:S(2)}) collective-permute-start(bf16[288,768]{1,0:T(8,128)(2,1)S(1)} %constant_dynamic-update-slice_fusion.2.refs_0_), channel_id=1, source_target_pairs={{0,12},{4,8},{8,4},{12,0},{1,13},{5,9},{9,5},{13,1},{2,14},{6,10},... | collective-permute-start | bytes 1327112 | tf_op jit(solution)/shard_map/ppermute | solution.py:22
  59.7 9.6 %slice-start = ((f32[384]{0:T(512)}), f32[96]{0:T(128)S(1)}, s32[]{:S(2)}) async-start(f32[384]{0:T(512)} %copy-done.3), calls=%async_computation | async-start | bytes 1024 | tf_op jit(solution)/shard_map/slice | solution.py:431
  67.2 9.1 %collective-permute-start.17 = (bf16[192,768]{1,0:T(8,128)(2,1)S(1)}, bf16[192,768]{1,0:T(8,128)(2,1)S(1)}, u32[]{:S(2)}, u32[]{:S(2)}) collective-permute-start(bf16[192,768]{1,0:T(8,128)(2,1)S(1)} %get-tuple-element.59), channel_id=1, source_target_pairs={{0,4},{4,0},{8,12},{12,8},{1,5},{5,1},{9,13},{13,9},{2,6},{6,2},{1... | collective-permute-start | bytes 884744 | tf_op jit(solution)/shard_map/ppermute | solution.py:22
  69.0 8.8 %collective-permute-start.18 = (bf16[192,768]{1,0:T(8,128)(2,1)S(1)}, bf16[192,768]{1,0:T(8,128)(2,1)S(1)}, u32[]{:S(2)}, u32[]{:S(2)}) collective-permute-start(bf16[192,768]{1,0:T(8,128)(2,1)S(1)} %get-tuple-element.60), channel_id=1, source_target_pairs={{0,8},{4,12},{8,0},{12,4},{1,9},{5,13},{9,1},{13,5},{2,10},{6,14},... | collective-permute-start | bytes 884744 | tf_op jit(solution)/shard_map/ppermute | solution.py:22
  74.5 12.6 %collective-permute-start.20 = (bf16[384,1024]{1,0:T(8,128)(2,1)S(1)}, bf16[384,1024]{1,0:T(8,128)(2,1)S(1)}, u32[]{:S(2)}, u32[]{:S(2)}) collective-permute-start(bf16[384,1024]{1,0:T(8,128)(2,1)S(1)} %get-tuple-element.69), channel_id=1, source_target_pairs={{0,16},{16,0},{1,17},{17,1},{2,18},{18,2},{3,19},{19,3},{4,20},{20... | collective-permute-start | bytes 2359304 | tf_op jit(solution)/shard_map/ppermute | solution.py:22
  82.6 4.6 %collective-permute-start.21 = (bf16[384,1024]{1,0:T(8,128)(2,1)S(1)}, bf16[384,1024]{1,0:T(8,128)(2,1)S(1)}, u32[]{:S(2)}, u32[]{:S(2)}) collective-permute-start(bf16[384,1024]{1,0:T(8,128)(2,1)S(1)} %get-tuple-element.63), channel_id=1, source_target_pairs={{0,16},{16,0},{1,17},{17,1},{2,18},{18,2},{3,19},{19,3},{4,20},{20... | collective-permute-start | bytes 2359304 | tf_op jit(solution)/shard_map/ppermute | solution.py:22
  82.7 24.4 %collective-permute-start.24 = (bf16[384,768]{1,0:T(8,128)(2,1)S(1)}, bf16[384,768]{1,0:T(8,128)(2,1)S(1)}, u32[]{:S(2)}, u32[]{:S(2)}) collective-permute-start(bf16[384,768]{1,0:T(8,128)(2,1)S(1)} %get-tuple-element.61), channel_id=1, source_target_pairs={{0,4},{4,0},{8,12},{12,8},{1,5},{5,1},{9,13},{13,9},{2,6},{6,2},{1... | collective-permute-start | bytes 1769480 | tf_op jit(solution)/shard_map/ppermute | solution.py:22
  83.1 24.0 %collective-permute-start.25 = (bf16[384,768]{1,0:T(8,128)(2,1)S(1)}, bf16[384,768]{1,0:T(8,128)(2,1)S(1)}, u32[]{:S(2)}, u32[]{:S(2)}) collective-permute-start(bf16[384,768]{1,0:T(8,128)(2,1)S(1)} %get-tuple-element.77), channel_id=1, source_target_pairs={{0,8},{4,12},{8,0},{12,4},{1,9},{5,13},{9,1},{13,5},{2,10},{6,14},... | collective-permute-start | bytes 1769480 | tf_op jit(solution)/shard_map/ppermute | solution.py:22
  92.8 12.0 %collective-permute-start.22 = (bf16[192,768]{1,0:T(8,128)(2,1)S(1)}, bf16[192,768]{1,0:T(8,128)(2,1)S(1)}, u32[]{:S(2)}, u32[]{:S(2)}) collective-permute-start(bf16[192,768]{1,0:T(8,128)(2,1)S(1)} %get-tuple-element.73), channel_id=1, source_target_pairs={{0,4},{4,0},{8,12},{12,8},{1,5},{5,1},{9,13},{13,9},{2,6},{6,2},{1... | collective-permute-start | bytes 884744 | tf_op jit(solution)/shard_map/ppermute | solution.py:22
  94.5 10.3 %collective-permute-start.23 = (bf16[192,768]{1,0:T(8,128)(2,1)S(1)}, bf16[192,768]{1,0:T(8,128)(2,1)S(1)}, u32[]{:S(2)}, u32[]{:S(2)}) collective-permute-start(bf16[192,768]{1,0:T(8,128)(2,1)S(1)} %get-tuple-element.74), channel_id=1, source_target_pairs={{0,8},{4,12},{8,0},{12,4},{1,9},{5,13},{9,1},{13,5},{2,10},{6,14},... | collective-permute-start | bytes 884744 | tf_op jit(solution)/shard_map/ppermute | solution.py:22
  105.0 14.9 %collective-permute-start.29 = (bf16[384,768]{1,0:T(8,128)(2,1)S(1)}, bf16[384,768]{1,0:T(8,128)(2,1)S(1)}, u32[]{:S(2)}, u32[]{:S(2)}) collective-permute-start(bf16[384,768]{1,0:T(8,128)(2,1)S(1)} %get-tuple-element.75), channel_id=1, source_target_pairs={{0,4},{4,0},{8,12},{12,8},{1,5},{5,1},{9,13},{13,9},{2,6},{6,2},{1... | collective-permute-start | bytes 1769480 | tf_op jit(solution)/shard_map/ppermute | solution.py:22
  106.7 14.3 %collective-permute-start.30 = (bf16[384,768]{1,0:T(8,128)(2,1)S(1)}, bf16[384,768]{1,0:T(8,128)(2,1)S(1)}, u32[]{:S(2)}, u32[]{:S(2)}) collective-permute-start(bf16[384,768]{1,0:T(8,128)(2,1)S(1)} %get-tuple-element.79), channel_id=1, source_target_pairs={{0,8},{4,12},{8,0},{12,4},{1,9},{5,13},{9,1},{13,5},{2,10},{6,14},... | collective-permute-start | bytes 1769480 | tf_op jit(solution)/shard_map/ppermute | solution.py:22
  107.3 15.0 %collective-permute-start.26 = (bf16[96,768]{1,0:T(8,128)(2,1)S(1)}, bf16[96,768]{1,0:T(8,128)(2,1)S(1)}, u32[]{:S(2)}, u32[]{:S(2)}) collective-permute-start(bf16[96,768]{1,0:T(8,128)(2,1)S(1)} %get-tuple-element.94), channel_id=1, source_target_pairs={{0,1},{1,0},{2,3},{3,2},{4,5},{5,4},{6,7},{7,6},{8,9},{9,8},{10,11... | collective-permute-start | bytes 442376 | tf_op jit(solution)/shard_map/ppermute | solution.py:22
  107.4 17.4 %collective-permute-start.27 = (bf16[96,768]{1,0:T(8,128)(2,1)S(1)}, bf16[96,768]{1,0:T(8,128)(2,1)S(1)}, u32[]{:S(2)}, u32[]{:S(2)}) collective-permute-start(bf16[96,768]{1,0:T(8,128)(2,1)S(1)} %get-tuple-element.93), channel_id=1, source_target_pairs={{0,2},{1,3},{2,0},{3,1},{4,6},{5,7},{6,4},{7,5},{8,10},{9,11},{10,... | collective-permute-start | bytes 442376 | tf_op jit(solution)/shard_map/ppermute | solution.py:22
  108.4 16.5 %collective-permute-start.28 = (bf16[96,768]{1,0:T(8,128)(2,1)S(1)}, bf16[96,768]{1,0:T(8,128)(2,1)S(1)}, u32[]{:S(2)}, u32[]{:S(2)}) collective-permute-start(bf16[96,768]{1,0:T(8,128)(2,1)S(1)} %get-tuple-element.92), channel_id=1, source_target_pairs={{0,3},{1,2},{2,1},{3,0},{4,7},{5,6},{6,5},{7,4},{8,11},{9,10},{10,... | collective-permute-start | bytes 442376 | tf_op jit(solution)/shard_map/ppermute | solution.py:22
  121.3 6.8 %collective-permute-start.31 = (bf16[96,768]{1,0:T(8,128)(2,1)S(1)}, bf16[96,768]{1,0:T(8,128)(2,1)S(1)}, u32[]{:S(2)}, u32[]{:S(2)}) collective-permute-start(bf16[96,768]{1,0:T(8,128)(2,1)S(1)} %get-tuple-element.91), channel_id=1, source_target_pairs={{0,1},{1,0},{2,3},{3,2},{4,5},{5,4},{6,7},{7,6},{8,9},{9,8},{10,11... | collective-permute-start | bytes 442376 | tf_op jit(solution)/shard_map/ppermute | solution.py:22
  121.4 11.1 %collective-permute-start.35 = (bf16[96,768]{1,0:T(8,128)(2,1)S(1)}, bf16[96,768]{1,0:T(8,128)(2,1)S(1)}, u32[]{:S(2)}, u32[]{:S(2)}) collective-permute-start(bf16[96,768]{1,0:T(8,128)(2,1)S(1)} %get-tuple-element.90), channel_id=1, source_target_pairs={{0,2},{1,3},{2,0},{3,1},{4,6},{5,7},{6,4},{7,5},{8,10},{9,11},{10,... | collective-permute-start | bytes 442376 | tf_op jit(solution)/shard_map/ppermute | solution.py:22
  122.4 13.4 %collective-permute-start.36 = (bf16[96,768]{1,0:T(8,128)(2,1)S(1)}, bf16[96,768]{1,0:T(8,128)(2,1)S(1)}, u32[]{:S(2)}, u32[]{:S(2)}) collective-permute-start(bf16[96,768]{1,0:T(8,128)(2,1)S(1)} %get-tuple-element.89), channel_id=1, source_target_pairs={{0,3},{1,2},{2,1},{3,0},{4,7},{5,6},{6,5},{7,4},{8,11},{9,10},{10,... | collective-permute-start | bytes 442376 | tf_op jit(solution)/shard_map/ppermute | solution.py:22
  129.0 9.1 %collective-permute-start.32 = (bf16[128,768]{1,0:T(8,128)(2,1)S(1)}, bf16[128,768]{1,0:T(8,128)(2,1)S(1)}, u32[]{:S(2)}, u32[]{:S(2)}) collective-permute-start(bf16[128,768]{1,0:T(8,128)(2,1)S(1)} %get-tuple-element.87.refs_0_), channel_id=1, source_target_pairs={{0,4},{4,0},{8,12},{12,8},{1,5},{5,1},{9,13},{13,9},{2,6},{6,2},{1... | collective-permute-start | bytes 589832 | tf_op jit(solution)/shard_map/ppermute | solution.py:22
  129.6 10.3 %collective-permute-start.33 = (bf16[128,768]{1,0:T(8,128)(2,1)S(1)}, bf16[128,768]{1,0:T(8,128)(2,1)S(1)}, u32[]{:S(2)}, u32[]{:S(2)}) collective-permute-start(bf16[128,768]{1,0:T(8,128)(2,1)S(1)} %get-tuple-element.87.refs_0_), channel_id=1, source_target_pairs={{0,8},{4,12},{8,0},{12,4},{1,9},{5,13},{9,1},{13,5},{2,10},{6,14},... | collective-permute-start | bytes 589832 | tf_op jit(solution)/shard_map/ppermute | solution.py:22
  130.0 17.8 %collective-permute-start.34 = (bf16[128,768]{1,0:T(8,128)(2,1)S(1)}, bf16[128,768]{1,0:T(8,128)(2,1)S(1)}, u32[]{:S(2)}, u32[]{:S(2)}) collective-permute-start(bf16[128,768]{1,0:T(8,128)(2,1)S(1)} %get-tuple-element.87.refs_0_), channel_id=1, source_target_pairs={{0,12},{4,8},{8,4},{12,0},{1,13},{5,9},{9,5},{13,1},{2,14},{6,10},... | collective-permute-start | bytes 589832 | tf_op jit(solution)/shard_map/ppermute | solution.py:22
  136.4 12.4 %collective-permute-start.37 = (bf16[128,768]{1,0:T(8,128)(2,1)S(1)}, bf16[128,768]{1,0:T(8,128)(2,1)S(1)}, u32[]{:S(2)}, u32[]{:S(2)}) collective-permute-start(bf16[128,768]{1,0:T(8,128)(2,1)S(1)} %fusion.4.refs_0_), channel_id=1, source_target_pairs={{0,4},{4,0},{8,12},{12,8},{1,5},{5,1},{9,13},{13,9},{2,6},{6,2},{1... | collective-permute-start | bytes 589832 | tf_op jit(solution)/shard_map/ppermute | solution.py:22
  137.3 11.5 %collective-permute-start.38 = (bf16[128,768]{1,0:T(8,128)(2,1)S(1)}, bf16[128,768]{1,0:T(8,128)(2,1)S(1)}, u32[]{:S(2)}, u32[]{:S(2)}) collective-permute-start(bf16[128,768]{1,0:T(8,128)(2,1)S(1)} %fusion.4.refs_0_), channel_id=1, source_target_pairs={{0,8},{4,12},{8,0},{12,4},{1,9},{5,13},{9,1},{13,5},{2,10},{6,14},... | collective-permute-start | bytes 589832 | tf_op jit(solution)/shard_map/ppermute | solution.py:22
  138.1 10.7 %collective-permute-start.39 = (bf16[128,768]{1,0:T(8,128)(2,1)S(1)}, bf16[128,768]{1,0:T(8,128)(2,1)S(1)}, u32[]{:S(2)}, u32[]{:S(2)}) collective-permute-start(bf16[128,768]{1,0:T(8,128)(2,1)S(1)} %fusion.4.refs_0_), channel_id=1, source_target_pairs={{0,12},{4,8},{8,4},{12,0},{1,13},{5,9},{9,5},{13,1},{2,14},{6,10},... | collective-permute-start | bytes 589832 | tf_op jit(solution)/shard_map/ppermute | solution.py:22
  140.0 1.2 collective-permute-start.40
  141.2 5.1 %collective-permute-start.41 = (f32[2,128]{1,0:T(2,128)S(1)}, f32[2,128]{1,0:T(2,128)S(1)}, u32[]{:S(2)}, u32[]{:S(2)}) collective-permute-start(f32[2,128]{1,0:T(2,128)S(1)} %add.49), channel_id=1, source_target_pairs={{0,4},{4,0},{8,12},{12,8},{1,5},{5,1},{9,13},{13,9},{2,6},{6,2},{1... | collective-permute-start | bytes 3080 | tf_op jit(solution)/shard_map/ppermute | solution.py:22
  146.3 3.6 %collective-permute-start.42 = (f32[2,128]{1,0:T(2,128)S(1)}, f32[2,128]{1,0:T(2,128)S(1)}, u32[]{:S(2)}, u32[]{:S(2)}) collective-permute-start(f32[2,128]{1,0:T(2,128)S(1)} %add.50), channel_id=1, source_target_pairs={{0,8},{4,12},{8,0},{12,4},{1,9},{5,13},{9,1},{13,5},{2,10},{6,14},... | collective-permute-start | bytes 3080 | tf_op jit(solution)/shard_map/ppermute | solution.py:22
  (1 other events, 2.6 us)

commit v10 on v7

--- a/solution.py
+++ b/solution.py
@@ -197,7 +197,7 @@
     )
 
 
-STRIP = 32
+STRIP = 16
 LIMIT = 8
 
 

time: 150 us -> 150 us (level)
  no operation moved by 1% of the time
where the time goes in v10:
time: 150 us; the launch traced here: 149 us
  Pallas kernels  61.8 us (41%)
  starting transfers between devices  45.3 us (30%)
  waiting for transfers between devices  34.7 us (23%)
  other arithmetic  3.53 us (2%)
  matrix products  2.49 us (2%)
    pallas_call x14, Pallas kernels, call(): pl.pallas_call(kernel, in_specs=[SMEM] + [VMEM] * (len(ins) - far) + [HBM...  57.1 us
    ppermute x43, starting transfers between devices, exchange(): return lax.ppermute(array, axis, [(i, i ^ bit) for i in range(size)])  45.3 us
    ppermute x43, waiting for transfers between devices, exchange(): return lax.ppermute(array, axis, [(i, i ^ bit) for i in range(size)])  34.7 us
    pallas_call x1, Pallas kernels, fetch(): pl.pallas_call(kernel, in_specs=[HBM], out_specs=VMEM, out_shape=pltpu.VM...  4.66 us
  transfers between devices with their start and end apart: 43, of which 18 were waited for; matrix products, arithmetic and copies ran while one was open for 2% of the time, Pallas kernels for 41%

profile of v10, /device:TPU:16, one launch (start us, length us, event | category | flops | bytes accessed | tf_op | source)
XLA Modules:
  0.0 149.3 jit_solution(6332498166509249176)
XLA Ops:
  3.6 1.6 %collective-permute-start.2 = (bf16[96,768]{1,0:T(8,128)(2,1)S(1)}, bf16[96,768]{1,0:T(8,128)(2,1)S(1)}, u32[]{:S(2)}, u32[]{:S(2)}) collective-permute-start(bf16[96,768]{1,0:T(8,128)(2,1)S(1)} %get-tuple-element.97), channel_id=1, source_target_pairs={{0,1},{1,0},{2,3},{3,2},{4,5},{5,4},{6,7},{7,6},{8,9},{9,8},{10,11... | collective-permute-start | bytes 442376 | tf_op jit(solution)/shard_map/ppermute | solution.py:22
  5.5 1.6 %collective-permute-start.1 = (bf16[96,768]{1,0:T(8,128)(2,1)S(1)}, bf16[96,768]{1,0:T(8,128)(2,1)S(1)}, u32[]{:S(2)}, u32[]{:S(2)}) collective-permute-start(bf16[96,768]{1,0:T(8,128)(2,1)S(1)} %get-tuple-element.98), channel_id=1, source_target_pairs={{0,3},{1,2},{2,1},{3,0},{4,7},{5,6},{6,5},{7,4},{8,11},{9,10},{10,... | collective-permute-start | bytes 442376 | tf_op jit(solution)/shard_map/ppermute | solution.py:22
  7.1 3.2 %collective-permute-done.2.refs_0_ = bf16[96,768]{1,0:T(8,128)(2,1)S(1)} collective-permute-done((bf16[96,768]{1,0:T(8,128)(2,1)S(1)}, bf16[96,768]{1,0:T(8,128)(2,1)S(1)}, u32[]{:S(2)}, u32[]{:S(2)}) %collective-permute-start.2) | collective-permute-done | bytes 147488 | tf_op jit(solution)/shard_map/ppermute | solution.py:22
  10.4 1.5 %collective-permute-start.3 = (bf16[96,768]{1,0:T(8,128)(2,1)S(1)}, bf16[96,768]{1,0:T(8,128)(2,1)S(1)}, u32[]{:S(2)}, u32[]{:S(2)}) collective-permute-start(bf16[96,768]{1,0:T(8,128)(2,1)S(1)} %collective-permute-done.2.refs_0_), channel_id=1, source_target_pairs={{0,4},{4,0},{8,12},{12,8},{1,5},{5,1},{9,13},{13,9},{2,6},{6,2},{1... | collective-permute-start | bytes 442376 | tf_op jit(solution)/shard_map/ppermute | solution.py:22
  11.9 1.5 %collective-permute-start.4 = (bf16[96,768]{1,0:T(8,128)(2,1)S(1)}, bf16[96,768]{1,0:T(8,128)(2,1)S(1)}, u32[]{:S(2)}, u32[]{:S(2)}) collective-permute-start(bf16[96,768]{1,0:T(8,128)(2,1)S(1)} %collective-permute-done.2.refs_0_), channel_id=1, source_target_pairs={{0,8},{4,12},{8,0},{12,4},{1,9},{5,13},{9,1},{13,5},{2,10},{6,14},... | collective-permute-start | bytes 442376 | tf_op jit(solution)/shard_map/ppermute | solution.py:22
  13.9 4.7 %fetch.1.refs_9_ = bf16[3072,2048]{1,0:T(8,128)(2,1)S(1)} custom-call(bf16[3072,2048]{1,0:T(8,128)(2,1)} %bitcast.38), custom_call_target="tpu_custom_call" | custom-call | bytes 12582912 | tf_op jit(solution)/shard_map/fetch/pallas_call | solution.py:65
  18.8 1.2 collective-permute-done.1
  20.0 1.6 %collective-permute-start.9 = (bf16[192,768]{1,0:T(8,128)(2,1)S(1)}, bf16[192,768]{1,0:T(8,128)(2,1)S(1)}, u32[]{:S(2)}, u32[]{:S(2)}) collective-permute-start(bf16[192,768]{1,0:T(8,128)(2,1)S(1)} %constant_dynamic-update-slice_fusion.refs_1_), channel_id=1, source_target_pairs={{0,8},{4,12},{8,0},{12,4},{1,9},{5,13},{9,1},{13,5},{2,10},{6,14},... | collective-permute-start | bytes 884744 | tf_op jit(solution)/shard_map/ppermute | solution.py:22
  21.6 1.5 collective-permute-start.11
  23.4 1.3 collective-permute-start.6
  25.4 1.6 %collective-permute-start.8 = (bf16[96,768]{1,0:T(8,128)(2,1)S(1)}, bf16[96,768]{1,0:T(8,128)(2,1)S(1)}, u32[]{:S(2)}, u32[]{:S(2)}) collective-permute-start(bf16[96,768]{1,0:T(8,128)(2,1)S(1)} %get-tuple-element.94), channel_id=1, source_target_pairs={{0,3},{1,2},{2,1},{3,0},{4,7},{5,6},{6,5},{7,4},{8,11},{9,10},{10,... | collective-permute-start | bytes 442376 | tf_op jit(solution)/shard_map/ppermute | solution.py:22
  27.9 1.6 %collective-permute-start.10 = (bf16[96,768]{1,0:T(8,128)(2,1)S(1)}, bf16[96,768]{1,0:T(8,128)(2,1)S(1)}, u32[]{:S(2)}, u32[]{:S(2)}) collective-permute-start(bf16[96,768]{1,0:T(8,128)(2,1)S(1)} %slice.108), channel_id=1, source_target_pairs={{0,4},{4,0},{8,12},{12,8},{1,5},{5,1},{9,13},{13,9},{2,6},{6,2},{1... | collective-permute-start | bytes 442376 | tf_op jit(solution)/shard_map/ppermute | solution.py:22
  29.6 1.4 collective-permute-start.12
  31.0 3.4 %collective-permute-done.7 = bf16[96,768]{1,0:T(8,128)(2,1)S(1)} collective-permute-done((bf16[96,768]{1,0:T(8,128)(2,1)S(1)}, bf16[96,768]{1,0:T(8,128)(2,1)S(1)}, u32[]{:S(2)}, u32[]{:S(2)}) %collective-permute-start.7) | collective-permute-done | bytes 147488 | tf_op jit(solution)/shard_map/ppermute | solution.py:22
  34.4 3.8 %collective-permute-done.8 = bf16[96,768]{1,0:T(8,128)(2,1)S(1)} collective-permute-done((bf16[96,768]{1,0:T(8,128)(2,1)S(1)}, bf16[96,768]{1,0:T(8,128)(2,1)S(1)}, u32[]{:S(2)}, u32[]{:S(2)}) %collective-permute-start.8) | collective-permute-done | bytes 147488 | tf_op jit(solution)/shard_map/ppermute | solution.py:22
  39.9 6.8 %pre_acts.2 = (f32[384,1024]{1,0:T(8,128)S(1)}, f32[384,1024]{1,0:T(8,128)S(1)}, bf16[384,2048]{1,0:T(8,128)(2,1)S(1)}) custom-call(s32[1]{0:T(128)} %bitcast.t_ref, bf16[96,3072]{1,0:T(8,128)(2,1)S(1)} %convolution_convert_fusion.own_ref, bf16[96,768]{1,0:T(8,128)(2,1)S(1)} %collective-permute-done.2.refs_0_, ...), custom_call_target="tpu_custom_call" | custom-call | flops 2415919104 | bytes 1048576 | tf_op jit(solution)/shard_map/pre_acts/pallas_call | solution.py:47
  46.7 2.9 %collective-permute-done.14.refs_1_ = bf16[288,768]{1,0:T(8,128)(2,1)S(1)} collective-permute-done((bf16[288,768]{1,0:T(8,128)(2,1)S(1)}, bf16[288,768]{1,0:T(8,128)(2,1)S(1)}, u32[]{:S(2)}, u32[]{:S(2)}) %collective-permute-start.14) | collective-permute-done | bytes 442400 | tf_op jit(solution)/shard_map/ppermute | solution.py:22
  49.7 6.6 %pre_acts.3 = (f32[384,1024]{1,0:T(8,128)S(1)}, f32[384,1024]{1,0:T(8,128)S(1)}, bf16[384,2048]{1,0:T(8,128)(2,1)S(1)}) custom-call(s32[1]{0:T(128)} %bitcast.t_ref, bf16[96,3072]{1,0:T(8,128)(2,1)S(1)} %convolution_convert_fusion.own_ref, bf16[96,768]{1,0:T(8,128)(2,1)S(1)} %collective-permute-done.2.refs_0_, ...), custom_call_target="tpu_custom_call" | custom-call | flops 2415919104 | bytes 1048576 | tf_op jit(solution)/shard_map/pre_acts/pallas_call | solution.py:47
  56.3 1.6 %collective-permute-start.19 = (bf16[288,768]{1,0:T(8,128)(2,1)S(1)}, bf16[288,768]{1,0:T(8,128)(2,1)S(1)}, u32[]{:S(2)}, u32[]{:S(2)}) collective-permute-start(bf16[288,768]{1,0:T(8,128)(2,1)S(1)} %constant_dynamic-update-slice_fusion.2.refs_0_), channel_id=1, source_target_pairs={{0,12},{4,8},{8,4},{12,0},{1,13},{5,9},{9,5},{13,1},{2,14},{6,10},... | collective-permute-start | bytes 1327112 | tf_op jit(solution)/shard_map/ppermute | solution.py:22
  57.9 1.8 %collective-permute-done.16.refs_5_.refs_7_ = bf16[384,2048]{1,0:T(8,128)(2,1)S(1)} collective-permute-done((bf16[384,2048]{1,0:T(8,128)(2,1)S(1)}, bf16[384,2048]{1,0:T(8,128)(2,1)S(1)}, u32[]{:S(2)}, u32[]{:S(2)}) %collective-permute-start.16) | collective-permute-done | bytes 1572896 | tf_op jit(solution)/shard_map/ppermute | solution.py:22
  59.7 3.7 %project_first.1 = (bf16[192,768]{1,0:T(8,128)(2,1)S(1)}, bf16[192,768]{1,0:T(8,128)(2,1)S(1)}, bf16[384,2048]{1,0:T(8,128)(2,1)S(1)}) custom-call(s32[1]{0:T(128)} %bitcast.t_ref, f32[384,1024]{1,0:T(8,128)S(1)} %get-tuple-element.50.refs_0_, f32[384,1024]{1,0:T(8,128)S(1)} %get-tuple-element.51.refs_1_, ...), custom_call_target="tpu_custom_call" | custom-call | flops 603979776 | bytes 1048576 | tf_op jit(solution)/shard_map/project_first/pallas_call | solution.py:47
  63.4 1.7 %collective-permute-start.17 = (bf16[192,768]{1,0:T(8,128)(2,1)S(1)}, bf16[192,768]{1,0:T(8,128)(2,1)S(1)}, u32[]{:S(2)}, u32[]{:S(2)}) collective-permute-start(bf16[192,768]{1,0:T(8,128)(2,1)S(1)} %get-tuple-element.58), channel_id=1, source_target_pairs={{0,4},{4,0},{8,12},{12,8},{1,5},{5,1},{9,13},{13,9},{2,6},{6,2},{1... | collective-permute-start | bytes 884744 | tf_op jit(solution)/shard_map/ppermute | solution.py:22
  65.9 5.4 %project_send.1.both_ref = f32[2,384,768]{2,1,0:T(8,128)S(1)} custom-call(s32[1]{0:T(128)} %bitcast.t_ref, bf16[384,2048]{1,0:T(8,128)(2,1)S(1)} %get-tuple-element.57.refs_0_, bf16[2048,3072]{1,0:T(8,128)(2,1)} %bitcast.29), custom_call_target="tpu_custom_call" | custom-call | flops 1207959552 | bytes 1048576 | tf_op jit(solution)/shard_map/project_send/pallas_call | solution.py:47
  71.3 4.7 %grad_hidden.3 = (f32[384,1024]{1,0:T(8,128)S(1)}, bf16[384,1024]{1,0:T(8,128)(2,1)S(1)}) custom-call(s32[1]{0:T(128)} %bitcast.t_ref, bf16[96,3072]{1,0:T(8,128)(2,1)S(1)} %fusion.own_ref, bf16[288,768]{1,0:T(8,128)(2,1)S(1)} %constant_dynamic-update-slice_fusion.2.refs_0_, bf16[288,768]{1,0:T(8,128)(2,1)S(1)} %collective-permute-done.14.refs_1_, ...), custom_call_target="tpu_custom_call" | custom-call | flops 1207959552 | bytes 1048576 | tf_op jit(solution)/shard_map/grad_hidden/pallas_call | solution.py:47
  76.3 4.7 %grad_hidden.2 = (f32[384,1024]{1,0:T(8,128)S(1)}, bf16[384,1024]{1,0:T(8,128)(2,1)S(1)}) custom-call(s32[1]{0:T(128)} %bitcast.t_ref, bf16[96,3072]{1,0:T(8,128)(2,1)S(1)} %fusion.own_ref, bf16[288,768]{1,0:T(8,128)(2,1)S(1)} %constant_dynamic-update-slice_fusion.2.refs_0_, bf16[288,768]{1,0:T(8,128)(2,1)S(1)} %collective-permute-done.14.refs_1_, ...), custom_call_target="tpu_custom_call" | custom-call | flops 1207959552 | bytes 1048576 | tf_op jit(solution)/shard_map/grad_hidden/pallas_call | solution.py:47
  81.5 1.3 collective-permute-start.24
  83.5 3.6 %project_keep.1 = f32[1,384,768]{2,1,0:T(8,128)S(1)} custom-call(s32[1]{0:T(128)} %bitcast.t_ref, bf16[384,2048]{1,0:T(8,128)(2,1)S(1)} %get-tuple-element.57.refs_0_, bf16[2048,3072]{1,0:T(8,128)(2,1)} %bitcast.32), custom_call_target="tpu_custom_call" | custom-call | flops 603979776 | bytes 1048576 | tf_op jit(solution)/shard_map/project_keep/pallas_call | solution.py:47
  87.2 5.6 %rows_first.1 = (bf16[192,768]{1,0:T(8,128)(2,1)S(1)}, bf16[192,768]{1,0:T(8,128)(2,1)S(1)}, bf16[384,2048]{1,0:T(8,128)(2,1)S(1)}, bf16[384,2048]{1,0:T(8,128)(2,1)S(1)}) custom-call(s32[1]{0:T(128)} %bitcast.t_ref, f32[384,1024]{1,0:T(8,128)S(1)} %get-tuple-element.50.refs_0_, f32[384,1024]{1,0:T(8,128)S(1)} %get-tuple-element.51.refs_1_, ...), custom_call_target="tpu_custom_call" | custom-call | flops 1207959552 | bytes 1048576 | tf_op jit(solution)/shard_map/rows_first/pallas_call | solution.py:47
  92.8 1.7 %collective-permute-start.22 = (bf16[192,768]{1,0:T(8,128)(2,1)S(1)}, bf16[192,768]{1,0:T(8,128)(2,1)S(1)}, u32[]{:S(2)}, u32[]{:S(2)}) collective-permute-start(bf16[192,768]{1,0:T(8,128)(2,1)S(1)} %get-tuple-element.71), channel_id=1, source_target_pairs={{0,4},{4,0},{8,12},{12,8},{1,5},{5,1},{9,13},{13,9},{2,6},{6,2},{1... | collective-permute-start | bytes 884744 | tf_op jit(solution)/shard_map/ppermute | solution.py:22
  94.9 8.6 %rows_send.1.both_ref = f32[2,384,768]{2,1,0:T(8,128)S(1)} custom-call(s32[1]{0:T(128)} %bitcast.t_ref, bf16[384,2048]{1,0:T(8,128)(2,1)S(1)} %get-tuple-element.69.refs_0_, bf16[384,2048]{1,0:T(8,128)(2,1)S(1)} %get-tuple-element.70.refs_1_, bf16[3072,2048]{1,0:T(8,128)(2,1)} %bitcast.40, bf16[3072,2048]{1,0:T(8,128)(2,1)} %bitcast.36), custom_call_target="tpu_custom_call" | custom-call | flops 2415919104 | bytes 1048576 | tf_op jit(solution)/shard_map/rows_send/pallas_call | solution.py:47
  103.6 1.0 collective-permute-done.23.low_ref
  105.1 1.6 %collective-permute-start.30 = (bf16[384,768]{1,0:T(8,128)(2,1)S(1)}, bf16[384,768]{1,0:T(8,128)(2,1)S(1)}, u32[]{:S(2)}, u32[]{:S(2)}) collective-permute-start(bf16[384,768]{1,0:T(8,128)(2,1)S(1)} %get-tuple-element.77), channel_id=1, source_target_pairs={{0,8},{4,12},{8,0},{12,4},{1,9},{5,13},{9,1},{13,5},{2,10},{6,14},... | collective-permute-start | bytes 1769480 | tf_op jit(solution)/shard_map/ppermute | solution.py:22
  107.1 1.0 collective-permute-start.27
  108.1 2.5 %collective-permute-start.28 = (bf16[96,768]{1,0:T(8,128)(2,1)S(1)}, bf16[96,768]{1,0:T(8,128)(2,1)S(1)}, u32[]{:S(2)}, u32[]{:S(2)}) collective-permute-start(bf16[96,768]{1,0:T(8,128)(2,1)S(1)} %get-tuple-element.90), channel_id=1, source_target_pairs={{0,3},{1,2},{2,1},{3,0},{4,7},{5,6},{6,5},{7,4},{8,11},{9,10},{10,... | collective-permute-start | bytes 442376 | tf_op jit(solution)/shard_map/ppermute | solution.py:22
  110.6 5.2 %rows_keep.1 = f32[1,384,768]{2,1,0:T(8,128)S(1)} custom-call(s32[1]{0:T(128)} %bitcast.t_ref, bf16[384,2048]{1,0:T(8,128)(2,1)S(1)} %get-tuple-element.69.refs_0_, bf16[384,2048]{1,0:T(8,128)(2,1)S(1)} %get-tuple-element.70.refs_1_, bf16[3072,2048]{1,0:T(8,128)(2,1)} %bitcast.41, bf16[3072,2048]{1,0:T(8,128)(2,1)} %bitcast.37), custom_call_target="tpu_custom_call" | custom-call | flops 1207959552 | bytes 1048576 | tf_op jit(solution)/shard_map/rows_keep/pallas_call | solution.py:47
  115.8 3.6 %collective-permute-done.29 = bf16[384,768]{1,0:T(8,128)(2,1)S(1)} collective-permute-done((bf16[384,768]{1,0:T(8,128)(2,1)S(1)}, bf16[384,768]{1,0:T(8,128)(2,1)S(1)}, u32[]{:S(2)}, u32[]{:S(2)}) %collective-permute-start.29) | collective-permute-done | bytes 589856 | tf_op jit(solution)/shard_map/ppermute | solution.py:22
  120.0 1.0 collective-permute-start.35
  121.0 2.5 %collective-permute-start.36 = (bf16[96,768]{1,0:T(8,128)(2,1)S(1)}, bf16[96,768]{1,0:T(8,128)(2,1)S(1)}, u32[]{:S(2)}, u32[]{:S(2)}) collective-permute-start(bf16[96,768]{1,0:T(8,128)(2,1)S(1)} %get-tuple-element.87), channel_id=1, source_target_pairs={{0,3},{1,2},{2,1},{3,0},{4,7},{5,6},{6,5},{7,4},{8,11},{9,10},{10,... | collective-permute-start | bytes 442376 | tf_op jit(solution)/shard_map/ppermute | solution.py:22
  123.5 3.3 %collective-permute-done.31 = bf16[96,768]{1,0:T(8,128)(2,1)S(1)} collective-permute-done((bf16[96,768]{1,0:T(8,128)(2,1)S(1)}, bf16[96,768]{1,0:T(8,128)(2,1)S(1)}, u32[]{:S(2)}, u32[]{:S(2)}) %collective-permute-start.31) | collective-permute-done | bytes 147488 | tf_op jit(solution)/shard_map/ppermute | solution.py:22
  127.6 1.5 collective-permute-start.32
  129.6 1.6 %collective-permute-start.34 = (bf16[128,768]{1,0:T(8,128)(2,1)S(1)}, bf16[128,768]{1,0:T(8,128)(2,1)S(1)}, u32[]{:S(2)}, u32[]{:S(2)}) collective-permute-start(bf16[128,768]{1,0:T(8,128)(2,1)S(1)} %get-tuple-element.85.refs_0_), channel_id=1, source_target_pairs={{0,12},{4,8},{8,4},{12,0},{1,13},{5,9},{9,5},{13,1},{2,14},{6,10},... | collective-permute-start | bytes 589832 | tf_op jit(solution)/shard_map/ppermute | solution.py:22
  131.2 3.4 %collective-permute-done.36 = bf16[96,768]{1,0:T(8,128)(2,1)S(1)} collective-permute-done((bf16[96,768]{1,0:T(8,128)(2,1)S(1)}, bf16[96,768]{1,0:T(8,128)(2,1)S(1)}, u32[]{:S(2)}, u32[]{:S(2)}) %collective-permute-start.36) | collective-permute-done | bytes 147488 | tf_op jit(solution)/shard_map/ppermute | solution.py:22
  135.3 1.3 collective-permute-start.37
  137.5 1.4 collective-permute-start.39
  138.9 1.1 collective-permute-done.40
  140.1 1.2 collective-permute-start.41
  141.3 3.9 %collective-permute-done.41 = f32[2,128]{1,0:T(2,128)S(1)} collective-permute-done((f32[2,128]{1,0:T(2,128)S(1)}, f32[2,128]{1,0:T(2,128)S(1)}, u32[]{:S(2)}, u32[]{:S(2)}) %collective-permute-start.41) | collective-permute-done | bytes 1056 | tf_op jit(solution)/shard_map/ppermute | solution.py:22
  145.2 1.3 collective-permute-start.42
  (106 shorter events, 17.7 us)
Async XLA Ops:
  0.6 13.2 %copy-start.4 = (f32[128,2]{0,1:T(2,128)S(1)}, f32[128,2]{0,1:T(2,128)}, u32[]{:S(2)}) copy-start(f32[128,2]{0,1:T(2,128)} %param.9) | copy-start | bytes 3076
  3.6 6.8 %collective-permute-start.2 = (bf16[96,768]{1,0:T(8,128)(2,1)S(1)}, bf16[96,768]{1,0:T(8,128)(2,1)S(1)}, u32[]{:S(2)}, u32[]{:S(2)}) collective-permute-start(bf16[96,768]{1,0:T(8,128)(2,1)S(1)} %get-tuple-element.97), channel_id=1, source_target_pairs={{0,1},{1,0},{2,3},{3,2},{4,5},{5,4},{6,7},{7,6},{8,9},{9,8},{10,11... | collective-permute-start | bytes 442376 | tf_op jit(solution)/shard_map/ppermute | solution.py:22
  5.2 13.6 %collective-permute-start = (bf16[96,768]{1,0:T(8,128)(2,1)S(1)}, bf16[96,768]{1,0:T(8,128)(2,1)S(1)}, u32[]{:S(2)}, u32[]{:S(2)}) collective-permute-start(bf16[96,768]{1,0:T(8,128)(2,1)S(1)} %get-tuple-element.99), channel_id=1, source_target_pairs={{0,2},{1,3},{2,0},{3,1},{4,6},{5,7},{6,4},{7,5},{8,10},{9,11},{10,... | collective-permute-start | bytes 442376 | tf_op jit(solution)/shard_map/ppermute | solution.py:22
  5.5 14.4 %collective-permute-start.1 = (bf16[96,768]{1,0:T(8,128)(2,1)S(1)}, bf16[96,768]{1,0:T(8,128)(2,1)S(1)}, u32[]{:S(2)}, u32[]{:S(2)}) collective-permute-start(bf16[96,768]{1,0:T(8,128)(2,1)S(1)} %get-tuple-element.98), channel_id=1, source_target_pairs={{0,3},{1,2},{2,1},{3,0},{4,7},{5,6},{6,5},{7,4},{8,11},{9,10},{10,... | collective-permute-start | bytes 442376 | tf_op jit(solution)/shard_map/ppermute | solution.py:22
  10.4 9.6 %collective-permute-start.3 = (bf16[96,768]{1,0:T(8,128)(2,1)S(1)}, bf16[96,768]{1,0:T(8,128)(2,1)S(1)}, u32[]{:S(2)}, u32[]{:S(2)}) collective-permute-start(bf16[96,768]{1,0:T(8,128)(2,1)S(1)} %collective-permute-done.2.refs_0_), channel_id=1, source_target_pairs={{0,4},{4,0},{8,12},{12,8},{1,5},{5,1},{9,13},{13,9},{2,6},{6,2},{1... | collective-permute-start | bytes 442376 | tf_op jit(solution)/shard_map/ppermute | solution.py:22
  11.9 8.1 %collective-permute-start.4 = (bf16[96,768]{1,0:T(8,128)(2,1)S(1)}, bf16[96,768]{1,0:T(8,128)(2,1)S(1)}, u32[]{:S(2)}, u32[]{:S(2)}) collective-permute-start(bf16[96,768]{1,0:T(8,128)(2,1)S(1)} %collective-permute-done.2.refs_0_), channel_id=1, source_target_pairs={{0,8},{4,12},{8,0},{12,4},{1,9},{5,13},{9,1},{13,5},{2,10},{6,14},... | collective-permute-start | bytes 442376 | tf_op jit(solution)/shard_map/ppermute | solution.py:22
  13.4 6.6 %collective-permute-start.5 = (bf16[96,768]{1,0:T(8,128)(2,1)S(1)}, bf16[96,768]{1,0:T(8,128)(2,1)S(1)}, u32[]{:S(2)}, u32[]{:S(2)}) collective-permute-start(bf16[96,768]{1,0:T(8,128)(2,1)S(1)} %collective-permute-done.2.refs_0_), channel_id=1, source_target_pairs={{0,12},{4,8},{8,4},{12,0},{1,13},{5,9},{9,5},{13,1},{2,14},{6,10},... | collective-permute-start | bytes 442376 | tf_op jit(solution)/shard_map/ppermute | solution.py:22
  13.9 9.2 %copy-start.2 = (bf16[128,3072]{1,0:T(8,128)(2,1)S(1)}, bf16[128,3072]{1,0:T(8,128)(2,1)}, u32[]{:S(2)}) copy-start(bf16[128,3072]{1,0:T(8,128)(2,1)} %param.13) | copy-start | bytes 2359300
  18.7 39.2 %copy-start.3 = (f32[384]{0:T(512)}, f32[384]{0:T(512)S(1)}, u32[]{:S(2)}) copy-start(f32[384]{0:T(512)S(1)} %add_reduce_fusion) | copy-start | bytes 4612
  20.0 7.9 %collective-permute-start.9 = (bf16[192,768]{1,0:T(8,128)(2,1)S(1)}, bf16[192,768]{1,0:T(8,128)(2,1)S(1)}, u32[]{:S(2)}, u32[]{:S(2)}) collective-permute-start(bf16[192,768]{1,0:T(8,128)(2,1)S(1)} %constant_dynamic-update-slice_fusion.refs_1_), channel_id=1, source_target_pairs={{0,8},{4,12},{8,0},{12,4},{1,9},{5,13},{9,1},{13,5},{2,10},{6,14},... | collective-permute-start | bytes 884744 | tf_op jit(solution)/shard_map/ppermute | solution.py:22
  21.6 8.0 %collective-permute-start.11 = (bf16[192,768]{1,0:T(8,128)(2,1)S(1)}, bf16[192,768]{1,0:T(8,128)(2,1)S(1)}, u32[]{:S(2)}, u32[]{:S(2)}) collective-permute-start(bf16[192,768]{1,0:T(8,128)(2,1)S(1)} %constant_dynamic-update-slice_fusion.refs_1_), channel_id=1, source_target_pairs={{0,4},{4,0},{8,12},{12,8},{1,5},{5,1},{9,13},{13,9},{2,6},{6,2},{1... | collective-permute-start | bytes 884744 | tf_op jit(solution)/shard_map/ppermute | solution.py:22
  23.4 7.6 %collective-permute-start.6 = (bf16[96,768]{1,0:T(8,128)(2,1)S(1)}, bf16[96,768]{1,0:T(8,128)(2,1)S(1)}, u32[]{:S(2)}, u32[]{:S(2)}) collective-permute-start(bf16[96,768]{1,0:T(8,128)(2,1)S(1)} %get-tuple-element.96), channel_id=1, source_target_pairs={{0,1},{1,0},{2,3},{3,2},{4,5},{5,4},{6,7},{7,6},{8,9},{9,8},{10,11... | collective-permute-start | bytes 442376 | tf_op jit(solution)/shard_map/ppermute | solution.py:22
  24.6 9.7 %collective-permute-start.7 = (bf16[96,768]{1,0:T(8,128)(2,1)S(1)}, bf16[96,768]{1,0:T(8,128)(2,1)S(1)}, u32[]{:S(2)}, u32[]{:S(2)}) collective-permute-start(bf16[96,768]{1,0:T(8,128)(2,1)S(1)} %get-tuple-element.95), channel_id=1, source_target_pairs={{0,2},{1,3},{2,0},{3,1},{4,6},{5,7},{6,4},{7,5},{8,10},{9,11},{10,... | collective-permute-start | bytes 442376 | tf_op jit(solution)/shard_map/ppermute | solution.py:22
  25.4 12.9 %collective-permute-start.8 = (bf16[96,768]{1,0:T(8,128)(2,1)S(1)}, bf16[96,768]{1,0:T(8,128)(2,1)S(1)}, u32[]{:S(2)}, u32[]{:S(2)}) collective-permute-start(bf16[96,768]{1,0:T(8,128)(2,1)S(1)} %get-tuple-element.94), channel_id=1, source_target_pairs={{0,3},{1,2},{2,1},{3,0},{4,7},{5,6},{6,5},{7,4},{8,11},{9,10},{10,... | collective-permute-start | bytes 442376 | tf_op jit(solution)/shard_map/ppermute | solution.py:22
  27.9 10.4 %collective-permute-start.10 = (bf16[96,768]{1,0:T(8,128)(2,1)S(1)}, bf16[96,768]{1,0:T(8,128)(2,1)S(1)}, u32[]{:S(2)}, u32[]{:S(2)}) collective-permute-start(bf16[96,768]{1,0:T(8,128)(2,1)S(1)} %slice.108), channel_id=1, source_target_pairs={{0,4},{4,0},{8,12},{12,8},{1,5},{5,1},{9,13},{13,9},{2,6},{6,2},{1... | collective-permute-start | bytes 442376 | tf_op jit(solution)/shard_map/ppermute | solution.py:22
  29.6 8.6 %collective-permute-start.12 = (bf16[96,768]{1,0:T(8,128)(2,1)S(1)}, bf16[96,768]{1,0:T(8,128)(2,1)S(1)}, u32[]{:S(2)}, u32[]{:S(2)}) collective-permute-start(bf16[96,768]{1,0:T(8,128)(2,1)S(1)} %slice.109), channel_id=1, source_target_pairs={{0,8},{4,12},{8,0},{12,4},{1,9},{5,13},{9,1},{13,5},{2,10},{6,14},... | collective-permute-start | bytes 442376 | tf_op jit(solution)/shard_map/ppermute | solution.py:22
  38.3 11.3 %collective-permute-start.14 = (bf16[288,768]{1,0:T(8,128)(2,1)S(1)}, bf16[288,768]{1,0:T(8,128)(2,1)S(1)}, u32[]{:S(2)}, u32[]{:S(2)}) collective-permute-start(bf16[288,768]{1,0:T(8,128)(2,1)S(1)} %constant_dynamic-update-slice_fusion.2.refs_0_), channel_id=1, source_target_pairs={{0,4},{4,0},{8,12},{12,8},{1,5},{5,1},{9,13},{13,9},{2,6},{6,2},{1... | collective-permute-start | bytes 1327112 | tf_op jit(solution)/shard_map/ppermute | solution.py:22
  38.9 10.8 %collective-permute-start.15 = (bf16[288,768]{1,0:T(8,128)(2,1)S(1)}, bf16[288,768]{1,0:T(8,128)(2,1)S(1)}, u32[]{:S(2)}, u32[]{:S(2)}) collective-permute-start(bf16[288,768]{1,0:T(8,128)(2,1)S(1)} %constant_dynamic-update-slice_fusion.2.refs_0_), channel_id=1, source_target_pairs={{0,8},{4,12},{8,0},{12,4},{1,9},{5,13},{9,1},{13,5},{2,10},{6,14},... | collective-permute-start | bytes 1327112 | tf_op jit(solution)/shard_map/ppermute | solution.py:22
  46.7 11.3 %collective-permute-start.13 = (bf16[384,2048]{1,0:T(8,128)(2,1)S(1)}, bf16[384,2048]{1,0:T(8,128)(2,1)S(1)}, u32[]{:S(2)}, u32[]{:S(2)}) collective-permute-start(bf16[384,2048]{1,0:T(8,128)(2,1)S(1)} %get-tuple-element.52), channel_id=1, source_target_pairs={{0,16},{16,0},{1,17},{17,1},{2,18},{18,2},{3,19},{19,3},{4,20},{20... | collective-permute-start | bytes 4718600 | tf_op jit(solution)/shard_map/ppermute | solution.py:22
  56.3 3.5 %collective-permute-start.16 = (bf16[384,2048]{1,0:T(8,128)(2,1)S(1)}, bf16[384,2048]{1,0:T(8,128)(2,1)S(1)}, u32[]{:S(2)}, u32[]{:S(2)}) collective-permute-start(bf16[384,2048]{1,0:T(8,128)(2,1)S(1)} %get-tuple-element.56), channel_id=1, source_target_pairs={{0,16},{16,0},{1,17},{17,1},{2,18},{18,2},{3,19},{19,3},{4,20},{20... | collective-permute-start | bytes 4718600 | tf_op jit(solution)/shard_map/ppermute | solution.py:22
  56.3 14.9 %collective-permute-start.19 = (bf16[288,768]{1,0:T(8,128)(2,1)S(1)}, bf16[288,768]{1,0:T(8,128)(2,1)S(1)}, u32[]{:S(2)}, u32[]{:S(2)}) collective-permute-start(bf16[288,768]{1,0:T(8,128)(2,1)S(1)} %constant_dynamic-update-slice_fusion.2.refs_0_), channel_id=1, source_target_pairs={{0,12},{4,8},{8,4},{12,0},{1,13},{5,9},{9,5},{13,1},{2,14},{6,10},... | collective-permute-start | bytes 1327112 | tf_op jit(solution)/shard_map/ppermute | solution.py:22
  59.7 5.8 %slice-start = ((f32[384]{0:T(512)}), f32[96]{0:T(128)S(1)}, s32[]{:S(2)}) async-start(f32[384]{0:T(512)} %copy-done.3), calls=%async_computation | async-start | bytes 1024 | tf_op jit(solution)/shard_map/slice | solution.py:419
  63.4 12.7 %collective-permute-start.17 = (bf16[192,768]{1,0:T(8,128)(2,1)S(1)}, bf16[192,768]{1,0:T(8,128)(2,1)S(1)}, u32[]{:S(2)}, u32[]{:S(2)}) collective-permute-start(bf16[192,768]{1,0:T(8,128)(2,1)S(1)} %get-tuple-element.58), channel_id=1, source_target_pairs={{0,4},{4,0},{8,12},{12,8},{1,5},{5,1},{9,13},{13,9},{2,6},{6,2},{1... | collective-permute-start | bytes 884744 | tf_op jit(solution)/shard_map/ppermute | solution.py:22
  65.2 11.0 %collective-permute-start.18 = (bf16[192,768]{1,0:T(8,128)(2,1)S(1)}, bf16[192,768]{1,0:T(8,128)(2,1)S(1)}, u32[]{:S(2)}, u32[]{:S(2)}) collective-permute-start(bf16[192,768]{1,0:T(8,128)(2,1)S(1)} %get-tuple-element.59), channel_id=1, source_target_pairs={{0,8},{4,12},{8,0},{12,4},{1,9},{5,13},{9,1},{13,5},{2,10},{6,14},... | collective-permute-start | bytes 884744 | tf_op jit(solution)/shard_map/ppermute | solution.py:22
  76.0 11.2 %collective-permute-start.20 = (bf16[384,1024]{1,0:T(8,128)(2,1)S(1)}, bf16[384,1024]{1,0:T(8,128)(2,1)S(1)}, u32[]{:S(2)}, u32[]{:S(2)}) collective-permute-start(bf16[384,1024]{1,0:T(8,128)(2,1)S(1)} %get-tuple-element.67), channel_id=1, source_target_pairs={{0,16},{16,0},{1,17},{17,1},{2,18},{18,2},{3,19},{19,3},{4,20},{20... | collective-permute-start | bytes 2359304 | tf_op jit(solution)/shard_map/ppermute | solution.py:22
  81.0 6.2 %collective-permute-start.21 = (bf16[384,1024]{1,0:T(8,128)(2,1)S(1)}, bf16[384,1024]{1,0:T(8,128)(2,1)S(1)}, u32[]{:S(2)}, u32[]{:S(2)}) collective-permute-start(bf16[384,1024]{1,0:T(8,128)(2,1)S(1)} %get-tuple-element.62), channel_id=1, source_target_pairs={{0,16},{16,0},{1,17},{17,1},{2,18},{18,2},{3,19},{19,3},{4,20},{20... | collective-permute-start | bytes 2359304 | tf_op jit(solution)/shard_map/ppermute | solution.py:22
  81.5 25.2 %collective-permute-start.24 = (bf16[384,768]{1,0:T(8,128)(2,1)S(1)}, bf16[384,768]{1,0:T(8,128)(2,1)S(1)}, u32[]{:S(2)}, u32[]{:S(2)}) collective-permute-start(bf16[384,768]{1,0:T(8,128)(2,1)S(1)} %get-tuple-element.60), channel_id=1, source_target_pairs={{0,4},{4,0},{8,12},{12,8},{1,5},{5,1},{9,13},{13,9},{2,6},{6,2},{1... | collective-permute-start | bytes 1769480 | tf_op jit(solution)/shard_map/ppermute | solution.py:22
  82.8 23.9 %collective-permute-start.25 = (bf16[384,768]{1,0:T(8,128)(2,1)S(1)}, bf16[384,768]{1,0:T(8,128)(2,1)S(1)}, u32[]{:S(2)}, u32[]{:S(2)}) collective-permute-start(bf16[384,768]{1,0:T(8,128)(2,1)S(1)} %get-tuple-element.75), channel_id=1, source_target_pairs={{0,8},{4,12},{8,0},{12,4},{1,9},{5,13},{9,1},{13,5},{2,10},{6,14},... | collective-permute-start | bytes 1769480 | tf_op jit(solution)/shard_map/ppermute | solution.py:22
  92.8 10.7 %collective-permute-start.22 = (bf16[192,768]{1,0:T(8,128)(2,1)S(1)}, bf16[192,768]{1,0:T(8,128)(2,1)S(1)}, u32[]{:S(2)}, u32[]{:S(2)}) collective-permute-start(bf16[192,768]{1,0:T(8,128)(2,1)S(1)} %get-tuple-element.71), channel_id=1, source_target_pairs={{0,4},{4,0},{8,12},{12,8},{1,5},{5,1},{9,13},{13,9},{2,6},{6,2},{1... | collective-permute-start | bytes 884744 | tf_op jit(solution)/shard_map/ppermute | solution.py:22
  94.6 10.0 %collective-permute-start.23 = (bf16[192,768]{1,0:T(8,128)(2,1)S(1)}, bf16[192,768]{1,0:T(8,128)(2,1)S(1)}, u32[]{:S(2)}, u32[]{:S(2)}) collective-permute-start(bf16[192,768]{1,0:T(8,128)(2,1)S(1)} %get-tuple-element.72), channel_id=1, source_target_pairs={{0,8},{4,12},{8,0},{12,4},{1,9},{5,13},{9,1},{13,5},{2,10},{6,14},... | collective-permute-start | bytes 884744 | tf_op jit(solution)/shard_map/ppermute | solution.py:22
  104.7 14.6 %collective-permute-start.29 = (bf16[384,768]{1,0:T(8,128)(2,1)S(1)}, bf16[384,768]{1,0:T(8,128)(2,1)S(1)}, u32[]{:S(2)}, u32[]{:S(2)}) collective-permute-start(bf16[384,768]{1,0:T(8,128)(2,1)S(1)} %get-tuple-element.73), channel_id=1, source_target_pairs={{0,4},{4,0},{8,12},{12,8},{1,5},{5,1},{9,13},{13,9},{2,6},{6,2},{1... | collective-permute-start | bytes 1769480 | tf_op jit(solution)/shard_map/ppermute | solution.py:22
  105.1 14.6 %collective-permute-start.30 = (bf16[384,768]{1,0:T(8,128)(2,1)S(1)}, bf16[384,768]{1,0:T(8,128)(2,1)S(1)}, u32[]{:S(2)}, u32[]{:S(2)}) collective-permute-start(bf16[384,768]{1,0:T(8,128)(2,1)S(1)} %get-tuple-element.77), channel_id=1, source_target_pairs={{0,8},{4,12},{8,0},{12,4},{1,9},{5,13},{9,1},{13,5},{2,10},{6,14},... | collective-permute-start | bytes 1769480 | tf_op jit(solution)/shard_map/ppermute | solution.py:22
  107.0 14.0 %collective-permute-start.26 = (bf16[96,768]{1,0:T(8,128)(2,1)S(1)}, bf16[96,768]{1,0:T(8,128)(2,1)S(1)}, u32[]{:S(2)}, u32[]{:S(2)}) collective-permute-start(bf16[96,768]{1,0:T(8,128)(2,1)S(1)} %get-tuple-element.92), channel_id=1, source_target_pairs={{0,1},{1,0},{2,3},{3,2},{4,5},{5,4},{6,7},{7,6},{8,9},{9,8},{10,11... | collective-permute-start | bytes 442376 | tf_op jit(solution)/shard_map/ppermute | solution.py:22
  107.1 16.4 %collective-permute-start.27 = (bf16[96,768]{1,0:T(8,128)(2,1)S(1)}, bf16[96,768]{1,0:T(8,128)(2,1)S(1)}, u32[]{:S(2)}, u32[]{:S(2)}) collective-permute-start(bf16[96,768]{1,0:T(8,128)(2,1)S(1)} %get-tuple-element.91), channel_id=1, source_target_pairs={{0,2},{1,3},{2,0},{3,1},{4,6},{5,7},{6,4},{7,5},{8,10},{9,11},{10,... | collective-permute-start | bytes 442376 | tf_op jit(solution)/shard_map/ppermute | solution.py:22
  108.1 15.5 %collective-permute-start.28 = (bf16[96,768]{1,0:T(8,128)(2,1)S(1)}, bf16[96,768]{1,0:T(8,128)(2,1)S(1)}, u32[]{:S(2)}, u32[]{:S(2)}) collective-permute-start(bf16[96,768]{1,0:T(8,128)(2,1)S(1)} %get-tuple-element.90), channel_id=1, source_target_pairs={{0,3},{1,2},{2,1},{3,0},{4,7},{5,6},{6,5},{7,4},{8,11},{9,10},{10,... | collective-permute-start | bytes 442376 | tf_op jit(solution)/shard_map/ppermute | solution.py:22
  120.0 6.9 %collective-permute-start.31 = (bf16[96,768]{1,0:T(8,128)(2,1)S(1)}, bf16[96,768]{1,0:T(8,128)(2,1)S(1)}, u32[]{:S(2)}, u32[]{:S(2)}) collective-permute-start(bf16[96,768]{1,0:T(8,128)(2,1)S(1)} %get-tuple-element.89), channel_id=1, source_target_pairs={{0,1},{1,0},{2,3},{3,2},{4,5},{5,4},{6,7},{7,6},{8,9},{9,8},{10,11... | collective-permute-start | bytes 442376 | tf_op jit(solution)/shard_map/ppermute | solution.py:22
  120.0 11.2 %collective-permute-start.35 = (bf16[96,768]{1,0:T(8,128)(2,1)S(1)}, bf16[96,768]{1,0:T(8,128)(2,1)S(1)}, u32[]{:S(2)}, u32[]{:S(2)}) collective-permute-start(bf16[96,768]{1,0:T(8,128)(2,1)S(1)} %get-tuple-element.88), channel_id=1, source_target_pairs={{0,2},{1,3},{2,0},{3,1},{4,6},{5,7},{6,4},{7,5},{8,10},{9,11},{10,... | collective-permute-start | bytes 442376 | tf_op jit(solution)/shard_map/ppermute | solution.py:22
  121.0 13.6 %collective-permute-start.36 = (bf16[96,768]{1,0:T(8,128)(2,1)S(1)}, bf16[96,768]{1,0:T(8,128)(2,1)S(1)}, u32[]{:S(2)}, u32[]{:S(2)}) collective-permute-start(bf16[96,768]{1,0:T(8,128)(2,1)S(1)} %get-tuple-element.87), channel_id=1, source_target_pairs={{0,3},{1,2},{2,1},{3,0},{4,7},{5,6},{6,5},{7,4},{8,11},{9,10},{10,... | collective-permute-start | bytes 442376 | tf_op jit(solution)/shard_map/ppermute | solution.py:22
  127.6 9.8 %collective-permute-start.32 = (bf16[128,768]{1,0:T(8,128)(2,1)S(1)}, bf16[128,768]{1,0:T(8,128)(2,1)S(1)}, u32[]{:S(2)}, u32[]{:S(2)}) collective-permute-start(bf16[128,768]{1,0:T(8,128)(2,1)S(1)} %get-tuple-element.85.refs_0_), channel_id=1, source_target_pairs={{0,4},{4,0},{8,12},{12,8},{1,5},{5,1},{9,13},{13,9},{2,6},{6,2},{1... | collective-permute-start | bytes 589832 | tf_op jit(solution)/shard_map/ppermute | solution.py:22
  129.1 9.7 %collective-permute-start.33 = (bf16[128,768]{1,0:T(8,128)(2,1)S(1)}, bf16[128,768]{1,0:T(8,128)(2,1)S(1)}, u32[]{:S(2)}, u32[]{:S(2)}) collective-permute-start(bf16[128,768]{1,0:T(8,128)(2,1)S(1)} %get-tuple-element.85.refs_0_), channel_id=1, source_target_pairs={{0,8},{4,12},{8,0},{12,4},{1,9},{5,13},{9,1},{13,5},{2,10},{6,14},... | collective-permute-start | bytes 589832 | tf_op jit(solution)/shard_map/ppermute | solution.py:22
  129.6 16.9 %collective-permute-start.34 = (bf16[128,768]{1,0:T(8,128)(2,1)S(1)}, bf16[128,768]{1,0:T(8,128)(2,1)S(1)}, u32[]{:S(2)}, u32[]{:S(2)}) collective-permute-start(bf16[128,768]{1,0:T(8,128)(2,1)S(1)} %get-tuple-element.85.refs_0_), channel_id=1, source_target_pairs={{0,12},{4,8},{8,4},{12,0},{1,13},{5,9},{9,5},{13,1},{2,14},{6,10},... | collective-permute-start | bytes 589832 | tf_op jit(solution)/shard_map/ppermute | solution.py:22
  135.3 12.2 %collective-permute-start.37 = (bf16[128,768]{1,0:T(8,128)(2,1)S(1)}, bf16[128,768]{1,0:T(8,128)(2,1)S(1)}, u32[]{:S(2)}, u32[]{:S(2)}) collective-permute-start(bf16[128,768]{1,0:T(8,128)(2,1)S(1)} %fusion.4.refs_0_), channel_id=1, source_target_pairs={{0,4},{4,0},{8,12},{12,8},{1,5},{5,1},{9,13},{13,9},{2,6},{6,2},{1... | collective-permute-start | bytes 589832 | tf_op jit(solution)/shard_map/ppermute | solution.py:22
  136.5 10.9 %collective-permute-start.38 = (bf16[128,768]{1,0:T(8,128)(2,1)S(1)}, bf16[128,768]{1,0:T(8,128)(2,1)S(1)}, u32[]{:S(2)}, u32[]{:S(2)}) collective-permute-start(bf16[128,768]{1,0:T(8,128)(2,1)S(1)} %fusion.4.refs_0_), channel_id=1, source_target_pairs={{0,8},{4,12},{8,0},{12,4},{1,9},{5,13},{9,1},{13,5},{2,10},{6,14},... | collective-permute-start | bytes 589832 | tf_op jit(solution)/shard_map/ppermute | solution.py:22
  137.5 10.0 %collective-permute-start.39 = (bf16[128,768]{1,0:T(8,128)(2,1)S(1)}, bf16[128,768]{1,0:T(8,128)(2,1)S(1)}, u32[]{:S(2)}, u32[]{:S(2)}) collective-permute-start(bf16[128,768]{1,0:T(8,128)(2,1)S(1)} %fusion.4.refs_0_), channel_id=1, source_target_pairs={{0,12},{4,8},{8,4},{12,0},{1,13},{5,9},{9,5},{13,1},{2,14},{6,10},... | collective-permute-start | bytes 589832 | tf_op jit(solution)/shard_map/ppermute | solution.py:22
  138.9 1.2 collective-permute-start.40
  140.1 5.1 %collective-permute-start.41 = (f32[2,128]{1,0:T(2,128)S(1)}, f32[2,128]{1,0:T(2,128)S(1)}, u32[]{:S(2)}, u32[]{:S(2)}) collective-permute-start(f32[2,128]{1,0:T(2,128)S(1)} %add.49), channel_id=1, source_target_pairs={{0,4},{4,0},{8,12},{12,8},{1,5},{5,1},{9,13},{13,9},{2,6},{6,2},{1... | collective-permute-start | bytes 3080 | tf_op jit(solution)/shard_map/ppermute | solution.py:22
  145.2 3.6 %collective-permute-start.42 = (f32[2,128]{1,0:T(2,128)S(1)}, f32[2,128]{1,0:T(2,128)S(1)}, u32[]{:S(2)}, u32[]{:S(2)}) collective-permute-start(f32[2,128]{1,0:T(2,128)S(1)} %add.50), channel_id=1, source_target_pairs={{0,8},{4,12},{8,0},{12,4},{1,9},{5,13},{9,1},{13,5},{2,10},{6,14},... | collective-permute-start | bytes 3080 | tf_op jit(solution)/shard_map/ppermute | solution.py:22
  146.5 2.8 %copy-start.1 = (bf16[128,3072]{1,0:T(8,128)(2,1)S(1)}, bf16[128,3072]{1,0:T(8,128)(2,1)}, u32[]{:S(2)}) copy-start(bf16[128,3072]{1,0:T(8,128)(2,1)} %param.7) | copy-start | bytes 2359300
  (1 other events, 2.6 us)

commit v11 on v9

--- a/solution.py
+++ b/solution.py
@@ -197,7 +197,7 @@
     )
 
 
-STRIP = 32
+STRIP = 16
 LIMIT = 8
 
 

time: 151 us -> 151 us (level)
  no operation moved by 1% of the time
where the time goes in v11:
time: 151 us; the launch traced here: 150 us
  Pallas kernels  60.2 us (40%)
  starting transfers between devices  44.7 us (30%)
  waiting for transfers between devices  37.8 us (25%)
  other arithmetic  3.53 us (2%)
  matrix products  2.47 us (2%)
    pallas_call x13, Pallas kernels, call(): pl.pallas_call(kernel, in_specs=[SMEM] + [VMEM] * (len(ins) - far) + [HBM...  55.5 us
    ppermute x43, starting transfers between devices, exchange(): return lax.ppermute(array, axis, [(i, i ^ bit) for i in range(size)])  44.7 us
    ppermute x43, waiting for transfers between devices, exchange(): return lax.ppermute(array, axis, [(i, i ^ bit) for i in range(size)])  37.8 us
    pallas_call x1, Pallas kernels, fetch(): pl.pallas_call(kernel, in_specs=[HBM], out_specs=VMEM, out_shape=pltpu.VM...  4.66 us
  transfers between devices with their start and end apart: 43, of which 19 were waited for; matrix products, arithmetic and copies ran while one was open for 2% of the time, Pallas kernels for 40%

profile of v11, /device:TPU:16, one launch (start us, length us, event | category | flops | bytes accessed | tf_op | source)
XLA Modules:
  0.0 150.4 jit_solution(7711144436902722930)
XLA Ops:
  3.6 1.6 %collective-permute-start.2 = (bf16[96,768]{1,0:T(8,128)(2,1)S(1)}, bf16[96,768]{1,0:T(8,128)(2,1)S(1)}, u32[]{:S(2)}, u32[]{:S(2)}) collective-permute-start(bf16[96,768]{1,0:T(8,128)(2,1)S(1)} %get-tuple-element.99), channel_id=1, source_target_pairs={{0,1},{1,0},{2,3},{3,2},{4,5},{5,4},{6,7},{7,6},{8,9},{9,8},{10,11... | collective-permute-start | bytes 442376 | tf_op jit(solution)/shard_map/ppermute | solution.py:22
  5.5 1.6 %collective-permute-start.1 = (bf16[96,768]{1,0:T(8,128)(2,1)S(1)}, bf16[96,768]{1,0:T(8,128)(2,1)S(1)}, u32[]{:S(2)}, u32[]{:S(2)}) collective-permute-start(bf16[96,768]{1,0:T(8,128)(2,1)S(1)} %get-tuple-element.100), channel_id=1, source_target_pairs={{0,3},{1,2},{2,1},{3,0},{4,7},{5,6},{6,5},{7,4},{8,11},{9,10},{10,... | collective-permute-start | bytes 442376 | tf_op jit(solution)/shard_map/ppermute | solution.py:22
  7.1 3.2 %collective-permute-done.2.refs_0_ = bf16[96,768]{1,0:T(8,128)(2,1)S(1)} collective-permute-done((bf16[96,768]{1,0:T(8,128)(2,1)S(1)}, bf16[96,768]{1,0:T(8,128)(2,1)S(1)}, u32[]{:S(2)}, u32[]{:S(2)}) %collective-permute-start.2) | collective-permute-done | bytes 147488 | tf_op jit(solution)/shard_map/ppermute | solution.py:22
  10.4 1.5 collective-permute-start.3
  11.9 1.5 %collective-permute-start.4 = (bf16[96,768]{1,0:T(8,128)(2,1)S(1)}, bf16[96,768]{1,0:T(8,128)(2,1)S(1)}, u32[]{:S(2)}, u32[]{:S(2)}) collective-permute-start(bf16[96,768]{1,0:T(8,128)(2,1)S(1)} %collective-permute-done.2.refs_0_), channel_id=1, source_target_pairs={{0,8},{4,12},{8,0},{12,4},{1,9},{5,13},{9,1},{13,5},{2,10},{6,14},... | collective-permute-start | bytes 442376 | tf_op jit(solution)/shard_map/ppermute | solution.py:22
  13.9 4.7 %fetch.1.refs_9_ = bf16[3072,2048]{1,0:T(8,128)(2,1)S(1)} custom-call(bf16[3072,2048]{1,0:T(8,128)(2,1)} %bitcast.37), custom_call_target="tpu_custom_call" | custom-call | bytes 12582912 | tf_op jit(solution)/shard_map/fetch/pallas_call | solution.py:65
  18.8 1.2 collective-permute-done.1
  20.0 1.6 %collective-permute-start.9 = (bf16[192,768]{1,0:T(8,128)(2,1)S(1)}, bf16[192,768]{1,0:T(8,128)(2,1)S(1)}, u32[]{:S(2)}, u32[]{:S(2)}) collective-permute-start(bf16[192,768]{1,0:T(8,128)(2,1)S(1)} %constant_dynamic-update-slice_fusion.refs_1_), channel_id=1, source_target_pairs={{0,8},{4,12},{8,0},{12,4},{1,9},{5,13},{9,1},{13,5},{2,10},{6,14},... | collective-permute-start | bytes 884744 | tf_op jit(solution)/shard_map/ppermute | solution.py:22
  21.6 1.5 collective-permute-start.11
  23.4 1.3 collective-permute-start.6
  25.4 1.6 %collective-permute-start.8 = (bf16[96,768]{1,0:T(8,128)(2,1)S(1)}, bf16[96,768]{1,0:T(8,128)(2,1)S(1)}, u32[]{:S(2)}, u32[]{:S(2)}) collective-permute-start(bf16[96,768]{1,0:T(8,128)(2,1)S(1)} %get-tuple-element.96), channel_id=1, source_target_pairs={{0,3},{1,2},{2,1},{3,0},{4,7},{5,6},{6,5},{7,4},{8,11},{9,10},{10,... | collective-permute-start | bytes 442376 | tf_op jit(solution)/shard_map/ppermute | solution.py:22
  27.9 1.6 %collective-permute-start.10 = (bf16[96,768]{1,0:T(8,128)(2,1)S(1)}, bf16[96,768]{1,0:T(8,128)(2,1)S(1)}, u32[]{:S(2)}, u32[]{:S(2)}) collective-permute-start(bf16[96,768]{1,0:T(8,128)(2,1)S(1)} %slice.108), channel_id=1, source_target_pairs={{0,4},{4,0},{8,12},{12,8},{1,5},{5,1},{9,13},{13,9},{2,6},{6,2},{1... | collective-permute-start | bytes 442376 | tf_op jit(solution)/shard_map/ppermute | solution.py:22
  29.6 1.4 collective-permute-start.12
  31.0 3.4 %collective-permute-done.7 = bf16[96,768]{1,0:T(8,128)(2,1)S(1)} collective-permute-done((bf16[96,768]{1,0:T(8,128)(2,1)S(1)}, bf16[96,768]{1,0:T(8,128)(2,1)S(1)}, u32[]{:S(2)}, u32[]{:S(2)}) %collective-permute-start.7) | collective-permute-done | bytes 147488 | tf_op jit(solution)/shard_map/ppermute | solution.py:22
  34.4 3.8 %collective-permute-done.8 = bf16[96,768]{1,0:T(8,128)(2,1)S(1)} collective-permute-done((bf16[96,768]{1,0:T(8,128)(2,1)S(1)}, bf16[96,768]{1,0:T(8,128)(2,1)S(1)}, u32[]{:S(2)}, u32[]{:S(2)}) %collective-permute-start.8) | collective-permute-done | bytes 147488 | tf_op jit(solution)/shard_map/ppermute | solution.py:22
  39.9 6.8 %pre_acts.2 = (f32[384,1024]{1,0:T(8,128)S(1)}, f32[384,1024]{1,0:T(8,128)S(1)}, bf16[384,2048]{1,0:T(8,128)(2,1)S(1)}) custom-call(s32[1]{0:T(128)} %bitcast.t_ref, bf16[96,3072]{1,0:T(8,128)(2,1)S(1)} %convolution_convert_fusion.own_ref, bf16[96,768]{1,0:T(8,128)(2,1)S(1)} %collective-permute-done.2.refs_0_, ...), custom_call_target="tpu_custom_call" | custom-call | flops 2415919104 | bytes 1048576 | tf_op jit(solution)/shard_map/pre_acts/pallas_call | solution.py:47
  46.7 2.9 %collective-permute-done.14.refs_1_ = bf16[288,768]{1,0:T(8,128)(2,1)S(1)} collective-permute-done((bf16[288,768]{1,0:T(8,128)(2,1)S(1)}, bf16[288,768]{1,0:T(8,128)(2,1)S(1)}, u32[]{:S(2)}, u32[]{:S(2)}) %collective-permute-start.14) | collective-permute-done | bytes 442400 | tf_op jit(solution)/shard_map/ppermute | solution.py:22
  49.7 6.6 %pre_acts.3 = (f32[384,1024]{1,0:T(8,128)S(1)}, f32[384,1024]{1,0:T(8,128)S(1)}, bf16[384,2048]{1,0:T(8,128)(2,1)S(1)}) custom-call(s32[1]{0:T(128)} %bitcast.t_ref, bf16[96,3072]{1,0:T(8,128)(2,1)S(1)} %convolution_convert_fusion.own_ref, bf16[96,768]{1,0:T(8,128)(2,1)S(1)} %collective-permute-done.2.refs_0_, ...), custom_call_target="tpu_custom_call" | custom-call | flops 2415919104 | bytes 1048576 | tf_op jit(solution)/shard_map/pre_acts/pallas_call | solution.py:47
  56.3 1.6 %collective-permute-start.19 = (bf16[288,768]{1,0:T(8,128)(2,1)S(1)}, bf16[288,768]{1,0:T(8,128)(2,1)S(1)}, u32[]{:S(2)}, u32[]{:S(2)}) collective-permute-start(bf16[288,768]{1,0:T(8,128)(2,1)S(1)} %constant_dynamic-update-slice_fusion.2.refs_0_), channel_id=1, source_target_pairs={{0,12},{4,8},{8,4},{12,0},{1,13},{5,9},{9,5},{13,1},{2,14},{6,10},... | collective-permute-start | bytes 1327112 | tf_op jit(solution)/shard_map/ppermute | solution.py:22
  57.9 1.8 %collective-permute-done.16.refs_5_ = bf16[384,2048]{1,0:T(8,128)(2,1)S(1)} collective-permute-done((bf16[384,2048]{1,0:T(8,128)(2,1)S(1)}, bf16[384,2048]{1,0:T(8,128)(2,1)S(1)}, u32[]{:S(2)}, u32[]{:S(2)}) %collective-permute-start.16) | collective-permute-done | bytes 1572896 | tf_op jit(solution)/shard_map/ppermute | solution.py:22
  59.7 7.5 %project_send.1 = (bf16[192,768]{1,0:T(8,128)(2,1)S(1)}, bf16[192,768]{1,0:T(8,128)(2,1)S(1)}, bf16[384,2048]{1,0:T(8,128)(2,1)S(1)}, f32[2,384,768]{2,1,0:T(8,128)S(1)}) custom-call(s32[1]{0:T(128)} %bitcast.t_ref, f32[384,1024]{1,0:T(8,128)S(1)} %get-tuple-element.51.refs_0_, f32[384,1024]{1,0:T(8,128)S(1)} %get-tuple-element.52.refs_1_, ...), custom_call_target="tpu_custom_call" | custom-call | flops 1811939328 | bytes 1048576 | tf_op jit(solution)/shard_map/project_send/pallas_call | solution.py:47
  67.2 1.7 %collective-permute-start.17 = (bf16[192,768]{1,0:T(8,128)(2,1)S(1)}, bf16[192,768]{1,0:T(8,128)(2,1)S(1)}, u32[]{:S(2)}, u32[]{:S(2)}) collective-permute-start(bf16[192,768]{1,0:T(8,128)(2,1)S(1)} %get-tuple-element.59), channel_id=1, source_target_pairs={{0,4},{4,0},{8,12},{12,8},{1,5},{5,1},{9,13},{13,9},{2,6},{6,2},{1... | collective-permute-start | bytes 884744 | tf_op jit(solution)/shard_map/ppermute | solution.py:22
  69.8 4.7 %grad_hidden.3 = (f32[384,1024]{1,0:T(8,128)S(1)}, bf16[384,1024]{1,0:T(8,128)(2,1)S(1)}) custom-call(s32[1]{0:T(128)} %bitcast.t_ref, bf16[96,3072]{1,0:T(8,128)(2,1)S(1)} %fusion.own_ref, bf16[288,768]{1,0:T(8,128)(2,1)S(1)} %constant_dynamic-update-slice_fusion.2.refs_0_, bf16[288,768]{1,0:T(8,128)(2,1)S(1)} %collective-permute-done.14.refs_1_, ...), custom_call_target="tpu_custom_call" | custom-call | flops 2415919104 | bytes 1048576 | tf_op jit(solution)/shard_map/grad_hidden/pallas_call | solution.py:47
  74.6 1.7 %collective-permute-done.17.top_ref = bf16[192,768]{1,0:T(8,128)(2,1)S(1)} collective-permute-done((bf16[192,768]{1,0:T(8,128)(2,1)S(1)}, bf16[192,768]{1,0:T(8,128)(2,1)S(1)}, u32[]{:S(2)}, u32[]{:S(2)}) %collective-permute-start.17) | collective-permute-done | bytes 294944 | tf_op jit(solution)/shard_map/ppermute | solution.py:22
  76.3 1.4 collective-permute-done.18.low_ref
  77.9 4.7 %grad_hidden.2 = (f32[384,1024]{1,0:T(8,128)S(1)}, bf16[384,1024]{1,0:T(8,128)(2,1)S(1)}) custom-call(s32[1]{0:T(128)} %bitcast.t_ref, bf16[96,3072]{1,0:T(8,128)(2,1)S(1)} %fusion.own_ref, bf16[288,768]{1,0:T(8,128)(2,1)S(1)} %constant_dynamic-update-slice_fusion.2.refs_0_, bf16[288,768]{1,0:T(8,128)(2,1)S(1)} %collective-permute-done.14.refs_1_, ...), custom_call_target="tpu_custom_call" | custom-call | flops 2415919104 | bytes 1048576 | tf_op jit(solution)/shard_map/grad_hidden/pallas_call | solution.py:47
  83.5 3.6 %project_keep.1 = f32[1,384,768]{2,1,0:T(8,128)S(1)} custom-call(s32[1]{0:T(128)} %bitcast.t_ref, bf16[384,2048]{1,0:T(8,128)(2,1)S(1)} %get-tuple-element.65.refs_0_, bf16[2048,3072]{1,0:T(8,128)(2,1)} %bitcast.36), custom_call_target="tpu_custom_call" | custom-call | flops 603979776 | bytes 1048576 | tf_op jit(solution)/shard_map/project_keep/pallas_call | solution.py:47
  87.2 5.7 %rows_first.1 = (bf16[192,768]{1,0:T(8,128)(2,1)S(1)}, bf16[192,768]{1,0:T(8,128)(2,1)S(1)}, bf16[384,2048]{1,0:T(8,128)(2,1)S(1)}, bf16[384,2048]{1,0:T(8,128)(2,1)S(1)}) custom-call(s32[1]{0:T(128)} %bitcast.t_ref, f32[384,1024]{1,0:T(8,128)S(1)} %get-tuple-element.51.refs_0_, f32[384,1024]{1,0:T(8,128)S(1)} %get-tuple-element.52.refs_1_, ...), custom_call_target="tpu_custom_call" | custom-call | flops 1207959552 | bytes 1048576 | tf_op jit(solution)/shard_map/rows_first/pallas_call | solution.py:47
  92.8 1.7 %collective-permute-start.22 = (bf16[192,768]{1,0:T(8,128)(2,1)S(1)}, bf16[192,768]{1,0:T(8,128)(2,1)S(1)}, u32[]{:S(2)}, u32[]{:S(2)}) collective-permute-start(bf16[192,768]{1,0:T(8,128)(2,1)S(1)} %get-tuple-element.73), channel_id=1, source_target_pairs={{0,4},{4,0},{8,12},{12,8},{1,5},{5,1},{9,13},{13,9},{2,6},{6,2},{1... | collective-permute-start | bytes 884744 | tf_op jit(solution)/shard_map/ppermute | solution.py:22
  94.6 1.6 %collective-permute-start.23 = (bf16[192,768]{1,0:T(8,128)(2,1)S(1)}, bf16[192,768]{1,0:T(8,128)(2,1)S(1)}, u32[]{:S(2)}, u32[]{:S(2)}) collective-permute-start(bf16[192,768]{1,0:T(8,128)(2,1)S(1)} %get-tuple-element.74), channel_id=1, source_target_pairs={{0,8},{4,12},{8,0},{12,4},{1,9},{5,13},{9,1},{13,5},{2,10},{6,14},... | collective-permute-start | bytes 884744 | tf_op jit(solution)/shard_map/ppermute | solution.py:22
  96.2 8.6 %rows_send.1.both_ref = f32[2,384,768]{2,1,0:T(8,128)S(1)} custom-call(s32[1]{0:T(128)} %bitcast.t_ref, bf16[384,2048]{1,0:T(8,128)(2,1)S(1)} %get-tuple-element.71.refs_0_, bf16[384,2048]{1,0:T(8,128)(2,1)S(1)} %get-tuple-element.72.refs_1_, bf16[3072,2048]{1,0:T(8,128)(2,1)} %bitcast.39, bf16[3072,2048]{1,0:T(8,128)(2,1)} %bitcast.31), custom_call_target="tpu_custom_call" | custom-call | flops 2415919104 | bytes 1048576 | tf_op jit(solution)/shard_map/rows_send/pallas_call | solution.py:47
  105.0 1.7 %collective-permute-start.29 = (bf16[384,768]{1,0:T(8,128)(2,1)S(1)}, bf16[384,768]{1,0:T(8,128)(2,1)S(1)}, u32[]{:S(2)}, u32[]{:S(2)}) collective-permute-start(bf16[384,768]{1,0:T(8,128)(2,1)S(1)} %get-tuple-element.75), channel_id=1, source_target_pairs={{0,4},{4,0},{8,12},{12,8},{1,5},{5,1},{9,13},{13,9},{2,6},{6,2},{1... | collective-permute-start | bytes 1769480 | tf_op jit(solution)/shard_map/ppermute | solution.py:22
  107.4 1.0 collective-permute-start.27
  108.4 2.5 %collective-permute-start.28 = (bf16[96,768]{1,0:T(8,128)(2,1)S(1)}, bf16[96,768]{1,0:T(8,128)(2,1)S(1)}, u32[]{:S(2)}, u32[]{:S(2)}) collective-permute-start(bf16[96,768]{1,0:T(8,128)(2,1)S(1)} %get-tuple-element.92), channel_id=1, source_target_pairs={{0,3},{1,2},{2,1},{3,0},{4,7},{5,6},{6,5},{7,4},{8,11},{9,10},{10,... | collective-permute-start | bytes 442376 | tf_op jit(solution)/shard_map/ppermute | solution.py:22
  110.9 5.2 %rows_keep.1 = f32[1,384,768]{2,1,0:T(8,128)S(1)} custom-call(s32[1]{0:T(128)} %bitcast.t_ref, bf16[384,2048]{1,0:T(8,128)(2,1)S(1)} %get-tuple-element.71.refs_0_, bf16[384,2048]{1,0:T(8,128)(2,1)S(1)} %get-tuple-element.72.refs_1_, bf16[3072,2048]{1,0:T(8,128)(2,1)} %bitcast.40, bf16[3072,2048]{1,0:T(8,128)(2,1)} %bitcast.32), custom_call_target="tpu_custom_call" | custom-call | flops 1207959552 | bytes 1048576 | tf_op jit(solution)/shard_map/rows_keep/pallas_call | solution.py:47
  116.1 3.8 %collective-permute-done.29 = bf16[384,768]{1,0:T(8,128)(2,1)S(1)} collective-permute-done((bf16[384,768]{1,0:T(8,128)(2,1)S(1)}, bf16[384,768]{1,0:T(8,128)(2,1)S(1)}, u32[]{:S(2)}, u32[]{:S(2)}) %collective-permute-start.29) | collective-permute-done | bytes 589856 | tf_op jit(solution)/shard_map/ppermute | solution.py:22
  119.9 1.1 collective-permute-done.30
  121.4 1.0 collective-permute-start.35
  122.4 2.5 %collective-permute-start.36 = (bf16[96,768]{1,0:T(8,128)(2,1)S(1)}, bf16[96,768]{1,0:T(8,128)(2,1)S(1)}, u32[]{:S(2)}, u32[]{:S(2)}) collective-permute-start(bf16[96,768]{1,0:T(8,128)(2,1)S(1)} %get-tuple-element.89), channel_id=1, source_target_pairs={{0,3},{1,2},{2,1},{3,0},{4,7},{5,6},{6,5},{7,4},{8,11},{9,10},{10,... | collective-permute-start | bytes 442376 | tf_op jit(solution)/shard_map/ppermute | solution.py:22
  124.9 3.3 %collective-permute-done.31 = bf16[96,768]{1,0:T(8,128)(2,1)S(1)} collective-permute-done((bf16[96,768]{1,0:T(8,128)(2,1)S(1)}, bf16[96,768]{1,0:T(8,128)(2,1)S(1)}, u32[]{:S(2)}, u32[]{:S(2)}) %collective-permute-start.31) | collective-permute-done | bytes 147488 | tf_op jit(solution)/shard_map/ppermute | solution.py:22
  130.0 2.5 %collective-permute-start.34 = (bf16[128,768]{1,0:T(8,128)(2,1)S(1)}, bf16[128,768]{1,0:T(8,128)(2,1)S(1)}, u32[]{:S(2)}, u32[]{:S(2)}) collective-permute-start(bf16[128,768]{1,0:T(8,128)(2,1)S(1)} %get-tuple-element.87.refs_0_), channel_id=1, source_target_pairs={{0,12},{4,8},{8,4},{12,0},{1,13},{5,9},{9,5},{13,1},{2,14},{6,10},... | collective-permute-start | bytes 589832 | tf_op jit(solution)/shard_map/ppermute | solution.py:22
  132.5 3.2 %collective-permute-done.36 = bf16[96,768]{1,0:T(8,128)(2,1)S(1)} collective-permute-done((bf16[96,768]{1,0:T(8,128)(2,1)S(1)}, bf16[96,768]{1,0:T(8,128)(2,1)S(1)}, u32[]{:S(2)}, u32[]{:S(2)}) %collective-permute-start.36) | collective-permute-done | bytes 147488 | tf_op jit(solution)/shard_map/ppermute | solution.py:22
  138.1 1.9 %collective-permute-start.39 = (bf16[128,768]{1,0:T(8,128)(2,1)S(1)}, bf16[128,768]{1,0:T(8,128)(2,1)S(1)}, u32[]{:S(2)}, u32[]{:S(2)}) collective-permute-start(bf16[128,768]{1,0:T(8,128)(2,1)S(1)} %fusion.4.refs_0_), channel_id=1, source_target_pairs={{0,12},{4,8},{8,4},{12,0},{1,13},{5,9},{9,5},{13,1},{2,14},{6,10},... | collective-permute-start | bytes 589832 | tf_op jit(solution)/shard_map/ppermute | solution.py:22
  140.0 1.1 collective-permute-done.40
  142.0 4.3 %collective-permute-done.41 = f32[2,128]{1,0:T(2,128)S(1)} collective-permute-done((f32[2,128]{1,0:T(2,128)S(1)}, f32[2,128]{1,0:T(2,128)S(1)}, u32[]{:S(2)}, u32[]{:S(2)}) %collective-permute-start.41) | collective-permute-done | bytes 1056 | tf_op jit(solution)/shard_map/ppermute | solution.py:22
  146.3 1.5 %collective-permute-start.42 = (f32[2,128]{1,0:T(2,128)S(1)}, f32[2,128]{1,0:T(2,128)S(1)}, u32[]{:S(2)}, u32[]{:S(2)}) collective-permute-start(f32[2,128]{1,0:T(2,128)S(1)} %add.50), channel_id=1, source_target_pairs={{0,8},{4,12},{8,0},{12,4},{1,9},{5,13},{9,1},{13,5},{2,10},{6,14},... | collective-permute-start | bytes 3080 | tf_op jit(solution)/shard_map/ppermute | solution.py:22
  147.8 0.9 assemble.2
  148.8 0.9 assemble.3
  (105 shorter events, 16.8 us)
Async XLA Ops:
  0.6 2.6 %copy-start = (bf16[128,3072]{1,0:T(8,128)(2,1)S(1)}, bf16[128,3072]{1,0:T(8,128)(2,1)}, u32[]{:S(2)}) copy-start(bf16[128,3072]{1,0:T(8,128)(2,1)} %param.7) | copy-start | bytes 2359300
  0.6 13.2 %copy-start.4 = (f32[128,2]{0,1:T(2,128)S(1)}, f32[128,2]{0,1:T(2,128)}, u32[]{:S(2)}) copy-start(f32[128,2]{0,1:T(2,128)} %param.9) | copy-start | bytes 3076
  3.6 6.8 %collective-permute-start.2 = (bf16[96,768]{1,0:T(8,128)(2,1)S(1)}, bf16[96,768]{1,0:T(8,128)(2,1)S(1)}, u32[]{:S(2)}, u32[]{:S(2)}) collective-permute-start(bf16[96,768]{1,0:T(8,128)(2,1)S(1)} %get-tuple-element.99), channel_id=1, source_target_pairs={{0,1},{1,0},{2,3},{3,2},{4,5},{5,4},{6,7},{7,6},{8,9},{9,8},{10,11... | collective-permute-start | bytes 442376 | tf_op jit(solution)/shard_map/ppermute | solution.py:22
  5.2 13.6 %collective-permute-start = (bf16[96,768]{1,0:T(8,128)(2,1)S(1)}, bf16[96,768]{1,0:T(8,128)(2,1)S(1)}, u32[]{:S(2)}, u32[]{:S(2)}) collective-permute-start(bf16[96,768]{1,0:T(8,128)(2,1)S(1)} %get-tuple-element.101), channel_id=1, source_target_pairs={{0,2},{1,3},{2,0},{3,1},{4,6},{5,7},{6,4},{7,5},{8,10},{9,11},{10,... | collective-permute-start | bytes 442376 | tf_op jit(solution)/shard_map/ppermute | solution.py:22
  5.5 14.4 %collective-permute-start.1 = (bf16[96,768]{1,0:T(8,128)(2,1)S(1)}, bf16[96,768]{1,0:T(8,128)(2,1)S(1)}, u32[]{:S(2)}, u32[]{:S(2)}) collective-permute-start(bf16[96,768]{1,0:T(8,128)(2,1)S(1)} %get-tuple-element.100), channel_id=1, source_target_pairs={{0,3},{1,2},{2,1},{3,0},{4,7},{5,6},{6,5},{7,4},{8,11},{9,10},{10,... | collective-permute-start | bytes 442376 | tf_op jit(solution)/shard_map/ppermute | solution.py:22
  10.4 9.6 %collective-permute-start.3 = (bf16[96,768]{1,0:T(8,128)(2,1)S(1)}, bf16[96,768]{1,0:T(8,128)(2,1)S(1)}, u32[]{:S(2)}, u32[]{:S(2)}) collective-permute-start(bf16[96,768]{1,0:T(8,128)(2,1)S(1)} %collective-permute-done.2.refs_0_), channel_id=1, source_target_pairs={{0,4},{4,0},{8,12},{12,8},{1,5},{5,1},{9,13},{13,9},{2,6},{6,2},{1... | collective-permute-start | bytes 442376 | tf_op jit(solution)/shard_map/ppermute | solution.py:22
  11.9 8.1 %collective-permute-start.4 = (bf16[96,768]{1,0:T(8,128)(2,1)S(1)}, bf16[96,768]{1,0:T(8,128)(2,1)S(1)}, u32[]{:S(2)}, u32[]{:S(2)}) collective-permute-start(bf16[96,768]{1,0:T(8,128)(2,1)S(1)} %collective-permute-done.2.refs_0_), channel_id=1, source_target_pairs={{0,8},{4,12},{8,0},{12,4},{1,9},{5,13},{9,1},{13,5},{2,10},{6,14},... | collective-permute-start | bytes 442376 | tf_op jit(solution)/shard_map/ppermute | solution.py:22
  13.4 6.6 %collective-permute-start.5 = (bf16[96,768]{1,0:T(8,128)(2,1)S(1)}, bf16[96,768]{1,0:T(8,128)(2,1)S(1)}, u32[]{:S(2)}, u32[]{:S(2)}) collective-permute-start(bf16[96,768]{1,0:T(8,128)(2,1)S(1)} %collective-permute-done.2.refs_0_), channel_id=1, source_target_pairs={{0,12},{4,8},{8,4},{12,0},{1,13},{5,9},{9,5},{13,1},{2,14},{6,10},... | collective-permute-start | bytes 442376 | tf_op jit(solution)/shard_map/ppermute | solution.py:22
  13.9 9.2 %copy-start.2 = (bf16[128,3072]{1,0:T(8,128)(2,1)S(1)}, bf16[128,3072]{1,0:T(8,128)(2,1)}, u32[]{:S(2)}) copy-start(bf16[128,3072]{1,0:T(8,128)(2,1)} %param.13) | copy-start | bytes 2359300
  18.7 39.2 %copy-start.3 = (f32[384]{0:T(512)}, f32[384]{0:T(512)S(1)}, u32[]{:S(2)}) copy-start(f32[384]{0:T(512)S(1)} %add_reduce_fusion) | copy-start | bytes 4612
  20.0 7.9 %collective-permute-start.9 = (bf16[192,768]{1,0:T(8,128)(2,1)S(1)}, bf16[192,768]{1,0:T(8,128)(2,1)S(1)}, u32[]{:S(2)}, u32[]{:S(2)}) collective-permute-start(bf16[192,768]{1,0:T(8,128)(2,1)S(1)} %constant_dynamic-update-slice_fusion.refs_1_), channel_id=1, source_target_pairs={{0,8},{4,12},{8,0},{12,4},{1,9},{5,13},{9,1},{13,5},{2,10},{6,14},... | collective-permute-start | bytes 884744 | tf_op jit(solution)/shard_map/ppermute | solution.py:22
  21.6 8.0 %collective-permute-start.11 = (bf16[192,768]{1,0:T(8,128)(2,1)S(1)}, bf16[192,768]{1,0:T(8,128)(2,1)S(1)}, u32[]{:S(2)}, u32[]{:S(2)}) collective-permute-start(bf16[192,768]{1,0:T(8,128)(2,1)S(1)} %constant_dynamic-update-slice_fusion.refs_1_), channel_id=1, source_target_pairs={{0,4},{4,0},{8,12},{12,8},{1,5},{5,1},{9,13},{13,9},{2,6},{6,2},{1... | collective-permute-start | bytes 884744 | tf_op jit(solution)/shard_map/ppermute | solution.py:22
  23.4 7.6 %collective-permute-start.6 = (bf16[96,768]{1,0:T(8,128)(2,1)S(1)}, bf16[96,768]{1,0:T(8,128)(2,1)S(1)}, u32[]{:S(2)}, u32[]{:S(2)}) collective-permute-start(bf16[96,768]{1,0:T(8,128)(2,1)S(1)} %get-tuple-element.98), channel_id=1, source_target_pairs={{0,1},{1,0},{2,3},{3,2},{4,5},{5,4},{6,7},{7,6},{8,9},{9,8},{10,11... | collective-permute-start | bytes 442376 | tf_op jit(solution)/shard_map/ppermute | solution.py:22
  24.6 9.7 %collective-permute-start.7 = (bf16[96,768]{1,0:T(8,128)(2,1)S(1)}, bf16[96,768]{1,0:T(8,128)(2,1)S(1)}, u32[]{:S(2)}, u32[]{:S(2)}) collective-permute-start(bf16[96,768]{1,0:T(8,128)(2,1)S(1)} %get-tuple-element.97), channel_id=1, source_target_pairs={{0,2},{1,3},{2,0},{3,1},{4,6},{5,7},{6,4},{7,5},{8,10},{9,11},{10,... | collective-permute-start | bytes 442376 | tf_op jit(solution)/shard_map/ppermute | solution.py:22
  25.4 12.9 %collective-permute-start.8 = (bf16[96,768]{1,0:T(8,128)(2,1)S(1)}, bf16[96,768]{1,0:T(8,128)(2,1)S(1)}, u32[]{:S(2)}, u32[]{:S(2)}) collective-permute-start(bf16[96,768]{1,0:T(8,128)(2,1)S(1)} %get-tuple-element.96), channel_id=1, source_target_pairs={{0,3},{1,2},{2,1},{3,0},{4,7},{5,6},{6,5},{7,4},{8,11},{9,10},{10,... | collective-permute-start | bytes 442376 | tf_op jit(solution)/shard_map/ppermute | solution.py:22
  27.9 10.4 %collective-permute-start.10 = (bf16[96,768]{1,0:T(8,128)(2,1)S(1)}, bf16[96,768]{1,0:T(8,128)(2,1)S(1)}, u32[]{:S(2)}, u32[]{:S(2)}) collective-permute-start(bf16[96,768]{1,0:T(8,128)(2,1)S(1)} %slice.108), channel_id=1, source_target_pairs={{0,4},{4,0},{8,12},{12,8},{1,5},{5,1},{9,13},{13,9},{2,6},{6,2},{1... | collective-permute-start | bytes 442376 | tf_op jit(solution)/shard_map/ppermute | solution.py:22
  29.6 8.6 %collective-permute-start.12 = (bf16[96,768]{1,0:T(8,128)(2,1)S(1)}, bf16[96,768]{1,0:T(8,128)(2,1)S(1)}, u32[]{:S(2)}, u32[]{:S(2)}) collective-permute-start(bf16[96,768]{1,0:T(8,128)(2,1)S(1)} %slice.109), channel_id=1, source_target_pairs={{0,8},{4,12},{8,0},{12,4},{1,9},{5,13},{9,1},{13,5},{2,10},{6,14},... | collective-permute-start | bytes 442376 | tf_op jit(solution)/shard_map/ppermute | solution.py:22
  38.3 11.3 %collective-permute-start.14 = (bf16[288,768]{1,0:T(8,128)(2,1)S(1)}, bf16[288,768]{1,0:T(8,128)(2,1)S(1)}, u32[]{:S(2)}, u32[]{:S(2)}) collective-permute-start(bf16[288,768]{1,0:T(8,128)(2,1)S(1)} %constant_dynamic-update-slice_fusion.2.refs_0_), channel_id=1, source_target_pairs={{0,4},{4,0},{8,12},{12,8},{1,5},{5,1},{9,13},{13,9},{2,6},{6,2},{1... | collective-permute-start | bytes 1327112 | tf_op jit(solution)/shard_map/ppermute | solution.py:22
  38.9 10.8 %collective-permute-start.15 = (bf16[288,768]{1,0:T(8,128)(2,1)S(1)}, bf16[288,768]{1,0:T(8,128)(2,1)S(1)}, u32[]{:S(2)}, u32[]{:S(2)}) collective-permute-start(bf16[288,768]{1,0:T(8,128)(2,1)S(1)} %constant_dynamic-update-slice_fusion.2.refs_0_), channel_id=1, source_target_pairs={{0,8},{4,12},{8,0},{12,4},{1,9},{5,13},{9,1},{13,5},{2,10},{6,14},... | collective-permute-start | bytes 1327112 | tf_op jit(solution)/shard_map/ppermute | solution.py:22
  46.7 11.3 %collective-permute-start.13 = (bf16[384,2048]{1,0:T(8,128)(2,1)S(1)}, bf16[384,2048]{1,0:T(8,128)(2,1)S(1)}, u32[]{:S(2)}, u32[]{:S(2)}) collective-permute-start(bf16[384,2048]{1,0:T(8,128)(2,1)S(1)} %get-tuple-element.53), channel_id=1, source_target_pairs={{0,16},{16,0},{1,17},{17,1},{2,18},{18,2},{3,19},{19,3},{4,20},{20... | collective-permute-start | bytes 4718600 | tf_op jit(solution)/shard_map/ppermute | solution.py:22
  56.3 3.5 %collective-permute-start.16 = (bf16[384,2048]{1,0:T(8,128)(2,1)S(1)}, bf16[384,2048]{1,0:T(8,128)(2,1)S(1)}, u32[]{:S(2)}, u32[]{:S(2)}) collective-permute-start(bf16[384,2048]{1,0:T(8,128)(2,1)S(1)} %get-tuple-element.57), channel_id=1, source_target_pairs={{0,16},{16,0},{1,17},{17,1},{2,18},{18,2},{3,19},{19,3},{4,20},{20... | collective-permute-start | bytes 4718600 | tf_op jit(solution)/shard_map/ppermute | solution.py:22
  56.3 13.5 %collective-permute-start.19 = (bf16[288,768]{1,0:T(8,128)(2,1)S(1)}, bf16[288,768]{1,0:T(8,128)(2,1)S(1)}, u32[]{:S(2)}, u32[]{:S(2)}) collective-permute-start(bf16[288,768]{1,0:T(8,128)(2,1)S(1)} %constant_dynamic-update-slice_fusion.2.refs_0_), channel_id=1, source_target_pairs={{0,12},{4,8},{8,4},{12,0},{1,13},{5,9},{9,5},{13,1},{2,14},{6,10},... | collective-permute-start | bytes 1327112 | tf_op jit(solution)/shard_map/ppermute | solution.py:22
  59.7 9.6 %slice-start = ((f32[384]{0:T(512)}), f32[96]{0:T(128)S(1)}, s32[]{:S(2)}) async-start(f32[384]{0:T(512)} %copy-done.3), calls=%async_computation | async-start | bytes 1024 | tf_op jit(solution)/shard_map/slice | solution.py:431
  67.2 9.1 %collective-permute-start.17 = (bf16[192,768]{1,0:T(8,128)(2,1)S(1)}, bf16[192,768]{1,0:T(8,128)(2,1)S(1)}, u32[]{:S(2)}, u32[]{:S(2)}) collective-permute-start(bf16[192,768]{1,0:T(8,128)(2,1)S(1)} %get-tuple-element.59), channel_id=1, source_target_pairs={{0,4},{4,0},{8,12},{12,8},{1,5},{5,1},{9,13},{13,9},{2,6},{6,2},{1... | collective-permute-start | bytes 884744 | tf_op jit(solution)/shard_map/ppermute | solution.py:22
  69.0 8.8 %collective-permute-start.18 = (bf16[192,768]{1,0:T(8,128)(2,1)S(1)}, bf16[192,768]{1,0:T(8,128)(2,1)S(1)}, u32[]{:S(2)}, u32[]{:S(2)}) collective-permute-start(bf16[192,768]{1,0:T(8,128)(2,1)S(1)} %get-tuple-element.60), channel_id=1, source_target_pairs={{0,8},{4,12},{8,0},{12,4},{1,9},{5,13},{9,1},{13,5},{2,10},{6,14},... | collective-permute-start | bytes 884744 | tf_op jit(solution)/shard_map/ppermute | solution.py:22
  74.5 12.6 %collective-permute-start.20 = (bf16[384,1024]{1,0:T(8,128)(2,1)S(1)}, bf16[384,1024]{1,0:T(8,128)(2,1)S(1)}, u32[]{:S(2)}, u32[]{:S(2)}) collective-permute-start(bf16[384,1024]{1,0:T(8,128)(2,1)S(1)} %get-tuple-element.69), channel_id=1, source_target_pairs={{0,16},{16,0},{1,17},{17,1},{2,18},{18,2},{3,19},{19,3},{4,20},{20... | collective-permute-start | bytes 2359304 | tf_op jit(solution)/shard_map/ppermute | solution.py:22
  82.6 4.6 %collective-permute-start.21 = (bf16[384,1024]{1,0:T(8,128)(2,1)S(1)}, bf16[384,1024]{1,0:T(8,128)(2,1)S(1)}, u32[]{:S(2)}, u32[]{:S(2)}) collective-permute-start(bf16[384,1024]{1,0:T(8,128)(2,1)S(1)} %get-tuple-element.63), channel_id=1, source_target_pairs={{0,16},{16,0},{1,17},{17,1},{2,18},{18,2},{3,19},{19,3},{4,20},{20... | collective-permute-start | bytes 2359304 | tf_op jit(solution)/shard_map/ppermute | solution.py:22
  82.7 24.4 %collective-permute-start.24 = (bf16[384,768]{1,0:T(8,128)(2,1)S(1)}, bf16[384,768]{1,0:T(8,128)(2,1)S(1)}, u32[]{:S(2)}, u32[]{:S(2)}) collective-permute-start(bf16[384,768]{1,0:T(8,128)(2,1)S(1)} %get-tuple-element.61), channel_id=1, source_target_pairs={{0,4},{4,0},{8,12},{12,8},{1,5},{5,1},{9,13},{13,9},{2,6},{6,2},{1... | collective-permute-start | bytes 1769480 | tf_op jit(solution)/shard_map/ppermute | solution.py:22
  83.1 24.0 %collective-permute-start.25 = (bf16[384,768]{1,0:T(8,128)(2,1)S(1)}, bf16[384,768]{1,0:T(8,128)(2,1)S(1)}, u32[]{:S(2)}, u32[]{:S(2)}) collective-permute-start(bf16[384,768]{1,0:T(8,128)(2,1)S(1)} %get-tuple-element.77), channel_id=1, source_target_pairs={{0,8},{4,12},{8,0},{12,4},{1,9},{5,13},{9,1},{13,5},{2,10},{6,14},... | collective-permute-start | bytes 1769480 | tf_op jit(solution)/shard_map/ppermute | solution.py:22
  92.8 12.0 %collective-permute-start.22 = (bf16[192,768]{1,0:T(8,128)(2,1)S(1)}, bf16[192,768]{1,0:T(8,128)(2,1)S(1)}, u32[]{:S(2)}, u32[]{:S(2)}) collective-permute-start(bf16[192,768]{1,0:T(8,128)(2,1)S(1)} %get-tuple-element.73), channel_id=1, source_target_pairs={{0,4},{4,0},{8,12},{12,8},{1,5},{5,1},{9,13},{13,9},{2,6},{6,2},{1... | collective-permute-start | bytes 884744 | tf_op jit(solution)/shard_map/ppermute | solution.py:22
  94.6 10.3 %collective-permute-start.23 = (bf16[192,768]{1,0:T(8,128)(2,1)S(1)}, bf16[192,768]{1,0:T(8,128)(2,1)S(1)}, u32[]{:S(2)}, u32[]{:S(2)}) collective-permute-start(bf16[192,768]{1,0:T(8,128)(2,1)S(1)} %get-tuple-element.74), channel_id=1, source_target_pairs={{0,8},{4,12},{8,0},{12,4},{1,9},{5,13},{9,1},{13,5},{2,10},{6,14},... | collective-permute-start | bytes 884744 | tf_op jit(solution)/shard_map/ppermute | solution.py:22
  105.0 14.9 %collective-permute-start.29 = (bf16[384,768]{1,0:T(8,128)(2,1)S(1)}, bf16[384,768]{1,0:T(8,128)(2,1)S(1)}, u32[]{:S(2)}, u32[]{:S(2)}) collective-permute-start(bf16[384,768]{1,0:T(8,128)(2,1)S(1)} %get-tuple-element.75), channel_id=1, source_target_pairs={{0,4},{4,0},{8,12},{12,8},{1,5},{5,1},{9,13},{13,9},{2,6},{6,2},{1... | collective-permute-start | bytes 1769480 | tf_op jit(solution)/shard_map/ppermute | solution.py:22
  106.7 14.3 %collective-permute-start.30 = (bf16[384,768]{1,0:T(8,128)(2,1)S(1)}, bf16[384,768]{1,0:T(8,128)(2,1)S(1)}, u32[]{:S(2)}, u32[]{:S(2)}) collective-permute-start(bf16[384,768]{1,0:T(8,128)(2,1)S(1)} %get-tuple-element.79), channel_id=1, source_target_pairs={{0,8},{4,12},{8,0},{12,4},{1,9},{5,13},{9,1},{13,5},{2,10},{6,14},... | collective-permute-start | bytes 1769480 | tf_op jit(solution)/shard_map/ppermute | solution.py:22
  107.3 15.0 %collective-permute-start.26 = (bf16[96,768]{1,0:T(8,128)(2,1)S(1)}, bf16[96,768]{1,0:T(8,128)(2,1)S(1)}, u32[]{:S(2)}, u32[]{:S(2)}) collective-permute-start(bf16[96,768]{1,0:T(8,128)(2,1)S(1)} %get-tuple-element.94), channel_id=1, source_target_pairs={{0,1},{1,0},{2,3},{3,2},{4,5},{5,4},{6,7},{7,6},{8,9},{9,8},{10,11... | collective-permute-start | bytes 442376 | tf_op jit(solution)/shard_map/ppermute | solution.py:22
  107.4 17.4 %collective-permute-start.27 = (bf16[96,768]{1,0:T(8,128)(2,1)S(1)}, bf16[96,768]{1,0:T(8,128)(2,1)S(1)}, u32[]{:S(2)}, u32[]{:S(2)}) collective-permute-start(bf16[96,768]{1,0:T(8,128)(2,1)S(1)} %get-tuple-element.93), channel_id=1, source_target_pairs={{0,2},{1,3},{2,0},{3,1},{4,6},{5,7},{6,4},{7,5},{8,10},{9,11},{10,... | collective-permute-start | bytes 442376 | tf_op jit(solution)/shard_map/ppermute | solution.py:22
  108.4 16.5 %collective-permute-start.28 = (bf16[96,768]{1,0:T(8,128)(2,1)S(1)}, bf16[96,768]{1,0:T(8,128)(2,1)S(1)}, u32[]{:S(2)}, u32[]{:S(2)}) collective-permute-start(bf16[96,768]{1,0:T(8,128)(2,1)S(1)} %get-tuple-element.92), channel_id=1, source_target_pairs={{0,3},{1,2},{2,1},{3,0},{4,7},{5,6},{6,5},{7,4},{8,11},{9,10},{10,... | collective-permute-start | bytes 442376 | tf_op jit(solution)/shard_map/ppermute | solution.py:22
  121.3 6.8 %collective-permute-start.31 = (bf16[96,768]{1,0:T(8,128)(2,1)S(1)}, bf16[96,768]{1,0:T(8,128)(2,1)S(1)}, u32[]{:S(2)}, u32[]{:S(2)}) collective-permute-start(bf16[96,768]{1,0:T(8,128)(2,1)S(1)} %get-tuple-element.91), channel_id=1, source_target_pairs={{0,1},{1,0},{2,3},{3,2},{4,5},{5,4},{6,7},{7,6},{8,9},{9,8},{10,11... | collective-permute-start | bytes 442376 | tf_op jit(solution)/shard_map/ppermute | solution.py:22
  121.4 11.1 %collective-permute-start.35 = (bf16[96,768]{1,0:T(8,128)(2,1)S(1)}, bf16[96,768]{1,0:T(8,128)(2,1)S(1)}, u32[]{:S(2)}, u32[]{:S(2)}) collective-permute-start(bf16[96,768]{1,0:T(8,128)(2,1)S(1)} %get-tuple-element.90), channel_id=1, source_target_pairs={{0,2},{1,3},{2,0},{3,1},{4,6},{5,7},{6,4},{7,5},{8,10},{9,11},{10,... | collective-permute-start | bytes 442376 | tf_op jit(solution)/shard_map/ppermute | solution.py:22
  122.4 13.4 %collective-permute-start.36 = (bf16[96,768]{1,0:T(8,128)(2,1)S(1)}, bf16[96,768]{1,0:T(8,128)(2,1)S(1)}, u32[]{:S(2)}, u32[]{:S(2)}) collective-permute-start(bf16[96,768]{1,0:T(8,128)(2,1)S(1)} %get-tuple-element.89), channel_id=1, source_target_pairs={{0,3},{1,2},{2,1},{3,0},{4,7},{5,6},{6,5},{7,4},{8,11},{9,10},{10,... | collective-permute-start | bytes 442376 | tf_op jit(solution)/shard_map/ppermute | solution.py:22
  129.0 9.1 %collective-permute-start.32 = (bf16[128,768]{1,0:T(8,128)(2,1)S(1)}, bf16[128,768]{1,0:T(8,128)(2,1)S(1)}, u32[]{:S(2)}, u32[]{:S(2)}) collective-permute-start(bf16[128,768]{1,0:T(8,128)(2,1)S(1)} %get-tuple-element.87.refs_0_), channel_id=1, source_target_pairs={{0,4},{4,0},{8,12},{12,8},{1,5},{5,1},{9,13},{13,9},{2,6},{6,2},{1... | collective-permute-start | bytes 589832 | tf_op jit(solution)/shard_map/ppermute | solution.py:22
  129.6 10.3 %collective-permute-start.33 = (bf16[128,768]{1,0:T(8,128)(2,1)S(1)}, bf16[128,768]{1,0:T(8,128)(2,1)S(1)}, u32[]{:S(2)}, u32[]{:S(2)}) collective-permute-start(bf16[128,768]{1,0:T(8,128)(2,1)S(1)} %get-tuple-element.87.refs_0_), channel_id=1, source_target_pairs={{0,8},{4,12},{8,0},{12,4},{1,9},{5,13},{9,1},{13,5},{2,10},{6,14},... | collective-permute-start | bytes 589832 | tf_op jit(solution)/shard_map/ppermute | solution.py:22
  130.0 17.8 %collective-permute-start.34 = (bf16[128,768]{1,0:T(8,128)(2,1)S(1)}, bf16[128,768]{1,0:T(8,128)(2,1)S(1)}, u32[]{:S(2)}, u32[]{:S(2)}) collective-permute-start(bf16[128,768]{1,0:T(8,128)(2,1)S(1)} %get-tuple-element.87.refs_0_), channel_id=1, source_target_pairs={{0,12},{4,8},{8,4},{12,0},{1,13},{5,9},{9,5},{13,1},{2,14},{6,10},... | collective-permute-start | bytes 589832 | tf_op jit(solution)/shard_map/ppermute | solution.py:22
  136.4 12.4 %collective-permute-start.37 = (bf16[128,768]{1,0:T(8,128)(2,1)S(1)}, bf16[128,768]{1,0:T(8,128)(2,1)S(1)}, u32[]{:S(2)}, u32[]{:S(2)}) collective-permute-start(bf16[128,768]{1,0:T(8,128)(2,1)S(1)} %fusion.4.refs_0_), channel_id=1, source_target_pairs={{0,4},{4,0},{8,12},{12,8},{1,5},{5,1},{9,13},{13,9},{2,6},{6,2},{1... | collective-permute-start | bytes 589832 | tf_op jit(solution)/shard_map/ppermute | solution.py:22
  137.2 11.5 %collective-permute-start.38 = (bf16[128,768]{1,0:T(8,128)(2,1)S(1)}, bf16[128,768]{1,0:T(8,128)(2,1)S(1)}, u32[]{:S(2)}, u32[]{:S(2)}) collective-permute-start(bf16[128,768]{1,0:T(8,128)(2,1)S(1)} %fusion.4.refs_0_), channel_id=1, source_target_pairs={{0,8},{4,12},{8,0},{12,4},{1,9},{5,13},{9,1},{13,5},{2,10},{6,14},... | collective-permute-start | bytes 589832 | tf_op jit(solution)/shard_map/ppermute | solution.py:22
  138.1 10.7 %collective-permute-start.39 = (bf16[128,768]{1,0:T(8,128)(2,1)S(1)}, bf16[128,768]{1,0:T(8,128)(2,1)S(1)}, u32[]{:S(2)}, u32[]{:S(2)}) collective-permute-start(bf16[128,768]{1,0:T(8,128)(2,1)S(1)} %fusion.4.refs_0_), channel_id=1, source_target_pairs={{0,12},{4,8},{8,4},{12,0},{1,13},{5,9},{9,5},{13,1},{2,14},{6,10},... | collective-permute-start | bytes 589832 | tf_op jit(solution)/shard_map/ppermute | solution.py:22
  140.0 1.2 collective-permute-start.40
  141.2 5.1 %collective-permute-start.41 = (f32[2,128]{1,0:T(2,128)S(1)}, f32[2,128]{1,0:T(2,128)S(1)}, u32[]{:S(2)}, u32[]{:S(2)}) collective-permute-start(f32[2,128]{1,0:T(2,128)S(1)} %add.49), channel_id=1, source_target_pairs={{0,4},{4,0},{8,12},{12,8},{1,5},{5,1},{9,13},{13,9},{2,6},{6,2},{1... | collective-permute-start | bytes 3080 | tf_op jit(solution)/shard_map/ppermute | solution.py:22
  146.3 3.6 %collective-permute-start.42 = (f32[2,128]{1,0:T(2,128)S(1)}, f32[2,128]{1,0:T(2,128)S(1)}, u32[]{:S(2)}, u32[]{:S(2)}) collective-permute-start(f32[2,128]{1,0:T(2,128)S(1)} %add.50), channel_id=1, source_target_pairs={{0,8},{4,12},{8,0},{12,4},{1,9},{5,13},{9,1},{13,5},{2,10},{6,14},... | collective-permute-start | bytes 3080 | tf_op jit(solution)/shard_map/ppermute | solution.py:22
  (1 other events, 2.6 us)
